TPU v7x, 32 devices: a whole 2x2x4 slice. The times are simulated.
32 devices in a mesh: fsdp: 32 (over z, y, x, core).
Axes of the slice: x: 2, y: 2, z: 4, core: 2. Of those that a mesh axis runs over, the one named last changes fastest.
Arguments:
- tokens: bfloat16 [12288, 1024], P('fsdp'), may hold values from -6 to 6
- seq_lengths: int32 [96], replicated, may hold values from 0 to 384, as said below
- seq_owner: int32 [96], replicated, may hold values from 0 to 31, as said below
- g_attn: bfloat16 [1024], P('fsdp'), may hold values from 0.099609375 to 1.8984375
- w_query: bfloat16 [1024, 2048], P('fsdp'), may hold values from -0.1875 to 0.1875
- key_projection: bfloat16 [1024, 1024], P('fsdp'), may hold values from -0.1875 to 0.1875
- value_projection: bfloat16 [1024, 1024], P('fsdp'), may hold values from -0.1875 to 0.1875
- query_norm_gain: bfloat16 [128], P('fsdp'), may hold values from 0.099609375 to 1.8984375
- g_key: bfloat16 [128], P('fsdp'), may hold values from 0.099609375 to 1.8984375
- w_out: bfloat16 [2048, 1024], P('fsdp'), may hold values from -0.625 to 0.625
- g_ffn: bfloat16 [1024], P('fsdp'), may hold values from 0.099609375 to 1.8984375
- w_gate: bfloat16 [1024, 3072], P('fsdp'), may hold values from -0.1875 to 0.1875
- w_up: bfloat16 [1024, 3072], P('fsdp'), may hold values from -0.1875 to 0.1875
- w_down: bfloat16 [3072, 1024], P('fsdp'), may hold values from -0.109375 to 0.109375
- cotangent: bfloat16 [12288, 1024], P('fsdp'), may hold values from -6 to 6
Outputs:
- mixed: bfloat16 [12288, 1024], P('fsdp')
- grad_tokens: bfloat16 [12288, 1024], P('fsdp')
- grad_g_attn: float32 [1024], P('fsdp')
- grad_w_query: float32 [1024, 2048], P('fsdp')
- grad_w_key: float32 [1024, 1024], P('fsdp')
- grad_w_value: float32 [1024, 1024], P('fsdp')
- grad_g_query: float32 [128], P('fsdp')
- grad_g_key: float32 [128], P('fsdp')
- grad_w_out: float32 [2048, 1024], P('fsdp')
- grad_g_ffn: float32 [1024], P('fsdp')
- grad_w_gate: float32 [1024, 3072], P('fsdp')
- grad_w_up: float32 [1024, 3072], P('fsdp')
- grad_w_down: float32 [3072, 1024], P('fsdp')
Inputs may be any that keep to these rules, and one draw needn't show every extreme that they name: `seq_lengths`: the slots of each device have lengths that add up to exactly 384; some slot is 384 long. `seq_owner`: every device holds exactly 3 slots.
All inputs are finite; a program needn't handle non-finite values.
Results may differ from a plain program's by a relative error of at most 0.015.
Values may be sent and summed in bfloat16 or wider, within the bound.
No kernel may reach another device: no remote copies, remote signals or barrier semaphores. Data moves between devices by JAX's collectives and lax.ppermute only.
A program may use at most 256 MiB of HBM per device.

v0:
```python
import math

import jax
import jax.numpy as jnp
from jax import lax
from jax.sharding import PartitionSpec as P

QUERY_HEADS = 16
KEY_VALUE_HEADS = 8
HEAD_SIZE = 128


epsilon = 1e-06
rope_base = 1000000.0


def layout(seq_lengths, seq_owner, device, row_total_count):
    seq_index = jnp.arange(seq_lengths.shape[0], dtype=jnp.int32)
    same_owner = seq_owner[:, None] == seq_owner[None, :]
    before = seq_index[None, :] < seq_index[:, None]
    starts = jnp.sum(jnp.where(same_owner & before, seq_lengths[None, :], 0), axis=1)
    places = jnp.arange(row_total_count, dtype=jnp.int32)
    member = (
        (seq_owner[None, :] == device)
        & (starts[None, :] <= places[:, None])
        & (places[:, None] < (starts + seq_lengths)[None, :])
    )
    seq_id = jnp.sum(jnp.where(member, seq_index[None, :], 0), axis=1)
    token_position = jnp.sum(jnp.where(member, places[:, None] - starts[None, :], 0), axis=1)
    return (seq_id, token_position)


def rotation_table(values, token_position, direction):
    half_width = HEAD_SIZE // 2
    frequency = jnp.exp(
        jnp.arange(half_width, dtype=jnp.float32) * (-2.0 * math.log(rope_base) / HEAD_SIZE)
    )
    angles = token_position.astype(jnp.float32)[:, None] * frequency[None, :]
    cosine = jnp.cos(angles)[:, None, :]
    sine_part = jnp.sin(angles)[:, None, :] * direction
    first_half = values[..., :half_width]
    second = values[..., half_width:]
    return jnp.concatenate(
        [first_half * cosine - second * sine_part, second * cosine + first_half * sine_part],
        axis=-1,
    )


def norm_forward(values, gain):
    inverse = lax.rsqrt(jnp.mean(values * values, axis=-1, keepdims=True) + epsilon)
    unit_rows = values * inverse
    return (unit_rows * gain, unit_rows, inverse)


def norm_backward(grad_out, unit_rows, inverse, gain, axes):
    grad_gain = jnp.sum(grad_out * unit_rows, axis=axes)
    scaled = grad_out * gain
    grad_in = inverse * (scaled - unit_rows * jnp.mean(scaled * unit_rows, axis=-1, keepdims=True))
    return (grad_in, grad_gain)


def gather_attention(
    g_attn, w_query, key_projection, value_projection, query_norm_gain, g_key, w_out, g_ffn
):
    return (
        lax.all_gather(g_attn, "fsdp", axis=0, tiled=True),
        lax.all_gather(w_query, "fsdp", axis=0, tiled=True),
        lax.all_gather(key_projection, "fsdp", axis=0, tiled=True),
        lax.all_gather(value_projection, "fsdp", axis=0, tiled=True),
        lax.all_gather(query_norm_gain, "fsdp", axis=0, tiled=True),
        lax.all_gather(g_key, "fsdp", axis=0, tiled=True),
        lax.all_gather(w_out, "fsdp", axis=0, tiled=True),
        lax.all_gather(g_ffn, "fsdp", axis=0, tiled=True),
    )


def gather_ffn(w_gate, w_up, w_down):
    return (
        lax.all_gather(w_gate, "fsdp", axis=0, tiled=True),
        lax.all_gather(w_up, "fsdp", axis=0, tiled=True),
        lax.all_gather(w_down, "fsdp", axis=0, tiled=True),
    )


def head_scores(query_group, key_rows, allowed, score_scale):
    scores = (
        jnp.einsum("qgd,sd->gqs", query_group, key_rows, preferred_element_type=jnp.float32)
        * score_scale
    )
    return jnp.where(allowed[None], scores, -1e30)


def on_device(
    tokens,
    seq_lengths,
    seq_owner,
    g_attn,
    w_query,
    key_projection,
    value_projection,
    query_norm_gain,
    g_key,
    w_out,
    g_ffn,
    w_gate,
    w_up,
    w_down,
    cotangent,
):
    row_total_count = tokens.shape[0]
    query_group_count = QUERY_HEADS // KEY_VALUE_HEADS
    score_scale = 1.0 / math.sqrt(HEAD_SIZE)
    seq_id, token_position = layout(seq_lengths, seq_owner, lax.axis_index("fsdp"), row_total_count)
    places = jnp.arange(row_total_count, dtype=jnp.int32)
    allowed = (seq_id[:, None] == seq_id[None, :]) & (places[None, :] <= places[:, None])
    inputs = tokens.astype(jnp.float32)
    attention_set = gather_attention(
        g_attn, w_query, key_projection, value_projection, query_norm_gain, g_key, w_out, g_ffn
    )
    gain_one = attention_set[0].astype(jnp.float32)
    gain_query = attention_set[4].astype(jnp.float32)
    gain_key = attention_set[5].astype(jnp.float32)
    gain_two = attention_set[7].astype(jnp.float32)
    normed_in, unit_one, inverse_one = norm_forward(inputs, gain_one)
    normed_low = normed_in.astype(jnp.bfloat16)
    query_unnormed = jnp.dot(
        normed_low, attention_set[1], preferred_element_type=jnp.float32
    ).reshape(row_total_count, QUERY_HEADS, HEAD_SIZE)
    key_unnormed = jnp.dot(
        normed_low, attention_set[2], preferred_element_type=jnp.float32
    ).reshape(row_total_count, KEY_VALUE_HEADS, HEAD_SIZE)
    value_low = (
        jnp.dot(normed_low, attention_set[3], preferred_element_type=jnp.float32)
        .astype(jnp.bfloat16)
        .reshape(row_total_count, KEY_VALUE_HEADS, HEAD_SIZE)
    )
    query_normed, unit_query, inverse_query = norm_forward(query_unnormed, gain_query)
    query_matrix = rotation_table(query_normed, token_position, 1.0).astype(jnp.bfloat16)
    key_normed, unit_key, inverse_key = norm_forward(key_unnormed, gain_key)
    keys = rotation_table(key_normed, token_position, 1.0).astype(jnp.bfloat16)
    head_outputs = []
    log_totals = []
    for shared_key_head in range(KEY_VALUE_HEADS):
        query_group = query_matrix[
            :, shared_key_head * query_group_count : (shared_key_head + 1) * query_group_count, :
        ]
        scores = head_scores(query_group, keys[:, shared_key_head, :], allowed, score_scale)
        row_max = jnp.max(scores, axis=-1, keepdims=True)
        log_total = row_max + jnp.log(jnp.sum(jnp.exp(scores - row_max), axis=-1, keepdims=True))
        probs_low = jnp.exp(scores - log_total).astype(jnp.bfloat16)
        head_outputs.append(
            jnp.einsum(
                "gqs,sd->qgd",
                probs_low,
                value_low[:, shared_key_head, :],
                preferred_element_type=jnp.float32,
            )
        )
        log_totals.append(log_total)
    attended = (
        jnp.concatenate(head_outputs, axis=1)
        .reshape(row_total_count, QUERY_HEADS * HEAD_SIZE)
        .astype(jnp.bfloat16)
    )
    residual = inputs + jnp.dot(attended, attention_set[6], preferred_element_type=jnp.float32)
    ffn_set = gather_ffn(w_gate, w_up, w_down)
    normed_mid, unit_two, inverse_two = norm_forward(residual, gain_two)
    normed_two = normed_mid.astype(jnp.bfloat16)
    gate_rows = jnp.dot(normed_two, ffn_set[0], preferred_element_type=jnp.float32)
    up_rows = jnp.dot(normed_two, ffn_set[1], preferred_element_type=jnp.float32)
    sigmoid_gate = jax.nn.sigmoid(gate_rows)
    silu_gate = gate_rows * sigmoid_gate
    hidden = (silu_gate * up_rows).astype(jnp.bfloat16)
    ffn_rows = jnp.dot(hidden, ffn_set[2], preferred_element_type=jnp.float32)
    mixed = (residual + ffn_rows).astype(jnp.bfloat16)
    back_ffn = gather_ffn(w_gate, w_up, w_down)
    back_set = gather_attention(
        g_attn, w_query, key_projection, value_projection, query_norm_gain, g_key, w_out, g_ffn
    )
    grad_out = cotangent.astype(jnp.float32)
    grad_w_down = jnp.einsum("rf,rd->fd", hidden, cotangent, preferred_element_type=jnp.float32)
    grad_hidden = jnp.einsum(
        "rd,fd->rf", cotangent, back_ffn[2], preferred_element_type=jnp.float32
    )
    grad_gate = (
        grad_hidden * up_rows * sigmoid_gate * (1.0 + gate_rows * (1.0 - sigmoid_gate))
    ).astype(jnp.bfloat16)
    grad_up = (grad_hidden * silu_gate).astype(jnp.bfloat16)
    grad_w_gate = jnp.einsum("rd,rf->df", normed_two, grad_gate, preferred_element_type=jnp.float32)
    grad_w_up = jnp.einsum("rd,rf->df", normed_two, grad_up, preferred_element_type=jnp.float32)
    grad_normed_two = jnp.einsum(
        "rf,df->rd", grad_gate, back_ffn[0], preferred_element_type=jnp.float32
    )
    grad_normed_two = grad_normed_two + jnp.einsum(
        "rf,df->rd", grad_up, back_ffn[1], preferred_element_type=jnp.float32
    )
    grad_mid, grad_gain_two = norm_backward(grad_normed_two, unit_two, inverse_two, gain_two, (0,))
    ffn_grads = (
        lax.psum_scatter(grad_gain_two, "fsdp", scatter_dimension=0, tiled=True),
        lax.psum_scatter(grad_w_gate, "fsdp", scatter_dimension=0, tiled=True),
        lax.psum_scatter(grad_w_up, "fsdp", scatter_dimension=0, tiled=True),
        lax.psum_scatter(grad_w_down, "fsdp", scatter_dimension=0, tiled=True),
    )
    grad_residual = grad_out + grad_mid
    grad_res_low = grad_residual.astype(jnp.bfloat16)
    query_weight = back_set[1]
    key_weight = back_set[2]
    value_weight = back_set[3]
    out_weight = back_set[6]
    grad_w_out = jnp.einsum("ra,rd->ad", attended, grad_res_low, preferred_element_type=jnp.float32)
    grad_attended = jnp.einsum(
        "rd,ad->ra", grad_res_low, out_weight, preferred_element_type=jnp.float32
    )
    grad_attended = grad_attended.astype(jnp.bfloat16).reshape(
        row_total_count, QUERY_HEADS, HEAD_SIZE
    )
    grad_query_parts = []
    grad_key_parts = []
    value_gradient_pieces = []
    for shared_key_head in range(KEY_VALUE_HEADS):
        query_group = query_matrix[
            :, shared_key_head * query_group_count : (shared_key_head + 1) * query_group_count, :
        ]
        key_rows = keys[:, shared_key_head, :]
        scores = head_scores(query_group, key_rows, allowed, score_scale)
        probs = jnp.exp(scores - log_totals[shared_key_head])
        probs_low = probs.astype(jnp.bfloat16)
        grad_heads = grad_attended[
            :, shared_key_head * query_group_count : (shared_key_head + 1) * query_group_count, :
        ]
        grad_probs = jnp.einsum(
            "qgd,sd->gqs",
            grad_heads,
            value_low[:, shared_key_head, :],
            preferred_element_type=jnp.float32,
        )
        value_gradient_pieces.append(
            jnp.einsum("gqs,qgd->sd", probs_low, grad_heads, preferred_element_type=jnp.float32)
        )
        inner_sum = jnp.sum(probs * grad_probs, axis=-1, keepdims=True)
        grad_scores = (probs * (grad_probs - inner_sum)).astype(jnp.bfloat16)
        grad_query_parts.append(
            jnp.einsum("gqs,sd->qgd", grad_scores, key_rows, preferred_element_type=jnp.float32)
            * score_scale
        )
        grad_key_parts.append(
            jnp.einsum("gqs,qgd->sd", grad_scores, query_group, preferred_element_type=jnp.float32)
            * score_scale
        )
    grad_queries = jnp.concatenate(grad_query_parts, axis=1)
    grad_keys = jnp.stack(grad_key_parts, axis=1)
    grad_value_low = (
        jnp.stack(value_gradient_pieces, axis=1)
        .reshape(row_total_count, KEY_VALUE_HEADS * HEAD_SIZE)
        .astype(jnp.bfloat16)
    )
    grad_query_raw, grad_gain_query = norm_backward(
        rotation_table(grad_queries, token_position, -1.0),
        unit_query,
        inverse_query,
        gain_query,
        (0, 1),
    )
    key_gradient_unnormed, grad_gain_key = norm_backward(
        rotation_table(grad_keys, token_position, -1.0), unit_key, inverse_key, gain_key, (0, 1)
    )
    grad_query_low = grad_query_raw.reshape(row_total_count, QUERY_HEADS * HEAD_SIZE).astype(
        jnp.bfloat16
    )
    key_gradient_lowered = key_gradient_unnormed.reshape(
        row_total_count, KEY_VALUE_HEADS * HEAD_SIZE
    ).astype(jnp.bfloat16)
    grad_w_query = jnp.einsum(
        "rd,ra->da", normed_low, grad_query_low, preferred_element_type=jnp.float32
    )
    grad_w_key = jnp.einsum(
        "rd,ra->da", normed_low, key_gradient_lowered, preferred_element_type=jnp.float32
    )
    grad_w_value = jnp.einsum(
        "rd,ra->da", normed_low, grad_value_low, preferred_element_type=jnp.float32
    )
    grad_normed = jnp.einsum(
        "ra,da->rd", grad_query_low, query_weight, preferred_element_type=jnp.float32
    )
    grad_normed = grad_normed + jnp.einsum(
        "ra,da->rd", key_gradient_lowered, key_weight, preferred_element_type=jnp.float32
    )
    grad_normed = grad_normed + jnp.einsum(
        "ra,da->rd", grad_value_low, value_weight, preferred_element_type=jnp.float32
    )
    grad_first, grad_gain_one = norm_backward(grad_normed, unit_one, inverse_one, gain_one, (0,))
    grad_tokens = (grad_residual + grad_first).astype(jnp.bfloat16)
    attention_grads = (
        lax.psum_scatter(grad_gain_one, "fsdp", scatter_dimension=0, tiled=True),
        lax.psum_scatter(grad_w_query, "fsdp", scatter_dimension=0, tiled=True),
        lax.psum_scatter(grad_w_key, "fsdp", scatter_dimension=0, tiled=True),
        lax.psum_scatter(grad_w_value, "fsdp", scatter_dimension=0, tiled=True),
        lax.psum_scatter(grad_gain_query, "fsdp", scatter_dimension=0, tiled=True),
        lax.psum_scatter(grad_gain_key, "fsdp", scatter_dimension=0, tiled=True),
        lax.psum_scatter(grad_w_out, "fsdp", scatter_dimension=0, tiled=True),
    )
    return (
        mixed,
        grad_tokens,
        attention_grads[0],
        attention_grads[1],
        attention_grads[2],
        attention_grads[3],
        attention_grads[4],
        attention_grads[5],
        attention_grads[6],
        ffn_grads[0],
        ffn_grads[1],
        ffn_grads[2],
        ffn_grads[3],
    )


def solution(mesh):
    return jax.shard_map(
        on_device,
        mesh=mesh,
        in_specs=(
            P("fsdp", None),
            P(),
            P(),
            P("fsdp"),
            P("fsdp", None),
            P("fsdp", None),
            P("fsdp", None),
            P("fsdp"),
            P("fsdp"),
            P("fsdp", None),
            P("fsdp"),
            P("fsdp", None),
            P("fsdp", None),
            P("fsdp", None),
            P("fsdp", None),
        ),
        out_specs=(
            P("fsdp", None),
            P("fsdp", None),
            P("fsdp"),
            P("fsdp", None),
            P("fsdp", None),
            P("fsdp", None),
            P("fsdp"),
            P("fsdp"),
            P("fsdp", None),
            P("fsdp"),
            P("fsdp", None),
            P("fsdp", None),
            P("fsdp", None),
        ),
        check_vma=False,
    )
```

profile of v0, /device:TPU:0, one launch (start us, length us, event | category | flops | bytes accessed | tf_op | source)
XLA Modules:
  0.0 1582.2 jit_solution(5710588042076673058)
XLA Ops:
  15.4 42.3 %all-reduce.9 = (bf16[1024]{0:T(1024)(128)(2,1)S(1)}, bf16[128]{0:T(256)(128)(2,1)S(1)}, bf16[128]{0:T(256)(128)(2,1)S(1)}, bf16[1024]{0:T(1024)(128)(2,1)S(1)}) all-reduce(bf16[1024]{0:T(1024)(128)(2,1)S(1)} %dynamic-update-slice, bf16[128]{0:T(256)(128)(2,1)S(1)} %dynamic-update-slice.1, ...), channel_id=1, replica_groups=mesh['fsdp'=32] {'fsdp'}, use_global_device_ids=true, to_apply=%add | all-reduce | flops 2304 | bytes 9216
  61.1 9.0 all-gather.10.cloned.1.call-done
  70.0 2.6 fusion.234
  73.6 54.7 %all-gather.8.cloned.1.call-done = bf16[1024,1024]{1,0:T(8,128)(2,1)} async-done(((bf16[32,1024]{1,0:T(8,128)(2,1)}), bf16[1024,1024]{1,0:T(8,128)(2,1)}) %all-gather.8.cloned.1.call-update) | async-done | bytes 2097168 | tf_op jit(solution)/shard_map/all_gather | solution.py:69
  128.2 3.5 convolution_convert_fusion.1
  131.7 2.3 copy.662
  137.8 54.2 %all-gather.12.cloned.1.call-done = bf16[1024,2048]{1,0:T(8,128)(2,1)} async-done(((bf16[32,2048]{1,0:T(8,128)(2,1)}), bf16[1024,2048]{1,0:T(8,128)(2,1)}) %all-gather.12.cloned.1.call-update) | async-done | bytes 4194320 | tf_op jit(solution)/shard_map/all_gather | solution.py:67
  192.0 4.3 fusion.232
  197.0 1.6 multiply_reduce_fusion.1
  198.5 1.6 copy.455
  219.3 36.1 %all-gather.14.cloned.1.call-done = bf16[2048,1024]{1,0:T(8,128)(2,1)} async-done(((bf16[64,1024]{1,0:T(8,128)(2,1)}), bf16[2048,1024]{1,0:T(8,128)(2,1)}) %all-gather.14.cloned.1.call-update) | async-done | bytes 4194320 | tf_op jit(solution)/shard_map/all_gather | solution.py:72
  255.3 4.7 multiply_reduce_fusion.5
  262.4 63.8 %all-gather.16.cloned.1.call-done = bf16[1024,3072]{1,0:T(8,128)(2,1)} async-done(((bf16[32,3072]{1,0:T(8,128)(2,1)}), bf16[1024,3072]{1,0:T(8,128)(2,1)}) %all-gather.16.cloned.1.call-update) | async-done | bytes 6291472 | tf_op jit(solution)/shard_map/all_gather | solution.py:79
  326.1 7.7 fusion.246
  333.9 63.0 %all-gather.18.cloned.1.call-done = bf16[1024,3072]{1,0:T(8,128)(2,1)} async-done(((bf16[32,3072]{1,0:T(8,128)(2,1)}), bf16[1024,3072]{1,0:T(8,128)(2,1)}) %all-gather.18.cloned.1.call-update) | async-done | bytes 6291472 | tf_op jit(solution)/shard_map/all_gather | solution.py:80
  396.9 8.0 fusion.247
  404.9 62.9 %all-gather.20.cloned.1.call-done = bf16[3072,1024]{1,0:T(8,128)(2,1)} async-done(((bf16[96,1024]{1,0:T(8,128)(2,1)}), bf16[3072,1024]{1,0:T(8,128)(2,1)}) %all-gather.20.cloned.1.call-update) | async-done | bytes 6291472 | tf_op jit(solution)/shard_map/all_gather | solution.py:81
  467.8 9.6 multiply_convert_fusion
  477.5 6.5 fusion.248
  484.3 3.0 multiply_reduce_fusion.2
  487.7 1.7 copy-done.104
  489.5 1.9 fusion.22
  511.2 2.3 fusion.130
  516.2 3.4 fusion.228
  519.7 1.8 fusion.119
  527.4 3.5 fusion.226
  541.7 4.0 fusion.120
  546.5 1.8 mul.698
  550.3 3.5 fusion.4
  554.9 5.7 fusion.230
  562.5 6.4 fusion.251
  569.1 1.6 copy-done.73
  570.6 6.5 fusion.252
  578.5 7.1 fusion.131
  586.7 8.2 fusion.253
  596.0 2.7 fusion.250
  598.8 4.2 fusion.249
  603.0 2.5 fusion.16
  605.5 39.6 %all-reduce.8 = (f32[1024]{0:T(1024)S(1)}, f32[128]{0:T(128)S(1)}, f32[128]{0:T(128)S(1)}, f32[1024]{0:T(1024)S(1)}) all-reduce(f32[1024]{0:T(1024)S(1)} %get-tuple-element.15, f32[128]{0:T(128)S(1)} %bitcast_reduce_fusion, f32[128]{0:T(128)S(1)} %bitcast_reduce_fusion.1, ...), channel_id=2, replica_groups=mesh['fsdp'=32] {'fsdp'}, use_global_device_ids=true, to_apply=%region_36.37.clone | all-reduce | flops 2304 | bytes 18432
  647.4 2.9 fusion.15
  650.3 6.4 add_convert_fusion.1
  656.7 2.4 reduce-scatter.10.cloned.1.call-done
  659.1 139.9 %reduce-scatter.12.cloned.1.call-done = f32[32,1024]{1,0:T(8,128)} async-done(((f32[1024,1024]{1,0:T(8,128)}), f32[32,1024]{1,0:T(8,128)}) %reduce-scatter.12.cloned.1.call-update) | async-done | bytes 131088 | tf_op jit(solution)/shard_map/reduce_scatter | solution.py:297
  799.0 147.4 %reduce-scatter.8.cloned.1.call-done = f32[32,2048]{1,0:T(8,128)} async-done(((f32[1024,2048]{1,0:T(8,128)}), f32[32,2048]{1,0:T(8,128)}) %reduce-scatter.8.cloned.1.call-update) | async-done | bytes 262160 | tf_op jit(solution)/shard_map/reduce_scatter | solution.py:295
  946.3 157.9 %reduce-scatter.16.cloned.1.call-done = f32[32,3072]{1,0:T(8,128)} async-done(((f32[1024,3072]{1,0:T(8,128)}), f32[32,3072]{1,0:T(8,128)}) %reduce-scatter.16.cloned.1.call-update) | async-done | bytes 393232 | tf_op jit(solution)/shard_map/reduce_scatter | solution.py:200
  1104.3 162.4 %reduce-scatter.18.cloned.1.call-done = f32[32,3072]{1,0:T(8,128)} async-done(((f32[1024,3072]{1,0:T(8,128)}), f32[32,3072]{1,0:T(8,128)}) %reduce-scatter.18.cloned.1.call-update) | async-done | bytes 393232 | tf_op jit(solution)/shard_map/reduce_scatter | solution.py:201
  1266.7 150.8 %reduce-scatter.14.cloned.1.call-done = f32[64,1024]{1,0:T(8,128)} async-done(((f32[2048,1024]{1,0:T(8,128)}), f32[64,1024]{1,0:T(8,128)}) %reduce-scatter.14.cloned.1.call-update) | async-done | bytes 262160 | tf_op jit(solution)/shard_map/reduce_scatter | solution.py:300
  1417.4 158.1 %reduce-scatter.20.cloned.1.call-done = f32[96,1024]{1,0:T(8,128)} async-done(((f32[3072,1024]{1,0:T(8,128)}), f32[96,1024]{1,0:T(8,128)}) %reduce-scatter.20.cloned.1.call-update) | async-done | bytes 393232 | tf_op jit(solution)/shard_map/reduce_scatter | solution.py:202
  (368 shorter events, 89.1 us)
Async XLA Ops:
  7.2 62.8 %copy-start.8 = (bf16[384,1024]{1,0:T(8,128)(2,1)S(1)}, bf16[384,1024]{1,0:T(8,128)(2,1)}, u32[]{:S(2)}) copy-start(bf16[384,1024]{1,0:T(8,128)(2,1)} %param.15) | copy-start | bytes 2359300
  7.2 51.9 %copy-start.101 = (s32[96]{0:T(128)S(1)}, s32[96]{0:T(128)}, u32[]{:S(2)}) copy-start(s32[96]{0:T(128)} %param.17) | copy-start | bytes 1156
  7.2 51.9 %copy-start.102 = (s32[96]{0:T(128)S(1)}, s32[96]{0:T(128)}, u32[]{:S(2)}) copy-start(s32[96]{0:T(128)} %param.16) | copy-start | bytes 1156
  7.2 62.8 %all-gather.10.cloned.1.call-start = ((), (), s32[]{:S(2)}) async-start(), calls=%async_computation.8 | async-start | bytes 2162688 | tf_op jit(solution)/shard_map/all_gather | solution.py:68
  7.9 120.3 %all-gather.8.cloned.1.call-start = ((), (), s32[]{:S(2)}) async-start(), calls=%async_computation.7 | async-start | bytes 2162688 | tf_op jit(solution)/shard_map/all_gather | solution.py:69
  8.7 183.3 %all-gather.12.cloned.1.call-start = ((), (), s32[]{:S(2)}) async-start(), calls=%async_computation.9 | async-start | bytes 4325376 | tf_op jit(solution)/shard_map/all_gather | solution.py:67
  9.4 245.9 %all-gather.14.cloned.1.call-start = ((), (), s32[]{:S(2)}) async-start(), calls=%async_computation.10 | async-start | bytes 4325376 | tf_op jit(solution)/shard_map/all_gather | solution.py:72
  10.0 316.1 %all-gather.16.cloned.1.call-start = ((), (), s32[]{:S(2)}) async-start(), calls=%async_computation.11 | async-start | bytes 6488064 | tf_op jit(solution)/shard_map/all_gather | solution.py:79
  10.6 386.3 %all-gather.18.cloned.1.call-start = ((), (), s32[]{:S(2)}) async-start(), calls=%async_computation.12 | async-start | bytes 6488064 | tf_op jit(solution)/shard_map/all_gather | solution.py:80
  11.2 456.7 %all-gather.20.cloned.1.call-start = ((), (), s32[]{:S(2)}) async-start(), calls=%async_computation.13 | async-start | bytes 6488064 | tf_op jit(solution)/shard_map/all_gather | solution.py:81
  11.9 647.1 %reduce-scatter.10.cloned.1.call-start = ((), (), s32[]{:S(2)}) async-start(), calls=%async_computation.15 | async-start | bytes 4325376 | tf_op jit(solution)/shard_map/reduce_scatter | solution.py:296
  61.1 74.2 %copy-start.93 = (f32[384,64]{1,0:T(8,128)}, f32[384,64]{1,0:T(8,128)S(1)}, u32[]{:S(2)}) copy-start(f32[384,64]{1,0:T(8,128)S(1)} %get-tuple-element.55) | copy-start | bytes 294916
  72.6 62.2 %copy-start.35 = (f32[384,1024]{1,0:T(8,128)}, f32[384,1024]{1,0:T(8,128)S(1)}, u32[]{:S(2)}) copy-start(f32[384,1024]{1,0:T(8,128)S(1)} %fusion.234) | copy-start | bytes 4718596
  196.3 4.6 copy-start.6
  204.8 13.5 copy-start.12
  206.5 10.8 copy-start.15
  207.1 9.2 copy-start.18
  207.8 7.5 copy-start.21
  208.4 5.8 copy-start.24
  209.0 4.2 copy-start.27
  210.3 2.9 copy-start.33
  477.4 6.5 copy-start.74
  477.4 6.5 copy-start.72
  477.4 6.5 copy-start.44
  477.5 6.8 copy-start.103
  484.3 3.0 copy-start.69
  493.0 3.3 copy-start.87
  493.0 3.8 copy-start.85
  493.0 5.0 copy-start.83
  493.1 5.5 copy-start.81
  493.1 6.7 copy-start.79
  493.1 7.2 copy-start.77
  516.1 3.4 copy-start.67
  519.6 3.3 copy-start.29
  519.6 279.4 %reduce-scatter.12.cloned.1.call-start = ((), (), s32[]{:S(2)}) async-start(), calls=%async_computation.16 | async-start | bytes 4325376 | tf_op jit(solution)/shard_map/reduce_scatter | solution.py:297
  519.6 3.2 copy-start.88
  530.9 415.4 %reduce-scatter.8.cloned.1.call-start = ((), (), s32[]{:S(2)}) async-start(), calls=%async_computation.14 | async-start | bytes 8650752 | tf_op jit(solution)/shard_map/reduce_scatter | solution.py:295
  550.3 4.7 copy-start.10
  560.6 543.6 %reduce-scatter.16.cloned.1.call-start = ((), (), s32[]{:S(2)}) async-start(), calls=%async_computation.18 | async-start | bytes 12976128 | tf_op jit(solution)/shard_map/reduce_scatter | solution.py:200
  569.0 697.6 %reduce-scatter.18.cloned.1.call-start = ((), (), s32[]{:S(2)}) async-start(), calls=%async_computation.19 | async-start | bytes 12976128 | tf_op jit(solution)/shard_map/reduce_scatter | solution.py:201
  577.2 840.2 %reduce-scatter.14.cloned.1.call-start = ((), (), s32[]{:S(2)}) async-start(), calls=%async_computation.17 | async-start | bytes 8650752 | tf_op jit(solution)/shard_map/reduce_scatter | solution.py:300
  585.6 989.8 %reduce-scatter.20.cloned.1.call-start = ((), (), s32[]{:S(2)}) async-start(), calls=%async_computation.20 | async-start | bytes 12976128 | tf_op jit(solution)/shard_map/reduce_scatter | solution.py:202
  596.0 2.7 copy-start.47
  598.8 4.2 copy-start.11
  598.8 4.2 copy-start.66
  598.8 4.2 copy-start.76
  647.4 2.9 copy-start.45
  647.4 2.9 copy-start.71
  (71 other events, 94.1 us)
Sparse Core Ops, SparseCore 0:
  10.9 59.0 all-gather.9
  72.9 55.2 all-gather.7
  131.1 60.8 all-gather.11
  194.7 60.5 all-gather.13
  258.0 68.0 all-gather.15
  328.9 68.0 all-gather.17
  399.8 68.0 all-gather.19
  519.7 139.3 reduce-scatter.9
  661.9 137.0 reduce-scatter.11
  801.7 144.5 reduce-scatter.7
  952.9 151.2 reduce-scatter.15
  1111.7 154.8 reduce-scatter.17
  1269.5 147.8 reduce-scatter.13
  1423.9 151.5 reduce-scatter.19
where the time goes:
time: 1590 us; the launch traced here: 1580 us
  waiting for transfers between devices  1270 us (80%)
  matrix products  135 us (8%)
  blocking collectives  81.9 us (5%)
  local copies, waits for them, and re-layouts  50.1 us (3%)
  other arithmetic  31.9 us (2%)
    reduce_scatter x1, waiting for transfers between devices, on_device(): lax.psum_scatter(grad_w_up, 'fsdp', scatter_dimension=0, tiled=True)  162 us
    reduce_scatter x1, waiting for transfers between devices, on_device(): lax.psum_scatter(grad_w_down, 'fsdp', scatter_dimension=0, tiled=True)  158 us
    reduce_scatter x1, waiting for transfers between devices, on_device(): lax.psum_scatter(grad_w_gate, 'fsdp', scatter_dimension=0, tiled=True)  158 us
    reduce_scatter x1, waiting for transfers between devices, on_device(): lax.psum_scatter(grad_w_out, 'fsdp', scatter_dimension=0, tiled=True)  151 us
    reduce_scatter x1, waiting for transfers between devices, on_device(): lax.psum_scatter(grad_w_query, 'fsdp', scatter_dimension=0, tiled=True)  147 us
    reduce_scatter x1, waiting for transfers between devices, on_device(): lax.psum_scatter(grad_w_value, 'fsdp', scatter_dimension=0, tiled=True)  140 us
    unnamed x2, blocking collectives  81.9 us
    all_gather x1, waiting for transfers between devices, gather_ffn(): lax.all_gather(w_gate, 'fsdp', axis=0, tiled=True)  63.8 us
  transfers between devices with their start and end apart: 14, of which 14 were waited for; matrix products, arithmetic and copies ran while one was open for 9% of the time, Pallas kernels for 0%

commit v1 on v0

--- a/solution.py
+++ b/solution.py
@@ -59,27 +59,37 @@
     return (grad_in, grad_gain)
 
 
-def gather_attention(
-    g_attn, w_query, key_projection, value_projection, query_norm_gain, g_key, w_out, g_ffn
-):
-    return (
-        lax.all_gather(g_attn, "fsdp", axis=0, tiled=True),
-        lax.all_gather(w_query, "fsdp", axis=0, tiled=True),
-        lax.all_gather(key_projection, "fsdp", axis=0, tiled=True),
-        lax.all_gather(value_projection, "fsdp", axis=0, tiled=True),
-        lax.all_gather(query_norm_gain, "fsdp", axis=0, tiled=True),
-        lax.all_gather(g_key, "fsdp", axis=0, tiled=True),
-        lax.all_gather(w_out, "fsdp", axis=0, tiled=True),
-        lax.all_gather(g_ffn, "fsdp", axis=0, tiled=True),
-    )
-
-
-def gather_ffn(w_gate, w_up, w_down):
-    return (
-        lax.all_gather(w_gate, "fsdp", axis=0, tiled=True),
-        lax.all_gather(w_up, "fsdp", axis=0, tiled=True),
-        lax.all_gather(w_down, "fsdp", axis=0, tiled=True),
-    )
+def exchange(values, count, mask):
+    return lax.ppermute(values, "fsdp", [(source, source ^ mask) for source in range(count)])
+
+
+def scatter_sum(grad, device, count, flip):
+    bits = count.bit_length() - 1
+    columns = grad.shape[1]
+    held = grad.astype(jnp.bfloat16).reshape((4,) + (2,) * (bits - 2) + (grad.shape[0] // count, columns))
+    middle = list(range(1, bits - 2))
+    if flip:
+        middle = middle[::-1]
+    left = list(range(bits - 3, -1, -1))
+    for bit in [0] + middle:
+        axis = 1 + left.index(bit)
+        left.remove(bit)
+        mine = (device >> bit) & 1
+        sent = lax.dynamic_index_in_dim(held, 1 - mine, axis, keepdims=False)
+        kept = lax.dynamic_index_in_dim(held, mine, axis, keepdims=False)
+        came = exchange(sent, count, 1 << bit)
+        held = (kept.astype(jnp.float32) + came.astype(jnp.float32)).astype(jnp.bfloat16)
+    top = device >> (bits - 2)
+    total = lax.dynamic_index_in_dim(held, top, 0, keepdims=False).astype(jnp.float32)
+    for step in (1, 2, 3):
+        sent = lax.dynamic_index_in_dim(held, top ^ step, 0, keepdims=False)
+        total = total + exchange(sent, count, step << (bits - 2)).astype(jnp.float32)
+    return total
+
+
+def gain_columns(first, second, third, fourth, rows):
+    columns = [jnp.pad(v, (0, rows - v.shape[0]))[:, None] for v in (first, second, third, fourth)]
+    return jnp.pad(jnp.concatenate(columns, axis=1), ((0, 0), (0, 124)))
 
 
 def head_scores(query_group, key_rows, allowed, score_scale):
@@ -114,25 +124,35 @@
     places = jnp.arange(row_total_count, dtype=jnp.int32)
     allowed = (seq_id[:, None] == seq_id[None, :]) & (places[None, :] <= places[:, None])
     inputs = tokens.astype(jnp.float32)
-    attention_set = gather_attention(
-        g_attn, w_query, key_projection, value_projection, query_norm_gain, g_key, w_out, g_ffn
-    )
-    gain_one = attention_set[0].astype(jnp.float32)
-    gain_query = attention_set[4].astype(jnp.float32)
-    gain_key = attention_set[5].astype(jnp.float32)
-    gain_two = attention_set[7].astype(jnp.float32)
+    count = lax.axis_size("fsdp")
+    device = lax.axis_index("fsdp")
+    shard = g_attn.shape[0]
+    head_shard = query_norm_gain.shape[0]
+    gains = gain_columns(g_attn, g_ffn, query_norm_gain, g_key, shard)
+    projections = lax.all_gather(
+        jnp.concatenate([w_query, key_projection, value_projection, gains], axis=1), "fsdp", axis=0, tiled=True
+    )
+    back_rows = lax.all_gather(jnp.concatenate([w_out, w_down], axis=0), "fsdp", axis=0, tiled=False)
+    gate_up = lax.all_gather(jnp.concatenate([w_gate, w_up], axis=1), "fsdp", axis=0, tiled=True)
+    out_rows = w_out.shape[0]
+    out_weight = back_rows[:, :out_rows].reshape(count * out_rows, -1)
+    down_weight = back_rows[:, out_rows:].reshape(count * w_down.shape[0], -1)
+    query_width = w_query.shape[1]
+    key_width = key_projection.shape[1]
+    qkv_width = query_width + 2 * key_width
+    gain_block = projections[:, qkv_width:].astype(jnp.float32)
+    gain_one = gain_block[:, 0]
+    gain_two = gain_block[:, 1]
+    head_gains = gain_block.reshape(count, shard, 128)[:, :head_shard, 2:4]
+    gain_query = head_gains[..., 0].reshape(-1)
+    gain_key = head_gains[..., 1].reshape(-1)
     normed_in, unit_one, inverse_one = norm_forward(inputs, gain_one)
     normed_low = normed_in.astype(jnp.bfloat16)
-    query_unnormed = jnp.dot(
-        normed_low, attention_set[1], preferred_element_type=jnp.float32
-    ).reshape(row_total_count, QUERY_HEADS, HEAD_SIZE)
-    key_unnormed = jnp.dot(
-        normed_low, attention_set[2], preferred_element_type=jnp.float32
-    ).reshape(row_total_count, KEY_VALUE_HEADS, HEAD_SIZE)
+    raw = jnp.dot(normed_low, projections[:, :qkv_width], preferred_element_type=jnp.float32)
+    query_unnormed = raw[:, :query_width].reshape(row_total_count, QUERY_HEADS, HEAD_SIZE)
+    key_unnormed = raw[:, query_width : query_width + key_width].reshape(row_total_count, KEY_VALUE_HEADS, HEAD_SIZE)
     value_low = (
-        jnp.dot(normed_low, attention_set[3], preferred_element_type=jnp.float32)
-        .astype(jnp.bfloat16)
-        .reshape(row_total_count, KEY_VALUE_HEADS, HEAD_SIZE)
+        raw[:, query_width + key_width :].astype(jnp.bfloat16).reshape(row_total_count, KEY_VALUE_HEADS, HEAD_SIZE)
     )
     query_normed, unit_query, inverse_query = norm_forward(query_unnormed, gain_query)
     query_matrix = rotation_table(query_normed, token_position, 1.0).astype(jnp.bfloat16)
@@ -162,51 +182,36 @@
         .reshape(row_total_count, QUERY_HEADS * HEAD_SIZE)
         .astype(jnp.bfloat16)
     )
-    residual = inputs + jnp.dot(attended, attention_set[6], preferred_element_type=jnp.float32)
-    ffn_set = gather_ffn(w_gate, w_up, w_down)
+    residual = inputs + jnp.dot(attended, out_weight, preferred_element_type=jnp.float32)
     normed_mid, unit_two, inverse_two = norm_forward(residual, gain_two)
     normed_two = normed_mid.astype(jnp.bfloat16)
-    gate_rows = jnp.dot(normed_two, ffn_set[0], preferred_element_type=jnp.float32)
-    up_rows = jnp.dot(normed_two, ffn_set[1], preferred_element_type=jnp.float32)
+    hidden_width = w_gate.shape[1]
+    both_rows = jnp.dot(normed_two, gate_up, preferred_element_type=jnp.float32)
+    gate_rows = both_rows[:, :hidden_width]
+    up_rows = both_rows[:, hidden_width:]
     sigmoid_gate = jax.nn.sigmoid(gate_rows)
     silu_gate = gate_rows * sigmoid_gate
     hidden = (silu_gate * up_rows).astype(jnp.bfloat16)
-    ffn_rows = jnp.dot(hidden, ffn_set[2], preferred_element_type=jnp.float32)
+    ffn_rows = jnp.dot(hidden, down_weight, preferred_element_type=jnp.float32)
     mixed = (residual + ffn_rows).astype(jnp.bfloat16)
-    back_ffn = gather_ffn(w_gate, w_up, w_down)
-    back_set = gather_attention(
-        g_attn, w_query, key_projection, value_projection, query_norm_gain, g_key, w_out, g_ffn
-    )
     grad_out = cotangent.astype(jnp.float32)
     grad_w_down = jnp.einsum("rf,rd->fd", hidden, cotangent, preferred_element_type=jnp.float32)
     grad_hidden = jnp.einsum(
-        "rd,fd->rf", cotangent, back_ffn[2], preferred_element_type=jnp.float32
+        "rd,fd->rf", cotangent, down_weight, preferred_element_type=jnp.float32
     )
     grad_gate = (
         grad_hidden * up_rows * sigmoid_gate * (1.0 + gate_rows * (1.0 - sigmoid_gate))
     ).astype(jnp.bfloat16)
     grad_up = (grad_hidden * silu_gate).astype(jnp.bfloat16)
-    grad_w_gate = jnp.einsum("rd,rf->df", normed_two, grad_gate, preferred_element_type=jnp.float32)
-    grad_w_up = jnp.einsum("rd,rf->df", normed_two, grad_up, preferred_element_type=jnp.float32)
-    grad_normed_two = jnp.einsum(
-        "rf,df->rd", grad_gate, back_ffn[0], preferred_element_type=jnp.float32
-    )
-    grad_normed_two = grad_normed_two + jnp.einsum(
-        "rf,df->rd", grad_up, back_ffn[1], preferred_element_type=jnp.float32
-    )
+    grad_both = jnp.concatenate([grad_gate, grad_up], axis=1)
+    grad_gate_up = jnp.einsum("rd,rf->df", normed_two, grad_both, preferred_element_type=jnp.float32)
+    grad_normed_two = jnp.einsum("rf,df->rd", grad_both, gate_up, preferred_element_type=jnp.float32)
     grad_mid, grad_gain_two = norm_backward(grad_normed_two, unit_two, inverse_two, gain_two, (0,))
-    ffn_grads = (
-        lax.psum_scatter(grad_gain_two, "fsdp", scatter_dimension=0, tiled=True),
-        lax.psum_scatter(grad_w_gate, "fsdp", scatter_dimension=0, tiled=True),
-        lax.psum_scatter(grad_w_up, "fsdp", scatter_dimension=0, tiled=True),
-        lax.psum_scatter(grad_w_down, "fsdp", scatter_dimension=0, tiled=True),
-    )
+    sum_down = scatter_sum(grad_w_down, device, count, False)
+    sum_gate = scatter_sum(grad_gate_up[:, :hidden_width], device, count, True)
+    sum_up = scatter_sum(grad_gate_up[:, hidden_width:], device, count, False)
     grad_residual = grad_out + grad_mid
     grad_res_low = grad_residual.astype(jnp.bfloat16)
-    query_weight = back_set[1]
-    key_weight = back_set[2]
-    value_weight = back_set[3]
-    out_weight = back_set[6]
     grad_w_out = jnp.einsum("ra,rd->ad", attended, grad_res_low, preferred_element_type=jnp.float32)
     grad_attended = jnp.einsum(
         "rd,ad->ra", grad_res_low, out_weight, preferred_element_type=jnp.float32
@@ -270,49 +275,41 @@
     key_gradient_lowered = key_gradient_unnormed.reshape(
         row_total_count, KEY_VALUE_HEADS * HEAD_SIZE
     ).astype(jnp.bfloat16)
-    grad_w_query = jnp.einsum(
-        "rd,ra->da", normed_low, grad_query_low, preferred_element_type=jnp.float32
-    )
-    grad_w_key = jnp.einsum(
-        "rd,ra->da", normed_low, key_gradient_lowered, preferred_element_type=jnp.float32
-    )
-    grad_w_value = jnp.einsum(
-        "rd,ra->da", normed_low, grad_value_low, preferred_element_type=jnp.float32
-    )
+    grad_raw = jnp.concatenate([grad_query_low, key_gradient_lowered, grad_value_low], axis=1)
+    grad_projections = jnp.einsum("rd,ra->da", normed_low, grad_raw, preferred_element_type=jnp.float32)
     grad_normed = jnp.einsum(
-        "ra,da->rd", grad_query_low, query_weight, preferred_element_type=jnp.float32
-    )
-    grad_normed = grad_normed + jnp.einsum(
-        "ra,da->rd", key_gradient_lowered, key_weight, preferred_element_type=jnp.float32
-    )
-    grad_normed = grad_normed + jnp.einsum(
-        "ra,da->rd", grad_value_low, value_weight, preferred_element_type=jnp.float32
+        "ra,da->rd", grad_raw, projections[:, :qkv_width], preferred_element_type=jnp.float32
     )
     grad_first, grad_gain_one = norm_backward(grad_normed, unit_one, inverse_one, gain_one, (0,))
     grad_tokens = (grad_residual + grad_first).astype(jnp.bfloat16)
-    attention_grads = (
-        lax.psum_scatter(grad_gain_one, "fsdp", scatter_dimension=0, tiled=True),
-        lax.psum_scatter(grad_w_query, "fsdp", scatter_dimension=0, tiled=True),
-        lax.psum_scatter(grad_w_key, "fsdp", scatter_dimension=0, tiled=True),
-        lax.psum_scatter(grad_w_value, "fsdp", scatter_dimension=0, tiled=True),
-        lax.psum_scatter(grad_gain_query, "fsdp", scatter_dimension=0, tiled=True),
-        lax.psum_scatter(grad_gain_key, "fsdp", scatter_dimension=0, tiled=True),
-        lax.psum_scatter(grad_w_out, "fsdp", scatter_dimension=0, tiled=True),
-    )
+    sum_out = scatter_sum(grad_w_out, device, count, True)
+    sum_query = scatter_sum(grad_projections[:, :query_width], device, count, False)
+    head_pad = ((0, 0), (0, shard - head_shard))
+    gain_grads = gain_columns(
+        grad_gain_one,
+        grad_gain_two,
+        jnp.pad(grad_gain_query.reshape(count, head_shard), head_pad).reshape(-1),
+        jnp.pad(grad_gain_key.reshape(count, head_shard), head_pad).reshape(-1),
+        count * shard,
+    )
+    sum_rest = scatter_sum(
+        jnp.concatenate([grad_projections[:, query_width:], gain_grads], axis=1), device, count, True
+    )
+    sum_gains = sum_rest[:, 2 * key_width :]
     return (
         mixed,
         grad_tokens,
-        attention_grads[0],
-        attention_grads[1],
-        attention_grads[2],
-        attention_grads[3],
-        attention_grads[4],
-        attention_grads[5],
-        attention_grads[6],
-        ffn_grads[0],
-        ffn_grads[1],
-        ffn_grads[2],
-        ffn_grads[3],
+        sum_gains[:, 0],
+        sum_query,
+        sum_rest[:, :key_width],
+        sum_rest[:, key_width : 2 * key_width],
+        sum_gains[:head_shard, 2],
+        sum_gains[:head_shard, 3],
+        sum_out,
+        sum_gains[:, 1],
+        sum_gate,
+        sum_up,
+        sum_down,
     )
 
 

time: 1590 us -> 682 us (0.43)
  waiting for transfers between devices: 1270 us -> 335 us
  blocking collectives: 81.9 us -> 0 us
  starting transfers between devices: 0.77 us -> 53 us
  other arithmetic: 31.9 us -> 68.5 us
  local copies, waits for them, and re-layouts: 50.1 us -> 81.5 us
    reduce_scatter x7 -> x0, waiting for transfers between devices: 919 us -> none  [the longest x1 162 us: on_device(): lax.psum_scatter(grad_w_up, 'fsdp', scatter_dimension=0, tiled=True)]
    all_gather x7 -> x3, waiting for transfers between devices: 344 us -> 203 us  [the longest x1 82.7 us: on_device(): lax.all_gather(jnp.concatenate([w_gate, w_up], axis=1), 'fsdp', axis=0, t...]
    ppermute x0 -> x36, waiting for transfers between devices: none -> 132 us  [exchange(): lax.ppermute(values, 'fsdp', [(source, source ^ mask) for source in range...]
    unnamed x2 -> x0, blocking collectives: 81.9 us -> none
    ppermute x0 -> x36, starting transfers between devices: none -> 52.8 us  [exchange(): lax.ppermute(values, 'fsdp', [(source, source ^ mask) for source in range...]
    dot_general x18 -> x9, matrix products: 91.2 us -> 67.3 us  [the longest x1 13.3 us: on_device(): jnp.einsum('rf,df->rd', grad_both, gate_up, preferred_element_type=jnp.fl...]
    slice x0 -> x10, local copies, waits for them, and re-layouts: none -> 20.1 us  [the longest x1 8.07 us: on_device(): down_weight = back_rows[:, out_rows:].reshape(count * w_down.shape[0], -1)]
    convert_element_type x5 -> x19, other arithmetic: 1.11 us -> 19.9 us  [the longest x18 18.9 us: scatter_sum(): (kept.astype(jnp.float32) + came.astype(jnp.float32)).astype(jnp.bfloat16)]
  transfers between devices with their start and end apart: 14 -> 39, of which waited for: 14 -> 20; matrix products, arithmetic and copies ran while one was open for 9% -> 17% of each run, Pallas kernels for 0% -> 0%
where the time goes in v1:
time: 682 us; the launch traced here: 678 us
  waiting for transfers between devices  335 us (49%)
  matrix products  123 us (18%)
  local copies, waits for them, and re-layouts  81.5 us (12%)
  other arithmetic  68.5 us (10%)
  starting transfers between devices  53 us (8%)
  between operations  16.6 us (2%)
    ppermute x36, waiting for transfers between devices, exchange(): lax.ppermute(values, 'fsdp', [(source, source ^ mask) for source in range...  132 us
    all_gather x1, waiting for transfers between devices, on_device(): lax.all_gather(jnp.concatenate([w_gate, w_up], axis=1), 'fsdp', axis=0, t...  82.7 us
    all_gather x1, waiting for transfers between devices, on_device(): lax.all_gather(jnp.concatenate([w_query, key_projection, value_projection...  77.1 us
    ppermute x36, starting transfers between devices, exchange(): lax.ppermute(values, 'fsdp', [(source, source ^ mask) for source in range...  52.8 us
    all_gather x1, waiting for transfers between devices, on_device(): lax.all_gather(jnp.concatenate([w_out, w_down], axis=0), 'fsdp', axis=0,...  43.6 us
    unnamed x292, local copies, waits for them, and re-layouts  27.9 us
    convert_element_type x18, other arithmetic, scatter_sum(): (kept.astype(jnp.float32) + came.astype(jnp.float32)).astype(jnp.bfloat16)  18.9 us
    dot_general x8, matrix products, on_device(): jnp.einsum('qgd,sd->gqs', grad_heads, value_low[:, shared_key_head, :], p...  14.2 us
  transfers between devices with their start and end apart: 39, of which 20 were waited for; matrix products, arithmetic and copies ran while one was open for 17% of the time, Pallas kernels for 0%

profile of v1, /device:TPU:0, one launch (start us, length us, event | category | flops | bytes accessed | tf_op | source)
XLA Modules:
  0.0 677.7 jit_solution(16873184653569265932)
XLA Ops:
  15.7 77.1 %all-gather.5.cloned.1.call-done = bf16[1024,4224]{1,0:T(8,128)(2,1)} async-done(((bf16[32,4224]{1,0:T(8,128)(2,1)}), bf16[1024,4224]{1,0:T(8,128)(2,1)}) %all-gather.5.cloned.1.call-update) | async-done | bytes 8650768 | tf_op jit(solution)/shard_map/all_gather | solution.py:132
  94.6 6.3 fusion.2
  107.7 2.8 slice_bitcast_fusion.3
  137.9 43.6 %all-gather.9.cloned.1.call-done = bf16[5120,1024]{1,0:T(8,128)(2,1)} async-done(((bf16[160,1024]{1,0:T(8,128)(2,1)}), bf16[5120,1024]{1,0:T(8,128)(2,1)}) %all-gather.9.cloned.1.call-update) | async-done | bytes 10485776 | tf_op jit(solution)/shard_map/all_gather | solution.py:135
  181.5 2.6 slice.338
  184.2 8.1 %slice.342 = bf16[32,96,1024]{2,1,0:T(8,128)(2,1)} slice(bf16[32,160,1024]{2,1,0:T(8,128)(2,1)} %bitcast.773), slice={[0:32], [64:160], [0:1024]} | slice | bytes 12582912 | tf_op jit(solution)/shard_map/slice | solution.py:139
  192.3 4.5 multiply_reduce_fusion.5
  196.8 82.7 %all-gather.7.cloned.1.call-done = bf16[1024,6144]{1,0:T(8,128)(2,1)} async-done(((bf16[32,6144]{1,0:T(8,128)(2,1)}), bf16[1024,6144]{1,0:T(8,128)(2,1)}) %all-gather.7.cloned.1.call-update) | async-done | bytes 12582928 | tf_op jit(solution)/shard_map/all_gather | solution.py:136
  279.5 8.7 %fusion.238 = f32[384,6144]{1,0:T(8,128)S(1)} fusion(bf16[1024,6144]{1,0:T(8,128)(2,1)} %all-gather.7.cloned.1.call-done, f32[384,1024]{1,0:T(8,128)} %get-tuple-element.114, f32[1024]{0:T(1024)S(1)} %get-tuple-element.17, f32[384]{0:T(512)S(1)} %add_rsqrt_fusion.2), kind=kOutput, calls=%fused_computation.515 | convolution fusion | flops 4833017856 | bytes 23598592 | tf_op jit(solution)/shard_map/dot_general | solution.py:189
  288.2 6.6 fusion.9
  294.9 13.3 %multiply_reduce_fusion.2 = (bf16[1024]{0:T(1024)(128)(2,1)}, f32[384]{0:T(512)S(1)}, f32[384,1024]{1,0:T(8,128)}) fusion(f32[384,1024]{1,0:T(8,128)} %get-tuple-element.114, f32[384]{0:T(512)S(1)} %add_rsqrt_fusion.2, f32[1024]{0:T(1024)S(1)} %get-tuple-element.17, bf16[1024,6144]{1,0:T(8,128)(2,1)} %all-gather.7.cloned.1.call-done, ...), kind=kOutput, calls=%fused_computation.117 | convolution fusion | flops 4843633152 | bytes 20456448 | tf_op jit(solution)/shard_map/rf,df->rd/dot_general | solution.py:208
  308.2 2.7 multiply_add_fusion.2
  318.8 5.9 convolution_convert_fusion.3
  324.7 10.3 %convolution_convert_fusion = bf16[1024,6144]{1,0:T(8,128)(2,1)} fusion(bf16[384,3072]{1,0:T(8,128)(2,1)S(1)} %copy-done.70, bf16[384,3072]{1,0:T(8,128)(2,1)S(1)} %copy-done.69, f32[384,1024]{1,0:T(8,128)S(1)} %copy-done.43, f32[1024]{0:T(1024)S(1)} %get-tuple-element.17, f32[384]{0:T(512)S(1)} %add_rsqrt_fusion.2), kind=kOutput, calls=%fused_computation | convolution fusion | flops 4848746496 | bytes 18880000 | tf_op jit(solution)/shard_map/rd,rf->df/dot_general | solution.py:207
  383.1 4.1 multiply_subtract_fusion
  387.2 3.8 fusion.141
  392.6 2.8 fusion.44
  398.2 3.5 fusion.18
  401.9 5.5 convolution_convert_fusion.1
  407.4 3.8 fusion.268
  411.6 8.6 %fusion.39 = (bf16[1024]{0:T(1024)(128)(2,1)S(1)}, f32[384]{0:T(512)S(1)}, f32[384,1024]{1,0:T(8,128)}) fusion(bf16[384,1024]{1,0:T(8,128)(2,1)S(1)} %copy-done.68, f32[384]{0:T(512)S(1)} %copy-done.125, f32[1024]{0:T(1024)S(1)} %copy-done.113, bf16[1024,4224]{1,0:T(8,128)(2,1)} %all-gather.5.cloned.1.call-done, bf16[384,1024]{1,0:T(8,128)(2,1)S(1)} %copy-done.85, ...), kind=kOutput, calls=%fused_computation.95 | convolution fusion | flops 3233413632 | bytes 13902848 | tf_op jit(solution)/shard_map/ra,da->rd/dot_general | solution.py:280
  420.5 2.7 fusion.29
  443.5 5.8 convolution_convert_fusion.2
  450.6 3.7 constant_dynamic-slice_fusion.1
  456.4 3.5 add_convert_fusion.1
  464.2 2.6 fusion.13
  470.6 17.5 %collective-permute-done.7 = bf16[4,2,32,2048]{3,2,0,1:T(8,128)(2,1)S(1)} collective-permute-done((bf16[4,2,32,2048]{3,2,0,1:T(8,128)(2,1)S(1)}, bf16[4,2,32,2048]{3,2,0,1:T(8,128)(2,1)S(1)}, u32[]{:S(2)}, u32[]{:S(2)}) %collective-permute-start.7) | collective-permute-done | bytes 1048608 | tf_op jit(solution)/shard_map/ppermute | solution.py:63
  495.6 3.0 fusion.6
  501.9 3.0 fusion.5
  505.1 11.7 %collective-permute-done.1 = bf16[4,2,32,2176]{3,2,0,1:T(8,128)(2,1)S(1)} collective-permute-done((bf16[4,2,32,2176]{3,2,0,1:T(8,128)(2,1)S(1)}, bf16[4,2,32,2176]{3,2,0,1:T(8,128)(2,1)S(1)}, u32[]{:S(2)}, u32[]{:S(2)}) %collective-permute-start.1) | collective-permute-done | bytes 1114144 | tf_op jit(solution)/shard_map/ppermute | solution.py:63
  518.7 9.3 %collective-permute-done.8 = bf16[4,32,2048]{2,1,0:T(8,128)(2,1)S(1)} collective-permute-done((bf16[4,32,2048]{2,1,0:T(8,128)(2,1)}, bf16[4,32,2048]{2,1,0:T(8,128)(2,1)S(1)}, u32[]{:S(2)}, u32[]{:S(2)}) %collective-permute-start.8) | collective-permute-done | bytes 524320 | tf_op jit(solution)/shard_map/ppermute | solution.py:63
  532.9 3.6 collective-permute-done.11
  537.9 3.3 collective-permute-done.10
  541.1 2.4 collective-permute-start.17
  546.5 2.4 collective-permute-done.17
  548.9 2.8 collective-permute-start.5
  551.7 7.8 %collective-permute-done.16 = bf16[64,1024]{1,0:T(8,128)(2,1)S(1)} collective-permute-done((bf16[64,1024]{1,0:T(8,128)(2,1)S(1)}, bf16[64,1024]{1,0:T(8,128)(2,1)S(1)}, u32[]{:S(2)}, u32[]{:S(2)}) %collective-permute-start.16) | collective-permute-done | bytes 131104 | tf_op jit(solution)/shard_map/ppermute | solution.py:63
  559.6 3.2 collective-permute-start.3
  563.5 3.3 collective-permute-done.4
  570.9 3.0 collective-permute-done.25
  576.0 31.5 %collective-permute-done.31 = bf16[4,2,96,1024]{3,2,0,1:T(8,128)(2,1)S(1)} collective-permute-done((bf16[4,2,96,1024]{3,2,0,1:T(8,128)(2,1)S(1)}, bf16[4,2,96,1024]{3,2,0,1:T(8,128)(2,1)S(1)}, u32[]{:S(2)}, u32[]{:S(2)}) %collective-permute-start.31) | collective-permute-done | bytes 1572896 | tf_op jit(solution)/shard_map/ppermute | solution.py:63
  609.8 9.7 %collective-permute-done.20 = bf16[4,32,3072]{2,1,0:T(8,128)(2,1)S(1)} collective-permute-done((bf16[4,32,3072]{2,1,0:T(8,128)(2,1)S(1)}, bf16[4,32,3072]{2,1,0:T(8,128)(2,1)S(1)}, u32[]{:S(2)}, u32[]{:S(2)}) %collective-permute-start.20) | collective-permute-done | bytes 786464 | tf_op jit(solution)/shard_map/ppermute | solution.py:63
  621.5 2.8 collective-permute-start.22
  625.0 2.4 collective-permute-start.29
  629.6 9.5 %collective-permute-start.27 = (bf16[32,3072]{1,0:T(8,128)(2,1)S(1)}, bf16[32,3072]{1,0:T(8,128)(2,1)S(1)}, u32[]{:S(2)}, u32[]{:S(2)}) collective-permute-start(bf16[32,3072]{1,0:T(8,128)(2,1)S(1)} %get-tuple-element.77), channel_id=1, source_target_pairs={{0,8},{1,9},{2,10},{3,11},{4,12},{5,13},{6,14},{7,15},{8,0},{9,1},... | collective-permute-start | bytes 589832 | tf_op jit(solution)/shard_map/ppermute | solution.py:63
  639.1 11.8 %collective-permute-done.22 = bf16[32,3072]{1,0:T(8,128)(2,1)S(1)} collective-permute-done((bf16[32,3072]{1,0:T(8,128)(2,1)S(1)}, bf16[32,3072]{1,0:T(8,128)(2,1)S(1)}, u32[]{:S(2)}, u32[]{:S(2)}) %collective-permute-start.22) | collective-permute-done | bytes 196640 | tf_op jit(solution)/shard_map/ppermute | solution.py:63
  656.1 7.4 %collective-permute-done.28 = bf16[32,3072]{1,0:T(8,128)(2,1)S(1)} collective-permute-done((bf16[32,3072]{1,0:T(8,128)(2,1)S(1)}, bf16[32,3072]{1,0:T(8,128)(2,1)S(1)}, u32[]{:S(2)}, u32[]{:S(2)}) %collective-permute-start.28) | collective-permute-done | bytes 196640 | tf_op jit(solution)/shard_map/ppermute | solution.py:63
  664.4 5.8 collective-permute-done.34
  (541 shorter events, 178.4 us)
Async XLA Ops:
  7.2 85.5 %all-gather.5.cloned.1.call-start = ((), (), s32[]{:S(2)}) async-start(), calls=%async_computation | async-start | bytes 8921088 | tf_op jit(solution)/shard_map/all_gather | solution.py:132
  10.6 170.9 %all-gather.9.cloned.1.call-start = ((), (), s32[]{:S(2)}) async-start(), calls=%async_computation.2 | async-start | bytes 10813440 | tf_op jit(solution)/shard_map/all_gather | solution.py:135
  12.4 267.1 %all-gather.7.cloned.1.call-start = ((), (), s32[]{:S(2)}) async-start(), calls=%async_computation.1 | async-start | bytes 12976128 | tf_op jit(solution)/shard_map/all_gather | solution.py:136
  14.0 86.9 %copy-start.124 = (f32[384]{0:T(512)}, f32[384]{0:T(512)S(1)}, u32[]{:S(2)}) copy-start(f32[384]{0:T(512)S(1)} %add_rsqrt_fusion.3) | copy-start | bytes 4612
  94.1 34.5 %copy-start.122 = (f32[128]{0:T(128)}, f32[128]{0:T(128)S(1)}, u32[]{:S(2)}) copy-start(f32[128]{0:T(128)S(1)} %mul.621) | copy-start | bytes 1540
  103.8 16.7 %copy-start.28 = (f32[48,16,8,128]{3,2,1,0:T(8,128)}, f32[48,16,8,128]{3,2,1,0:T(8,128)S(1)}, u32[]{:S(2)}) copy-start(f32[48,16,8,128]{3,2,1,0:T(8,128)S(1)} %get-tuple-element.47) | copy-start | bytes 9437188
  107.7 10.0 %copy-start.126 = (f32[128]{0:T(128)}, f32[128]{0:T(128)S(1)}, u32[]{:S(2)}) copy-start(f32[128]{0:T(128)S(1)} %mul.605) | copy-start | bytes 1540
  127.6 9.3 %copy-start.6 = (f32[2,384,384]{1,2,0:T(8,128)}, f32[2,384,384]{1,2,0:T(8,128)S(1)}, u32[]{:S(2)}) copy-start(f32[2,384,384]{1,2,0:T(8,128)S(1)} %get-tuple-element.112) | copy-start | bytes 3538948
  324.7 10.3 %copy-start.25 = (f32[2,384,384]{1,2,0:T(8,128)S(1)}, f32[2,384,384]{1,2,0:T(8,128)}, u32[]{:S(2)}) copy-start(f32[2,384,384]{1,2,0:T(8,128)} %copy-done.24) | copy-start | bytes 3538948
  324.7 10.3 %copy-start.107 = (f32[2,384]{1,0:T(2,128)S(1)}, f32[2,384]{1,0:T(2,128)}, u32[]{:S(2)}) copy-start(f32[2,384]{1,0:T(2,128)} %copy-done.106) | copy-start | bytes 9220
  387.2 10.0 %slice-start.3 = ((s8[6291456]{0:T(1024)(128)(4,1)}), s8[2097152]{0:T(1024)(128)(4,1)S(1)}, s32[]{:S(2)}) async-start(s8[6291456]{0:T(1024)(128)(4,1)} %bitcast.767), calls=%async_computation.6 | async-start | bytes 4194304
  424.9 42.0 %collective-permute-start = (bf16[4,2,2,32,2176]{4,3,0,2,1:T(8,128)(2,1)}, bf16[4,2,2,32,2176]{4,3,0,2,1:T(8,128)(2,1)}, u32[]{:S(2)}, u32[]{:S(2)}) collective-permute-start(bf16[4,2,2,32,2176]{4,3,0,2,1:T(8,128)(2,1)} %bitcast.758), channel_id=1, source_target_pairs={{0,1},{1,0},{2,3},{3,2},{4,5},{5,4},{6,7},{7,6},{8,9},{9,8},{10,11... | collective-permute-start | bytes 6684680 | tf_op jit(solution)/shard_map/ppermute | solution.py:63
  429.8 30.2 %collective-permute-start.6 = (bf16[4,2,2,32,2048]{4,3,0,1,2:T(8,128)(2,1)}, bf16[4,2,2,32,2048]{4,3,0,1,2:T(8,128)(2,1)}, u32[]{:S(2)}, u32[]{:S(2)}) collective-permute-start(bf16[4,2,2,32,2048]{4,3,0,1,2:T(8,128)(2,1)} %bitcast.760), channel_id=1, source_target_pairs={{0,1},{1,0},{2,3},{3,2},{4,5},{5,4},{6,7},{7,6},{8,9},{9,8},{10,11... | collective-permute-start | bytes 6291464 | tf_op jit(solution)/shard_map/ppermute | solution.py:63
  434.7 28.0 %collective-permute-start.12 = (bf16[4,2,2,64,1024]{4,3,0,2,1:T(8,128)(2,1)}, bf16[4,2,2,64,1024]{4,3,0,2,1:T(8,128)(2,1)}, u32[]{:S(2)}, u32[]{:S(2)}) collective-permute-start(bf16[4,2,2,64,1024]{4,3,0,2,1:T(8,128)(2,1)} %bitcast.759), channel_id=1, source_target_pairs={{0,1},{1,0},{2,3},{3,2},{4,5},{5,4},{6,7},{7,6},{8,9},{9,8},{10,11... | collective-permute-start | bytes 6291464 | tf_op jit(solution)/shard_map/ppermute | solution.py:63
  439.4 55.4 %collective-permute-start.18 = (bf16[4,2,2,32,3072]{4,3,0,2,1:T(8,128)(2,1)}, bf16[4,2,2,32,3072]{4,3,0,2,1:T(8,128)(2,1)}, u32[]{:S(2)}, u32[]{:S(2)}) collective-permute-start(bf16[4,2,2,32,3072]{4,3,0,2,1:T(8,128)(2,1)} %bitcast.757), channel_id=1, source_target_pairs={{0,1},{1,0},{2,3},{3,2},{4,5},{5,4},{6,7},{7,6},{8,9},{9,8},{10,11... | collective-permute-start | bytes 9437192 | tf_op jit(solution)/shard_map/ppermute | solution.py:63
  442.3 59.6 %collective-permute-start.24 = (bf16[4,2,2,32,3072]{4,3,0,1,2:T(8,128)(2,1)}, bf16[4,2,2,32,3072]{4,3,0,1,2:T(8,128)(2,1)}, u32[]{:S(2)}, u32[]{:S(2)}) collective-permute-start(bf16[4,2,2,32,3072]{4,3,0,1,2:T(8,128)(2,1)} %bitcast.756), channel_id=1, source_target_pairs={{0,1},{1,0},{2,3},{3,2},{4,5},{5,4},{6,7},{7,6},{8,9},{9,8},{10,11... | collective-permute-start | bytes 9437192 | tf_op jit(solution)/shard_map/ppermute | solution.py:63
  443.5 11.2 %slice-start.5 = ((s8[6291456]{0:T(1024)(128)(4,1)}), s8[4194304]{0:T(1024)(128)(4,1)S(1)}, s32[]{:S(2)}) async-start(s8[6291456]{0:T(1024)(128)(4,1)} %bitcast.791), calls=%async_computation.8 | async-start | bytes 8388608
  459.9 38.8 %collective-permute-start.30 = (bf16[4,2,2,96,1024]{4,3,0,1,2:T(8,128)(2,1)S(1)}, bf16[4,2,2,96,1024]{4,3,0,1,2:T(8,128)(2,1)S(1)}, u32[]{:S(2)}, u32[]{:S(2)}) collective-permute-start(bf16[4,2,2,96,1024]{4,3,0,1,2:T(8,128)(2,1)S(1)} %bitcast.803), channel_id=1, source_target_pairs={{0,1},{1,0},{2,3},{3,2},{4,5},{5,4},{6,7},{7,6},{8,9},{9,8},{10,11... | collective-permute-start | bytes 9437192 | tf_op jit(solution)/shard_map/ppermute | solution.py:63
  462.7 25.4 %collective-permute-start.7 = (bf16[4,2,32,2048]{3,2,0,1:T(8,128)(2,1)S(1)}, bf16[4,2,32,2048]{3,2,0,1:T(8,128)(2,1)S(1)}, u32[]{:S(2)}, u32[]{:S(2)}) collective-permute-start(bf16[4,2,32,2048]{3,2,0,1:T(8,128)(2,1)S(1)} %dynamic-slice_bitcast_fusion.5), channel_id=1, source_target_pairs={{0,2},{1,3},{2,0},{3,1},{4,6},{5,7},{6,4},{7,5},{8,10},{9,11},{10,... | collective-permute-start | bytes 3145736 | tf_op jit(solution)/shard_map/ppermute | solution.py:63
  466.8 26.1 %collective-permute-start.13 = (bf16[4,2,64,1024]{3,2,0,1:T(8,128)(2,1)S(1)}, bf16[4,2,64,1024]{3,2,0,1:T(8,128)(2,1)S(1)}, u32[]{:S(2)}, u32[]{:S(2)}) collective-permute-start(bf16[4,2,64,1024]{3,2,0,1:T(8,128)(2,1)S(1)} %dynamic-slice_bitcast_fusion.4), channel_id=1, source_target_pairs={{0,4},{1,5},{2,6},{3,7},{4,0},{5,1},{6,2},{7,3},{8,12},{9,13},{10,... | collective-permute-start | bytes 3145736 | tf_op jit(solution)/shard_map/ppermute | solution.py:63
  488.1 28.7 %collective-permute-start.1 = (bf16[4,2,32,2176]{3,2,0,1:T(8,128)(2,1)S(1)}, bf16[4,2,32,2176]{3,2,0,1:T(8,128)(2,1)S(1)}, u32[]{:S(2)}, u32[]{:S(2)}) collective-permute-start(bf16[4,2,32,2176]{3,2,0,1:T(8,128)(2,1)S(1)} %dynamic-slice_bitcast_fusion.3), channel_id=1, source_target_pairs={{0,4},{1,5},{2,6},{3,7},{4,0},{5,1},{6,2},{7,3},{8,12},{9,13},{10,... | collective-permute-start | bytes 3342344 | tf_op jit(solution)/shard_map/ppermute | solution.py:63
  492.9 35.1 %collective-permute-start.8 = (bf16[4,32,2048]{2,1,0:T(8,128)(2,1)}, bf16[4,32,2048]{2,1,0:T(8,128)(2,1)S(1)}, u32[]{:S(2)}, u32[]{:S(2)}) collective-permute-start(bf16[4,32,2048]{2,1,0:T(8,128)(2,1)} %dynamic-slice_bitcast_fusion.11), channel_id=1, source_target_pairs={{0,4},{1,5},{2,6},{3,7},{4,0},{5,1},{6,2},{7,3},{8,12},{9,13},{10,... | collective-permute-start | bytes 1572872 | tf_op jit(solution)/shard_map/ppermute | solution.py:63
  494.8 35.8 %collective-permute-start.14 = (bf16[4,64,1024]{2,1,0:T(8,128)(2,1)S(1)}, bf16[4,64,1024]{2,1,0:T(8,128)(2,1)S(1)}, u32[]{:S(2)}, u32[]{:S(2)}) collective-permute-start(bf16[4,64,1024]{2,1,0:T(8,128)(2,1)S(1)} %dynamic-slice_bitcast_fusion.10), channel_id=1, source_target_pairs={{0,2},{1,3},{2,0},{3,1},{4,6},{5,7},{6,4},{7,5},{8,10},{9,11},{10,... | collective-permute-start | bytes 1572872 | tf_op jit(solution)/shard_map/ppermute | solution.py:63
  498.7 70.8 %collective-permute-start.19 = (bf16[4,2,32,3072]{3,2,0,1:T(8,128)(2,1)S(1)}, bf16[4,2,32,3072]{3,2,0,1:T(8,128)(2,1)S(1)}, u32[]{:S(2)}, u32[]{:S(2)}) collective-permute-start(bf16[4,2,32,3072]{3,2,0,1:T(8,128)(2,1)S(1)} %dynamic-slice_bitcast_fusion.2), channel_id=1, source_target_pairs={{0,4},{1,5},{2,6},{3,7},{4,0},{5,1},{6,2},{7,3},{8,12},{9,13},{10,... | collective-permute-start | bytes 4718600 | tf_op jit(solution)/shard_map/ppermute | solution.py:63
  517.3 27.0 %collective-permute-start.2 = (bf16[4,32,2176]{2,1,0:T(8,128)(2,1)S(1)}, bf16[4,32,2176]{2,1,0:T(8,128)(2,1)S(1)}, u32[]{:S(2)}, u32[]{:S(2)}) collective-permute-start(bf16[4,32,2176]{2,1,0:T(8,128)(2,1)S(1)} %dynamic-slice_bitcast_fusion.9), channel_id=1, source_target_pairs={{0,2},{1,3},{2,0},{3,1},{4,6},{5,7},{6,4},{7,5},{8,10},{9,11},{10,... | collective-permute-start | bytes 1671176 | tf_op jit(solution)/shard_map/ppermute | solution.py:63
  528.2 8.3 %collective-permute-start.11 = (bf16[32,2048]{1,0:T(8,128)(2,1)S(1)}, bf16[32,2048]{1,0:T(8,128)(2,1)S(1)}, u32[]{:S(2)}, u32[]{:S(2)}) collective-permute-start(bf16[32,2048]{1,0:T(8,128)(2,1)S(1)} %get-tuple-element.90), channel_id=1, source_target_pairs={{0,24},{1,25},{2,26},{3,27},{4,28},{5,29},{6,30},{7,31},{8,16},{9,... | collective-permute-start | bytes 393224 | tf_op jit(solution)/shard_map/ppermute | solution.py:63
  529.8 11.3 %collective-permute-start.10 = (bf16[32,2048]{1,0:T(8,128)(2,1)S(1)}, bf16[32,2048]{1,0:T(8,128)(2,1)S(1)}, u32[]{:S(2)}, u32[]{:S(2)}) collective-permute-start(bf16[32,2048]{1,0:T(8,128)(2,1)S(1)} %get-tuple-element.91), channel_id=1, source_target_pairs={{0,16},{1,17},{2,18},{3,19},{4,20},{5,21},{6,22},{7,23},{8,24},{9,... | collective-permute-start | bytes 393224 | tf_op jit(solution)/shard_map/ppermute | solution.py:63
  530.6 12.9 %collective-permute-start.9 = (bf16[32,2048]{1,0:T(8,128)(2,1)S(1)}, bf16[32,2048]{1,0:T(8,128)(2,1)S(1)}, u32[]{:S(2)}, u32[]{:S(2)}) collective-permute-start(bf16[32,2048]{1,0:T(8,128)(2,1)S(1)} %get-tuple-element.89), channel_id=1, source_target_pairs={{0,8},{1,9},{2,10},{3,11},{4,12},{5,13},{6,14},{7,15},{8,0},{9,1},... | collective-permute-start | bytes 393224 | tf_op jit(solution)/shard_map/ppermute | solution.py:63
  536.5 37.3 %collective-permute-start.25 = (bf16[4,2,32,3072]{3,2,0,1:T(8,128)(2,1)S(1)}, bf16[4,2,32,3072]{3,2,0,1:T(8,128)(2,1)S(1)}, u32[]{:S(2)}, u32[]{:S(2)}) collective-permute-start(bf16[4,2,32,3072]{3,2,0,1:T(8,128)(2,1)S(1)} %dynamic-slice_bitcast_fusion.1), channel_id=1, source_target_pairs={{0,2},{1,3},{2,0},{3,1},{4,6},{5,7},{6,4},{7,5},{8,10},{9,11},{10,... | collective-permute-start | bytes 4718600 | tf_op jit(solution)/shard_map/ppermute | solution.py:63
  541.1 7.8 %collective-permute-start.17 = (bf16[64,1024]{1,0:T(8,128)(2,1)S(1)}, bf16[64,1024]{1,0:T(8,128)(2,1)S(1)}, u32[]{:S(2)}, u32[]{:S(2)}) collective-permute-start(bf16[64,1024]{1,0:T(8,128)(2,1)S(1)} %get-tuple-element.87), channel_id=1, source_target_pairs={{0,24},{1,25},{2,26},{3,27},{4,28},{5,29},{6,30},{7,31},{8,16},{9,... | collective-permute-start | bytes 393224 | tf_op jit(solution)/shard_map/ppermute | solution.py:63
  543.5 16.0 %collective-permute-start.16 = (bf16[64,1024]{1,0:T(8,128)(2,1)S(1)}, bf16[64,1024]{1,0:T(8,128)(2,1)S(1)}, u32[]{:S(2)}, u32[]{:S(2)}) collective-permute-start(bf16[64,1024]{1,0:T(8,128)(2,1)S(1)} %get-tuple-element.88), channel_id=1, source_target_pairs={{0,16},{1,17},{2,18},{3,19},{4,20},{5,21},{6,22},{7,23},{8,24},{9,... | collective-permute-start | bytes 393224 | tf_op jit(solution)/shard_map/ppermute | solution.py:63
  544.3 15.3 %collective-permute-start.15 = (bf16[64,1024]{1,0:T(8,128)(2,1)S(1)}, bf16[64,1024]{1,0:T(8,128)(2,1)S(1)}, u32[]{:S(2)}, u32[]{:S(2)}) collective-permute-start(bf16[64,1024]{1,0:T(8,128)(2,1)S(1)} %get-tuple-element.86), channel_id=1, source_target_pairs={{0,8},{1,9},{2,10},{3,11},{4,12},{5,13},{6,14},{7,15},{8,0},{9,1},... | collective-permute-start | bytes 393224 | tf_op jit(solution)/shard_map/ppermute | solution.py:63
  548.9 14.6 %collective-permute-start.5 = (bf16[32,2176]{1,0:T(8,128)(2,1)S(1)}, bf16[32,2176]{1,0:T(8,128)(2,1)S(1)}, u32[]{:S(2)}, u32[]{:S(2)}) collective-permute-start(bf16[32,2176]{1,0:T(8,128)(2,1)S(1)} %get-tuple-element.84), channel_id=1, source_target_pairs={{0,24},{1,25},{2,26},{3,27},{4,28},{5,29},{6,30},{7,31},{8,16},{9,... | collective-permute-start | bytes 417800 | tf_op jit(solution)/shard_map/ppermute | solution.py:63
  559.6 7.3 %collective-permute-start.4 = (bf16[32,2176]{1,0:T(8,128)(2,1)S(1)}, bf16[32,2176]{1,0:T(8,128)(2,1)S(1)}, u32[]{:S(2)}, u32[]{:S(2)}) collective-permute-start(bf16[32,2176]{1,0:T(8,128)(2,1)S(1)} %get-tuple-element.85), channel_id=1, source_target_pairs={{0,16},{1,17},{2,18},{3,19},{4,20},{5,21},{6,22},{7,23},{8,24},{9,... | collective-permute-start | bytes 417800 | tf_op jit(solution)/shard_map/ppermute | solution.py:63
  559.6 7.7 %collective-permute-start.3 = (bf16[32,2176]{1,0:T(8,128)(2,1)S(1)}, bf16[32,2176]{1,0:T(8,128)(2,1)S(1)}, u32[]{:S(2)}, u32[]{:S(2)}) collective-permute-start(bf16[32,2176]{1,0:T(8,128)(2,1)S(1)} %get-tuple-element.83), channel_id=1, source_target_pairs={{0,8},{1,9},{2,10},{3,11},{4,12},{5,13},{6,14},{7,15},{8,0},{9,1},... | collective-permute-start | bytes 417800 | tf_op jit(solution)/shard_map/ppermute | solution.py:63
  563.5 44.0 %collective-permute-start.31 = (bf16[4,2,96,1024]{3,2,0,1:T(8,128)(2,1)S(1)}, bf16[4,2,96,1024]{3,2,0,1:T(8,128)(2,1)S(1)}, u32[]{:S(2)}, u32[]{:S(2)}) collective-permute-start(bf16[4,2,96,1024]{3,2,0,1:T(8,128)(2,1)S(1)} %dynamic-slice_bitcast_fusion), channel_id=1, source_target_pairs={{0,2},{1,3},{2,0},{3,1},{4,6},{5,7},{6,4},{7,5},{8,10},{9,11},{10,... | collective-permute-start | bytes 4718600 | tf_op jit(solution)/shard_map/ppermute | solution.py:63
  570.2 49.4 %collective-permute-start.20 = (bf16[4,32,3072]{2,1,0:T(8,128)(2,1)S(1)}, bf16[4,32,3072]{2,1,0:T(8,128)(2,1)S(1)}, u32[]{:S(2)}, u32[]{:S(2)}) collective-permute-start(bf16[4,32,3072]{2,1,0:T(8,128)(2,1)S(1)} %dynamic-slice_bitcast_fusion.8), channel_id=1, source_target_pairs={{0,2},{1,3},{2,0},{3,1},{4,6},{5,7},{6,4},{7,5},{8,10},{9,11},{10,... | collective-permute-start | bytes 2359304 | tf_op jit(solution)/shard_map/ppermute | solution.py:63
  574.5 50.3 %collective-permute-start.26 = (bf16[4,32,3072]{2,1,0:T(8,128)(2,1)S(1)}, bf16[4,32,3072]{2,1,0:T(8,128)(2,1)S(1)}, u32[]{:S(2)}, u32[]{:S(2)}) collective-permute-start(bf16[4,32,3072]{2,1,0:T(8,128)(2,1)S(1)} %dynamic-slice_bitcast_fusion.7), channel_id=1, source_target_pairs={{0,4},{1,5},{2,6},{3,7},{4,0},{5,1},{6,2},{7,3},{8,12},{9,13},{10,... | collective-permute-start | bytes 2359304 | tf_op jit(solution)/shard_map/ppermute | solution.py:63
  608.3 19.1 %collective-permute-start.32 = (bf16[4,96,1024]{2,1,0:T(8,128)(2,1)S(1)}, bf16[4,96,1024]{2,1,0:T(8,128)(2,1)S(1)}, u32[]{:S(2)}, u32[]{:S(2)}) collective-permute-start(bf16[4,96,1024]{2,1,0:T(8,128)(2,1)S(1)} %dynamic-slice_bitcast_fusion.6), channel_id=1, source_target_pairs={{0,4},{1,5},{2,6},{3,7},{4,0},{5,1},{6,2},{7,3},{8,12},{9,13},{10,... | collective-permute-start | bytes 2359304 | tf_op jit(solution)/shard_map/ppermute | solution.py:63
  619.8 9.7 %collective-permute-start.23 = (bf16[32,3072]{1,0:T(8,128)(2,1)S(1)}, bf16[32,3072]{1,0:T(8,128)(2,1)S(1)}, u32[]{:S(2)}, u32[]{:S(2)}) collective-permute-start(bf16[32,3072]{1,0:T(8,128)(2,1)S(1)} %get-tuple-element.81), channel_id=1, source_target_pairs={{0,24},{1,25},{2,26},{3,27},{4,28},{5,29},{6,30},{7,31},{8,16},{9,... | collective-permute-start | bytes 589832 | tf_op jit(solution)/shard_map/ppermute | solution.py:63
  621.5 29.4 %collective-permute-start.22 = (bf16[32,3072]{1,0:T(8,128)(2,1)S(1)}, bf16[32,3072]{1,0:T(8,128)(2,1)S(1)}, u32[]{:S(2)}, u32[]{:S(2)}) collective-permute-start(bf16[32,3072]{1,0:T(8,128)(2,1)S(1)} %get-tuple-element.82), channel_id=1, source_target_pairs={{0,16},{1,17},{2,18},{3,19},{4,20},{5,21},{6,22},{7,23},{8,24},{9,... | collective-permute-start | bytes 589832 | tf_op jit(solution)/shard_map/ppermute | solution.py:63
  624.3 28.9 %collective-permute-start.21 = (bf16[32,3072]{1,0:T(8,128)(2,1)S(1)}, bf16[32,3072]{1,0:T(8,128)(2,1)S(1)}, u32[]{:S(2)}, u32[]{:S(2)}) collective-permute-start(bf16[32,3072]{1,0:T(8,128)(2,1)S(1)} %get-tuple-element.80), channel_id=1, source_target_pairs={{0,8},{1,9},{2,10},{3,11},{4,12},{5,13},{6,14},{7,15},{8,0},{9,1},... | collective-permute-start | bytes 589832 | tf_op jit(solution)/shard_map/ppermute | solution.py:63
  625.0 29.0 %collective-permute-start.29 = (bf16[32,3072]{1,0:T(8,128)(2,1)S(1)}, bf16[32,3072]{1,0:T(8,128)(2,1)S(1)}, u32[]{:S(2)}, u32[]{:S(2)}) collective-permute-start(bf16[32,3072]{1,0:T(8,128)(2,1)S(1)} %get-tuple-element.78), channel_id=1, source_target_pairs={{0,24},{1,25},{2,26},{3,27},{4,28},{5,29},{6,30},{7,31},{8,16},{9,... | collective-permute-start | bytes 589832 | tf_op jit(solution)/shard_map/ppermute | solution.py:63
  627.5 36.1 %collective-permute-start.28 = (bf16[32,3072]{1,0:T(8,128)(2,1)S(1)}, bf16[32,3072]{1,0:T(8,128)(2,1)S(1)}, u32[]{:S(2)}, u32[]{:S(2)}) collective-permute-start(bf16[32,3072]{1,0:T(8,128)(2,1)S(1)} %get-tuple-element.79), channel_id=1, source_target_pairs={{0,16},{1,17},{2,18},{3,19},{4,20},{5,21},{6,22},{7,23},{8,24},{9,... | collective-permute-start | bytes 589832 | tf_op jit(solution)/shard_map/ppermute | solution.py:63
  629.6 33.9 %collective-permute-start.27 = (bf16[32,3072]{1,0:T(8,128)(2,1)S(1)}, bf16[32,3072]{1,0:T(8,128)(2,1)S(1)}, u32[]{:S(2)}, u32[]{:S(2)}) collective-permute-start(bf16[32,3072]{1,0:T(8,128)(2,1)S(1)} %get-tuple-element.77), channel_id=1, source_target_pairs={{0,8},{1,9},{2,10},{3,11},{4,12},{5,13},{6,14},{7,15},{8,0},{9,1},... | collective-permute-start | bytes 589832 | tf_op jit(solution)/shard_map/ppermute | solution.py:63
  650.9 13.5 %collective-permute-start.35 = (bf16[96,1024]{1,0:T(8,128)(2,1)S(1)}, bf16[96,1024]{1,0:T(8,128)(2,1)S(1)}, u32[]{:S(2)}, u32[]{:S(2)}) collective-permute-start(bf16[96,1024]{1,0:T(8,128)(2,1)S(1)} %get-tuple-element.75), channel_id=1, source_target_pairs={{0,24},{1,25},{2,26},{3,27},{4,28},{5,29},{6,30},{7,31},{8,16},{9,... | collective-permute-start | bytes 589832 | tf_op jit(solution)/shard_map/ppermute | solution.py:63
  653.1 17.0 %collective-permute-start.34 = (bf16[96,1024]{1,0:T(8,128)(2,1)S(1)}, bf16[96,1024]{1,0:T(8,128)(2,1)S(1)}, u32[]{:S(2)}, u32[]{:S(2)}) collective-permute-start(bf16[96,1024]{1,0:T(8,128)(2,1)S(1)} %get-tuple-element.76), channel_id=1, source_target_pairs={{0,16},{1,17},{2,18},{3,19},{4,20},{5,21},{6,22},{7,23},{8,24},{9,... | collective-permute-start | bytes 589832 | tf_op jit(solution)/shard_map/ppermute | solution.py:63
  654.0 16.2 %collective-permute-start.33 = (bf16[96,1024]{1,0:T(8,128)(2,1)S(1)}, bf16[96,1024]{1,0:T(8,128)(2,1)S(1)}, u32[]{:S(2)}, u32[]{:S(2)}) collective-permute-start(bf16[96,1024]{1,0:T(8,128)(2,1)S(1)} %get-tuple-element.74), channel_id=1, source_target_pairs={{0,8},{1,9},{2,10},{3,11},{4,12},{5,13},{6,14},{7,15},{8,0},{9,1},... | collective-permute-start | bytes 589832 | tf_op jit(solution)/shard_map/ppermute | solution.py:63
  (132 other events, 443.2 us)
Sparse Core Ops, SparseCore 0:
  11.5 81.1 all-gather.4
  96.1 85.3 all-gather.8
  185.0 94.4 all-gather.6

commit v2 on v1

v2 whole, which is shorter than its diff:
```python
import functools
import math

import jax
import jax.numpy as jnp
from jax import lax
from jax.experimental import pallas as pl
from jax.experimental.pallas import tpu as pltpu
from jax.sharding import PartitionSpec as P

QUERY_HEADS = 16
KEY_VALUE_HEADS = 8
HEAD_SIZE = 128


epsilon = 1e-06
rope_base = 1000000.0


def layout(seq_lengths, seq_owner, device, row_total_count):
    seq_index = jnp.arange(seq_lengths.shape[0], dtype=jnp.int32)
    same_owner = seq_owner[:, None] == seq_owner[None, :]
    before = seq_index[None, :] < seq_index[:, None]
    starts = jnp.sum(jnp.where(same_owner & before, seq_lengths[None, :], 0), axis=1)
    places = jnp.arange(row_total_count, dtype=jnp.int32)
    member = (
        (seq_owner[None, :] == device)
        & (starts[None, :] <= places[:, None])
        & (places[:, None] < (starts + seq_lengths)[None, :])
    )
    seq_id = jnp.sum(jnp.where(member, seq_index[None, :], 0), axis=1)
    token_position = jnp.sum(jnp.where(member, places[:, None] - starts[None, :], 0), axis=1)
    return (seq_id, token_position)


def rotation_factors(token_position):
    half_width = HEAD_SIZE // 2
    frequency = jnp.exp(
        jnp.arange(half_width, dtype=jnp.float32) * (-2.0 * math.log(rope_base) / HEAD_SIZE)
    )
    angles = token_position.astype(jnp.float32)[:, None] * frequency[None, :]
    cosine = jnp.cos(angles)
    sine = jnp.sin(angles)
    return jnp.concatenate([cosine, cosine], axis=1), jnp.concatenate([-sine, sine], axis=1)


def norm_forward(values, gain):
    inverse = lax.rsqrt(jnp.mean(values * values, axis=-1, keepdims=True) + epsilon)
    unit_rows = values * inverse
    return (unit_rows * gain, unit_rows, inverse)


def norm_backward(grad_out, unit_rows, inverse, gain, axes):
    grad_gain = jnp.sum(grad_out * unit_rows, axis=axes)
    scaled = grad_out * gain
    grad_in = inverse * (scaled - unit_rows * jnp.mean(scaled * unit_rows, axis=-1, keepdims=True))
    return (grad_in, grad_gain)


def exchange(values, count, mask):
    return lax.ppermute(values, "fsdp", [(source, source ^ mask) for source in range(count)])


def middle_bits(count, flip):
    bits = list(range(1, count.bit_length() - 3))
    return bits[::-1] if flip else bits


def row_order(count, flip):
    bits = count.bit_length() - 1
    sequence = [0] + middle_bits(count, flip)
    order = []
    for place_index in range(count):
        mask = (place_index & 3) << (bits - 2)
        for step, bit in enumerate(sequence):
            mask |= ((place_index >> (bits - 1 - step)) & 1) << bit
        order.append(mask)
    return order


def turn_body(device_ref, values_ref, out_ref, turned_ref, *, order):
    turned_ref[...] = values_ref[...].astype(turned_ref.dtype).T
    device = device_ref[0]
    rows = out_ref.shape[0] // len(order)
    group = max(1, 16 // rows)
    for first in range(0, len(order), group):
        blocks = [
            turned_ref[pl.ds(pl.multiple_of((device ^ mask) * rows, rows), rows), :]
            for mask in order[first : first + group]
        ]
        block = blocks[0] if group == 1 else jnp.concatenate(blocks, axis=0)
        out_ref[first * rows : (first + group) * rows, :] = block.astype(out_ref.dtype)


def turn(values, device, count, flip):
    rows, columns = values.shape
    held = jnp.bfloat16 if columns // count % 16 == 0 else jnp.float32
    return pl.pallas_call(
        functools.partial(turn_body, order=row_order(count, flip)),
        grid_spec=pltpu.PrefetchScalarGridSpec(
            num_scalar_prefetch=1,
            grid=(1,),
            in_specs=[pl.BlockSpec((rows, columns), lambda i, d: (0, 0))],
            out_specs=pl.BlockSpec((columns, rows), lambda i, d: (0, 0)),
            scratch_shapes=[pltpu.VMEM((columns, rows), held)],
        ),
        out_shape=jax.ShapeDtypeStruct((columns, rows), values.dtype),
        compiler_params=pltpu.CompilerParams(vmem_limit_bytes=40 * 1024 * 1024),
        name="turn",
    )(device.reshape(1), values)


def add_low(first, second):
    return (first.astype(jnp.float32) + second.astype(jnp.float32)).astype(jnp.bfloat16)


def product_low(left, right):
    return jnp.dot(left, right, preferred_element_type=jnp.float32).astype(jnp.bfloat16)


def sum_start(turned, right, count, extra=None):
    half = turned.shape[0] // 2
    sent = product_low(turned[half:], right)
    kept = product_low(turned[:half], right)
    if extra is not None:
        sent = jnp.concatenate([sent, extra[half:]], axis=1)
        kept = jnp.concatenate([kept, extra[:half]], axis=1)
    return (kept, exchange(sent, count, 1))


def sum_fold(pair, count, bits):
    for bit in bits:
        kept, came = pair
        half = kept.shape[0] // 2
        sent = add_low(kept[half:], came[half:])
        pair = (add_low(kept[:half], came[:half]), exchange(sent, count, 1 << bit))
    return pair


def sum_end(pair, count):
    kept, came = pair
    rows = kept.shape[0] // 4
    total = kept[:rows].astype(jnp.float32) + came[:rows].astype(jnp.float32)
    for step in (1, 2, 3):
        part = slice(step * rows, (step + 1) * rows)
        sent = add_low(kept[part], came[part])
        total = total + exchange(sent, count, step * (count // 4)).astype(jnp.float32)
    return total


def place_body(device_ref, *refs):
    parts = refs[:-2]
    out_ref, semaphores = refs[-2:]
    device = device_ref[0]
    copies = [
        pltpu.make_async_copy(part, out_ref.at[:, device ^ mask], semaphores.at[mask])
        for mask, part in enumerate(parts)
    ]
    for copy in copies:
        copy.start()
    for copy in copies:
        copy.wait()


def place(parts, inner):
    top, rows, columns = parts[0].shape
    return pl.pallas_call(
        place_body,
        grid_spec=pltpu.PrefetchScalarGridSpec(
            num_scalar_prefetch=1,
            grid=(1,),
            in_specs=[pl.BlockSpec(memory_space=pl.ANY)] * len(parts),
            out_specs=pl.BlockSpec((top, len(parts), rows, columns), lambda i, d: (0, 0, 0, 0)),
            scratch_shapes=[pltpu.SemaphoreType.DMA((len(parts),))],
        ),
        out_shape=jax.ShapeDtypeStruct((top, len(parts), rows, columns), parts[0].dtype),
        compiler_params=pltpu.CompilerParams(vmem_limit_bytes=40 * 1024 * 1024),
        name="place",
    )(inner.reshape(1), *parts).reshape(top * len(parts) * rows, columns)


def gather_rows(block, device, count, flip):
    quarter = count // 4
    tops = [block[None]] + [exchange(block, count, step * quarter)[None] for step in (1, 2, 3)]
    parts = {0: place(tops, device // quarter).reshape((4,) + block.shape)}
    for bit in middle_bits(count, flip) + [0]:
        for mask in list(parts):
            parts[mask | (1 << bit)] = exchange(parts[mask], count, 1 << bit)
    return place([parts[mask] for mask in range(quarter)], device & (quarter - 1))


def gain_columns(first, second, third, fourth, rows):
    columns = [jnp.pad(v, (0, rows - v.shape[0]))[:, None] for v in (first, second, third, fourth)]
    return jnp.pad(jnp.concatenate(columns, axis=1), ((0, 0), (0, 124)))


def swap_halves(head):
    return pltpu.roll(head, HEAD_SIZE // 2, 1)


def unit_head(raw):
    inverse = lax.rsqrt(jnp.mean(raw * raw, axis=-1, keepdims=True) + epsilon)
    return raw * inverse, inverse


def contract(left, right, left_axis, right_axis):
    return lax.dot_general(
        left, right, (((left_axis,), (right_axis,)), ((), ())), preferred_element_type=jnp.float32
    )


def block_scores(group, key_rows, first_row, row_start):
    scores = contract(group, key_rows, 1, 1) * (1.0 / math.sqrt(HEAD_SIZE))
    rows = lax.broadcasted_iota(jnp.int32, scores.shape, 0)
    half = scores.shape[0] // 2
    rows = jnp.where(rows >= half, rows - half, rows) + row_start
    columns = lax.broadcasted_iota(jnp.int32, scores.shape, 1)
    return jnp.where((columns <= rows) & (columns >= first_row), scores, -1e30)


def head_pair(ref, block):
    return jnp.concatenate([ref[block, :HEAD_SIZE], ref[block, HEAD_SIZE:]], axis=0)


def pair_rows(first_row_ref, block):
    rows = first_row_ref[block, :]
    return jnp.concatenate([rows, rows], axis=0)


def attend_body(
    normed_ref, wq_ref, wk_ref, wv_ref, gains_ref, cosine_ref, sine_ref, first_ref,
    attended_ref, query_ref, key_ref, value_ref, raw_query_ref, raw_key_ref, total_ref,
):
    normed = normed_ref[...]
    cosine = cosine_ref[...]
    sine = sine_ref[...]

    def turned(raw, gain):
        scaled = unit_head(raw)[0] * gain
        return (scaled * cosine + swap_halves(scaled) * sine).astype(jnp.bfloat16)

    raw_query = jnp.dot(normed, wq_ref[...], preferred_element_type=jnp.float32)
    raw_query_ref[...] = raw_query
    for head in range(2):
        part = slice(head * HEAD_SIZE, (head + 1) * HEAD_SIZE)
        query_ref[:, part] = turned(raw_query[:, part], gains_ref[0:1, :])
    raw_key = jnp.dot(normed, wk_ref[...], preferred_element_type=jnp.float32)
    raw_key_ref[...] = raw_key
    key_ref[...] = turned(raw_key, gains_ref[1:2, :])
    value_ref[...] = jnp.dot(normed, wv_ref[...], preferred_element_type=jnp.float32).astype(jnp.bfloat16)
    step = 128
    for start in range(0, normed.shape[0], step):
        block = slice(start, start + step)
        seen = slice(0, start + step)
        scores = block_scores(head_pair(query_ref, block), key_ref[seen, :], pair_rows(first_ref, block), start)
        top = jnp.max(scores, axis=-1, keepdims=True)
        log_total = top + jnp.log(jnp.sum(jnp.exp(scores - top), axis=-1, keepdims=True))
        probs_low = jnp.exp(scores - log_total).astype(jnp.bfloat16)
        out = jnp.dot(probs_low, value_ref[seen, :], preferred_element_type=jnp.float32).astype(jnp.bfloat16)
        attended_ref[block, :HEAD_SIZE] = out[:step]
        attended_ref[block, HEAD_SIZE:] = out[step:]
        total_ref[0, block, 0:1] = log_total[:step]
        total_ref[0, block, 1:2] = log_total[step:]


def attend(normed, query_weight, rest_weight, head_gains, cosine, sine, first_row):
    rows, width = normed.shape
    whole = lambda shape: pl.BlockSpec(shape, lambda h: (0, 0))
    columns = lambda size, shift: pl.BlockSpec((rows, size), lambda h: (0, h + shift))
    pair = 2 * HEAD_SIZE
    low = lambda size: jax.ShapeDtypeStruct((rows, size), jnp.bfloat16)
    full = lambda size: jax.ShapeDtypeStruct((rows, size), jnp.float32)
    return pl.pallas_call(
        attend_body,
        grid=(KEY_VALUE_HEADS,),
        in_specs=[
            whole((rows, width)),
            pl.BlockSpec((width, pair), lambda h: (0, h)),
            pl.BlockSpec((width, HEAD_SIZE), lambda h: (0, h)),
            pl.BlockSpec((width, HEAD_SIZE), lambda h: (0, h + KEY_VALUE_HEADS)),
            whole((2, HEAD_SIZE)),
            whole((rows, HEAD_SIZE)),
            whole((rows, HEAD_SIZE)),
            whole((rows, 1)),
        ],
        out_specs=[
            columns(pair, 0),
            columns(pair, 0),
            columns(HEAD_SIZE, 0),
            columns(HEAD_SIZE, 0),
            columns(pair, 0),
            columns(HEAD_SIZE, 0),
            pl.BlockSpec((1, rows, 2), lambda h: (h, 0, 0)),
        ],
        out_shape=[
            low(QUERY_HEADS * HEAD_SIZE),
            low(QUERY_HEADS * HEAD_SIZE),
            low(KEY_VALUE_HEADS * HEAD_SIZE),
            low(KEY_VALUE_HEADS * HEAD_SIZE),
            full(QUERY_HEADS * HEAD_SIZE),
            full(KEY_VALUE_HEADS * HEAD_SIZE),
            jax.ShapeDtypeStruct((KEY_VALUE_HEADS, rows, 2), jnp.float32),
        ],
        compiler_params=pltpu.CompilerParams(vmem_limit_bytes=40 * 1024 * 1024),
        cost_estimate=pl.CostEstimate(flops=10_000_000_000, bytes_accessed=20_000_000, transcendentals=4_000_000),
        name="attend",
    )(normed, query_weight, rest_weight, rest_weight, head_gains, cosine, sine, first_row)


def attend_back_body(
    residual_ref, wo_ref, query_ref, key_ref, value_ref, raw_query_ref, raw_key_ref, total_ref,
    gains_ref, cosine_ref, sine_ref, first_ref,
    grad_query_ref, grad_key_ref, grad_value_ref, grad_gains_ref,
    grad_out_ref, query_sum_ref, key_sum_ref, value_sum_ref,
):
    scale = 1.0 / math.sqrt(HEAD_SIZE)

    @pl.when(pl.program_id(0) == 0)
    def _():
        grad_gains_ref[...] = jnp.zeros_like(grad_gains_ref)

    grad_out_ref[...] = contract(residual_ref[...], wo_ref[...], 1, 1).astype(jnp.bfloat16)
    key_sum_ref[...] = jnp.zeros_like(key_sum_ref)
    value_sum_ref[...] = jnp.zeros_like(value_sum_ref)
    step = 128
    for start in range(0, residual_ref.shape[0], step):
        block = slice(start, start + step)
        seen = slice(0, start + step)
        group = head_pair(query_ref, block)
        grad_out = head_pair(grad_out_ref, block)
        key_rows = key_ref[seen, :]
        scores = block_scores(group, key_rows, pair_rows(first_ref, block), start)
        log_total = jnp.concatenate([total_ref[0, block, 0:1], total_ref[0, block, 1:2]], axis=0)
        probs = jnp.exp(scores - log_total)
        grad_probs = contract(grad_out, value_ref[seen, :], 1, 1)
        value_sum_ref[seen, :] += contract(probs.astype(jnp.bfloat16), grad_out, 0, 0)
        inner = jnp.sum(probs * grad_probs, axis=-1, keepdims=True)
        grad_scores = (probs * (grad_probs - inner)).astype(jnp.bfloat16)
        grad_group = jnp.dot(grad_scores, key_rows, preferred_element_type=jnp.float32) * scale
        query_sum_ref[block, :HEAD_SIZE] = grad_group[:step]
        query_sum_ref[block, HEAD_SIZE:] = grad_group[step:]
        key_sum_ref[seen, :] += contract(grad_scores, group, 0, 0)
    grad_value_ref[...] = value_sum_ref[...].astype(jnp.bfloat16)
    cosine = cosine_ref[...]
    sine = sine_ref[...]

    def back(grad, raw, gain):
        turned = grad * cosine - swap_halves(grad) * sine
        unit, inverse = unit_head(raw)
        product = turned * unit
        scaled = turned * gain
        grad_raw = inverse * (scaled - unit * jnp.mean(product * gain, axis=-1, keepdims=True))
        return grad_raw.astype(jnp.bfloat16), jnp.sum(product, axis=0, keepdims=True)

    for head in range(2):
        part = slice(head * HEAD_SIZE, (head + 1) * HEAD_SIZE)
        low, gain_sum = back(query_sum_ref[:, part], raw_query_ref[:, part], gains_ref[0:1, :])
        grad_query_ref[:, part] = low
        grad_gains_ref[0:1, :] += gain_sum
    low, gain_sum = back(key_sum_ref[...] * scale, raw_key_ref[...], gains_ref[1:2, :])
    grad_key_ref[...] = low
    grad_gains_ref[1:2, :] += gain_sum


def attend_back(residual_low, out_weight, saved, head_gains, cosine, sine, first_row):
    rows, width = residual_low.shape
    query, key, value, raw_query, raw_key, totals = saved
    whole = lambda shape: pl.BlockSpec(shape, lambda h: (0, 0))
    columns = lambda size: pl.BlockSpec((rows, size), lambda h: (0, h))
    pair = 2 * HEAD_SIZE
    low = lambda size: jax.ShapeDtypeStruct((rows, size), jnp.bfloat16)
    return pl.pallas_call(
        attend_back_body,
        grid=(KEY_VALUE_HEADS,),
        in_specs=[
            whole((rows, width)),
            pl.BlockSpec((pair, width), lambda h: (h, 0)),
            columns(pair),
            columns(HEAD_SIZE),
            columns(HEAD_SIZE),
            columns(pair),
            columns(HEAD_SIZE),
            pl.BlockSpec((1, rows, 2), lambda h: (h, 0, 0)),
            whole((2, HEAD_SIZE)),
            whole((rows, HEAD_SIZE)),
            whole((rows, HEAD_SIZE)),
            whole((rows, 1)),
        ],
        out_specs=[columns(pair), columns(HEAD_SIZE), columns(HEAD_SIZE), whole((2, HEAD_SIZE))],
        out_shape=[
            low(QUERY_HEADS * HEAD_SIZE),
            low(KEY_VALUE_HEADS * HEAD_SIZE),
            low(KEY_VALUE_HEADS * HEAD_SIZE),
            jax.ShapeDtypeStruct((2, HEAD_SIZE), jnp.float32),
        ],
        scratch_shapes=[
            pltpu.VMEM((rows, pair), jnp.bfloat16),
            pltpu.VMEM((rows, pair), jnp.float32),
            pltpu.VMEM((rows, HEAD_SIZE), jnp.float32),
            pltpu.VMEM((rows, HEAD_SIZE), jnp.float32),
        ],
        compiler_params=pltpu.CompilerParams(vmem_limit_bytes=40 * 1024 * 1024),
        cost_estimate=pl.CostEstimate(flops=16_000_000_000, bytes_accessed=20_000_000, transcendentals=4_000_000),
        name="attend_back",
    )(
        residual_low, out_weight, query, key, value, raw_query, raw_key, totals,
        head_gains, cosine, sine, first_row,
    )


def on_device(
    tokens,
    seq_lengths,
    seq_owner,
    g_attn,
    w_query,
    key_projection,
    value_projection,
    query_norm_gain,
    g_key,
    w_out,
    g_ffn,
    w_gate,
    w_up,
    w_down,
    cotangent,
):
    row_total_count = tokens.shape[0]
    seq_id, token_position = layout(seq_lengths, seq_owner, lax.axis_index("fsdp"), row_total_count)
    first_row = (jnp.arange(row_total_count, dtype=jnp.int32) - token_position)[:, None]
    cosine, sine = rotation_factors(token_position)
    inputs = tokens.astype(jnp.float32)
    count = lax.axis_size("fsdp")
    device = lax.axis_index("fsdp")
    shard = g_attn.shape[0]
    head_shard = query_norm_gain.shape[0]
    gains = gain_columns(g_attn, g_ffn, query_norm_gain, g_key, shard)
    query_weight = gather_rows(w_query, device, count, False)
    rest_weight = gather_rows(
        jnp.concatenate([key_projection, value_projection, gains], axis=1), device, count, True
    )
    out_weight = gather_rows(w_out, device, count, False)
    down_weight = gather_rows(w_down, device, count, True)
    gate_up = lax.all_gather(jnp.concatenate([w_gate, w_up], axis=1), "fsdp", axis=0, tiled=True)
    key_width = key_projection.shape[1]
    gain_block = rest_weight[:, 2 * key_width :].astype(jnp.float32)
    gain_one = gain_block[:, 0]
    gain_two = gain_block[:, 1]
    head_gains = gain_block.reshape(count, shard, 128)[:, :head_shard, 2:4].reshape(HEAD_SIZE, 2).T
    normed_in, unit_one, inverse_one = norm_forward(inputs, gain_one)
    normed_low = normed_in.astype(jnp.bfloat16)
    attended, *saved = attend(normed_low, query_weight, rest_weight, head_gains, cosine, sine, first_row)
    residual = inputs + jnp.dot(attended, out_weight, preferred_element_type=jnp.float32)
    normed_mid, unit_two, inverse_two = norm_forward(residual, gain_two)
    normed_two = normed_mid.astype(jnp.bfloat16)
    hidden_width = w_gate.shape[1]
    both_rows = jnp.dot(normed_two, gate_up, preferred_element_type=jnp.float32)
    gate_rows = both_rows[:, :hidden_width]
    up_rows = both_rows[:, hidden_width:]
    sigmoid_gate = jax.nn.sigmoid(gate_rows)
    silu_gate = gate_rows * sigmoid_gate
    hidden = (silu_gate * up_rows).astype(jnp.bfloat16)
    ffn_rows = jnp.dot(hidden, down_weight, preferred_element_type=jnp.float32)
    mixed = (residual + ffn_rows).astype(jnp.bfloat16)
    grad_out = cotangent.astype(jnp.float32)
    grad_hidden = jnp.einsum(
        "rd,fd->rf", cotangent, down_weight, preferred_element_type=jnp.float32
    )
    grad_gate = (
        grad_hidden * up_rows * sigmoid_gate * (1.0 + gate_rows * (1.0 - sigmoid_gate))
    ).astype(jnp.bfloat16)
    grad_up = (grad_hidden * silu_gate).astype(jnp.bfloat16)
    grad_both = jnp.concatenate([grad_gate, grad_up], axis=1)
    early = middle_bits(count, False)
    late = middle_bits(count, True)
    cut = len(early) // 2
    turned_two = turn(normed_two, device, count, False)
    sum_down = sum_start(turn(hidden, device, count, True), cotangent, count)
    sum_gate = sum_start(turned_two, grad_gate, count)
    grad_both, sum_down, sum_gate = lax.optimization_barrier((grad_both, sum_down, sum_gate))
    sum_up = sum_start(turned_two, grad_up, count)
    sum_down = sum_fold(sum_down, count, late[:cut])
    sum_gate = sum_fold(sum_gate, count, early[:cut])
    grad_normed_two = jnp.einsum("rf,df->rd", grad_both, gate_up, preferred_element_type=jnp.float32)
    grad_mid, grad_gain_two = norm_backward(grad_normed_two, unit_two, inverse_two, gain_two, (0,))
    grad_residual = grad_out + grad_mid
    grad_res_low = grad_residual.astype(jnp.bfloat16)
    sum_out = sum_start(turn(attended, device, count, True), grad_res_low, count)
    grad_res_tied, sum_down, sum_gate, sum_up, sum_out = lax.optimization_barrier(
        (grad_res_low, sum_down, sum_gate, sum_up, sum_out)
    )
    grad_query_low, grad_key_low, grad_value_low, grad_head_gains = attend_back(
        grad_res_tied, out_weight, saved, head_gains, cosine, sine, first_row
    )
    grad_gain_query = grad_head_gains[0]
    grad_gain_key = grad_head_gains[1]
    grad_rest_low = jnp.concatenate([grad_key_low, grad_value_low], axis=1)
    sum_down = sum_fold(sum_down, count, late[cut:])
    sum_gate = sum_fold(sum_gate, count, early[cut:])
    sum_up = sum_fold(sum_up, count, early[:cut])
    sum_out = sum_fold(sum_out, count, late[:cut])
    sum_down = sum_end(sum_down, count)
    sum_gate = sum_end(sum_gate, count)
    sum_up = sum_fold(sum_up, count, early[cut:])
    sum_out = sum_fold(sum_out, count, late[cut:])
    grad_query_low, grad_rest_low, sum_down, sum_gate, sum_up, sum_out = lax.optimization_barrier(
        (grad_query_low, grad_rest_low, sum_down, sum_gate, sum_up, sum_out)
    )
    sum_query = sum_start(turn(normed_low, device, count, False), grad_query_low, count)
    sum_up = sum_end(sum_up, count)
    sum_out = sum_end(sum_out, count)
    grad_normed = jnp.einsum("ra,da->rd", grad_query_low, query_weight, preferred_element_type=jnp.float32)
    grad_normed = grad_normed + jnp.einsum(
        "ra,da->rd", grad_rest_low, rest_weight[:, : 2 * key_width], preferred_element_type=jnp.float32
    )
    grad_first, grad_gain_one = norm_backward(grad_normed, unit_one, inverse_one, gain_one, (0,))
    grad_tokens = (grad_residual + grad_first).astype(jnp.bfloat16)
    head_pad = ((0, 0), (0, shard - head_shard))
    gain_grads = gain_columns(
        grad_gain_one,
        grad_gain_two,
        jnp.pad(grad_gain_query.reshape(count, head_shard), head_pad).reshape(-1),
        jnp.pad(grad_gain_key.reshape(count, head_shard), head_pad).reshape(-1),
        count * shard,
    )
    order = jnp.asarray(row_order(count, True), jnp.int32) ^ device
    gain_grads = gain_grads.astype(jnp.bfloat16).reshape(count, shard, 128)[order].reshape(count * shard, 128)
    sum_rest = sum_start(turn(normed_low, device, count, True), grad_rest_low, count, gain_grads)
    sum_query = sum_end(sum_fold(sum_query, count, early), count)
    sum_rest = sum_end(sum_fold(sum_rest, count, late), count)
    sum_gains = sum_rest[:, 2 * key_width :]
    return (
        mixed,
        grad_tokens,
        sum_gains[:, 0],
        sum_query,
        sum_rest[:, :key_width],
        sum_rest[:, key_width : 2 * key_width],
        sum_gains[:head_shard, 2],
        sum_gains[:head_shard, 3],
        sum_out,
        sum_gains[:, 1],
        sum_gate,
        sum_up,
        sum_down,
    )


def solution(mesh):
    return jax.shard_map(
        on_device,
        mesh=mesh,
        in_specs=(
            P("fsdp", None),
            P(),
            P(),
            P("fsdp"),
            P("fsdp", None),
            P("fsdp", None),
            P("fsdp", None),
            P("fsdp"),
            P("fsdp"),
            P("fsdp", None),
            P("fsdp"),
            P("fsdp", None),
            P("fsdp", None),
            P("fsdp", None),
            P("fsdp", None),
        ),
        out_specs=(
            P("fsdp", None),
            P("fsdp", None),
            P("fsdp"),
            P("fsdp", None),
            P("fsdp", None),
            P("fsdp", None),
            P("fsdp"),
            P("fsdp"),
            P("fsdp", None),
            P("fsdp"),
            P("fsdp", None),
            P("fsdp", None),
            P("fsdp", None),
        ),
        check_vma=False,
    )
```

time: 682 us -> 583 us (0.85)
  waiting for transfers between devices: 335 us -> 209 us
  starting transfers between devices: 53 us -> 108 us
  Pallas kernels: 0 us -> 53.6 us
  local copies, waits for them, and re-layouts: 81.5 us -> 39 us
  matrix products: 123 us -> 83.8 us
    all_gather x2 -> x0, waiting for transfers between devices: 121 us -> none  [the longest x1 77.1 us: on_device(): lax.all_gather(jnp.concatenate([w_query, key_projection, value_projection...]
    all_gather x1, waiting for transfers between devices: 82.7 us -> 0.01 us  [on_device(): lax.all_gather(jnp.concatenate([w_gate, w_up], axis=1), 'fsdp', axis=0, t...]
    ppermute x36 -> x76, waiting for transfers between devices: 132 us -> 209 us  [exchange(): lax.ppermute(values, 'fsdp', [(source, source ^ mask) for source in range...]
    ppermute x36 -> x76, starting transfers between devices: 52.8 us -> 108 us  [exchange(): lax.ppermute(values, 'fsdp', [(source, source ^ mask) for source in range...]
    pallas_call x0 -> x15, Pallas kernels: none -> 53.6 us  [the longest x1 21.8 us: attend_back(): pl.pallas_call(attend_back_body, grid=(KEY_VALUE_HEADS,), in_specs=[whole...]
    dot_general x55 -> x14, matrix products: 86.2 us -> 39.7 us  [the longest x12 34.1 us: product_low(): jnp.dot(left, right, preferred_element_type=jnp.float32)]
    convert_element_type x28 -> x23, other arithmetic: 23.6 us -> 40.8 us  [the longest x18 38.7 us: add_low(): (first.astype(jnp.float32) + second.astype(jnp.float32)).astype(jnp.bfloa...]
    dynamic_slice x10 -> x0, local copies, waits for them, and re-layouts: 16.3 us -> none  [the longest x5 8.85 us: scatter_sum(): kept = lax.dynamic_index_in_dim(held, mine, axis, keepdims=False)]
  transfers between devices with their start and end apart: 39 -> 77, of which waited for: 20 -> 23; matrix products, arithmetic and copies ran while one was open for 17% -> 20% of each run, Pallas kernels for 0% -> 9%
where the time goes in v2:
time: 583 us; the launch traced here: 573 us
  waiting for transfers between devices  209 us (36%)
  starting transfers between devices  108 us (19%)
  matrix products  83.8 us (14%)
  other arithmetic  64.2 us (11%)
  Pallas kernels  53.6 us (9%)
  local copies, waits for them, and re-layouts  39 us (7%)
  between operations  15.7 us (3%)
    ppermute x76, waiting for transfers between devices, exchange(): lax.ppermute(values, 'fsdp', [(source, source ^ mask) for source in range...  209 us
    ppermute x76, starting transfers between devices, exchange(): lax.ppermute(values, 'fsdp', [(source, source ^ mask) for source in range...  108 us
    convert_element_type x18, other arithmetic, add_low(): (first.astype(jnp.float32) + second.astype(jnp.float32)).astype(jnp.bfloa...  38.7 us
    dot_general x12, matrix products, product_low(): jnp.dot(left, right, preferred_element_type=jnp.float32)  34.1 us
    unnamed x190, local copies, waits for them, and re-layouts  30.5 us
    pallas_call x1, Pallas kernels, attend_back(): pl.pallas_call(attend_back_body, grid=(KEY_VALUE_HEADS,), in_specs=[whole...  21.8 us
    pallas_call x1, Pallas kernels, attend(): pl.pallas_call(attend_body, grid=(KEY_VALUE_HEADS,), in_specs=[whole((row...  20.8 us
    dot_general x1, matrix products, on_device(): jnp.einsum('rf,df->rd', grad_both, gate_up, preferred_element_type=jnp.fl...  19.4 us
  transfers between devices with their start and end apart: 77, of which 23 were waited for; matrix products, arithmetic and copies ran while one was open for 20% of the time, Pallas kernels for 9%

profile of v2, /device:TPU:0, one launch (start us, length us, event | category | flops | bytes accessed | tf_op | source)
XLA Modules:
  0.0 572.8 jit_solution(2953070813213636422)
XLA Ops:
  9.1 3.1 collective-permute-start.10
  15.7 3.5 collective-permute-start.21
  25.4 16.1 %collective-permute-start.1 = (bf16[32,2176]{1,0:T(8,128)(2,1)S(1)}, bf16[32,2176]{1,0:T(8,128)(2,1)S(1)}, u32[]{:S(2)}, u32[]{:S(2)}) collective-permute-start(bf16[32,2176]{1,0:T(8,128)(2,1)S(1)} %get-tuple-element.138), channel_id=1, source_target_pairs={{0,16},{1,17},{2,18},{3,19},{4,20},{5,21},{6,22},{7,23},{8,24},{9,... | collective-permute-start | bytes 417800 | tf_op jit(solution)/shard_map/ppermute | solution.py:61
  41.5 6.6 %collective-permute-done.21 = bf16[64,1024]{1,0:T(8,128)(2,1)S(1)} collective-permute-done((bf16[64,1024]{1,0:T(8,128)(2,1)}, bf16[64,1024]{1,0:T(8,128)(2,1)S(1)}, u32[]{:S(2)}, u32[]{:S(2)}) %collective-permute-start.21) | collective-permute-done | bytes 131104 | tf_op jit(solution)/shard_map/ppermute | solution.py:61
  52.4 19.2 %collective-permute-done.1 = bf16[32,2176]{1,0:T(8,128)(2,1)S(1)} collective-permute-done((bf16[32,2176]{1,0:T(8,128)(2,1)S(1)}, bf16[32,2176]{1,0:T(8,128)(2,1)S(1)}, u32[]{:S(2)}, u32[]{:S(2)}) %collective-permute-start.1) | collective-permute-done | bytes 139296 | tf_op jit(solution)/shard_map/ppermute | solution.py:61
  71.6 3.4 collective-permute-start.32
  78.8 6.1 %collective-permute-done.31 = bf16[96,1024]{1,0:T(8,128)(2,1)S(1)} collective-permute-done((bf16[96,1024]{1,0:T(8,128)(2,1)}, bf16[96,1024]{1,0:T(8,128)(2,1)S(1)}, u32[]{:S(2)}, u32[]{:S(2)}) %collective-permute-start.31) | collective-permute-done | bytes 196640 | tf_op jit(solution)/shard_map/ppermute | solution.py:61
  91.0 13.8 %collective-permute-done.24.refs_2_ = bf16[4,64,1024]{2,1,0:T(8,128)(2,1)S(1)} collective-permute-done((bf16[4,64,1024]{2,1,0:T(8,128)(2,1)S(1)}, bf16[4,64,1024]{2,1,0:T(8,128)(2,1)S(1)}, u32[]{:S(2)}, u32[]{:S(2)}) %collective-permute-start.24) | collective-permute-done | bytes 524320 | tf_op jit(solution)/shard_map/ppermute | solution.py:61
  109.2 19.1 %collective-permute-done.4.refs_2_ = bf16[4,32,2176]{2,1,0:T(8,128)(2,1)} collective-permute-done((bf16[4,32,2176]{2,1,0:T(8,128)(2,1)S(1)}, bf16[4,32,2176]{2,1,0:T(8,128)(2,1)}, u32[]{:S(2)}, u32[]{:S(2)}) %collective-permute-start.4) | collective-permute-done | bytes 557088 | tf_op jit(solution)/shard_map/ppermute | solution.py:61
  134.3 18.2 %collective-permute-done.36.refs_4_ = bf16[4,96,1024]{2,1,0:T(8,128)(2,1)S(1)} collective-permute-done((bf16[4,96,1024]{2,1,0:T(8,128)(2,1)S(1)}, bf16[4,96,1024]{2,1,0:T(8,128)(2,1)S(1)}, u32[]{:S(2)}, u32[]{:S(2)}) %collective-permute-start.36) | collective-permute-done | bytes 786464 | tf_op jit(solution)/shard_map/ppermute | solution.py:61
  155.9 7.7 %collective-permute-done.18.refs_6_ = bf16[4,32,2048]{2,1,0:T(8,128)(2,1)S(1)} collective-permute-done((bf16[4,32,2048]{2,1,0:T(8,128)(2,1)S(1)}, bf16[4,32,2048]{2,1,0:T(8,128)(2,1)S(1)}, u32[]{:S(2)}, u32[]{:S(2)}) %collective-permute-start.18) | collective-permute-done | bytes 524320 | tf_op jit(solution)/shard_map/ppermute | solution.py:61
  164.5 9.7 %collective-permute-done.28.refs_6_ = bf16[4,64,1024]{2,1,0:T(8,128)(2,1)S(1)} collective-permute-done((bf16[4,64,1024]{2,1,0:T(8,128)(2,1)S(1)}, bf16[4,64,1024]{2,1,0:T(8,128)(2,1)S(1)}, u32[]{:S(2)}, u32[]{:S(2)}) %collective-permute-start.28) | collective-permute-done | bytes 524320 | tf_op jit(solution)/shard_map/ppermute | solution.py:61
  198.2 15.0 %collective-permute-done.38.refs_6_ = bf16[4,96,1024]{2,1,0:T(8,128)(2,1)} collective-permute-done((bf16[4,96,1024]{2,1,0:T(8,128)(2,1)S(1)}, bf16[4,96,1024]{2,1,0:T(8,128)(2,1)}, u32[]{:S(2)}, u32[]{:S(2)}) %collective-permute-start.38) | collective-permute-done | bytes 786464 | tf_op jit(solution)/shard_map/ppermute | solution.py:61
  219.4 20.8 %attend.1 = (bf16[384,2048]{1,0:T(8,128)(2,1)S(1)}, bf16[384,2048]{1,0:T(8,128)(2,1)S(1)}, bf16[384,1024]{1,0:T(8,128)(2,1)S(1)}, bf16[384,1024]{1,0:T(8,128)(2,...) custom-call(bf16[384,1024]{1,0:T(8,128)(2,1)S(1)} %fusion.11.normed_ref.values_ref, ...), custom_call_target="tpu_custom_call" | custom-call | flops 10000000000 | bytes 20000000 | tf_op jit(solution)/shard_map/attend/pallas_call | solution.py:273
  251.0 12.1 %fusion.41 = f32[384,6144]{1,0:T(8,128)} fusion(bf16[384,1024]{1,0:T(8,128)(2,1)S(1)} %multiply_convert_fusion.1.values_ref, bf16[1024,6144]{1,0:T(8,128)(2,1)} %all-gather.2.cloned.1.call-done), kind=kOutput, calls=%fused_computation.157 | convolution fusion | flops 4831838208 | bytes 22806528 | tf_op jit(solution)/shard_map/dot_general | solution.py:457
  263.1 7.1 %fusion.2 = (bf16[384,3072]{1,0:T(8,128)(2,1)S(1)}, bf16[384,3072]{1,0:T(8,128)(2,1)S(1)}, bf16[384,3072]{1,0:T(8,128)(2,1)S(1)}) fusion(f32[384,6144]{1,0:T(8,128)} %fusion.41, bf16[3072,1024]{1,0:T(8,128)(2,1)S(1)} %bitcast.77, bf16[384,1024]{1,0:T(8,128)(2,1)S(1)} %copy-done.75), kind=kOutput, calls=%fused_computation.6 | convolution fusion | flops 2433613824 | bytes 23592960 | tf_op jit(solution)/shard_map/rd,fd->rf/dot_general | solution.py:466
  271.2 3.4 convolution_convert_fusion.4
  275.1 3.5 convolution_convert_fusion.2
  279.2 3.5 convolution_convert_fusion
  283.2 3.4 convolution_convert_fusion.5
  286.7 3.5 convolution_convert_fusion.3
  292.7 5.6 add_convert_fusion.4
  298.3 19.4 %multiply_reduce_fusion = (bf16[1024]{0:T(1024)(128)(2,1)S(1)}, f32[384]{0:T(512)S(1)}, f32[384,1024]{1,0:T(8,128)S(1)}) fusion(f32[384,1024]{1,0:T(8,128)S(1)} %copy-done.67, f32[384]{0:T(512)S(1)} %add_rsqrt_fusion, f32[1024]{0:T(1024)S(1)} %get-tuple-element.83, bf16[384,6144]{1,0:T(8,128)(2,1)} %pad_maximum_fusion, ...), kind=kOutput, calls=%fused_computation.56 | convolution fusion | flops 4834195968 | bytes 20456448 | tf_op jit(solution)/shard_map/rf,df->rd/dot_general | solution.py:484
  322.4 4.2 add_convert_fusion.2
  327.8 3.5 convolution_convert_fusion.1
  331.3 3.5 add_convert_fusion.18
  336.1 18.4 %collective-permute-done.42 = bf16[768,1024]{1,0:T(8,128)(2,1)} collective-permute-done((bf16[768,1024]{1,0:T(8,128)(2,1)}, bf16[768,1024]{1,0:T(8,128)(2,1)}, u32[]{:S(2)}, u32[]{:S(2)}) %collective-permute-start.42) | collective-permute-done | bytes 1572896 | tf_op jit(solution)/shard_map/ppermute | solution.py:61
  354.5 9.2 %collective-permute-done.43 = bf16[256,3072]{1,0:T(8,128)(2,1)} collective-permute-done((bf16[256,3072]{1,0:T(8,128)(2,1)}, bf16[256,3072]{1,0:T(8,128)(2,1)}, u32[]{:S(2)}, u32[]{:S(2)}) %collective-permute-start.43) | collective-permute-done | bytes 1572896 | tf_op jit(solution)/shard_map/ppermute | solution.py:61
  363.7 3.3 add_convert_fusion.17
  367.6 3.1 add_convert_fusion.15
  371.3 4.8 add_convert_fusion.1
  377.7 4.2 add_convert_fusion.11
  383.4 21.8 %attend_back.1 = (bf16[384,2048]{1,0:T(8,128)(2,1)S(1)}, bf16[384,1024]{1,0:T(8,128)(2,1)S(1)}, bf16[384,1024]{1,0:T(8,128)(2,1)S(1)}, f32[2,128]{1,0:T(2,128)S(1)}) custom-call(bf16[384,1024]{1,0:T(8,128)(2,1)S(1)} %fusion.39.residual_ref, bf16[2048,1024]{1,0:T(8,128)(2,1)} %bitcast.87, bf16[384,2048]{1,0:T(8,128)(2,1)S(1)} %copy-done.57, ...), custom_call_target="tpu_custom_call" | custom-call | flops 16000000000 | bytes 20000000 | tf_op jit(solution)/shard_map/attend_back/pallas_call | solution.py:372
  409.7 3.4 collective-permute-start.49
  413.1 10.9 %collective-permute-start.48 = (bf16[96,1024]{1,0:T(8,128)(2,1)S(1)}, bf16[96,1024]{1,0:T(8,128)(2,1)S(1)}, u32[]{:S(2)}, u32[]{:S(2)}) collective-permute-start(bf16[96,1024]{1,0:T(8,128)(2,1)S(1)} %get-tuple-element.126), channel_id=1, source_target_pairs={{0,16},{1,17},{2,18},{3,19},{4,20},{5,21},{6,22},{7,23},{8,24},{9,... | collective-permute-start | bytes 589832 | tf_op jit(solution)/shard_map/ppermute | solution.py:61
  428.2 14.2 %collective-permute-done.48 = bf16[96,1024]{1,0:T(8,128)(2,1)S(1)} collective-permute-done((bf16[96,1024]{1,0:T(8,128)(2,1)S(1)}, bf16[96,1024]{1,0:T(8,128)(2,1)S(1)}, u32[]{:S(2)}, u32[]{:S(2)}) %collective-permute-start.48) | collective-permute-done | bytes 196640 | tf_op jit(solution)/shard_map/ppermute | solution.py:61
  442.4 4.6 collective-permute-start.51
  456.0 8.8 %collective-permute-done.57 = bf16[256,1024]{1,0:T(8,128)(2,1)S(1)} collective-permute-done((bf16[256,1024]{1,0:T(8,128)(2,1)S(1)}, bf16[256,1024]{1,0:T(8,128)(2,1)S(1)}, u32[]{:S(2)}, u32[]{:S(2)}) %collective-permute-start.57) | collective-permute-done | bytes 524320 | tf_op jit(solution)/shard_map/ppermute | solution.py:61
  464.8 2.9 collective-permute-done.55
  471.4 3.8 fusion.17
  478.4 2.8 convolution_convert_fusion.8
  506.6 2.9 collective-permute-start.73
  511.3 12.9 %collective-permute-done.65 = bf16[256,2048]{1,0:T(8,128)(2,1)S(1)} collective-permute-done((bf16[256,2048]{1,0:T(8,128)(2,1)S(1)}, bf16[256,2048]{1,0:T(8,128)(2,1)S(1)}, u32[]{:S(2)}, u32[]{:S(2)}) %collective-permute-start.65) | collective-permute-done | bytes 1048608 | tf_op jit(solution)/shard_map/ppermute | solution.py:61
  525.2 4.8 collective-permute-done.59
  533.1 6.2 %collective-permute-done.66 = bf16[128,2048]{1,0:T(8,128)(2,1)S(1)} collective-permute-done((bf16[128,2048]{1,0:T(8,128)(2,1)S(1)}, bf16[128,2048]{1,0:T(8,128)(2,1)S(1)}, u32[]{:S(2)}, u32[]{:S(2)}) %collective-permute-start.66) | collective-permute-done | bytes 524320 | tf_op jit(solution)/shard_map/ppermute | solution.py:61
  547.7 6.5 %collective-permute-start.61 = (bf16[32,2176]{1,0:T(8,128)(2,1)S(1)}, bf16[32,2176]{1,0:T(8,128)(2,1)S(1)}, u32[]{:S(2)}, u32[]{:S(2)}) collective-permute-start(bf16[32,2176]{1,0:T(8,128)(2,1)S(1)} %get-tuple-element.127), channel_id=1, source_target_pairs={{0,8},{1,9},{2,10},{3,11},{4,12},{5,13},{6,14},{7,15},{8,0},{9,1},... | collective-permute-start | bytes 417800 | tf_op jit(solution)/shard_map/ppermute | solution.py:61
  554.2 5.0 collective-permute-done.68
  560.1 3.2 collective-permute-done.62
  (408 shorter events, 164.2 us)
Async XLA Ops:
  7.2 243.8 %all-gather.2.cloned.1.call-start = ((), (), s32[]{:S(2)}) async-start(), calls=%async_computation | async-start | bytes 12976128 | tf_op jit(solution)/shard_map/all_gather | solution.py:444
  14.8 26.6 %collective-permute-start.20 = (bf16[64,1024]{1,0:T(8,128)(2,1)}, bf16[64,1024]{1,0:T(8,128)(2,1)S(1)}, u32[]{:S(2)}, u32[]{:S(2)}) collective-permute-start(bf16[64,1024]{1,0:T(8,128)(2,1)} %param.25), channel_id=1, source_target_pairs={{0,8},{1,9},{2,10},{3,11},{4,12},{5,13},{6,14},{7,15},{8,0},{9,1},... | collective-permute-start | bytes 393224 | tf_op jit(solution)/shard_map/ppermute | solution.py:61
  15.7 32.3 %collective-permute-start.21 = (bf16[64,1024]{1,0:T(8,128)(2,1)}, bf16[64,1024]{1,0:T(8,128)(2,1)S(1)}, u32[]{:S(2)}, u32[]{:S(2)}) collective-permute-start(bf16[64,1024]{1,0:T(8,128)(2,1)} %param.25), channel_id=1, source_target_pairs={{0,16},{1,17},{2,18},{3,19},{4,20},{5,21},{6,22},{7,23},{8,24},{9,... | collective-permute-start | bytes 393224 | tf_op jit(solution)/shard_map/ppermute | solution.py:61
  20.7 29.0 %collective-permute-start.22 = (bf16[64,1024]{1,0:T(8,128)(2,1)}, bf16[64,1024]{1,0:T(8,128)(2,1)S(1)}, u32[]{:S(2)}, u32[]{:S(2)}) collective-permute-start(bf16[64,1024]{1,0:T(8,128)(2,1)} %param.25), channel_id=1, source_target_pairs={{0,24},{1,25},{2,26},{3,27},{4,28},{5,29},{6,30},{7,31},{8,16},{9,... | collective-permute-start | bytes 393224 | tf_op jit(solution)/shard_map/ppermute | solution.py:61
  25.4 24.4 %collective-permute-start = (bf16[32,2176]{1,0:T(8,128)(2,1)S(1)}, bf16[32,2176]{1,0:T(8,128)(2,1)S(1)}, u32[]{:S(2)}, u32[]{:S(2)}) collective-permute-start(bf16[32,2176]{1,0:T(8,128)(2,1)S(1)} %get-tuple-element.138), channel_id=1, source_target_pairs={{0,8},{1,9},{2,10},{3,11},{4,12},{5,13},{6,14},{7,15},{8,0},{9,1},... | collective-permute-start | bytes 417800 | tf_op jit(solution)/shard_map/ppermute | solution.py:61
  25.4 46.2 %collective-permute-start.1 = (bf16[32,2176]{1,0:T(8,128)(2,1)S(1)}, bf16[32,2176]{1,0:T(8,128)(2,1)S(1)}, u32[]{:S(2)}, u32[]{:S(2)}) collective-permute-start(bf16[32,2176]{1,0:T(8,128)(2,1)S(1)} %get-tuple-element.138), channel_id=1, source_target_pairs={{0,16},{1,17},{2,18},{3,19},{4,20},{5,21},{6,22},{7,23},{8,24},{9,... | collective-permute-start | bytes 417800 | tf_op jit(solution)/shard_map/ppermute | solution.py:61
  41.5 35.8 %collective-permute-start.30 = (bf16[96,1024]{1,0:T(8,128)(2,1)}, bf16[96,1024]{1,0:T(8,128)(2,1)S(1)}, u32[]{:S(2)}, u32[]{:S(2)}) collective-permute-start(bf16[96,1024]{1,0:T(8,128)(2,1)} %param.29), channel_id=1, source_target_pairs={{0,8},{1,9},{2,10},{3,11},{4,12},{5,13},{6,14},{7,15},{8,0},{9,1},... | collective-permute-start | bytes 589832 | tf_op jit(solution)/shard_map/ppermute | solution.py:61
  48.0 36.9 %collective-permute-start.31 = (bf16[96,1024]{1,0:T(8,128)(2,1)}, bf16[96,1024]{1,0:T(8,128)(2,1)S(1)}, u32[]{:S(2)}, u32[]{:S(2)}) collective-permute-start(bf16[96,1024]{1,0:T(8,128)(2,1)} %param.29), channel_id=1, source_target_pairs={{0,16},{1,17},{2,18},{3,19},{4,20},{5,21},{6,22},{7,23},{8,24},{9,... | collective-permute-start | bytes 589832 | tf_op jit(solution)/shard_map/ppermute | solution.py:61
  49.7 36.8 %collective-permute-start.13 = (bf16[4,32,2048]{2,1,0:T(8,128)(2,1)S(1)}, bf16[4,32,2048]{2,1,0:T(8,128)(2,1)S(1)}, u32[]{:S(2)}, u32[]{:S(2)}) collective-permute-start(bf16[4,32,2048]{2,1,0:T(8,128)(2,1)S(1)} %bitcast.97), channel_id=1, source_target_pairs={{0,1},{1,0},{2,3},{3,2},{4,5},{5,4},{6,7},{7,6},{8,9},{9,8},{10,11... | collective-permute-start | bytes 1572872 | tf_op jit(solution)/shard_map/ppermute | solution.py:61
  49.7 25.9 %collective-permute-start.2 = (bf16[32,2176]{1,0:T(8,128)(2,1)S(1)}, bf16[32,2176]{1,0:T(8,128)(2,1)S(1)}, u32[]{:S(2)}, u32[]{:S(2)}) collective-permute-start(bf16[32,2176]{1,0:T(8,128)(2,1)S(1)} %get-tuple-element.138), channel_id=1, source_target_pairs={{0,24},{1,25},{2,26},{3,27},{4,28},{5,29},{6,30},{7,31},{8,16},{9,... | collective-permute-start | bytes 417800 | tf_op jit(solution)/shard_map/ppermute | solution.py:61
  84.9 19.9 %collective-permute-start.24 = (bf16[4,64,1024]{2,1,0:T(8,128)(2,1)S(1)}, bf16[4,64,1024]{2,1,0:T(8,128)(2,1)S(1)}, u32[]{:S(2)}, u32[]{:S(2)}) collective-permute-start(bf16[4,64,1024]{2,1,0:T(8,128)(2,1)S(1)} %bitcast.102), channel_id=1, source_target_pairs={{0,2},{1,3},{2,0},{3,1},{4,6},{5,7},{6,4},{7,5},{8,10},{9,11},{10,... | collective-permute-start | bytes 1572872 | tf_op jit(solution)/shard_map/ppermute | solution.py:61
  86.4 21.4 %collective-permute-start.26 = (bf16[4,64,1024]{2,1,0:T(8,128)(2,1)S(1)}, bf16[4,64,1024]{2,1,0:T(8,128)(2,1)S(1)}, u32[]{:S(2)}, u32[]{:S(2)}) collective-permute-start(bf16[4,64,1024]{2,1,0:T(8,128)(2,1)S(1)} %bitcast.103), channel_id=1, source_target_pairs={{0,4},{1,5},{2,6},{3,7},{4,0},{5,1},{6,2},{7,3},{8,12},{9,13},{10,... | collective-permute-start | bytes 1572872 | tf_op jit(solution)/shard_map/ppermute | solution.py:61
  88.7 19.1 %collective-permute-start.3 = (bf16[4,32,2176]{2,1,0:T(8,128)(2,1)S(1)}, bf16[4,32,2176]{2,1,0:T(8,128)(2,1)S(1)}, u32[]{:S(2)}, u32[]{:S(2)}) collective-permute-start(bf16[4,32,2176]{2,1,0:T(8,128)(2,1)S(1)} %bitcast.93), channel_id=1, source_target_pairs={{0,1},{1,0},{2,3},{3,2},{4,5},{5,4},{6,7},{7,6},{8,9},{9,8},{10,11... | collective-permute-start | bytes 1671176 | tf_op jit(solution)/shard_map/ppermute | solution.py:61
  88.8 39.5 %collective-permute-start.4 = (bf16[4,32,2176]{2,1,0:T(8,128)(2,1)S(1)}, bf16[4,32,2176]{2,1,0:T(8,128)(2,1)}, u32[]{:S(2)}, u32[]{:S(2)}) collective-permute-start(bf16[4,32,2176]{2,1,0:T(8,128)(2,1)S(1)} %bitcast.94), channel_id=1, source_target_pairs={{0,2},{1,3},{2,0},{3,1},{4,6},{5,7},{6,4},{7,5},{8,10},{9,11},{10,... | collective-permute-start | bytes 1671176 | tf_op jit(solution)/shard_map/ppermute | solution.py:61
  89.4 42.3 %collective-permute-start.6 = (bf16[4,32,2176]{2,1,0:T(8,128)(2,1)S(1)}, bf16[4,32,2176]{2,1,0:T(8,128)(2,1)}, u32[]{:S(2)}, u32[]{:S(2)}) collective-permute-start(bf16[4,32,2176]{2,1,0:T(8,128)(2,1)S(1)} %bitcast.95), channel_id=1, source_target_pairs={{0,4},{1,5},{2,6},{3,7},{4,0},{5,1},{6,2},{7,3},{8,12},{9,13},{10,... | collective-permute-start | bytes 1671176 | tf_op jit(solution)/shard_map/ppermute | solution.py:61
  104.8 47.7 %collective-permute-start.36 = (bf16[4,96,1024]{2,1,0:T(8,128)(2,1)S(1)}, bf16[4,96,1024]{2,1,0:T(8,128)(2,1)S(1)}, u32[]{:S(2)}, u32[]{:S(2)}) collective-permute-start(bf16[4,96,1024]{2,1,0:T(8,128)(2,1)S(1)} %bitcast.89), channel_id=1, source_target_pairs={{0,4},{1,5},{2,6},{3,7},{4,0},{5,1},{6,2},{7,3},{8,12},{9,13},{10,... | collective-permute-start | bytes 2359304 | tf_op jit(solution)/shard_map/ppermute | solution.py:61
  107.8 45.4 %collective-permute-start.15 = (bf16[4,32,2048]{2,1,0:T(8,128)(2,1)S(1)}, bf16[4,32,2048]{2,1,0:T(8,128)(2,1)S(1)}, u32[]{:S(2)}, u32[]{:S(2)}) collective-permute-start(bf16[4,32,2048]{2,1,0:T(8,128)(2,1)S(1)} %collective-permute-done.14.refs_2_), channel_id=1, source_target_pairs={{0,1},{1,0},{2,3},{3,2},{4,5},{5,4},{6,7},{7,6},{8,9},{9,8},{10,11... | collective-permute-start | bytes 1572872 | tf_op jit(solution)/shard_map/ppermute | solution.py:61
  108.6 46.7 %collective-permute-start.17 = (bf16[4,32,2048]{2,1,0:T(8,128)(2,1)S(1)}, bf16[4,32,2048]{2,1,0:T(8,128)(2,1)S(1)}, u32[]{:S(2)}, u32[]{:S(2)}) collective-permute-start(bf16[4,32,2048]{2,1,0:T(8,128)(2,1)S(1)} %collective-permute-done.16.refs_4_), channel_id=1, source_target_pairs={{0,1},{1,0},{2,3},{3,2},{4,5},{5,4},{6,7},{7,6},{8,9},{9,8},{10,11... | collective-permute-start | bytes 1572872 | tf_op jit(solution)/shard_map/ppermute | solution.py:61
  128.3 35.4 %collective-permute-start.18 = (bf16[4,32,2048]{2,1,0:T(8,128)(2,1)S(1)}, bf16[4,32,2048]{2,1,0:T(8,128)(2,1)S(1)}, u32[]{:S(2)}, u32[]{:S(2)}) collective-permute-start(bf16[4,32,2048]{2,1,0:T(8,128)(2,1)S(1)} %collective-permute-done.14.refs_2_), channel_id=1, source_target_pairs={{0,4},{1,5},{2,6},{3,7},{4,0},{5,1},{6,2},{7,3},{8,12},{9,13},{10,... | collective-permute-start | bytes 1572872 | tf_op jit(solution)/shard_map/ppermute | solution.py:61
  131.7 42.5 %collective-permute-start.28 = (bf16[4,64,1024]{2,1,0:T(8,128)(2,1)S(1)}, bf16[4,64,1024]{2,1,0:T(8,128)(2,1)S(1)}, u32[]{:S(2)}, u32[]{:S(2)}) collective-permute-start(bf16[4,64,1024]{2,1,0:T(8,128)(2,1)S(1)} %collective-permute-done.24.refs_2_), channel_id=1, source_target_pairs={{0,4},{1,5},{2,6},{3,7},{4,0},{5,1},{6,2},{7,3},{8,12},{9,13},{10,... | collective-permute-start | bytes 1572872 | tf_op jit(solution)/shard_map/ppermute | solution.py:61
  152.5 22.9 %collective-permute-start.25 = (bf16[4,64,1024]{2,1,0:T(8,128)(2,1)S(1)}, bf16[4,64,1024]{2,1,0:T(8,128)(2,1)S(1)}, u32[]{:S(2)}, u32[]{:S(2)}) collective-permute-start(bf16[4,64,1024]{2,1,0:T(8,128)(2,1)S(1)} %collective-permute-done.24.refs_2_), channel_id=1, source_target_pairs={{0,1},{1,0},{2,3},{3,2},{4,5},{5,4},{6,7},{7,6},{8,9},{9,8},{10,11... | collective-permute-start | bytes 1572872 | tf_op jit(solution)/shard_map/ppermute | solution.py:61
  154.1 22.6 %collective-permute-start.27 = (bf16[4,64,1024]{2,1,0:T(8,128)(2,1)S(1)}, bf16[4,64,1024]{2,1,0:T(8,128)(2,1)S(1)}, u32[]{:S(2)}, u32[]{:S(2)}) collective-permute-start(bf16[4,64,1024]{2,1,0:T(8,128)(2,1)S(1)} %collective-permute-done.26.refs_4_), channel_id=1, source_target_pairs={{0,1},{1,0},{2,3},{3,2},{4,5},{5,4},{6,7},{7,6},{8,9},{9,8},{10,11... | collective-permute-start | bytes 1572872 | tf_op jit(solution)/shard_map/ppermute | solution.py:61
  155.4 25.2 %collective-permute-start.8 = (bf16[4,32,2176]{2,1,0:T(8,128)(2,1)}, bf16[4,32,2176]{2,1,0:T(8,128)(2,1)}, u32[]{:S(2)}, u32[]{:S(2)}) collective-permute-start(bf16[4,32,2176]{2,1,0:T(8,128)(2,1)} %collective-permute-done.6.refs_4_), channel_id=1, source_target_pairs={{0,2},{1,3},{2,0},{3,1},{4,6},{5,7},{6,4},{7,5},{8,10},{9,11},{10,... | collective-permute-start | bytes 1671176 | tf_op jit(solution)/shard_map/ppermute | solution.py:61
  176.2 20.9 %collective-permute-start.34 = (bf16[4,96,1024]{2,1,0:T(8,128)(2,1)S(1)}, bf16[4,96,1024]{2,1,0:T(8,128)(2,1)}, u32[]{:S(2)}, u32[]{:S(2)}) collective-permute-start(bf16[4,96,1024]{2,1,0:T(8,128)(2,1)S(1)} %bitcast.90), channel_id=1, source_target_pairs={{0,2},{1,3},{2,0},{3,1},{4,6},{5,7},{6,4},{7,5},{8,10},{9,11},{10,... | collective-permute-start | bytes 2359304 | tf_op jit(solution)/shard_map/ppermute | solution.py:61
  177.5 35.6 %collective-permute-start.38 = (bf16[4,96,1024]{2,1,0:T(8,128)(2,1)S(1)}, bf16[4,96,1024]{2,1,0:T(8,128)(2,1)}, u32[]{:S(2)}, u32[]{:S(2)}) collective-permute-start(bf16[4,96,1024]{2,1,0:T(8,128)(2,1)S(1)} %collective-permute-done.36.refs_4_), channel_id=1, source_target_pairs={{0,2},{1,3},{2,0},{3,1},{4,6},{5,7},{6,4},{7,5},{8,10},{9,11},{10,... | collective-permute-start | bytes 2359304 | tf_op jit(solution)/shard_map/ppermute | solution.py:61
  182.7 30.4 %collective-permute-start.9 = (bf16[4,32,2176]{2,1,0:T(8,128)(2,1)}, bf16[4,32,2176]{2,1,0:T(8,128)(2,1)}, u32[]{:S(2)}, u32[]{:S(2)}) collective-permute-start(bf16[4,32,2176]{2,1,0:T(8,128)(2,1)} %collective-permute-done.8.refs_6_), channel_id=1, source_target_pairs={{0,1},{1,0},{2,3},{3,2},{4,5},{5,4},{6,7},{7,6},{8,9},{9,8},{10,11... | collective-permute-start | bytes 1671176 | tf_op jit(solution)/shard_map/ppermute | solution.py:61
  197.1 48.7 %collective-permute-start.33 = (bf16[4,96,1024]{2,1,0:T(8,128)(2,1)S(1)}, bf16[4,96,1024]{2,1,0:T(8,128)(2,1)}, u32[]{:S(2)}, u32[]{:S(2)}) collective-permute-start(bf16[4,96,1024]{2,1,0:T(8,128)(2,1)S(1)} %bitcast.91), channel_id=1, source_target_pairs={{0,1},{1,0},{2,3},{3,2},{4,5},{5,4},{6,7},{7,6},{8,9},{9,8},{10,11... | collective-permute-start | bytes 2359304 | tf_op jit(solution)/shard_map/ppermute | solution.py:61
  197.6 48.2 %collective-permute-start.37 = (bf16[4,96,1024]{2,1,0:T(8,128)(2,1)S(1)}, bf16[4,96,1024]{2,1,0:T(8,128)(2,1)}, u32[]{:S(2)}, u32[]{:S(2)}) collective-permute-start(bf16[4,96,1024]{2,1,0:T(8,128)(2,1)S(1)} %collective-permute-done.36.refs_4_), channel_id=1, source_target_pairs={{0,1},{1,0},{2,3},{3,2},{4,5},{5,4},{6,7},{7,6},{8,9},{9,8},{10,11... | collective-permute-start | bytes 2359304 | tf_op jit(solution)/shard_map/ppermute | solution.py:61
  197.7 48.1 %collective-permute-start.35 = (bf16[4,96,1024]{2,1,0:T(8,128)(2,1)}, bf16[4,96,1024]{2,1,0:T(8,128)(2,1)}, u32[]{:S(2)}, u32[]{:S(2)}) collective-permute-start(bf16[4,96,1024]{2,1,0:T(8,128)(2,1)} %collective-permute-done.34.refs_2_), channel_id=1, source_target_pairs={{0,1},{1,0},{2,3},{3,2},{4,5},{5,4},{6,7},{7,6},{8,9},{9,8},{10,11... | collective-permute-start | bytes 2359304 | tf_op jit(solution)/shard_map/ppermute | solution.py:61
  213.1 32.7 %collective-permute-start.39 = (bf16[4,96,1024]{2,1,0:T(8,128)(2,1)}, bf16[4,96,1024]{2,1,0:T(8,128)(2,1)}, u32[]{:S(2)}, u32[]{:S(2)}) collective-permute-start(bf16[4,96,1024]{2,1,0:T(8,128)(2,1)} %collective-permute-done.38.refs_6_), channel_id=1, source_target_pairs={{0,1},{1,0},{2,3},{3,2},{4,5},{5,4},{6,7},{7,6},{8,9},{9,8},{10,11... | collective-permute-start | bytes 2359304 | tf_op jit(solution)/shard_map/ppermute | solution.py:61
  282.7 53.3 %collective-permute-start.44 = (bf16[512,3072]{1,0:T(8,128)(2,1)}, bf16[512,3072]{1,0:T(8,128)(2,1)}, u32[]{:S(2)}, u32[]{:S(2)}) collective-permute-start(bf16[512,3072]{1,0:T(8,128)(2,1)} %convolution_convert_fusion), channel_id=1, source_target_pairs={{0,1},{1,0},{2,3},{3,2},{4,5},{5,4},{6,7},{7,6},{8,9},{9,8},{10,11... | collective-permute-start | bytes 9437192 | tf_op jit(solution)/shard_map/ppermute | solution.py:61
  317.8 36.7 %collective-permute-start.42 = (bf16[768,1024]{1,0:T(8,128)(2,1)}, bf16[768,1024]{1,0:T(8,128)(2,1)}, u32[]{:S(2)}, u32[]{:S(2)}) collective-permute-start(bf16[768,1024]{1,0:T(8,128)(2,1)} %get-tuple-element.98), channel_id=1, source_target_pairs={{0,4},{1,5},{2,6},{3,7},{4,0},{5,1},{6,2},{7,3},{8,12},{9,13},{10,... | collective-permute-start | bytes 4718600 | tf_op jit(solution)/shard_map/ppermute | solution.py:61
  322.4 41.3 %collective-permute-start.45 = (bf16[1024,1024]{1,0:T(8,128)(2,1)}, bf16[1024,1024]{1,0:T(8,128)(2,1)}, u32[]{:S(2)}, u32[]{:S(2)}) collective-permute-start(bf16[1024,1024]{1,0:T(8,128)(2,1)} %convolution_convert_fusion.10), channel_id=1, source_target_pairs={{0,1},{1,0},{2,3},{3,2},{4,5},{5,4},{6,7},{7,6},{8,9},{9,8},{10,11... | collective-permute-start | bytes 6291464 | tf_op jit(solution)/shard_map/ppermute | solution.py:61
  326.6 37.1 %collective-permute-start.43 = (bf16[256,3072]{1,0:T(8,128)(2,1)}, bf16[256,3072]{1,0:T(8,128)(2,1)}, u32[]{:S(2)}, u32[]{:S(2)}) collective-permute-start(bf16[256,3072]{1,0:T(8,128)(2,1)} %get-tuple-element.96), channel_id=1, source_target_pairs={{0,2},{1,3},{2,0},{3,1},{4,6},{5,7},{6,4},{7,5},{8,10},{9,11},{10,... | collective-permute-start | bytes 4718600 | tf_op jit(solution)/shard_map/ppermute | solution.py:61
  367.0 40.0 %collective-permute-start.46 = (bf16[384,1024]{1,0:T(8,128)(2,1)}, bf16[384,1024]{1,0:T(8,128)(2,1)}, u32[]{:S(2)}, u32[]{:S(2)}) collective-permute-start(bf16[384,1024]{1,0:T(8,128)(2,1)} %get-tuple-element.111), channel_id=1, source_target_pairs={{0,2},{1,3},{2,0},{3,1},{4,6},{5,7},{6,4},{7,5},{8,10},{9,11},{10,... | collective-permute-start | bytes 2359304 | tf_op jit(solution)/shard_map/ppermute | solution.py:61
  370.7 53.4 %collective-permute-start.50 = (bf16[128,3072]{1,0:T(8,128)(2,1)}, bf16[128,3072]{1,0:T(8,128)(2,1)}, u32[]{:S(2)}, u32[]{:S(2)}) collective-permute-start(bf16[128,3072]{1,0:T(8,128)(2,1)} %get-tuple-element.109), channel_id=1, source_target_pairs={{0,4},{1,5},{2,6},{3,7},{4,0},{5,1},{6,2},{7,3},{8,12},{9,13},{10,... | collective-permute-start | bytes 2359304 | tf_op jit(solution)/shard_map/ppermute | solution.py:61
  376.2 72.7 %collective-permute-start.54 = (bf16[256,3072]{1,0:T(8,128)(2,1)}, bf16[256,3072]{1,0:T(8,128)(2,1)}, u32[]{:S(2)}, u32[]{:S(2)}) collective-permute-start(bf16[256,3072]{1,0:T(8,128)(2,1)} %get-tuple-element.95), channel_id=1, source_target_pairs={{0,2},{1,3},{2,0},{3,1},{4,6},{5,7},{6,4},{7,5},{8,10},{9,11},{10,... | collective-permute-start | bytes 4718600 | tf_op jit(solution)/shard_map/ppermute | solution.py:61
  381.9 69.6 %collective-permute-start.56 = (bf16[512,1024]{1,0:T(8,128)(2,1)}, bf16[512,1024]{1,0:T(8,128)(2,1)}, u32[]{:S(2)}, u32[]{:S(2)}) collective-permute-start(bf16[512,1024]{1,0:T(8,128)(2,1)} %get-tuple-element.105), channel_id=1, source_target_pairs={{0,4},{1,5},{2,6},{3,7},{4,0},{5,1},{6,2},{7,3},{8,12},{9,13},{10,... | collective-permute-start | bytes 3145736 | tf_op jit(solution)/shard_map/ppermute | solution.py:61
  413.1 29.3 %collective-permute-start.48 = (bf16[96,1024]{1,0:T(8,128)(2,1)S(1)}, bf16[96,1024]{1,0:T(8,128)(2,1)S(1)}, u32[]{:S(2)}, u32[]{:S(2)}) collective-permute-start(bf16[96,1024]{1,0:T(8,128)(2,1)S(1)} %get-tuple-element.126), channel_id=1, source_target_pairs={{0,16},{1,17},{2,18},{3,19},{4,20},{5,21},{6,22},{7,23},{8,24},{9,... | collective-permute-start | bytes 589832 | tf_op jit(solution)/shard_map/ppermute | solution.py:61
  424.1 18.4 %collective-permute-start.47 = (bf16[96,1024]{1,0:T(8,128)(2,1)S(1)}, bf16[96,1024]{1,0:T(8,128)(2,1)S(1)}, u32[]{:S(2)}, u32[]{:S(2)}) collective-permute-start(bf16[96,1024]{1,0:T(8,128)(2,1)S(1)} %get-tuple-element.124), channel_id=1, source_target_pairs={{0,8},{1,9},{2,10},{3,11},{4,12},{5,13},{6,14},{7,15},{8,0},{9,1},... | collective-permute-start | bytes 589832 | tf_op jit(solution)/shard_map/ppermute | solution.py:61
  425.8 28.4 %collective-permute-start.53 = (bf16[32,3072]{1,0:T(8,128)(2,1)S(1)}, bf16[32,3072]{1,0:T(8,128)(2,1)S(1)}, u32[]{:S(2)}, u32[]{:S(2)}) collective-permute-start(bf16[32,3072]{1,0:T(8,128)(2,1)S(1)} %get-tuple-element.122), channel_id=1, source_target_pairs={{0,24},{1,25},{2,26},{3,27},{4,28},{5,29},{6,30},{7,31},{8,16},{9,... | collective-permute-start | bytes 589832 | tf_op jit(solution)/shard_map/ppermute | solution.py:61
  499.7 24.6 %collective-permute-start.65 = (bf16[256,2048]{1,0:T(8,128)(2,1)S(1)}, bf16[256,2048]{1,0:T(8,128)(2,1)S(1)}, u32[]{:S(2)}, u32[]{:S(2)}) collective-permute-start(bf16[256,2048]{1,0:T(8,128)(2,1)S(1)} %get-tuple-element.103), channel_id=1, source_target_pairs={{0,2},{1,3},{2,0},{3,1},{4,6},{5,7},{6,4},{7,5},{8,10},{9,11},{10,... | collective-permute-start | bytes 3145736 | tf_op jit(solution)/shard_map/ppermute | solution.py:61
  502.5 27.6 %collective-permute-start.59 = (bf16[256,2176]{1,0:T(8,128)(2,1)S(1)}, bf16[256,2176]{1,0:T(8,128)(2,1)S(1)}, u32[]{:S(2)}, u32[]{:S(2)}) collective-permute-start(bf16[256,2176]{1,0:T(8,128)(2,1)S(1)} %get-tuple-element.101), channel_id=1, source_target_pairs={{0,4},{1,5},{2,6},{3,7},{4,0},{5,1},{6,2},{7,3},{8,12},{9,13},{10,... | collective-permute-start | bytes 3342344 | tf_op jit(solution)/shard_map/ppermute | solution.py:61
  505.2 27.1 %collective-permute-start.75 = (bf16[32,3072]{1,0:T(8,128)(2,1)S(1)}, bf16[32,3072]{1,0:T(8,128)(2,1)S(1)}, u32[]{:S(2)}, u32[]{:S(2)}) collective-permute-start(bf16[32,3072]{1,0:T(8,128)(2,1)S(1)} %get-tuple-element.119), channel_id=1, source_target_pairs={{0,24},{1,25},{2,26},{3,27},{4,28},{5,29},{6,30},{7,31},{8,16},{9,... | collective-permute-start | bytes 589832 | tf_op jit(solution)/shard_map/ppermute | solution.py:61
  505.2 27.0 %collective-permute-start.74 = (bf16[32,3072]{1,0:T(8,128)(2,1)S(1)}, bf16[32,3072]{1,0:T(8,128)(2,1)S(1)}, u32[]{:S(2)}, u32[]{:S(2)}) collective-permute-start(bf16[32,3072]{1,0:T(8,128)(2,1)S(1)} %get-tuple-element.120), channel_id=1, source_target_pairs={{0,16},{1,17},{2,18},{3,19},{4,20},{5,21},{6,22},{7,23},{8,24},{9,... | collective-permute-start | bytes 589832 | tf_op jit(solution)/shard_map/ppermute | solution.py:61
  506.6 25.6 %collective-permute-start.73 = (bf16[32,3072]{1,0:T(8,128)(2,1)S(1)}, bf16[32,3072]{1,0:T(8,128)(2,1)S(1)}, u32[]{:S(2)}, u32[]{:S(2)}) collective-permute-start(bf16[32,3072]{1,0:T(8,128)(2,1)S(1)} %get-tuple-element.118), channel_id=1, source_target_pairs={{0,8},{1,9},{2,10},{3,11},{4,12},{5,13},{6,14},{7,15},{8,0},{9,1},... | collective-permute-start | bytes 589832 | tf_op jit(solution)/shard_map/ppermute | solution.py:61
  539.8 19.5 %collective-permute-start.68 = (bf16[32,2048]{1,0:T(8,128)(2,1)S(1)}, bf16[32,2048]{1,0:T(8,128)(2,1)S(1)}, u32[]{:S(2)}, u32[]{:S(2)}) collective-permute-start(bf16[32,2048]{1,0:T(8,128)(2,1)S(1)} %get-tuple-element.135), channel_id=1, source_target_pairs={{0,16},{1,17},{2,18},{3,19},{4,20},{5,21},{6,22},{7,23},{8,24},{9,... | collective-permute-start | bytes 393224 | tf_op jit(solution)/shard_map/ppermute | solution.py:61
  544.4 18.9 %collective-permute-start.62 = (bf16[32,2176]{1,0:T(8,128)(2,1)S(1)}, bf16[32,2176]{1,0:T(8,128)(2,1)S(1)}, u32[]{:S(2)}, u32[]{:S(2)}) collective-permute-start(bf16[32,2176]{1,0:T(8,128)(2,1)S(1)} %get-tuple-element.129), channel_id=1, source_target_pairs={{0,16},{1,17},{2,18},{3,19},{4,20},{5,21},{6,22},{7,23},{8,24},{9,... | collective-permute-start | bytes 417800 | tf_op jit(solution)/shard_map/ppermute | solution.py:61
  (124 other events, 1597.6 us)
Sparse Core Ops, SparseCore 0:
  11.5 145.7 all-gather.1

commit v3 on v2

v3 whole, which is shorter than its diff:
```python
import functools
import math

import jax
import jax.numpy as jnp
from jax import lax
from jax.experimental import pallas as pl
from jax.experimental.pallas import tpu as pltpu
from jax.sharding import PartitionSpec as P

QUERY_HEADS = 16
KEY_VALUE_HEADS = 8
HEAD_SIZE = 128


SMALL = pl.CostEstimate(flops=1, bytes_accessed=1, transcendentals=0)

epsilon = 1e-06
rope_base = 1000000.0


def layout(seq_lengths, seq_owner, device, row_total_count):
    seq_index = jnp.arange(seq_lengths.shape[0], dtype=jnp.int32)
    same_owner = seq_owner[:, None] == seq_owner[None, :]
    before = seq_index[None, :] < seq_index[:, None]
    starts = jnp.sum(jnp.where(same_owner & before, seq_lengths[None, :], 0), axis=1)
    places = jnp.arange(row_total_count, dtype=jnp.int32)
    member = (
        (seq_owner[None, :] == device)
        & (starts[None, :] <= places[:, None])
        & (places[:, None] < (starts + seq_lengths)[None, :])
    )
    seq_id = jnp.sum(jnp.where(member, seq_index[None, :], 0), axis=1)
    token_position = jnp.sum(jnp.where(member, places[:, None] - starts[None, :], 0), axis=1)
    return (seq_id, token_position)


def rotation_factors(token_position):
    half_width = HEAD_SIZE // 2
    frequency = jnp.exp(
        jnp.arange(half_width, dtype=jnp.float32) * (-2.0 * math.log(rope_base) / HEAD_SIZE)
    )
    angles = token_position.astype(jnp.float32)[:, None] * frequency[None, :]
    cosine = jnp.cos(angles)
    sine = jnp.sin(angles)
    return jnp.concatenate([cosine, cosine], axis=1), jnp.concatenate([-sine, sine], axis=1)


def norm_forward(values, gain):
    inverse = lax.rsqrt(jnp.mean(values * values, axis=-1, keepdims=True) + epsilon)
    unit_rows = values * inverse
    return (unit_rows * gain, unit_rows, inverse)


def exchange(values, count, mask):
    return lax.ppermute(values, "fsdp", [(source, source ^ mask) for source in range(count)])


def middle_bits(count, flip):
    bits = list(range(1, count.bit_length() - 3))
    return bits[::-1] if flip else bits


def sum_bits(count, flip, top_early=False):
    bits = count.bit_length() - 1
    middle = middle_bits(count, flip)
    top = [bits - 2, bits - 1]
    return [0, middle[0]] + top + middle[1:] if top_early else [0] + middle + top


def row_order(count, sequence):
    bits = len(sequence)
    return [
        sum(((index >> (bits - 1 - step)) & 1) << bit for step, bit in enumerate(sequence)) for index in range(count)
    ]


def turn_body(device_ref, values_ref, out_ref, turned_ref, *, order):
    turned_ref[...] = values_ref[...].astype(turned_ref.dtype).T
    device = device_ref[0]
    rows = out_ref.shape[0] // len(order)
    group = max(1, 16 // rows)
    for first in range(0, len(order), group):
        blocks = [
            turned_ref[pl.ds(pl.multiple_of((device ^ mask) * rows, rows), rows), :]
            for mask in order[first : first + group]
        ]
        block = blocks[0] if group == 1 else jnp.concatenate(blocks, axis=0)
        out_ref[first * rows : (first + group) * rows, :] = block.astype(out_ref.dtype)


def turn(values, device, order):
    count = len(order)
    rows, columns = values.shape
    held = jnp.bfloat16 if columns // count % 16 == 0 else jnp.float32
    return pl.pallas_call(
        functools.partial(turn_body, order=order),
        grid_spec=pltpu.PrefetchScalarGridSpec(
            num_scalar_prefetch=1,
            grid=(1,),
            in_specs=[pl.BlockSpec((rows, columns), lambda i, d: (0, 0))],
            out_specs=pl.BlockSpec((columns, rows), lambda i, d: (0, 0)),
            scratch_shapes=[pltpu.VMEM((columns, rows), held)],
        ),
        out_shape=jax.ShapeDtypeStruct((columns, rows), values.dtype),
        compiler_params=pltpu.CompilerParams(vmem_limit_bytes=40 * 1024 * 1024),
        cost_estimate=SMALL,
        name="turn",
    )(device.reshape(1), values)


def add_body(first_ref, second_ref, out_ref):
    out_ref[...] = (first_ref[...].astype(jnp.float32) + second_ref[...].astype(jnp.float32)).astype(out_ref.dtype)


def add_half(first, second, half):
    rows, columns = first.shape[0] // 2, first.shape[1]
    steps = next(n for n in (4, 2, 1) if rows % (16 * n) == 0 or n == 1)
    spec = lambda shift: pl.BlockSpec((rows // steps, columns), lambda i: (i + shift, 0))
    return pl.pallas_call(
        add_body,
        grid=(steps,),
        in_specs=[spec(half * steps), spec(half * steps)],
        out_specs=spec(0),
        out_shape=jax.ShapeDtypeStruct((rows, columns), jnp.bfloat16),
        compiler_params=pltpu.CompilerParams(vmem_limit_bytes=40 * 1024 * 1024),
        cost_estimate=SMALL,
        name="add_half",
    )(first, second)


def product_body(left_ref, right_ref, out_ref):
    out_ref[...] = jnp.dot(left_ref[...], right_ref[...], preferred_element_type=jnp.float32).astype(jnp.bfloat16)


def product_half(left, right, half=None):
    rows, depth = left.shape
    if half is not None:
        rows //= 2
    columns = right.shape[1]
    row_tile, column_tile = min(rows, 512), min(columns, 512)
    shift = half * (rows // row_tile) if half else 0
    return pl.pallas_call(
        product_body,
        grid=(rows // row_tile, columns // column_tile),
        in_specs=[
            pl.BlockSpec((row_tile, depth), lambda i, j: (i + shift, 0)),
            pl.BlockSpec((depth, column_tile), lambda i, j: (0, j)),
        ],
        out_specs=pl.BlockSpec((row_tile, column_tile), lambda i, j: (i, j)),
        out_shape=jax.ShapeDtypeStruct((rows, columns), jnp.bfloat16),
        compiler_params=pltpu.CompilerParams(vmem_limit_bytes=40 * 1024 * 1024),
        cost_estimate=SMALL,
        name="product",
    )(left, right)


def sum_end(pair):
    return pair[0].astype(jnp.float32) + pair[1].astype(jnp.float32)


def place_body(device_ref, *refs):
    parts = refs[:-2]
    out_ref, semaphores = refs[-2:]
    device = device_ref[0]
    copies = [
        pltpu.make_async_copy(part, out_ref.at[:, device ^ mask], semaphores.at[mask])
        for mask, part in enumerate(parts)
    ]
    for copy in copies:
        copy.start()
    for copy in copies:
        copy.wait()


def place(parts, inner):
    top, rows, columns = parts[0].shape
    return pl.pallas_call(
        place_body,
        grid_spec=pltpu.PrefetchScalarGridSpec(
            num_scalar_prefetch=1,
            grid=(1,),
            in_specs=[pl.BlockSpec(memory_space=pl.ANY)] * len(parts),
            out_specs=pl.BlockSpec((top, len(parts), rows, columns), lambda i, d: (0, 0, 0, 0)),
            scratch_shapes=[pltpu.SemaphoreType.DMA((len(parts),))],
        ),
        out_shape=jax.ShapeDtypeStruct((top, len(parts), rows, columns), parts[0].dtype),
        compiler_params=pltpu.CompilerParams(vmem_limit_bytes=40 * 1024 * 1024),
        cost_estimate=SMALL,
        name="place",
    )(inner.reshape(1), *parts).reshape(top * len(parts) * rows, columns)


def gather_top(block, count):
    return [block[None]] + [exchange(block, count, step * (count // 4))[None] for step in (1, 2, 3)]


def lay_top(blocks, device, count):
    return {0: place(blocks, device // (count // 4)).reshape((4,) + blocks[0].shape[1:])}


def split_body(device_ref, *refs):
    parts = refs[:4]
    left_ref, right_ref, semaphores = refs[4:]
    width = left_ref.shape[-1]
    copies = []
    for mask, part in enumerate(parts):
        target = device_ref[0] ^ mask
        copies += [
            pltpu.make_async_copy(part.at[:, :width], left_ref.at[target], semaphores.at[2 * mask]),
            pltpu.make_async_copy(part.at[:, width:], right_ref.at[target], semaphores.at[2 * mask + 1]),
        ]
    for copy in copies:
        copy.start()
    for copy in copies:
        copy.wait()


def lay_top_split(blocks, device, count, width):
    rows, columns = blocks[0].shape[1:]
    shapes = [(4, rows, width), (4, rows, columns - width)]
    return pl.pallas_call(
        split_body,
        grid_spec=pltpu.PrefetchScalarGridSpec(
            num_scalar_prefetch=1,
            grid=(1,),
            in_specs=[pl.BlockSpec(memory_space=pl.ANY)] * 4,
            out_specs=[pl.BlockSpec(shape, lambda i, d: (0, 0, 0)) for shape in shapes],
            scratch_shapes=[pltpu.SemaphoreType.DMA((8,))],
        ),
        out_shape=[jax.ShapeDtypeStruct(shape, blocks[0].dtype) for shape in shapes],
        compiler_params=pltpu.CompilerParams(vmem_limit_bytes=40 * 1024 * 1024),
        cost_estimate=SMALL,
        name="lay_top_split",
    )((device // (count // 4)).reshape(1), *[block[0] for block in blocks])


def gather_bits(parts, count, bits):
    parts = dict(parts)
    for bit in bits:
        for mask in list(parts):
            parts[mask | (1 << bit)] = exchange(parts[mask], count, 1 << bit)
    return parts


def lay(parts, device, count):
    return place([parts[mask] for mask in range(count // 4)], device & (count // 4 - 1))


def gain_columns(first, second, third, fourth, rows):
    columns = [jnp.pad(v, (0, rows - v.shape[0]))[:, None] for v in (first, second, third, fourth)]
    return jnp.pad(jnp.concatenate(columns, axis=1), ((0, 0), (0, 124)))


def swap_halves(head):
    return pltpu.roll(head, HEAD_SIZE // 2, 1)


def unit_head(raw):
    inverse = lax.rsqrt(jnp.mean(raw * raw, axis=-1, keepdims=True) + epsilon)
    return raw * inverse, inverse


def contract(left, right, left_axis, right_axis):
    return lax.dot_general(
        left, right, (((left_axis,), (right_axis,)), ((), ())), preferred_element_type=jnp.float32
    )


def block_scores(group, key_rows, first_row, row_start):
    scores = contract(group, key_rows, 1, 1) * (1.0 / math.sqrt(HEAD_SIZE))
    rows = lax.broadcasted_iota(jnp.int32, scores.shape, 0)
    half = scores.shape[0] // 2
    rows = jnp.where(rows >= half, rows - half, rows) + row_start
    columns = lax.broadcasted_iota(jnp.int32, scores.shape, 1)
    return jnp.where((columns <= rows) & (columns >= first_row), scores, -1e30)


def head_pair(ref, block):
    return jnp.concatenate([ref[block, :HEAD_SIZE], ref[block, HEAD_SIZE:]], axis=0)


def pair_rows(first_row_ref, block):
    rows = first_row_ref[block, :]
    return jnp.concatenate([rows, rows], axis=0)


def attend_body(
    normed_ref, wq_ref, wk_ref, wv_ref, gains_ref, cosine_ref, sine_ref, first_ref,
    attended_ref, query_ref, key_ref, value_ref, raw_query_ref, raw_key_ref, total_ref,
):
    normed = normed_ref[...]
    cosine = cosine_ref[...]
    sine = sine_ref[...]

    def turned(raw, gain):
        scaled = unit_head(raw)[0] * gain
        return (scaled * cosine + swap_halves(scaled) * sine).astype(jnp.bfloat16)

    raw_query = jnp.dot(normed, wq_ref[...], preferred_element_type=jnp.float32)
    raw_query_ref[...] = raw_query
    for head in range(2):
        part = slice(head * HEAD_SIZE, (head + 1) * HEAD_SIZE)
        query_ref[:, part] = turned(raw_query[:, part], gains_ref[0:1, :])
    raw_key = jnp.dot(normed, wk_ref[...], preferred_element_type=jnp.float32)
    raw_key_ref[...] = raw_key
    key_ref[...] = turned(raw_key, gains_ref[1:2, :])
    value_ref[...] = jnp.dot(normed, wv_ref[...], preferred_element_type=jnp.float32).astype(jnp.bfloat16)
    step = 128
    for start in range(0, normed.shape[0], step):
        block = slice(start, start + step)
        seen = slice(0, start + step)
        scores = block_scores(head_pair(query_ref, block), key_ref[seen, :], pair_rows(first_ref, block), start)
        top = jnp.max(scores, axis=-1, keepdims=True)
        log_total = top + jnp.log(jnp.sum(jnp.exp(scores - top), axis=-1, keepdims=True))
        probs_low = jnp.exp(scores - log_total).astype(jnp.bfloat16)
        out = jnp.dot(probs_low, value_ref[seen, :], preferred_element_type=jnp.float32).astype(jnp.bfloat16)
        attended_ref[block, :HEAD_SIZE] = out[:step]
        attended_ref[block, HEAD_SIZE:] = out[step:]
        total_ref[0, block, 0:1] = log_total[:step]
        total_ref[0, block, 1:2] = log_total[step:]


def attend(normed, query_weight, rest_weight, head_gains, cosine, sine, first_row):
    rows, width = normed.shape
    whole = lambda shape: pl.BlockSpec(shape, lambda h: (0, 0))
    columns = lambda size, shift: pl.BlockSpec((rows, size), lambda h: (0, h + shift))
    pair = 2 * HEAD_SIZE
    low = lambda size: jax.ShapeDtypeStruct((rows, size), jnp.bfloat16)
    full = lambda size: jax.ShapeDtypeStruct((rows, size), jnp.float32)
    return pl.pallas_call(
        attend_body,
        grid=(KEY_VALUE_HEADS,),
        in_specs=[
            whole((rows, width)),
            pl.BlockSpec((width, pair), lambda h: (0, h)),
            pl.BlockSpec((width, HEAD_SIZE), lambda h: (0, h)),
            pl.BlockSpec((width, HEAD_SIZE), lambda h: (0, h + KEY_VALUE_HEADS)),
            whole((2, HEAD_SIZE)),
            whole((rows, HEAD_SIZE)),
            whole((rows, HEAD_SIZE)),
            whole((rows, 1)),
        ],
        out_specs=[
            columns(pair, 0),
            columns(pair, 0),
            columns(HEAD_SIZE, 0),
            columns(HEAD_SIZE, 0),
            columns(pair, 0),
            columns(HEAD_SIZE, 0),
            pl.BlockSpec((1, rows, 2), lambda h: (h, 0, 0)),
        ],
        out_shape=[
            low(QUERY_HEADS * HEAD_SIZE),
            low(QUERY_HEADS * HEAD_SIZE),
            low(KEY_VALUE_HEADS * HEAD_SIZE),
            low(KEY_VALUE_HEADS * HEAD_SIZE),
            full(QUERY_HEADS * HEAD_SIZE),
            full(KEY_VALUE_HEADS * HEAD_SIZE),
            jax.ShapeDtypeStruct((KEY_VALUE_HEADS, rows, 2), jnp.float32),
        ],
        compiler_params=pltpu.CompilerParams(vmem_limit_bytes=40 * 1024 * 1024),
        cost_estimate=SMALL,
        name="attend",
    )(normed, query_weight, rest_weight, rest_weight, head_gains, cosine, sine, first_row)


def attend_back_body(
    device_ref, residual_ref, wo_ref, query_ref, key_ref, value_ref, raw_query_ref, raw_key_ref, total_ref,
    gains_ref, cosine_ref, sine_ref, first_ref, turned_query_ref, turned_rest_ref, wq_ref, wk_ref, wv_ref,
    tokens_ref, gain_ref, grad_residual_ref, gain_two_ref,
    query_kept_ref, query_sent_ref, rest_kept_ref, rest_sent_ref, tokens_out_ref,
    grad_out_ref, query_sum_ref, key_sum_ref, value_sum_ref, grad_query_ref, head_gains_ref, normed_sum_ref, lines_ref,
    *, order, shard, head_shard,
):
    scale = 1.0 / math.sqrt(HEAD_SIZE)
    head = pl.program_id(0)

    @pl.when(head == 0)
    def _():
        head_gains_ref[...] = jnp.zeros_like(head_gains_ref)
        normed_sum_ref[...] = jnp.zeros_like(normed_sum_ref)

    grad_out_ref[...] = contract(residual_ref[...], wo_ref[...], 1, 1).astype(jnp.bfloat16)
    key_sum_ref[...] = jnp.zeros_like(key_sum_ref)
    value_sum_ref[...] = jnp.zeros_like(value_sum_ref)
    step = 128
    for start in range(0, residual_ref.shape[0], step):
        block = slice(start, start + step)
        seen = slice(0, start + step)
        group = head_pair(query_ref, block)
        grad_out = head_pair(grad_out_ref, block)
        key_rows = key_ref[seen, :]
        scores = block_scores(group, key_rows, pair_rows(first_ref, block), start)
        log_total = jnp.concatenate([total_ref[0, block, 0:1], total_ref[0, block, 1:2]], axis=0)
        probs = jnp.exp(scores - log_total)
        grad_probs = contract(grad_out, value_ref[seen, :], 1, 1)
        value_sum_ref[seen, :] += contract(probs.astype(jnp.bfloat16), grad_out, 0, 0)
        inner = jnp.sum(probs * grad_probs, axis=-1, keepdims=True)
        grad_scores = (probs * (grad_probs - inner)).astype(jnp.bfloat16)
        grad_group = jnp.dot(grad_scores, key_rows, preferred_element_type=jnp.float32) * scale
        query_sum_ref[block, :HEAD_SIZE] = grad_group[:step]
        query_sum_ref[block, HEAD_SIZE:] = grad_group[step:]
        key_sum_ref[seen, :] += contract(grad_scores, group, 0, 0)
    grad_value = value_sum_ref[...].astype(jnp.bfloat16)
    cosine = cosine_ref[...]
    sine = sine_ref[...]

    def back(grad, raw, gain):
        turned = grad * cosine - swap_halves(grad) * sine
        unit, inverse = unit_head(raw)
        product = turned * unit
        scaled = turned * gain
        grad_raw = inverse * (scaled - unit * jnp.mean(product * gain, axis=-1, keepdims=True))
        return grad_raw.astype(jnp.bfloat16), jnp.sum(product, axis=0, keepdims=True)

    for index in range(2):
        part = slice(index * HEAD_SIZE, (index + 1) * HEAD_SIZE)
        low, gain_sum = back(query_sum_ref[:, part], raw_query_ref[:, part], gains_ref[0:1, :])
        grad_query_ref[:, part] = low
        head_gains_ref[0:1, :] += gain_sum
    grad_key, gain_sum = back(key_sum_ref[...] * scale, raw_key_ref[...], gains_ref[1:2, :])
    head_gains_ref[1:2, :] += gain_sum
    grad_query = grad_query_ref[...]

    half = turned_query_ref.shape[0] // 2
    product = jnp.dot(turned_query_ref[...], grad_query, preferred_element_type=jnp.float32).astype(jnp.bfloat16)
    query_kept_ref[...] = product[:half]
    query_sent_ref[...] = product[half:]
    turned_rest = turned_rest_ref[...]
    for grad, shift in ((grad_key, 0), (grad_value, KEY_VALUE_HEADS)):
        product = jnp.dot(turned_rest, grad, preferred_element_type=jnp.float32).astype(jnp.bfloat16)
        columns = pl.ds(pl.multiple_of((head + shift) * HEAD_SIZE, HEAD_SIZE), HEAD_SIZE)
        rest_kept_ref[:, columns] = product[:half]
        rest_sent_ref[:, columns] = product[half:]
    normed_sum_ref[...] += (
        contract(grad_query, wq_ref[...], 1, 1)
        + contract(grad_key, wk_ref[...], 1, 1)
        + contract(grad_value, wv_ref[...], 1, 1)
    )

    @pl.when(head == pl.num_programs(0) - 1)
    def _():
        unit, inverse = unit_head(tokens_ref[...].astype(jnp.float32))
        grad = normed_sum_ref[...]
        scaled = grad * gain_ref[...]
        grad_first = inverse * (scaled - unit * jnp.mean(scaled * unit, axis=-1, keepdims=True))
        tokens_out_ref[...] = (grad_residual_ref[...] + grad_first).astype(jnp.bfloat16)
        width = grad.shape[1]
        source = lax.broadcasted_iota(jnp.int32, (HEAD_SIZE, width), 0)
        target = lax.broadcasted_iota(jnp.int32, (HEAD_SIZE, width), 1)
        spread = jnp.where(source // head_shard * shard + source % head_shard == target, 1.0, 0.0)
        heads = jnp.dot(
            head_gains_ref[...], spread, precision=lax.Precision.HIGHEST, preferred_element_type=jnp.float32
        )
        lines = jnp.concatenate(
            [
                jnp.sum(grad * unit, axis=0, keepdims=True),
                gain_two_ref[...],
                heads,
                jnp.zeros((124, width), jnp.float32),
            ],
            axis=0,
        )
        lines_ref[...] = lines.T
        device = device_ref[0]
        group = max(1, 16 // shard)
        last = slice(2 * KEY_VALUE_HEADS * HEAD_SIZE, None)
        for first in range(0, len(order), group):
            blocks = [
                lines_ref[pl.ds(pl.multiple_of((device ^ mask) * shard, shard), shard), :]
                for mask in order[first : first + group]
            ]
            block = (blocks[0] if group == 1 else jnp.concatenate(blocks, axis=0)).astype(jnp.bfloat16)
            row = first * shard
            target_ref = rest_kept_ref if row < half else rest_sent_ref
            target_ref[row % half : row % half + group * shard, last] = block


def attend_back(
    device, residual_low, out_weight, saved, head_gains, cosine, sine, first_row, turned_query, turned_rest,
    query_weight, rest_weight, tokens, gain, grad_residual, grad_gain_two, order, shard, head_shard,
):
    rows, width = residual_low.shape
    query, key, value, raw_query, raw_key, totals = saved
    whole = lambda shape: pl.BlockSpec(shape, lambda h, d: (0, 0))
    columns = lambda height, size, shift=0: pl.BlockSpec((height, size), lambda h, d: (0, h + shift))
    pair = 2 * HEAD_SIZE
    low = lambda height, size: jax.ShapeDtypeStruct((height, size), jnp.bfloat16)
    half = width // 2
    rest_width = rest_weight.shape[1]
    return pl.pallas_call(
        functools.partial(attend_back_body, order=order, shard=shard, head_shard=head_shard),
        grid_spec=pltpu.PrefetchScalarGridSpec(
            num_scalar_prefetch=1,
            grid=(KEY_VALUE_HEADS,),
            in_specs=[
                whole((rows, width)),
                pl.BlockSpec((pair, width), lambda h, d: (h, 0)),
                columns(rows, pair),
                columns(rows, HEAD_SIZE),
                columns(rows, HEAD_SIZE),
                columns(rows, pair),
                columns(rows, HEAD_SIZE),
                pl.BlockSpec((1, rows, 2), lambda h, d: (h, 0, 0)),
                whole((2, HEAD_SIZE)),
                whole((rows, HEAD_SIZE)),
                whole((rows, HEAD_SIZE)),
                whole((rows, 1)),
                whole((width, rows)),
                whole((width, rows)),
                columns(width, pair),
                columns(width, HEAD_SIZE),
                columns(width, HEAD_SIZE, KEY_VALUE_HEADS),
                whole((rows, width)),
                whole((1, width)),
                whole((rows, width)),
                whole((1, width)),
            ],
            out_specs=[
                columns(half, pair),
                columns(half, pair),
                whole((half, rest_width)),
                whole((half, rest_width)),
                whole((rows, width)),
            ],
            scratch_shapes=[
                pltpu.VMEM((rows, pair), jnp.bfloat16),
                pltpu.VMEM((rows, pair), jnp.float32),
                pltpu.VMEM((rows, HEAD_SIZE), jnp.float32),
                pltpu.VMEM((rows, HEAD_SIZE), jnp.float32),
                pltpu.VMEM((rows, pair), jnp.bfloat16),
                pltpu.VMEM((2, HEAD_SIZE), jnp.float32),
                pltpu.VMEM((rows, width), jnp.float32),
                pltpu.VMEM((width, 128), jnp.float32),
            ],
        ),
        out_shape=[
            low(half, QUERY_HEADS * HEAD_SIZE),
            low(half, QUERY_HEADS * HEAD_SIZE),
            low(half, rest_width),
            low(half, rest_width),
            low(rows, width),
        ],
        compiler_params=pltpu.CompilerParams(vmem_limit_bytes=48 * 1024 * 1024),
        cost_estimate=SMALL,
        name="attend_back",
    )(
        device.reshape(1), residual_low, out_weight, query, key, value, raw_query, raw_key, totals, head_gains, cosine,
        sine, first_row, turned_query, turned_rest, query_weight, rest_weight, rest_weight, tokens, gain,
        grad_residual, grad_gain_two,
    )


def feed_forward_body(
    residual_ref, gain_ref, cotangent_ref, gate_ref, up_ref, down_ref,
    mixed_ref, normed_ref, hidden_ref, grad_gate_ref, grad_up_ref, grad_residual_ref, grad_low_ref, grad_gain_ref,
    out_ref, back_ref, down_weight_ref,
):
    step = pl.program_id(0)

    @pl.when(step == 0)
    def _():
        unit, _ = unit_head(residual_ref[...])
        normed_ref[...] = (unit * gain_ref[...]).astype(jnp.bfloat16)
        out_ref[...] = jnp.zeros_like(out_ref)
        back_ref[...] = jnp.zeros_like(back_ref)

    normed = normed_ref[...]
    width = normed.shape[1]
    gate_weight = gate_ref[...].reshape(width, gate_ref.shape[-1])
    up_weight = up_ref[...].reshape(width, up_ref.shape[-1])
    devices, rows, _ = down_ref.shape
    pieces = down_ref.shape[2] // width
    for device in range(devices):
        for piece in range(pieces):
            first = (device * pieces + piece) * rows
            down_weight_ref[first : first + rows, :] = down_ref[device, :, piece * width : (piece + 1) * width]
    down_weight = down_weight_ref[...]
    gate = jnp.dot(normed, gate_weight, preferred_element_type=jnp.float32)
    up = jnp.dot(normed, up_weight, preferred_element_type=jnp.float32)
    grad_hidden = contract(cotangent_ref[...], down_weight, 1, 1)
    sigmoid = jax.nn.sigmoid(gate)
    silu = gate * sigmoid
    hidden = (silu * up).astype(jnp.bfloat16)
    grad_gate = (grad_hidden * up * sigmoid * (1.0 + gate * (1.0 - sigmoid))).astype(jnp.bfloat16)
    grad_up = (grad_hidden * silu).astype(jnp.bfloat16)
    hidden_ref[...] = hidden
    grad_gate_ref[...] = grad_gate
    grad_up_ref[...] = grad_up
    out_ref[...] += jnp.dot(hidden, down_weight, preferred_element_type=jnp.float32)
    back_ref[...] += contract(grad_gate, gate_weight, 1, 1) + contract(grad_up, up_weight, 1, 1)

    @pl.when(step == pl.num_programs(0) - 1)
    def _():
        residual = residual_ref[...]
        mixed_ref[...] = (residual + out_ref[...]).astype(jnp.bfloat16)
        unit, inverse = unit_head(residual)
        grad = back_ref[...]
        grad_gain_ref[...] = jnp.sum(grad * unit, axis=0, keepdims=True)
        scaled = grad * gain_ref[...]
        grad_mid = inverse * (scaled - unit * jnp.mean(scaled * unit, axis=-1, keepdims=True))
        grad_residual = cotangent_ref[...].astype(jnp.float32) + grad_mid
        grad_residual_ref[...] = grad_residual
        grad_low_ref[...] = grad_residual.astype(jnp.bfloat16)


def feed_forward(residual, gain, cotangent, weights, shard):
    rows, width = residual.shape
    count, _, hidden_width = weights.shape
    tile = 4 * hidden_width // 32
    tiles = hidden_width // tile
    whole = pl.BlockSpec((rows, width), lambda j: (0, 0))
    row = pl.BlockSpec((1, width), lambda j: (0, 0))
    columns = pl.BlockSpec((rows, tile), lambda j: (0, j))
    low = lambda size: jax.ShapeDtypeStruct((rows, size), jnp.bfloat16)
    if shard % 16 == 0:
        weight_args = [weights, weights, weights]
        weight_specs = [
            pl.BlockSpec((count, shard, tile), lambda j: (0, 0, j)),
            pl.BlockSpec((count, shard, tile), lambda j: (0, 1, j)),
            pl.BlockSpec((count // tiles, shard, hidden_width), lambda j: (j, 2, 0)),
        ]
    else:
        gate, up, down = (weights[:, part * shard : (part + 1) * shard] for part in range(3))
        down = down.reshape(count, shard, -1, width).transpose(0, 2, 1, 3).reshape(tiles, tile, width)
        weight_args = [gate.reshape(width, hidden_width), up.reshape(width, hidden_width), down]
        weight_specs = [
            pl.BlockSpec((width, tile), lambda j: (0, j)),
            pl.BlockSpec((width, tile), lambda j: (0, j)),
            pl.BlockSpec((1, tile, width), lambda j: (j, 0, 0)),
        ]
    return pl.pallas_call(
        feed_forward_body,
        grid=(tiles,),
        in_specs=[whole, row, whole] + weight_specs,
        out_specs=[whole, whole, columns, columns, columns, whole, whole, row],
        out_shape=[
            low(width),
            low(width),
            low(hidden_width),
            low(hidden_width),
            low(hidden_width),
            jax.ShapeDtypeStruct((rows, width), jnp.float32),
            low(width),
            jax.ShapeDtypeStruct((1, width), jnp.float32),
        ],
        scratch_shapes=[
            pltpu.VMEM((rows, width), jnp.float32),
            pltpu.VMEM((rows, width), jnp.float32),
            pltpu.VMEM((tile, width), jnp.bfloat16),
        ],
        compiler_params=pltpu.CompilerParams(vmem_limit_bytes=48 * 1024 * 1024),
        cost_estimate=SMALL,
        name="feed_forward",
    )(residual, gain, cotangent, *weight_args)


def on_device(
    tokens,
    seq_lengths,
    seq_owner,
    g_attn,
    w_query,
    key_projection,
    value_projection,
    query_norm_gain,
    g_key,
    w_out,
    g_ffn,
    w_gate,
    w_up,
    w_down,
    cotangent,
):
    row_total_count = tokens.shape[0]
    fence = lax.optimization_barrier
    count = lax.axis_size("fsdp")
    device = lax.axis_index("fsdp")
    early = middle_bits(count, False)
    late = middle_bits(count, True)
    cut_bits = len(early) // 2
    shard = g_attn.shape[0]
    head_shard = query_norm_gain.shape[0]
    key_width = key_projection.shape[1]

    pieces = w_down.shape[0] // shard
    down_pieces = w_down.reshape(pieces, shard, -1).transpose(1, 0, 2).reshape(shard, -1)
    ffn_weights = lax.all_gather(jnp.concatenate([w_gate, w_up, down_pieces], axis=0), "fsdp", axis=0, tiled=False)
    gains = gain_columns(g_attn, g_ffn, query_norm_gain, g_key, shard)
    projections = jnp.concatenate([w_query, key_projection, value_projection, gains], axis=1)
    top = gather_top(projections, count)
    top, w_out = fence((top, w_out))
    query_part, rest_part = lay_top_split(top, device, count, w_query.shape[1])
    query_parts = gather_bits({0: query_part}, count, early[:cut_bits])
    rest_parts = gather_bits({0: rest_part}, count, late[:cut_bits])
    out_top = gather_top(w_out, count)
    query_parts, rest_parts, out_top = fence((query_parts, rest_parts, out_top))
    query_parts = gather_bits(query_parts, count, early[cut_bits:])
    rest_parts = gather_bits(rest_parts, count, late[cut_bits:])
    out_parts = lay_top(out_top, device, count)
    query_parts, rest_parts, out_parts = fence((query_parts, rest_parts, out_parts))
    out_parts = gather_bits(out_parts, count, early[:cut_bits])
    query_parts = gather_bits(query_parts, count, [0])
    rest_parts = gather_bits(rest_parts, count, [0])
    query_parts, rest_parts = fence((query_parts, rest_parts))
    query_weight = lay(query_parts, device, count)
    rest_weight = lay(rest_parts, device, count)

    seq_id, token_position = layout(seq_lengths, seq_owner, device, row_total_count)
    first_row = (jnp.arange(row_total_count, dtype=jnp.int32) - token_position)[:, None]
    cosine, sine = rotation_factors(token_position)
    inputs = tokens.astype(jnp.float32)
    gain_block = rest_weight[:, 2 * key_width :].astype(jnp.float32)
    head_gains = gain_block.reshape(count, shard, 128)[:, :head_shard, 2:4].reshape(HEAD_SIZE, 2).T
    gain_one = gain_block[:, 0]
    gain_two = gain_block[:, 1]
    normed_low = norm_forward(inputs, gain_one)[0].astype(jnp.bfloat16)
    normed_low, out_parts = fence((normed_low, out_parts))
    out_parts = gather_bits(out_parts, count, early[cut_bits:])
    attended, *saved = attend(normed_low, query_weight, rest_weight, head_gains, cosine, sine, first_row)
    attended, out_parts = fence((attended, out_parts))
    out_parts = gather_bits(out_parts, count, [0])
    out_weight = lay(out_parts, device, count)
    residual = inputs + jnp.dot(attended, out_weight, preferred_element_type=jnp.float32)
    mixed, normed_two, hidden, grad_gate, grad_up, grad_residual, grad_res_low, grad_gain_two = feed_forward(
        residual, gain_two[None], cotangent, ffn_weights, shard
    )

    live = dict(
        hidden=hidden, two=normed_two, grad_gate=grad_gate, grad_up=grad_up, attended=attended, low=grad_res_low,
        one=normed_low,
    )
    flying = {}
    stages = dict(
        down=sum_bits(count, True, True),
        gate=sum_bits(count, False),
        out=sum_bits(count, False),
        query=sum_bits(count, False),
        rest=sum_bits(count, True),
    )
    orders = {name: row_order(count, bits) for name, bits in stages.items()}
    stages = {name: list(bits) for name, bits in stages.items()}

    def cut():
        live.update(fence(dict(live)))

    def fly(**sent):
        live.update({name + "_sent": value for name, value in sent.items()})
        cut()
        for name in sent:
            flying[name] = exchange(live.pop(name + "_sent"), count, 1 << stages[name].pop(0))

    def land(*names):
        live.update({name + "_came": flying.pop(name) for name in names})
        cut()

    def pass_on(*names):
        land(*names)
        fly(**{name: add_half(live[name], live[name + "_came"], 1) for name in names})

    def keep(name):
        live[name] = add_half(live[name], live.pop(name + "_came"), 0)

    live["up"] = product_half(turn(live["two"], jnp.zeros_like(device), list(range(count))), live["grad_up"])
    cut()
    sum_up = lax.psum_scatter(live.pop("up"), "fsdp", scatter_dimension=0, tiled=True)
    turned_down = turn(live["hidden"], device, orders["down"])
    fly(down=product_half(turned_down, cotangent, 1))
    turned_gate = turn(live["two"], device, orders["gate"])
    fly(gate=product_half(turned_gate, live["grad_gate"], 1))
    live["down"] = product_half(turned_down, cotangent, 0)
    pass_on("down")
    live["gate"] = product_half(turned_gate, live["grad_gate"], 0)
    pass_on("gate")
    keep("down")
    keep("gate")
    turned_query = turn(live["one"], device, orders["query"])
    turned_rest = turn(live["one"], device, orders["rest"])
    live["query"], query_sent, live["rest"], rest_sent, live["grad_tokens"] = attend_back(
        device, live["low"], out_weight, saved, head_gains, cosine, sine, first_row, turned_query, turned_rest,
        query_weight, rest_weight, tokens, gain_one[None], grad_residual, grad_gain_two, orders["rest"], shard,
        head_shard,
    )
    live["query_sent"], live["rest_sent"] = query_sent, rest_sent
    land("down", "gate")
    fly(
        down=add_half(live["down"], live["down_came"], 1),
        gate=add_half(live["gate"], live["gate_came"], 1),
        query=live["query_sent"],
        rest=live["rest_sent"],
    )
    pass_on("query", "rest")
    turned_out = turn(live["attended"], device, orders["out"])
    fly(out=product_half(turned_out, live["low"], 1))
    keep("down")
    keep("gate")
    keep("query")
    keep("rest")
    live["out"] = product_half(turned_out, live["low"], 0)
    pass_on("out")
    keep("out")
    grad_tokens = live.pop("grad_tokens")
    for name in ("hidden", "two", "grad_gate", "grad_up", "attended", "low", "one"):
        del live[name]
    sequence = [
        "down", "gate", "query", "gate", "down", "rest", "out", "query", "rest", "query", "out", "rest", "out",
    ]
    while any(stages.values()):
        name = sequence.pop(0) if sequence else max(stages, key=lambda n: len(stages[n]))
        if stages[name]:
            pass_on(name)
            keep(name)
    ends = {}
    for name in ("gate", "down", "out", "query", "rest"):
        land(name)
        ends[name] = sum_end((live.pop(name), live.pop(name + "_came")))
    sum_down, sum_gate, sum_out, sum_query, sum_rest = (
        ends[name] for name in ("down", "gate", "out", "query", "rest")
    )
    sum_gains = sum_rest[:, 2 * key_width :]
    return (
        mixed,
        grad_tokens,
        sum_gains[:, 0],
        sum_query,
        sum_rest[:, :key_width],
        sum_rest[:, key_width : 2 * key_width],
        sum_gains[:head_shard, 2],
        sum_gains[:head_shard, 3],
        sum_out,
        sum_gains[:, 1],
        sum_gate,
        sum_up.astype(jnp.float32),
        sum_down,
    )


def solution(mesh):
    return jax.shard_map(
        on_device,
        mesh=mesh,
        in_specs=(
            P("fsdp", None),
            P(),
            P(),
            P("fsdp"),
            P("fsdp", None),
            P("fsdp", None),
            P("fsdp", None),
            P("fsdp"),
            P("fsdp"),
            P("fsdp", None),
            P("fsdp"),
            P("fsdp", None),
            P("fsdp", None),
            P("fsdp", None),
            P("fsdp", None),
        ),
        out_specs=(
            P("fsdp", None),
            P("fsdp", None),
            P("fsdp"),
            P("fsdp", None),
            P("fsdp", None),
            P("fsdp", None),
            P("fsdp"),
            P("fsdp"),
            P("fsdp", None),
            P("fsdp"),
            P("fsdp", None),
            P("fsdp", None),
            P("fsdp", None),
        ),
        check_vma=False,
    )
```

time: 583 us -> 438 us (0.75); the launches traced: 573 us -> 437 us
  Pallas kernels: 53.6 us -> 157 us
  matrix products: 83.8 us -> 3.01 us
  waiting for transfers between devices: 209 us -> 139 us
  other arithmetic: 64.2 us -> 10.4 us
  starting transfers between devices: 108 us -> 79.1 us
  local copies, waits for them, and re-layouts: 39 us -> 32.8 us
    pallas_call x6 -> x56, Pallas kernels: 24.3 us -> 131 us  [the longest x1 39.3 us: attend_back(): pl.pallas_call(functools.partial(attend_back_body, order=order, shard=sha...]
    dot_general x18 -> x0, matrix products: 81.9 us -> none  [the longest x12 34.1 us: product_low(): jnp.dot(left, right, preferred_element_type=jnp.float32)]
    ppermute x76 -> x52, waiting for transfers between devices: 209 us -> 139 us  [exchange(): lax.ppermute(values, 'fsdp', [(source, source ^ mask) for source in range...]
    convert_element_type x22 -> x2, other arithmetic: 42.4 us -> 1.94 us  [the longest x1 1.7 us: on_device(): sum_up.astype(jnp.float32)]
    ppermute x76 -> x52, starting transfers between devices: 108 us -> 79 us  [exchange(): lax.ppermute(values, 'fsdp', [(source, source ^ mask) for source in range...]
    unnamed x190 -> x129, local copies, waits for them, and re-layouts: 30.5 us -> 28.7 us
  transfers between devices with their start and end apart: 77 -> 54, of which waited for: 23 -> 23; matrix products, arithmetic and copies ran while one was open for 20% -> 2% of each run, Pallas kernels for 9% -> 27%
where the time goes in v3:
time: 438 us; the launch traced here: 437 us
  Pallas kernels  157 us (36%)
  waiting for transfers between devices  139 us (32%)
  starting transfers between devices  79.1 us (18%)
  local copies, waits for them, and re-layouts  32.8 us (7%)
  between operations  15.3 us (3%)
  other arithmetic  10.4 us (2%)
    ppermute x52, waiting for transfers between devices, exchange(): lax.ppermute(values, 'fsdp', [(source, source ^ mask) for source in range...  139 us
    ppermute x52, starting transfers between devices, exchange(): lax.ppermute(values, 'fsdp', [(source, source ^ mask) for source in range...  79 us
    pallas_call x1, Pallas kernels, attend_back(): pl.pallas_call(functools.partial(attend_back_body, order=order, shard=sha...  39.3 us
    pallas_call x40, Pallas kernels, add_half(): pl.pallas_call(add_body, grid=(steps,), in_specs=[spec(half * steps), spe...  37.1 us
    unnamed x129, local copies, waits for them, and re-layouts  28.7 us
    pallas_call x1, Pallas kernels, feed_forward(): pl.pallas_call(feed_forward_body, grid=(tiles,), in_specs=[whole, row, wh...  26.4 us
    pallas_call x7, Pallas kernels, product_half(): pl.pallas_call(product_body, grid=(rows // row_tile, columns // column_ti...  25 us
    pallas_call x1, Pallas kernels, attend(): pl.pallas_call(attend_body, grid=(KEY_VALUE_HEADS,), in_specs=[whole((row...  20.7 us
  transfers between devices with their start and end apart: 54, of which 23 were waited for; matrix products, arithmetic and copies ran while one was open for 2% of the time, Pallas kernels for 27%

profile of v3, /device:TPU:0, one launch (start us, length us, event | category | flops | bytes accessed | tf_op | source)
XLA Modules:
  0.0 436.8 jit_solution(12890528169454461703)
XLA Ops:
  10.8 4.1 collective-permute-start.1
  16.5 14.8 %collective-permute-done.1 = bf16[32,4224]{1,0:T(8,128)(2,1)S(1)} collective-permute-done((bf16[32,4224]{1,0:T(8,128)(2,1)S(1)}, bf16[32,4224]{1,0:T(8,128)(2,1)S(1)}, u32[]{:S(2)}, u32[]{:S(2)}) %collective-permute-start.1) | collective-permute-done | bytes 270368 | tf_op jit(solution)/shard_map/ppermute | solution.py:56
  31.3 9.9 %collective-permute-done.2 = bf16[32,4224]{1,0:T(8,128)(2,1)S(1)} collective-permute-done((bf16[32,4224]{1,0:T(8,128)(2,1)S(1)}, bf16[32,4224]{1,0:T(8,128)(2,1)S(1)}, u32[]{:S(2)}, u32[]{:S(2)}) %collective-permute-start.2) | collective-permute-done | bytes 270368 | tf_op jit(solution)/shard_map/ppermute | solution.py:56
  44.7 3.2 collective-permute-start.7
  48.0 12.3 %collective-permute-start.6 = (bf16[64,1024]{1,0:T(8,128)(2,1)S(1)}, bf16[64,1024]{1,0:T(8,128)(2,1)S(1)}, u32[]{:S(2)}, u32[]{:S(2)}) collective-permute-start(bf16[64,1024]{1,0:T(8,128)(2,1)S(1)} %copy-done.51), channel_id=1, source_target_pairs={{0,16},{1,17},{2,18},{3,19},{4,20},{5,21},{6,22},{7,23},{8,24},{9,... | collective-permute-start | bytes 393224 | tf_op jit(solution)/shard_map/ppermute | solution.py:56
  60.9 18.3 %collective-permute-done.6 = bf16[64,1024]{1,0:T(8,128)(2,1)S(1)} collective-permute-done((bf16[64,1024]{1,0:T(8,128)(2,1)S(1)}, bf16[64,1024]{1,0:T(8,128)(2,1)S(1)}, u32[]{:S(2)}, u32[]{:S(2)}) %collective-permute-start.6) | collective-permute-done | bytes 131104 | tf_op jit(solution)/shard_map/ppermute | solution.py:56
  79.3 2.0 collective-permute-start.11
  81.3 2.0 collective-permute-start.9
  85.0 9.2 %collective-permute-done.8.refs_4_ = bf16[4,32,2048]{2,1,0:T(8,128)(2,1)S(1)} collective-permute-done((bf16[4,32,2048]{2,1,0:T(8,128)(2,1)S(1)}, bf16[4,32,2048]{2,1,0:T(8,128)(2,1)S(1)}, u32[]{:S(2)}, u32[]{:S(2)}) %collective-permute-start.8) | collective-permute-done | bytes 524320 | tf_op jit(solution)/shard_map/ppermute | solution.py:56
  94.2 5.7 %collective-permute-done.9.refs_6_ = bf16[4,32,2048]{2,1,0:T(8,128)(2,1)} collective-permute-done((bf16[4,32,2048]{2,1,0:T(8,128)(2,1)S(1)}, bf16[4,32,2048]{2,1,0:T(8,128)(2,1)}, u32[]{:S(2)}, u32[]{:S(2)}) %collective-permute-start.9) | collective-permute-done | bytes 524320 | tf_op jit(solution)/shard_map/ppermute | solution.py:56
  99.9 2.6 collective-permute-done.11.refs_6_
  112.5 2.0 copy-done
  115.4 18.6 %collective-permute-done.20.refs_2_ = bf16[4,64,1024]{2,1,0:T(8,128)(2,1)} collective-permute-done((bf16[4,64,1024]{2,1,0:T(8,128)(2,1)S(1)}, bf16[4,64,1024]{2,1,0:T(8,128)(2,1)}, u32[]{:S(2)}, u32[]{:S(2)}) %collective-permute-start.20) | collective-permute-done | bytes 524320 | tf_op jit(solution)/shard_map/ppermute | solution.py:56
  140.8 20.7 %attend.1 = (bf16[384,2048]{1,0:T(8,128)(2,1)S(1)}, bf16[384,2048]{1,0:T(8,128)(2,1)S(1)}, bf16[384,1024]{1,0:T(8,128)(2,1)S(1)}, bf16[384,1024]{1,0:T(8,128)(2,...) custom-call(bf16[384,1024]{1,0:T(8,128)(2,1)S(1)} %fusion.2.normed_ref.values_ref, ...), custom_call_target="tpu_custom_call" | custom-call | flops 1 | bytes 1 | tf_op jit(solution)/shard_map/attend/pallas_call | solution.py:331
  168.6 2.3 collective-permute-done.23.refs_1_
  176.5 3.0 convert_add_fusion.residual_ref
  180.9 26.4 %feed_forward.1 = (bf16[384,1024]{1,0:T(8,128)(2,1)}, bf16[384,1024]{1,0:T(8,128)(2,1)S(1)}, bf16[384,3072]{1,0:T(8,128)(2,1)}, bf16[384,3072]{1,0:T(8,128)(2,1)...) custom-call(f32[384,1024]{1,0:T(8,128)S(1)} %copy-done.34, ...), custom_call_target="tpu_custom_call" | custom-call | flops 1 | bytes 1 | tf_op jit(solution)/shard_map/feed_forward/pallas_call | solution.py:633
  211.0 6.0 %product.7 = bf16[1024,3072]{1,0:T(8,128)(2,1)S(1)} custom-call(bf16[1024,384]{1,0:T(8,128)(2,1)S(1)} %turn.6.left_ref, bf16[384,3072]{1,0:T(8,128)(2,1)S(1)} %copy-done.25), custom_call_target="tpu_custom_call" | custom-call | flops 1 | bytes 1 | tf_op jit(solution)/shard_map/product/pallas_call | solution.py:143
  217.1 2.6 copy-done.2
  222.5 4.4 %product.8 = bf16[1536,1024]{1,0:T(8,128)(2,1)} custom-call(bf16[3072,384]{1,0:T(8,128)(2,1)S(1)} %turn.7.left_ref, bf16[384,1024]{1,0:T(8,128)(2,1)S(1)} %copy-done.15), custom_call_target="tpu_custom_call" | custom-call | flops 1 | bytes 1 | tf_op jit(solution)/shard_map/product/pallas_call | solution.py:143
  227.3 4.5 %product.9 = bf16[512,3072]{1,0:T(8,128)(2,1)} custom-call(bf16[1024,384]{1,0:T(8,128)(2,1)S(1)} %turn.8.left_ref, bf16[384,3072]{1,0:T(8,128)(2,1)S(1)} %copy-done.4), custom_call_target="tpu_custom_call" | custom-call | flops 1 | bytes 1 | tf_op jit(solution)/shard_map/product/pallas_call | solution.py:143
  233.4 3.0 product.10.first_ref
  236.5 2.5 add_half.40
  240.2 3.0 product.11.first_ref
  243.2 3.7 add_half.41
  248.2 2.4 add_half.42.first_ref
  250.7 2.6 add_half.43.first_ref
  253.3 39.3 %attend_back.1 = (bf16[512,2048]{1,0:T(8,128)(2,1)}, bf16[512,2048]{1,0:T(8,128)(2,1)}, bf16[512,2176]{1,0:T(8,128)(2,1)}, bf16[512,2176]{1,0:T(8,128)(2,1)}, bf16[384,1024]{1,0:T(8,128)(2,1)}) custom-call(s32[1]{0:T(128)} %bitcast.27.device_ref, bf16[384,1024]{1,0:T(8,128)(2,1)S(1)} %copy-done.13, bf16[2048,1024]{1,0:T(8,128)(2,1)} %bitcast.46, ...), custom_call_target="tpu_custom_call" | custom-call | flops 1 | bytes 1 | tf_op jit(solution)/shard_map/attend_back/pallas_call | solution.py:492
  296.7 6.8 %collective-permute-done.31.second_ref = bf16[512,2048]{1,0:T(8,128)(2,1)S(1)} collective-permute-done((bf16[512,2048]{1,0:T(8,128)(2,1)S(1)}, bf16[512,2048]{1,0:T(8,128)(2,1)S(1)}, u32[]{:S(2)}, u32[]{:S(2)}) %collective-permute-start.31) | collective-permute-done | bytes 2097184 | tf_op jit(solution)/shard_map/ppermute | solution.py:56
  307.5 2.0 product.12
  311.4 10.7 %collective-permute-start.34 = (bf16[384,1024]{1,0:T(8,128)(2,1)}, bf16[384,1024]{1,0:T(8,128)(2,1)}, u32[]{:S(2)}, u32[]{:S(2)}) collective-permute-start(bf16[384,1024]{1,0:T(8,128)(2,1)} %add_half.44), channel_id=1, source_target_pairs={{0,8},{1,9},{2,10},{3,11},{4,12},{5,13},{6,14},{7,15},{8,0},{9,1},... | collective-permute-start | bytes 2359304 | tf_op jit(solution)/shard_map/ppermute | solution.py:56
  324.1 2.0 product.13.first_ref
  328.4 2.2 add_half.52
  332.2 2.1 add_half.53.first_ref
  334.3 14.2 %collective-permute-done.34.second_ref = bf16[384,1024]{1,0:T(8,128)(2,1)} collective-permute-done((bf16[384,1024]{1,0:T(8,128)(2,1)}, bf16[384,1024]{1,0:T(8,128)(2,1)}, u32[]{:S(2)}, u32[]{:S(2)}) %collective-permute-start.34) | collective-permute-done | bytes 786464 | tf_op jit(solution)/shard_map/ppermute | solution.py:56
  354.4 2.6 collective-permute-start.38
  357.2 2.0 add_half.58
  359.2 2.1 collective-permute-start.41
  363.2 12.2 %collective-permute-done.37.second_ref = bf16[64,3072]{1,0:T(8,128)(2,1)S(1)} collective-permute-done((bf16[64,3072]{1,0:T(8,128)(2,1)S(1)}, bf16[64,3072]{1,0:T(8,128)(2,1)S(1)}, u32[]{:S(2)}, u32[]{:S(2)}) %collective-permute-start.37) | collective-permute-done | bytes 393248 | tf_op jit(solution)/shard_map/ppermute | solution.py:56
  375.9 2.0 add_half.64
  379.5 2.0 add_half.65.first_ref
  383.7 3.5 collective-permute-start.43
  387.3 4.8 %collective-permute-done.42.second_ref = bf16[128,2176]{1,0:T(8,128)(2,1)S(1)} collective-permute-done((bf16[128,2176]{1,0:T(8,128)(2,1)S(1)}, bf16[128,2176]{1,0:T(8,128)(2,1)S(1)}, u32[]{:S(2)}, u32[]{:S(2)}) %collective-permute-start.42) | collective-permute-done | bytes 557088 | tf_op jit(solution)/shard_map/ppermute | solution.py:56
  395.0 3.3 collective-permute-start.46
  398.3 2.1 collective-permute-start.47
  403.6 3.3 collective-permute-done.45.second_ref
  407.0 3.2 collective-permute-start.51
  416.7 9.6 %collective-permute-done.49 = bf16[64,1024]{1,0:T(8,128)(2,1)S(1)} collective-permute-done((bf16[64,1024]{1,0:T(8,128)(2,1)S(1)}, bf16[64,1024]{1,0:T(8,128)(2,1)S(1)}, u32[]{:S(2)}, u32[]{:S(2)}) %collective-permute-start.49) | collective-permute-done | bytes 131104 | tf_op jit(solution)/shard_map/ppermute | solution.py:56
  (285 shorter events, 97.4 us)
Async XLA Ops:
  7.3 172.3 %all-gather.3.cloned.1.call-start = ((), (), s32[]{:S(2)}) async-start(), calls=%async_computation.2 | async-start | bytes 19464192 | tf_op jit(solution)/shard_map/all_gather | solution.py:689
  10.5 390.7 %reduce-scatter.2.cloned.1.call-start = ((), (), s32[]{:S(2)}) async-start(), calls=%async_computation.1 | async-start | bytes 6488064 | tf_op jit(solution)/shard_map/reduce_scatter | solution.py:767
  10.8 20.5 %collective-permute-start.1 = (bf16[32,4224]{1,0:T(8,128)(2,1)S(1)}, bf16[32,4224]{1,0:T(8,128)(2,1)S(1)}, u32[]{:S(2)}, u32[]{:S(2)}) collective-permute-start(bf16[32,4224]{1,0:T(8,128)(2,1)S(1)} %fusion.4), channel_id=1, source_target_pairs={{0,16},{1,17},{2,18},{3,19},{4,20},{5,21},{6,22},{7,23},{8,24},{9,... | collective-permute-start | bytes 811016 | tf_op jit(solution)/shard_map/ppermute | solution.py:56
  14.9 16.4 %collective-permute-start = (bf16[32,4224]{1,0:T(8,128)(2,1)S(1)}, bf16[32,4224]{1,0:T(8,128)(2,1)S(1)}, u32[]{:S(2)}, u32[]{:S(2)}) collective-permute-start(bf16[32,4224]{1,0:T(8,128)(2,1)S(1)} %fusion.4), channel_id=1, source_target_pairs={{0,8},{1,9},{2,10},{3,11},{4,12},{5,13},{6,14},{7,15},{8,0},{9,1},... | collective-permute-start | bytes 811016 | tf_op jit(solution)/shard_map/ppermute | solution.py:56
  16.4 24.7 %collective-permute-start.2 = (bf16[32,4224]{1,0:T(8,128)(2,1)S(1)}, bf16[32,4224]{1,0:T(8,128)(2,1)S(1)}, u32[]{:S(2)}, u32[]{:S(2)}) collective-permute-start(bf16[32,4224]{1,0:T(8,128)(2,1)S(1)} %fusion.4), channel_id=1, source_target_pairs={{0,24},{1,25},{2,26},{3,27},{4,28},{5,29},{6,30},{7,31},{8,16},{9,... | collective-permute-start | bytes 811016 | tf_op jit(solution)/shard_map/ppermute | solution.py:56
  41.6 37.6 %collective-permute-start.4 = (bf16[4,32,2176]{2,1,0:T(8,128)(2,1)S(1)}, bf16[4,32,2176]{2,1,0:T(8,128)(2,1)S(1)}, u32[]{:S(2)}, u32[]{:S(2)}) collective-permute-start(bf16[4,32,2176]{2,1,0:T(8,128)(2,1)S(1)} %get-tuple-element.413.refs_0_), channel_id=1, source_target_pairs={{0,4},{1,5},{2,6},{3,7},{4,0},{5,1},{6,2},{7,3},{8,12},{9,13},{10,... | collective-permute-start | bytes 1671176 | tf_op jit(solution)/shard_map/ppermute | solution.py:56
  43.2 36.0 %collective-permute-start.3 = (bf16[4,32,2048]{2,1,0:T(8,128)(2,1)S(1)}, bf16[4,32,2048]{2,1,0:T(8,128)(2,1)S(1)}, u32[]{:S(2)}, u32[]{:S(2)}) collective-permute-start(bf16[4,32,2048]{2,1,0:T(8,128)(2,1)S(1)} %get-tuple-element.423.refs_0_), channel_id=1, source_target_pairs={{0,2},{1,3},{2,0},{3,1},{4,6},{5,7},{6,4},{7,5},{8,10},{9,11},{10,... | collective-permute-start | bytes 1572872 | tf_op jit(solution)/shard_map/ppermute | solution.py:56
  44.7 16.1 %collective-permute-start.7 = (bf16[64,1024]{1,0:T(8,128)(2,1)S(1)}, bf16[64,1024]{1,0:T(8,128)(2,1)S(1)}, u32[]{:S(2)}, u32[]{:S(2)}) collective-permute-start(bf16[64,1024]{1,0:T(8,128)(2,1)S(1)} %copy-done.51), channel_id=1, source_target_pairs={{0,24},{1,25},{2,26},{3,27},{4,28},{5,29},{6,30},{7,31},{8,16},{9,... | collective-permute-start | bytes 393224 | tf_op jit(solution)/shard_map/ppermute | solution.py:56
  48.0 31.2 %collective-permute-start.6 = (bf16[64,1024]{1,0:T(8,128)(2,1)S(1)}, bf16[64,1024]{1,0:T(8,128)(2,1)S(1)}, u32[]{:S(2)}, u32[]{:S(2)}) collective-permute-start(bf16[64,1024]{1,0:T(8,128)(2,1)S(1)} %copy-done.51), channel_id=1, source_target_pairs={{0,16},{1,17},{2,18},{3,19},{4,20},{5,21},{6,22},{7,23},{8,24},{9,... | collective-permute-start | bytes 393224 | tf_op jit(solution)/shard_map/ppermute | solution.py:56
  60.3 18.9 %collective-permute-start.5 = (bf16[64,1024]{1,0:T(8,128)(2,1)S(1)}, bf16[64,1024]{1,0:T(8,128)(2,1)S(1)}, u32[]{:S(2)}, u32[]{:S(2)}) collective-permute-start(bf16[64,1024]{1,0:T(8,128)(2,1)S(1)} %copy-done.51), channel_id=1, source_target_pairs={{0,8},{1,9},{2,10},{3,11},{4,12},{5,13},{6,14},{7,15},{8,0},{9,1},... | collective-permute-start | bytes 393224 | tf_op jit(solution)/shard_map/ppermute | solution.py:56
  79.2 20.7 %collective-permute-start.10 = (bf16[4,32,2176]{2,1,0:T(8,128)(2,1)S(1)}, bf16[4,32,2176]{2,1,0:T(8,128)(2,1)S(1)}, u32[]{:S(2)}, u32[]{:S(2)}) collective-permute-start(bf16[4,32,2176]{2,1,0:T(8,128)(2,1)S(1)} %get-tuple-element.413.refs_0_), channel_id=1, source_target_pairs={{0,2},{1,3},{2,0},{3,1},{4,6},{5,7},{6,4},{7,5},{8,10},{9,11},{10,... | collective-permute-start | bytes 1671176 | tf_op jit(solution)/shard_map/ppermute | solution.py:56
  79.3 23.1 %collective-permute-start.11 = (bf16[4,32,2176]{2,1,0:T(8,128)(2,1)S(1)}, bf16[4,32,2176]{2,1,0:T(8,128)(2,1)S(1)}, u32[]{:S(2)}, u32[]{:S(2)}) collective-permute-start(bf16[4,32,2176]{2,1,0:T(8,128)(2,1)S(1)} %collective-permute-done.4.refs_4_), channel_id=1, source_target_pairs={{0,2},{1,3},{2,0},{3,1},{4,6},{5,7},{6,4},{7,5},{8,10},{9,11},{10,... | collective-permute-start | bytes 1671176 | tf_op jit(solution)/shard_map/ppermute | solution.py:56
  81.3 12.8 %collective-permute-start.8 = (bf16[4,32,2048]{2,1,0:T(8,128)(2,1)S(1)}, bf16[4,32,2048]{2,1,0:T(8,128)(2,1)S(1)}, u32[]{:S(2)}, u32[]{:S(2)}) collective-permute-start(bf16[4,32,2048]{2,1,0:T(8,128)(2,1)S(1)} %get-tuple-element.423.refs_0_), channel_id=1, source_target_pairs={{0,4},{1,5},{2,6},{3,7},{4,0},{5,1},{6,2},{7,3},{8,12},{9,13},{10,... | collective-permute-start | bytes 1572872 | tf_op jit(solution)/shard_map/ppermute | solution.py:56
  81.3 18.6 %collective-permute-start.9 = (bf16[4,32,2048]{2,1,0:T(8,128)(2,1)S(1)}, bf16[4,32,2048]{2,1,0:T(8,128)(2,1)}, u32[]{:S(2)}, u32[]{:S(2)}) collective-permute-start(bf16[4,32,2048]{2,1,0:T(8,128)(2,1)S(1)} %collective-permute-done.3.refs_2_), channel_id=1, source_target_pairs={{0,4},{1,5},{2,6},{3,7},{4,0},{5,1},{6,2},{7,3},{8,12},{9,13},{10,... | collective-permute-start | bytes 1572872 | tf_op jit(solution)/shard_map/ppermute | solution.py:56
  103.0 3.6 collective-permute-start.14
  103.8 4.5 %collective-permute-start.15 = (bf16[4,32,2048]{2,1,0:T(8,128)(2,1)}, bf16[4,32,2048]{2,1,0:T(8,128)(2,1)}, u32[]{:S(2)}, u32[]{:S(2)}) collective-permute-start(bf16[4,32,2048]{2,1,0:T(8,128)(2,1)} %collective-permute-done.9.refs_6_), channel_id=1, source_target_pairs={{0,1},{1,0},{2,3},{3,2},{4,5},{5,4},{6,7},{7,6},{8,9},{9,8},{10,11... | collective-permute-start | bytes 1572872 | tf_op jit(solution)/shard_map/ppermute | solution.py:56
  104.3 4.4 %collective-permute-start.16 = (bf16[4,32,2176]{2,1,0:T(8,128)(2,1)S(1)}, bf16[4,32,2176]{2,1,0:T(8,128)(2,1)}, u32[]{:S(2)}, u32[]{:S(2)}) collective-permute-start(bf16[4,32,2176]{2,1,0:T(8,128)(2,1)S(1)} %get-tuple-element.413.refs_0_), channel_id=1, source_target_pairs={{0,1},{1,0},{2,3},{3,2},{4,5},{5,4},{6,7},{7,6},{8,9},{9,8},{10,11... | collective-permute-start | bytes 1671176 | tf_op jit(solution)/shard_map/ppermute | solution.py:56
  108.3 25.6 %collective-permute-start.20 = (bf16[4,64,1024]{2,1,0:T(8,128)(2,1)S(1)}, bf16[4,64,1024]{2,1,0:T(8,128)(2,1)}, u32[]{:S(2)}, u32[]{:S(2)}) collective-permute-start(bf16[4,64,1024]{2,1,0:T(8,128)(2,1)S(1)} %bitcast.47), channel_id=1, source_target_pairs={{0,2},{1,3},{2,0},{3,1},{4,6},{5,7},{6,4},{7,5},{8,10},{9,11},{10,... | collective-permute-start | bytes 1572872 | tf_op jit(solution)/shard_map/ppermute | solution.py:56
  133.9 33.6 %collective-permute-start.21 = (bf16[4,64,1024]{2,1,0:T(8,128)(2,1)S(1)}, bf16[4,64,1024]{2,1,0:T(8,128)(2,1)}, u32[]{:S(2)}, u32[]{:S(2)}) collective-permute-start(bf16[4,64,1024]{2,1,0:T(8,128)(2,1)S(1)} %bitcast.48), channel_id=1, source_target_pairs={{0,4},{1,5},{2,6},{3,7},{4,0},{5,1},{6,2},{7,3},{8,12},{9,13},{10,... | collective-permute-start | bytes 1572872 | tf_op jit(solution)/shard_map/ppermute | solution.py:56
  135.4 32.1 %collective-permute-start.22 = (bf16[4,64,1024]{2,1,0:T(8,128)(2,1)}, bf16[4,64,1024]{2,1,0:T(8,128)(2,1)}, u32[]{:S(2)}, u32[]{:S(2)}) collective-permute-start(bf16[4,64,1024]{2,1,0:T(8,128)(2,1)} %collective-permute-done.20.refs_2_), channel_id=1, source_target_pairs={{0,4},{1,5},{2,6},{3,7},{4,0},{5,1},{6,2},{7,3},{8,12},{9,13},{10,... | collective-permute-start | bytes 1572872 | tf_op jit(solution)/shard_map/ppermute | solution.py:56
  167.6 3.6 collective-permute-start.24
  168.1 4.1 collective-permute-start.25
  168.2 4.8 %collective-permute-start.26 = (bf16[4,64,1024]{2,1,0:T(8,128)(2,1)}, bf16[4,64,1024]{2,1,0:T(8,128)(2,1)S(1)}, u32[]{:S(2)}, u32[]{:S(2)}) collective-permute-start(bf16[4,64,1024]{2,1,0:T(8,128)(2,1)} %collective-permute-done.22.refs_6_), channel_id=1, source_target_pairs={{0,1},{1,0},{2,3},{3,2},{4,5},{5,4},{6,7},{7,6},{8,9},{9,8},{10,11... | collective-permute-start | bytes 1572872 | tf_op jit(solution)/shard_map/ppermute | solution.py:56
  226.9 9.6 %collective-permute-start.27 = (bf16[1536,1024]{1,0:T(8,128)(2,1)}, bf16[1536,1024]{1,0:T(8,128)(2,1)}, u32[]{:S(2)}, u32[]{:S(2)}) collective-permute-start(bf16[1536,1024]{1,0:T(8,128)(2,1)} %product.8), channel_id=1, source_target_pairs={{0,1},{1,0},{2,3},{3,2},{4,5},{5,4},{6,7},{7,6},{8,9},{9,8},{10,11... | collective-permute-start | bytes 9437192 | tf_op jit(solution)/shard_map/ppermute | solution.py:56
  231.8 11.4 %collective-permute-start.28 = (bf16[512,3072]{1,0:T(8,128)(2,1)}, bf16[512,3072]{1,0:T(8,128)(2,1)}, u32[]{:S(2)}, u32[]{:S(2)}) collective-permute-start(bf16[512,3072]{1,0:T(8,128)(2,1)} %product.9), channel_id=1, source_target_pairs={{0,1},{1,0},{2,3},{3,2},{4,5},{5,4},{6,7},{7,6},{8,9},{9,8},{10,11... | collective-permute-start | bytes 9437192 | tf_op jit(solution)/shard_map/ppermute | solution.py:56
  239.0 53.6 %collective-permute-start.29 = (bf16[768,1024]{1,0:T(8,128)(2,1)S(1)}, bf16[768,1024]{1,0:T(8,128)(2,1)S(1)}, u32[]{:S(2)}, u32[]{:S(2)}) collective-permute-start(bf16[768,1024]{1,0:T(8,128)(2,1)S(1)} %add_half.40), channel_id=1, source_target_pairs={{0,4},{1,5},{2,6},{3,7},{4,0},{5,1},{6,2},{7,3},{8,12},{9,13},{10,... | collective-permute-start | bytes 4718600 | tf_op jit(solution)/shard_map/ppermute | solution.py:56
  247.0 45.6 %collective-permute-start.30 = (bf16[256,3072]{1,0:T(8,128)(2,1)}, bf16[256,3072]{1,0:T(8,128)(2,1)S(1)}, u32[]{:S(2)}, u32[]{:S(2)}) collective-permute-start(bf16[256,3072]{1,0:T(8,128)(2,1)} %add_half.41), channel_id=1, source_target_pairs={{0,2},{1,3},{2,0},{3,1},{4,6},{5,7},{6,4},{7,5},{8,10},{9,11},{10,... | collective-permute-start | bytes 4718600 | tf_op jit(solution)/shard_map/ppermute | solution.py:56
  296.2 7.3 %collective-permute-start.32 = (bf16[512,2176]{1,0:T(8,128)(2,1)S(1)}, bf16[512,2176]{1,0:T(8,128)(2,1)S(1)}, u32[]{:S(2)}, u32[]{:S(2)}) collective-permute-start(bf16[512,2176]{1,0:T(8,128)(2,1)S(1)} %copy-done.62), channel_id=1, source_target_pairs={{0,1},{1,0},{2,3},{3,2},{4,5},{5,4},{6,7},{7,6},{8,9},{9,8},{10,11... | collective-permute-start | bytes 6684680 | tf_op jit(solution)/shard_map/ppermute | solution.py:56
  296.7 6.9 %collective-permute-start.31 = (bf16[512,2048]{1,0:T(8,128)(2,1)S(1)}, bf16[512,2048]{1,0:T(8,128)(2,1)S(1)}, u32[]{:S(2)}, u32[]{:S(2)}) collective-permute-start(bf16[512,2048]{1,0:T(8,128)(2,1)S(1)} %copy-done.63), channel_id=1, source_target_pairs={{0,1},{1,0},{2,3},{3,2},{4,5},{5,4},{6,7},{7,6},{8,9},{9,8},{10,11... | collective-permute-start | bytes 6291464 | tf_op jit(solution)/shard_map/ppermute | solution.py:56
  309.6 18.8 %collective-permute-start.33 = (bf16[1024,1024]{1,0:T(8,128)(2,1)S(1)}, bf16[1024,1024]{1,0:T(8,128)(2,1)}, u32[]{:S(2)}, u32[]{:S(2)}) collective-permute-start(bf16[1024,1024]{1,0:T(8,128)(2,1)S(1)} %product.12), channel_id=1, source_target_pairs={{0,1},{1,0},{2,3},{3,2},{4,5},{5,4},{6,7},{7,6},{8,9},{9,8},{10,11... | collective-permute-start | bytes 6291464 | tf_op jit(solution)/shard_map/ppermute | solution.py:56
  309.8 47.4 %collective-permute-start.36 = (bf16[256,2048]{1,0:T(8,128)(2,1)}, bf16[256,2048]{1,0:T(8,128)(2,1)}, u32[]{:S(2)}, u32[]{:S(2)}) collective-permute-start(bf16[256,2048]{1,0:T(8,128)(2,1)} %add_half.46), channel_id=1, source_target_pairs={{0,2},{1,3},{2,0},{3,1},{4,6},{5,7},{6,4},{7,5},{8,10},{9,11},{10,... | collective-permute-start | bytes 3145736 | tf_op jit(solution)/shard_map/ppermute | solution.py:56
  311.4 37.2 %collective-permute-start.34 = (bf16[384,1024]{1,0:T(8,128)(2,1)}, bf16[384,1024]{1,0:T(8,128)(2,1)}, u32[]{:S(2)}, u32[]{:S(2)}) collective-permute-start(bf16[384,1024]{1,0:T(8,128)(2,1)} %add_half.44), channel_id=1, source_target_pairs={{0,8},{1,9},{2,10},{3,11},{4,12},{5,13},{6,14},{7,15},{8,0},{9,1},... | collective-permute-start | bytes 2359304 | tf_op jit(solution)/shard_map/ppermute | solution.py:56
  322.0 30.4 %collective-permute-start.35 = (bf16[128,3072]{1,0:T(8,128)(2,1)}, bf16[128,3072]{1,0:T(8,128)(2,1)S(1)}, u32[]{:S(2)}, u32[]{:S(2)}) collective-permute-start(bf16[128,3072]{1,0:T(8,128)(2,1)} %add_half.45), channel_id=1, source_target_pairs={{0,4},{1,5},{2,6},{3,7},{4,0},{5,1},{6,2},{7,3},{8,12},{9,13},{10,... | collective-permute-start | bytes 2359304 | tf_op jit(solution)/shard_map/ppermute | solution.py:56
  323.6 52.3 %collective-permute-start.39 = (bf16[256,2176]{1,0:T(8,128)(2,1)}, bf16[256,2176]{1,0:T(8,128)(2,1)}, u32[]{:S(2)}, u32[]{:S(2)}) collective-permute-start(bf16[256,2176]{1,0:T(8,128)(2,1)} %add_half.47), channel_id=1, source_target_pairs={{0,4},{1,5},{2,6},{3,7},{4,0},{5,1},{6,2},{7,3},{8,12},{9,13},{10,... | collective-permute-start | bytes 3342344 | tf_op jit(solution)/shard_map/ppermute | solution.py:56
  330.6 50.8 %collective-permute-start.40 = (bf16[512,1024]{1,0:T(8,128)(2,1)S(1)}, bf16[512,1024]{1,0:T(8,128)(2,1)S(1)}, u32[]{:S(2)}, u32[]{:S(2)}) collective-permute-start(bf16[512,1024]{1,0:T(8,128)(2,1)S(1)} %add_half.52), channel_id=1, source_target_pairs={{0,2},{1,3},{2,0},{3,1},{4,6},{5,7},{6,4},{7,5},{8,10},{9,11},{10,... | collective-permute-start | bytes 3145736 | tf_op jit(solution)/shard_map/ppermute | solution.py:56
  352.6 22.9 %collective-permute-start.37 = (bf16[64,3072]{1,0:T(8,128)(2,1)S(1)}, bf16[64,3072]{1,0:T(8,128)(2,1)S(1)}, u32[]{:S(2)}, u32[]{:S(2)}) collective-permute-start(bf16[64,3072]{1,0:T(8,128)(2,1)S(1)} %add_half.56), channel_id=1, source_target_pairs={{0,8},{1,9},{2,10},{3,11},{4,12},{5,13},{6,14},{7,15},{8,0},{9,1},... | collective-permute-start | bytes 1179656 | tf_op jit(solution)/shard_map/ppermute | solution.py:56
  354.4 21.2 %collective-permute-start.38 = (bf16[192,1024]{1,0:T(8,128)(2,1)S(1)}, bf16[192,1024]{1,0:T(8,128)(2,1)S(1)}, u32[]{:S(2)}, u32[]{:S(2)}) collective-permute-start(bf16[192,1024]{1,0:T(8,128)(2,1)S(1)} %add_half.54), channel_id=1, source_target_pairs={{0,16},{1,17},{2,18},{3,19},{4,20},{5,21},{6,22},{7,23},{8,24},{9,... | collective-permute-start | bytes 1179656 | tf_op jit(solution)/shard_map/ppermute | solution.py:56
  359.2 24.5 %collective-permute-start.41 = (bf16[128,2048]{1,0:T(8,128)(2,1)S(1)}, bf16[128,2048]{1,0:T(8,128)(2,1)S(1)}, u32[]{:S(2)}, u32[]{:S(2)}) collective-permute-start(bf16[128,2048]{1,0:T(8,128)(2,1)S(1)} %add_half.58), channel_id=1, source_target_pairs={{0,4},{1,5},{2,6},{3,7},{4,0},{5,1},{6,2},{7,3},{8,12},{9,13},{10,... | collective-permute-start | bytes 1572872 | tf_op jit(solution)/shard_map/ppermute | solution.py:56
  377.9 14.2 %collective-permute-start.42 = (bf16[128,2176]{1,0:T(8,128)(2,1)S(1)}, bf16[128,2176]{1,0:T(8,128)(2,1)S(1)}, u32[]{:S(2)}, u32[]{:S(2)}) collective-permute-start(bf16[128,2176]{1,0:T(8,128)(2,1)S(1)} %add_half.64), channel_id=1, source_target_pairs={{0,2},{1,3},{2,0},{3,1},{4,6},{5,7},{6,4},{7,5},{8,10},{9,11},{10,... | collective-permute-start | bytes 1671176 | tf_op jit(solution)/shard_map/ppermute | solution.py:56
  381.7 13.2 %collective-permute-start.44 = (bf16[256,1024]{1,0:T(8,128)(2,1)S(1)}, bf16[256,1024]{1,0:T(8,128)(2,1)S(1)}, u32[]{:S(2)}, u32[]{:S(2)}) collective-permute-start(bf16[256,1024]{1,0:T(8,128)(2,1)S(1)} %add_half.66), channel_id=1, source_target_pairs={{0,4},{1,5},{2,6},{3,7},{4,0},{5,1},{6,2},{7,3},{8,12},{9,13},{10,... | collective-permute-start | bytes 1572872 | tf_op jit(solution)/shard_map/ppermute | solution.py:56
  383.7 10.6 %collective-permute-start.43 = (bf16[64,2048]{1,0:T(8,128)(2,1)S(1)}, bf16[64,2048]{1,0:T(8,128)(2,1)S(1)}, u32[]{:S(2)}, u32[]{:S(2)}) collective-permute-start(bf16[64,2048]{1,0:T(8,128)(2,1)S(1)} %add_half.68), channel_id=1, source_target_pairs={{0,8},{1,9},{2,10},{3,11},{4,12},{5,13},{6,14},{7,15},{8,0},{9,1},... | collective-permute-start | bytes 786440 | tf_op jit(solution)/shard_map/ppermute | solution.py:56
  392.3 14.7 %collective-permute-start.45 = (bf16[64,2176]{1,0:T(8,128)(2,1)S(1)}, bf16[64,2176]{1,0:T(8,128)(2,1)S(1)}, u32[]{:S(2)}, u32[]{:S(2)}) collective-permute-start(bf16[64,2176]{1,0:T(8,128)(2,1)S(1)} %add_half.70), channel_id=1, source_target_pairs={{0,8},{1,9},{2,10},{3,11},{4,12},{5,13},{6,14},{7,15},{8,0},{9,1},... | collective-permute-start | bytes 835592 | tf_op jit(solution)/shard_map/ppermute | solution.py:56
  395.0 17.0 %collective-permute-start.46 = (bf16[128,1024]{1,0:T(8,128)(2,1)S(1)}, bf16[128,1024]{1,0:T(8,128)(2,1)S(1)}, u32[]{:S(2)}, u32[]{:S(2)}) collective-permute-start(bf16[128,1024]{1,0:T(8,128)(2,1)S(1)} %add_half.74), channel_id=1, source_target_pairs={{0,8},{1,9},{2,10},{3,11},{4,12},{5,13},{6,14},{7,15},{8,0},{9,1},... | collective-permute-start | bytes 786440 | tf_op jit(solution)/shard_map/ppermute | solution.py:56
  398.3 13.9 %collective-permute-start.47 = (bf16[32,3072]{1,0:T(8,128)(2,1)S(1)}, bf16[32,3072]{1,0:T(8,128)(2,1)}, u32[]{:S(2)}, u32[]{:S(2)}) collective-permute-start(bf16[32,3072]{1,0:T(8,128)(2,1)S(1)} %add_half.60), channel_id=1, source_target_pairs={{0,16},{1,17},{2,18},{3,19},{4,20},{5,21},{6,22},{7,23},{8,24},{9,... | collective-permute-start | bytes 589832 | tf_op jit(solution)/shard_map/ppermute | solution.py:56
  400.4 11.8 %collective-permute-start.48 = (bf16[96,1024]{1,0:T(8,128)(2,1)S(1)}, bf16[96,1024]{1,0:T(8,128)(2,1)}, u32[]{:S(2)}, u32[]{:S(2)}) collective-permute-start(bf16[96,1024]{1,0:T(8,128)(2,1)S(1)} %add_half.62), channel_id=1, source_target_pairs={{0,2},{1,3},{2,0},{3,1},{4,6},{5,7},{6,4},{7,5},{8,10},{9,11},{10,... | collective-permute-start | bytes 589832 | tf_op jit(solution)/shard_map/ppermute | solution.py:56
  402.8 23.5 %collective-permute-start.50 = (bf16[32,2048]{1,0:T(8,128)(2,1)S(1)}, bf16[32,2048]{1,0:T(8,128)(2,1)S(1)}, u32[]{:S(2)}, u32[]{:S(2)}) collective-permute-start(bf16[32,2048]{1,0:T(8,128)(2,1)S(1)} %add_half.72), channel_id=1, source_target_pairs={{0,16},{1,17},{2,18},{3,19},{4,20},{5,21},{6,22},{7,23},{8,24},{9,... | collective-permute-start | bytes 393224 | tf_op jit(solution)/shard_map/ppermute | solution.py:56
  407.0 19.4 %collective-permute-start.51 = (bf16[32,2176]{1,0:T(8,128)(2,1)S(1)}, bf16[32,2176]{1,0:T(8,128)(2,1)S(1)}, u32[]{:S(2)}, u32[]{:S(2)}) collective-permute-start(bf16[32,2176]{1,0:T(8,128)(2,1)S(1)} %add_half.76), channel_id=1, source_target_pairs={{0,16},{1,17},{2,18},{3,19},{4,20},{5,21},{6,22},{7,23},{8,24},{9,... | collective-permute-start | bytes 417800 | tf_op jit(solution)/shard_map/ppermute | solution.py:56
  412.2 14.1 %collective-permute-start.49 = (bf16[64,1024]{1,0:T(8,128)(2,1)S(1)}, bf16[64,1024]{1,0:T(8,128)(2,1)S(1)}, u32[]{:S(2)}, u32[]{:S(2)}) collective-permute-start(bf16[64,1024]{1,0:T(8,128)(2,1)S(1)} %add_half.78), channel_id=1, source_target_pairs={{0,16},{1,17},{2,18},{3,19},{4,20},{5,21},{6,22},{7,23},{8,24},{9,... | collective-permute-start | bytes 393224 | tf_op jit(solution)/shard_map/ppermute | solution.py:56
  (70 other events, 728.6 us)
Sparse Core Ops, SparseCore 0:
  11.6 167.4 all-gather.2
  232.4 139.5 reduce-scatter.1

commit v4 on v3

v4 whole, which is shorter than its diff:
```python
import functools
import math

import jax
import jax.numpy as jnp
from jax import lax
from jax.experimental import pallas as pl
from jax.experimental.pallas import tpu as pltpu
from jax.sharding import PartitionSpec as P

QUERY_HEADS = 16
KEY_VALUE_HEADS = 8
HEAD_SIZE = 128


SMALL = pl.CostEstimate(flops=1, bytes_accessed=1, transcendentals=0)


def far(shape, dtype):
    return pltpu.HBM(tuple(shape), dtype)


epsilon = 1e-06
rope_base = 1000000.0


def layout(seq_lengths, seq_owner, device, row_total_count):
    seq_index = jnp.arange(seq_lengths.shape[0], dtype=jnp.int32)
    same_owner = seq_owner[:, None] == seq_owner[None, :]
    before = seq_index[None, :] < seq_index[:, None]
    starts = jnp.sum(jnp.where(same_owner & before, seq_lengths[None, :], 0), axis=1)
    places = jnp.arange(row_total_count, dtype=jnp.int32)
    member = (
        (seq_owner[None, :] == device)
        & (starts[None, :] <= places[:, None])
        & (places[:, None] < (starts + seq_lengths)[None, :])
    )
    seq_id = jnp.sum(jnp.where(member, seq_index[None, :], 0), axis=1)
    token_position = jnp.sum(jnp.where(member, places[:, None] - starts[None, :], 0), axis=1)
    return (seq_id, token_position)


def rotation_factors(token_position):
    half_width = HEAD_SIZE // 2
    frequency = jnp.exp(
        jnp.arange(half_width, dtype=jnp.float32) * (-2.0 * math.log(rope_base) / HEAD_SIZE)
    )
    angles = token_position.astype(jnp.float32)[:, None] * frequency[None, :]
    cosine = jnp.cos(angles)
    sine = jnp.sin(angles)
    return jnp.concatenate([cosine, cosine], axis=1), jnp.concatenate([-sine, sine], axis=1)


def norm_forward(values, gain):
    inverse = lax.rsqrt(jnp.mean(values * values, axis=-1, keepdims=True) + epsilon)
    unit_rows = values * inverse
    return (unit_rows * gain, unit_rows, inverse)


def exchange(values, count, mask):
    return lax.ppermute(values, "fsdp", [(source, source ^ mask) for source in range(count)])


def middle_bits(count, flip):
    bits = list(range(1, count.bit_length() - 3))
    return bits[::-1] if flip else bits


def sum_bits(count):
    bits = count.bit_length() - 1
    middle = list(range(1, bits - 2))
    low, high = bits - 2, bits - 1
    return dict(
        down=[0, middle[-1], high, low] + middle[-2::-1],
        gate=[0] + middle + [low, high],
        up=[0, low, middle[-1], high] + middle[-2::-1],
        out=[0] + middle + [low, high],
        first=[0, low] + middle[::-1] + [high],
        second=[0] + middle + [low, high],
    )


def row_order(count, sequence):
    bits = len(sequence)
    return [
        sum(((index >> (bits - 1 - step)) & 1) << bit for step, bit in enumerate(sequence)) for index in range(count)
    ]


def turn_body(device_ref, *refs, order):
    values, (out_ref, turned_ref) = refs[:-2], refs[-2:]
    start = 0
    for ref in values:
        turned_ref[start : start + ref.shape[1], :] = ref[...].astype(turned_ref.dtype).T
        start += ref.shape[1]
    device = device_ref[0]
    rows = out_ref.shape[0] // len(order)
    group = max(1, 16 // rows)
    for first in range(0, len(order), group):
        blocks = [
            turned_ref[pl.ds(pl.multiple_of((device ^ mask) * rows, rows), rows), :]
            for mask in order[first : first + group]
        ]
        block = blocks[0] if group == 1 else jnp.concatenate(blocks, axis=0)
        out_ref[first * rows : (first + group) * rows, :] = block.astype(out_ref.dtype)


def turn(values, device, order):
    count = len(order)
    rows = values[0].shape[0]
    columns = sum(value.shape[1] for value in values)
    held = jnp.bfloat16 if columns // count % 16 == 0 else jnp.float32
    return pl.pallas_call(
        functools.partial(turn_body, order=order),
        grid_spec=pltpu.PrefetchScalarGridSpec(
            num_scalar_prefetch=1,
            grid=(1,),
            in_specs=[pl.BlockSpec(value.shape, lambda i, d: (0, 0)) for value in values],
            out_specs=pl.BlockSpec((columns, rows), lambda i, d: (0, 0)),
            scratch_shapes=[pltpu.VMEM((columns, rows), held)],
        ),
        out_shape=jax.ShapeDtypeStruct((columns, rows), values[0].dtype),
        compiler_params=pltpu.CompilerParams(vmem_limit_bytes=16 * 1024 * 1024),
        cost_estimate=SMALL,
        name="turn",
    )(device.reshape(1), *values)


def fold_body(*refs):
    pairs = len(refs) // 6

    def add(first, second):
        return (first[...].astype(jnp.float32) + second[...].astype(jnp.float32)).astype(jnp.bfloat16)

    for index in range(pairs):
        kept_first, kept_second, came_first, came_second = refs[4 * index : 4 * index + 4]
        kept_ref, sent_ref = refs[4 * pairs + 2 * index : 4 * pairs + 2 * index + 2]
        sent_ref[...] = add(kept_second, came_second)
        kept_ref[...] = add(kept_first, came_first)


def fold(*pairs):
    halves = [kept.shape[0] // 2 for kept, _ in pairs]
    steps = next(n for n in (4, 2, 1) if n == 1 or all(rows % (16 * n) == 0 for rows in halves))
    in_specs, out_specs, out_shape, operands = [], [], [], []
    for rows, (kept, came) in zip(halves, pairs):
        columns = kept.shape[1]
        first = pl.BlockSpec((rows // steps, columns), lambda i: (i, 0))
        second = pl.BlockSpec((rows // steps, columns), lambda i: (i + steps, 0))
        in_specs += [first, second, first, second]
        operands += [kept, kept, came, came]
        out_specs += [first, first]
        out_shape += [jax.ShapeDtypeStruct((rows, columns), jnp.bfloat16)] * 2
    block_bytes = sum(6 * 2 * (rows // steps) * kept.shape[1] for rows, (kept, _) in zip(halves, pairs))
    out = pl.pallas_call(
        fold_body,
        grid=(steps,),
        in_specs=in_specs,
        out_specs=out_specs,
        out_shape=out_shape,
        compiler_params=pltpu.CompilerParams(vmem_limit_bytes=2 * block_bytes + 6 * 1024 * 1024),
        cost_estimate=SMALL,
        name="fold",
    )(*operands)
    return [out[2 * index : 2 * index + 2] for index in range(len(pairs))]


def sum_end(pair):
    return pair[0].astype(jnp.float32) + pair[1].astype(jnp.float32)


def place_body(device_ref, *refs):
    parts = refs[:-2]
    out_ref, semaphores = refs[-2:]
    device = device_ref[0]
    copies = [
        pltpu.make_async_copy(part, out_ref.at[:, device ^ mask], semaphores.at[mask])
        for mask, part in enumerate(parts)
    ]
    for copy in copies:
        copy.start()
    for copy in copies:
        copy.wait()


def place(parts, inner):
    top, rows, columns = parts[0].shape
    return pl.pallas_call(
        place_body,
        grid_spec=pltpu.PrefetchScalarGridSpec(
            num_scalar_prefetch=1,
            grid=(1,),
            in_specs=[pl.BlockSpec(memory_space=pl.ANY)] * len(parts),
            out_specs=pl.BlockSpec((top, len(parts), rows, columns), lambda i, d: (0, 0, 0, 0)),
            scratch_shapes=[pltpu.SemaphoreType.DMA((len(parts),))],
        ),
        out_shape=far((top, len(parts), rows, columns), parts[0].dtype)
        if top > 1
        else jax.ShapeDtypeStruct((top, len(parts), rows, columns), parts[0].dtype),
        compiler_params=pltpu.CompilerParams(vmem_limit_bytes=14 * 1024 * 1024),
        cost_estimate=SMALL,
        name="place",
    )(inner.reshape(1), *parts).reshape(top * len(parts) * rows, columns)


def gather_top(block, count):
    return [block, exchange(block, count, count // 4), exchange(block, count, count // 2)]


def gather_top_rest(blocks, count):
    return [block[None] for block in blocks + [exchange(blocks[2], count, count // 4)]]


def join_body(query_ref, key_ref, value_ref, gains_ref, out_ref):
    groups = KEY_VALUE_HEADS
    pair = query_ref.shape[1] // groups
    one = key_ref.shape[1] // groups
    shift = 0
    for group in range(groups):
        for ref, size in ((query_ref, pair), (key_ref, one), (value_ref, one)):
            out_ref[:, shift : shift + size] = ref[:, group * size : (group + 1) * size]
            shift += size
        if group == groups // 2 - 1:
            out_ref[:, shift : shift + 128] = gains_ref[...]
            shift += 128


def join(w_query, key_projection, value_projection, gains):
    rows = w_query.shape[0]
    columns = w_query.shape[1] + 2 * key_projection.shape[1] + 128
    return pl.pallas_call(
        join_body,
        out_shape=jax.ShapeDtypeStruct((rows, columns), w_query.dtype),
        cost_estimate=SMALL,
        name="join",
    )(w_query, key_projection, value_projection, gains)


def lay_top(blocks, device, count):
    return {0: place(blocks, device // (count // 4)).reshape((4,) + blocks[0].shape[1:])}


def split_body(device_ref, *refs):
    parts = refs[:4]
    left_ref, right_ref, semaphores = refs[4:]
    width = left_ref.shape[-1]
    copies = []
    for mask, part in enumerate(parts):
        target = device_ref[0] ^ mask
        copies += [
            pltpu.make_async_copy(part.at[:, :width], left_ref.at[target], semaphores.at[2 * mask]),
            pltpu.make_async_copy(part.at[:, width:], right_ref.at[target], semaphores.at[2 * mask + 1]),
        ]
    for copy in copies:
        copy.start()
    for copy in copies:
        copy.wait()


def lay_top_split(blocks, device, count, width):
    rows, columns = blocks[0].shape[1:]
    shapes = [(4, rows, width), (4, rows, columns - width)]
    return pl.pallas_call(
        split_body,
        grid_spec=pltpu.PrefetchScalarGridSpec(
            num_scalar_prefetch=1,
            grid=(1,),
            in_specs=[pl.BlockSpec(memory_space=pl.ANY)] * 4,
            out_specs=[pl.BlockSpec(shape, lambda i, d: (0, 0, 0)) for shape in shapes],
            scratch_shapes=[pltpu.SemaphoreType.DMA((8,))],
        ),
        out_shape=[jax.ShapeDtypeStruct(shape, blocks[0].dtype) for shape in shapes],
        compiler_params=pltpu.CompilerParams(vmem_limit_bytes=10 * 1024 * 1024),
        cost_estimate=SMALL,
        name="lay_top_split",
    )((device // (count // 4)).reshape(1), *[block[0] for block in blocks])


def gather_bits(parts, count, bits):
    parts = dict(parts)
    for bit in bits:
        for mask in list(parts):
            parts[mask | (1 << bit)] = exchange(parts[mask], count, 1 << bit)
    return parts


def lay(parts, device, count):
    return place([parts[mask] for mask in range(count // 4)], device & (count // 4 - 1))


def gain_columns(first, second, third, fourth, rows):
    columns = [jnp.pad(v, (0, rows - v.shape[0]))[:, None] for v in (first, second, third, fourth)]
    return jnp.pad(jnp.concatenate(columns, axis=1), ((0, 0), (0, 124)))


def swap_halves(head):
    return pltpu.roll(head, HEAD_SIZE // 2, 1)


def unit_head(raw):
    inverse = lax.rsqrt(jnp.mean(raw * raw, axis=-1, keepdims=True) + epsilon)
    return raw * inverse, inverse


def contract(left, right, left_axis, right_axis):
    return lax.dot_general(
        left, right, (((left_axis,), (right_axis,)), ((), ())), preferred_element_type=jnp.float32
    )


def block_scores(group, key_rows, first_row, row_start):
    scores = contract(group, key_rows, 1, 1) * (1.0 / math.sqrt(HEAD_SIZE))
    rows = lax.broadcasted_iota(jnp.int32, scores.shape, 0)
    half = scores.shape[0] // 2
    rows = jnp.where(rows >= half, rows - half, rows) + row_start
    columns = lax.broadcasted_iota(jnp.int32, scores.shape, 1)
    return jnp.where((columns <= rows) & (columns >= first_row), scores, -1e30)


def head_pair(ref, block):
    return jnp.concatenate([ref[block, :HEAD_SIZE], ref[block, HEAD_SIZE:]], axis=0)


def pair_rows(first_row_ref, block):
    rows = first_row_ref[block, :]
    return jnp.concatenate([rows, rows], axis=0)


GROUP = 4 * HEAD_SIZE


def attend_body(
    normed_ref, weight_ref, gains_ref, cosine_ref, sine_ref, first_ref,
    attended_ref, query_ref, key_ref, value_ref, raw_ref, total_ref,
):
    cosine = cosine_ref[...]
    sine = sine_ref[...]

    def turned(raw, gain):
        scaled = unit_head(raw)[0] * gain
        return (scaled * cosine + swap_halves(scaled) * sine).astype(jnp.bfloat16)

    raw = jnp.dot(normed_ref[...], weight_ref[...], preferred_element_type=jnp.float32)
    raw_ref[...] = raw[:, : 3 * HEAD_SIZE]
    for head in range(2):
        part = slice(head * HEAD_SIZE, (head + 1) * HEAD_SIZE)
        query_ref[:, part] = turned(raw[:, part], gains_ref[0:1, :])
    key_ref[...] = turned(raw[:, 2 * HEAD_SIZE : 3 * HEAD_SIZE], gains_ref[1:2, :])
    value_ref[...] = raw[:, 3 * HEAD_SIZE :].astype(jnp.bfloat16)
    step = 128
    for start in range(0, raw.shape[0], step):
        block = slice(start, start + step)
        seen = slice(0, start + step)
        scores = block_scores(head_pair(query_ref, block), key_ref[seen, :], pair_rows(first_ref, block), start)
        top = jnp.max(scores, axis=-1, keepdims=True)
        log_total = top + jnp.log(jnp.sum(jnp.exp(scores - top), axis=-1, keepdims=True))
        probs_low = jnp.exp(scores - log_total).astype(jnp.bfloat16)
        out = jnp.dot(probs_low, value_ref[seen, :], preferred_element_type=jnp.float32).astype(jnp.bfloat16)
        attended_ref[block, :HEAD_SIZE] = out[:step]
        attended_ref[block, HEAD_SIZE:] = out[step:]
        total_ref[0, block, 0:1] = log_total[:step]
        total_ref[0, block, 1:2] = log_total[step:]


def attend(normed, weight, head_gains, cosine, sine, first_row):
    rows, width = normed.shape
    groups = KEY_VALUE_HEADS // 2
    whole = lambda *shape: pl.BlockSpec(shape, lambda h: (0, 0))
    columns = lambda size: pl.BlockSpec((rows, size), lambda h: (0, h))
    low = lambda size: jax.ShapeDtypeStruct((rows, groups * size), jnp.bfloat16)
    pair = 2 * HEAD_SIZE
    return pl.pallas_call(
        attend_body,
        grid=(groups,),
        in_specs=[
            whole(rows, width),
            pl.BlockSpec((width, GROUP), lambda h: (0, h)),
            whole(2, HEAD_SIZE),
            whole(rows, HEAD_SIZE),
            whole(rows, HEAD_SIZE),
            whole(rows, 1),
        ],
        out_specs=[
            columns(pair),
            columns(pair),
            columns(HEAD_SIZE),
            columns(HEAD_SIZE),
            columns(3 * HEAD_SIZE),
            pl.BlockSpec((1, rows, 2), lambda h: (h, 0, 0)),
        ],
        out_shape=[
            low(pair),
            low(pair),
            low(HEAD_SIZE),
            low(HEAD_SIZE),
            jax.ShapeDtypeStruct((rows, groups * 3 * HEAD_SIZE), jnp.float32),
            jax.ShapeDtypeStruct((groups, rows, 2), jnp.float32),
        ],
        compiler_params=pltpu.CompilerParams(vmem_limit_bytes=26 * 1024 * 1024),
        cost_estimate=SMALL,
        name="attend",
    )(normed, weight, head_gains, cosine, sine, first_row)


def attend_back_body(
    device_ref, residual_ref, wo_ref, query_ref, key_ref, value_ref, raw_ref, total_ref,
    gains_ref, cosine_ref, sine_ref, first_ref, turned_ref, weight_ref, *refs,
    order, shard, head_shard, last, head=None,
):
    if last:
        head_gains_in_ref, normed_in_ref = refs[:2]
        refs = refs[2:]
        tokens_ref, gain_ref, grad_residual_ref, gain_two_ref, kept_ref, sent_ref, tokens_out_ref = refs[:7]
        head_gains_ref, normed_sum_ref, lines_ref = refs[7:10]
        scratch = refs[10:]
    else:
        kept_ref, sent_ref, head_gains_ref, normed_sum_ref = refs[:4]
        scratch = refs[4:]
    grad_out_ref, query_sum_ref, key_sum_ref, value_sum_ref, grads_ref = scratch
    scale = 1.0 / math.sqrt(HEAD_SIZE)
    heads = KEY_VALUE_HEADS // 2
    if head is None:
        head = pl.program_id(0)

    @pl.when(head == 0)
    def _():
        head_gains_ref[...] = head_gains_in_ref[...] if last else jnp.zeros_like(head_gains_ref)
        normed_sum_ref[...] = normed_in_ref[...] if last else jnp.zeros_like(normed_sum_ref)

    grad_out_ref[...] = contract(residual_ref[...], wo_ref[...], 1, 1).astype(jnp.bfloat16)
    key_sum_ref[...] = jnp.zeros_like(key_sum_ref)
    value_sum_ref[...] = jnp.zeros_like(value_sum_ref)
    step = 128
    for start in range(0, residual_ref.shape[0], step):
        block = slice(start, start + step)
        seen = slice(0, start + step)
        group = head_pair(query_ref, block)
        grad_out = head_pair(grad_out_ref, block)
        key_rows = key_ref[seen, :]
        scores = block_scores(group, key_rows, pair_rows(first_ref, block), start)
        log_total = jnp.concatenate([total_ref[0, block, 0:1], total_ref[0, block, 1:2]], axis=0)
        probs = jnp.exp(scores - log_total)
        grad_probs = contract(grad_out, value_ref[seen, :], 1, 1)
        value_sum_ref[seen, :] += contract(probs.astype(jnp.bfloat16), grad_out, 0, 0)
        inner = jnp.sum(probs * grad_probs, axis=-1, keepdims=True)
        grad_scores = (probs * (grad_probs - inner)).astype(jnp.bfloat16)
        grad_group = jnp.dot(grad_scores, key_rows, preferred_element_type=jnp.float32) * scale
        query_sum_ref[block, :HEAD_SIZE] = grad_group[:step]
        query_sum_ref[block, HEAD_SIZE:] = grad_group[step:]
        key_sum_ref[seen, :] += contract(grad_scores, group, 0, 0)
    grads_ref[:, 3 * HEAD_SIZE :] = value_sum_ref[...].astype(jnp.bfloat16)
    cosine = cosine_ref[...]
    sine = sine_ref[...]

    def back(grad, part, gain):
        turned = grad * cosine - swap_halves(grad) * sine
        unit, inverse = unit_head(raw_ref[:, part])
        product = turned * unit
        scaled = turned * gain
        grad_raw = inverse * (scaled - unit * jnp.mean(product * gain, axis=-1, keepdims=True))
        grads_ref[:, part] = grad_raw.astype(jnp.bfloat16)
        return jnp.sum(product, axis=0, keepdims=True)

    for index in range(2):
        part = slice(index * HEAD_SIZE, (index + 1) * HEAD_SIZE)
        head_gains_ref[0:1, :] += back(query_sum_ref[:, part], part, gains_ref[0:1, :])
    part = slice(2 * HEAD_SIZE, 3 * HEAD_SIZE)
    head_gains_ref[1:2, :] += back(key_sum_ref[...] * scale, part, gains_ref[1:2, :])

    grads = grads_ref[...]
    half = turned_ref.shape[0] // 2
    product = jnp.dot(turned_ref[...], grads, preferred_element_type=jnp.float32).astype(jnp.bfloat16)
    columns = pl.ds(pl.multiple_of(head * GROUP, GROUP), GROUP)
    kept_ref[:, columns] = product[:half]
    sent_ref[:, columns] = product[half:]
    normed_sum_ref[...] += contract(grads, weight_ref[...], 1, 1)

    if not last:
        return

    @pl.when(head == heads - 1)
    def _():
        unit, inverse = unit_head(tokens_ref[...].astype(jnp.float32))
        grad = normed_sum_ref[...]
        scaled = grad * gain_ref[...]
        grad_first = inverse * (scaled - unit * jnp.mean(scaled * unit, axis=-1, keepdims=True))
        tokens_out_ref[...] = (grad_residual_ref[...] + grad_first).astype(jnp.bfloat16)
        width = grad.shape[1]
        source = lax.broadcasted_iota(jnp.int32, (HEAD_SIZE, width), 0)
        target = lax.broadcasted_iota(jnp.int32, (HEAD_SIZE, width), 1)
        spread = jnp.where(source // head_shard * shard + source % head_shard == target, 1.0, 0.0)
        heads = jnp.dot(
            head_gains_ref[...], spread, precision=lax.Precision.HIGHEST, preferred_element_type=jnp.float32
        )
        lines = jnp.concatenate(
            [
                jnp.sum(grad * unit, axis=0, keepdims=True),
                gain_two_ref[...],
                heads,
                jnp.zeros((124, width), jnp.float32),
            ],
            axis=0,
        )
        lines_ref[...] = lines.T
        device = device_ref[0]
        group = max(1, 16 // shard)
        end = slice(kept_ref.shape[1] - 128, None)
        for first in range(0, len(order), group):
            blocks = [
                lines_ref[pl.ds(pl.multiple_of((device ^ mask) * shard, shard), shard), :]
                for mask in order[first : first + group]
            ]
            block = (blocks[0] if group == 1 else jnp.concatenate(blocks, axis=0)).astype(jnp.bfloat16)
            row = first * shard
            target_ref = kept_ref if row < half else sent_ref
            target_ref[row % half : row % half + group * shard, end] = block


def attend_back_specs(rows, width, part, head):
    first = part * KEY_VALUE_HEADS // 2
    whole = lambda *shape: pl.BlockSpec(shape, lambda *j: (0, 0))
    columns = lambda height, size: pl.BlockSpec((height, size), lambda *j: (0, head(*j)))
    pair = 2 * HEAD_SIZE
    return [
        pl.BlockSpec((pair, width), lambda *j: (head(*j) + first, 0)),
        columns(rows, pair),
        columns(rows, HEAD_SIZE),
        columns(rows, HEAD_SIZE),
        columns(rows, 3 * HEAD_SIZE),
        pl.BlockSpec((1, rows, 2), lambda *j: (head(*j), 0, 0)),
        whole(2, HEAD_SIZE),
        whole(rows, HEAD_SIZE),
        whole(rows, HEAD_SIZE),
        whole(rows, 1),
        whole(width, rows),
        columns(width, GROUP),
    ]


def attend_back_scratch(rows):
    pair = 2 * HEAD_SIZE
    return [
        pltpu.VMEM((rows, pair), jnp.bfloat16),
        pltpu.VMEM((rows, pair), jnp.float32),
        pltpu.VMEM((rows, HEAD_SIZE), jnp.float32),
        pltpu.VMEM((rows, HEAD_SIZE), jnp.float32),
        pltpu.VMEM((rows, GROUP), jnp.bfloat16),
    ]


def attend_back_last(
    device, residual_low, operands, sums, tokens, gain, grad_residual, grad_gain_two, order, shard, head_shard
):
    rows, width = residual_low.shape
    whole = lambda *shape: pl.BlockSpec(shape, lambda *j: (0, 0))
    own_width = KEY_VALUE_HEADS * 2 * HEAD_SIZE + 128
    half = jax.ShapeDtypeStruct((width // 2, own_width), jnp.bfloat16)
    return pl.pallas_call(
        functools.partial(attend_back_body, order=order, shard=shard, head_shard=head_shard, last=True),
        grid_spec=pltpu.PrefetchScalarGridSpec(
            num_scalar_prefetch=1,
            grid=(KEY_VALUE_HEADS // 2,),
            in_specs=[whole(rows, width)]
            + attend_back_specs(rows, width, 1, lambda h, d: h)
            + [whole(2, HEAD_SIZE), whole(rows, width)]
            + [whole(rows, width), whole(1, width), whole(rows, width), whole(1, width)],
            out_specs=[whole(width // 2, own_width), whole(width // 2, own_width), whole(rows, width)],
            scratch_shapes=[
                pltpu.VMEM((2, HEAD_SIZE), jnp.float32),
                pltpu.VMEM((rows, width), jnp.float32),
                pltpu.VMEM((width, 128), jnp.float32),
            ]
            + attend_back_scratch(rows),
        ),
        out_shape=[half, half, jax.ShapeDtypeStruct((rows, width), jnp.bfloat16)],
        compiler_params=pltpu.CompilerParams(vmem_limit_bytes=38 * 1024 * 1024),
        cost_estimate=SMALL,
        name="attend_back_last",
    )(device.reshape(1), residual_low, *operands, *sums, tokens, gain, grad_residual, grad_gain_two)


def gather_down(down_ref, down_weight_ref, width):
    devices, rows, _ = down_ref.shape
    pieces = down_ref.shape[2] // width
    for index in range(devices):
        for piece in range(pieces):
            first = (index * pieces + piece) * rows
            down_weight_ref[first : first + rows, :] = down_ref[index, :, piece * width : (piece + 1) * width]


def feed_forward_body(
    device_ref, residual_ref, gain_ref, cotangent_ref, gate_ref, up_ref, down_ref,
    hidden_ref, grad_gate_ref, grad_up_ref, gate_kept_ref, gate_sent_ref, up_kept_ref, up_sent_ref,
    down_kept_ref, down_sent_ref, normed_ref, down_weight_ref, turned_ref, for_gate_ref, for_up_ref, product_ref,
    *, gate_order, up_order,
):
    device = device_ref[0]
    width = residual_ref.shape[1]

    @pl.when(pl.program_id(0) == 0)
    def _():
        unit, _ = unit_head(residual_ref[...])
        normed = (unit * gain_ref[...]).astype(jnp.bfloat16)
        normed_ref[...] = normed
        turned_ref[...] = normed.astype(turned_ref.dtype).T
        rows = width // len(gate_order)
        group = max(1, 16 // rows)
        for order, ref in ((gate_order, for_gate_ref), (up_order, for_up_ref)):
            for first in range(0, len(order), group):
                blocks = [
                    turned_ref[pl.ds(pl.multiple_of((device ^ mask) * rows, rows), rows), :]
                    for mask in order[first : first + group]
                ]
                block = blocks[0] if group == 1 else jnp.concatenate(blocks, axis=0)
                ref[first * rows : (first + group) * rows, :] = block.astype(jnp.bfloat16)

    normed = normed_ref[...]
    gather_down(down_ref, down_weight_ref, width)
    cotangent = cotangent_ref[...]
    gate = jnp.dot(normed, gate_ref[...].reshape(width, gate_ref.shape[-1]), preferred_element_type=jnp.float32)
    up = jnp.dot(normed, up_ref[...].reshape(width, up_ref.shape[-1]), preferred_element_type=jnp.float32)
    grad_hidden = contract(cotangent, down_weight_ref[...], 1, 1)
    sigmoid = jax.nn.sigmoid(gate)
    silu = gate * sigmoid
    hidden = (silu * up).astype(jnp.bfloat16)
    grad_gate = (grad_hidden * up * sigmoid * (1.0 + gate * (1.0 - sigmoid))).astype(jnp.bfloat16)
    hidden_ref[...] = hidden
    grad_gate_ref[...] = grad_gate
    grad_up = (grad_hidden * silu).astype(jnp.bfloat16)
    grad_up_ref[...] = grad_up

    for ordered_ref, grad, kept_ref, sent_ref in (
        (for_gate_ref, grad_gate, gate_kept_ref, gate_sent_ref),
        (for_up_ref, grad_up, up_kept_ref, up_sent_ref),
    ):
        product = jnp.dot(ordered_ref[...], grad, preferred_element_type=jnp.float32).astype(jnp.bfloat16)
        half = product.shape[0] // 2
        kept_ref[...] = product[:half]
        sent_ref[...] = product[half:]
    product_ref[...] = contract(hidden, cotangent, 0, 0).reshape(product_ref.shape)
    owners = product_ref.shape[0]
    low = device & (owners - 1)
    for target, core in ((down_kept_ref, 0), (down_sent_ref, 1)):
        blocks = [product_ref[low ^ (index | core)] for index in range(0, owners, 2)]
        target[...] = jnp.concatenate(blocks, axis=0).astype(jnp.bfloat16)


def ffn_operands(weights, shard, width, tiles, at):
    count, _, hidden_width = weights.shape
    tile = hidden_width // tiles
    if shard % 16 == 0:
        return [weights, weights, weights], [
            pl.BlockSpec((count, shard, tile), lambda *j: (0, 0, at(*j))),
            pl.BlockSpec((count, shard, tile), lambda *j: (0, 1, at(*j))),
            pl.BlockSpec((count // tiles, shard, hidden_width), lambda *j: (at(*j), 2, 0)),
        ]
    gate, up, down = (weights[:, part * shard : (part + 1) * shard] for part in range(3))
    down = down.reshape(count, shard, -1, width).transpose(0, 2, 1, 3).reshape(tiles, tile, width)
    return [gate.reshape(width, hidden_width), up.reshape(width, hidden_width), down], [
        pl.BlockSpec((width, tile), lambda *j: (0, at(*j))),
        pl.BlockSpec((width, tile), lambda *j: (0, at(*j))),
        pl.BlockSpec((1, tile, width), lambda *j: (at(*j), 0, 0)),
    ]


def feed_forward(device, residual, gain, cotangent, weights, shard, gate_order, up_order):
    rows, width = residual.shape
    count, _, hidden_width = weights.shape
    tiles = 8
    tile = hidden_width // tiles
    owners = count // tiles
    at = lambda j, d: j ^ (d[0] // owners)
    back = lambda j: (j & 1) * 4 + j // 2
    whole = pl.BlockSpec((rows, width), lambda j, d: (0, 0))
    row = pl.BlockSpec((1, width), lambda j, d: (0, 0))
    low = lambda height, size: jax.ShapeDtypeStruct((height, size), jnp.bfloat16)
    weight_args, weight_specs = ffn_operands(weights, shard, width, tiles, at)
    columns = lambda height: pl.BlockSpec((height, tile), lambda j, d: (0, at(j, d)))
    down_half = pl.BlockSpec((tile // 2, width), lambda j, d: (back(j), 0))
    return pl.pallas_call(
        functools.partial(feed_forward_body, gate_order=gate_order, up_order=up_order),
        grid_spec=pltpu.PrefetchScalarGridSpec(
            num_scalar_prefetch=1,
            grid=(tiles,),
            in_specs=[whole, row, whole] + weight_specs,
            out_specs=[
                columns(rows),
                columns(rows),
                columns(rows),
                columns(width // 2),
                columns(width // 2),
                columns(width // 2),
                columns(width // 2),
                down_half,
                down_half,
            ],
            scratch_shapes=[
                pltpu.VMEM((rows, width), jnp.bfloat16),
                pltpu.VMEM((tile, width), jnp.bfloat16),
                pltpu.VMEM((width, rows), jnp.bfloat16 if shard % 16 == 0 else jnp.float32),
                pltpu.VMEM((width, rows), jnp.bfloat16),
                pltpu.VMEM((width, rows), jnp.bfloat16),
                pltpu.VMEM((owners, tile // owners, width), jnp.float32),
            ],
        ),
        out_shape=[
            low(rows, hidden_width),
            low(rows, hidden_width),
            low(rows, hidden_width),
            low(width // 2, hidden_width),
            low(width // 2, hidden_width),
            low(width // 2, hidden_width),
            low(width // 2, hidden_width),
            low(hidden_width // 2, width),
            low(hidden_width // 2, width),
        ],
        compiler_params=pltpu.CompilerParams(vmem_limit_bytes=40 * 1024 * 1024),
        cost_estimate=SMALL,
        name="feed_forward",
    )(device.reshape(1), residual, gain, cotangent, *weight_args)


FFN_STEPS = 8


def back_body(device_ref, *refs):
    (
        residual_ref, gain_ref, cotangent_ref, grad_gate_ref, grad_up_ref, gate_ref, up_ref, turned_out_ref
    ), refs = refs[:8], refs[8:]
    operands, refs = refs[:12], refs[12:]
    (
        grad_residual_ref, grad_low_ref, grad_gain_ref, out_kept_ref, out_sent_ref, kept_ref, sent_ref, head_gains_ref,
        normed_sum_ref, back_ref,
    ), scratch = refs[:10], refs[10:]
    step = pl.program_id(0)
    width = residual_ref.shape[1]

    @pl.when(step == 0)
    def _():
        back_ref[...] = jnp.zeros_like(back_ref)

    @pl.when(step < FFN_STEPS)
    def _():
        back_ref[...] += contract(
            grad_gate_ref[...], gate_ref[...].reshape(width, gate_ref.shape[-1]), 1, 1
        ) + contract(grad_up_ref[...], up_ref[...].reshape(width, up_ref.shape[-1]), 1, 1)

    @pl.when(step == FFN_STEPS - 1)
    def _():
        unit, inverse = unit_head(residual_ref[...])
        grad = back_ref[...]
        grad_gain_ref[...] = jnp.sum(grad * unit, axis=0, keepdims=True)
        scaled = grad * gain_ref[...]
        grad_mid = inverse * (scaled - unit * jnp.mean(scaled * unit, axis=-1, keepdims=True))
        grad_residual = cotangent_ref[...].astype(jnp.float32) + grad_mid
        grad_residual_ref[...] = grad_residual
        grad_low = grad_residual.astype(jnp.bfloat16)
        grad_low_ref[...] = grad_low
        half = out_kept_ref.shape[0]
        for start in range(0, half, 512):
            for ref, shift in ((out_kept_ref, 0), (out_sent_ref, half)):
                rows = slice(start + shift, start + shift + 512)
                ref[start : start + 512, :] = jnp.dot(
                    turned_out_ref[rows, :], grad_low, preferred_element_type=jnp.float32
                ).astype(jnp.bfloat16)

    @pl.when(step >= FFN_STEPS)
    def _():
        attend_back_body(
            device_ref, grad_low_ref, *operands, kept_ref, sent_ref, head_gains_ref, normed_sum_ref, *scratch,
            order=None, shard=None, head_shard=None, last=False, head=step - FFN_STEPS,
        )


def back(device, residual, gain, cotangent, grad_gate, grad_up, weights, shard, turned_out, operands):
    rows, width = residual.shape
    tile = weights.shape[2] // FFN_STEPS
    at = lambda j, d: jnp.minimum(j, FFN_STEPS - 1)
    head = lambda j, d: jnp.maximum(j - FFN_STEPS, 0)
    whole = lambda *shape: pl.BlockSpec(shape, lambda *j: (0, 0))
    columns = pl.BlockSpec((rows, tile), lambda *j: (0, at(*j)))
    weight_args, weight_specs = ffn_operands(weights, shard, width, FFN_STEPS, at)
    out_rows = turned_out.shape[0]
    own_width = KEY_VALUE_HEADS * 2 * HEAD_SIZE
    low = lambda height, size: jax.ShapeDtypeStruct((height, size), jnp.bfloat16)
    wide = jax.ShapeDtypeStruct((rows, width), jnp.float32)
    return pl.pallas_call(
        back_body,
        grid_spec=pltpu.PrefetchScalarGridSpec(
            num_scalar_prefetch=1,
            grid=(FFN_STEPS + KEY_VALUE_HEADS // 2,),
            in_specs=[whole(rows, width), whole(1, width), whole(rows, width), columns, columns]
            + weight_specs[:2]
            + [whole(out_rows, rows)]
            + attend_back_specs(rows, width, 0, head),
            out_specs=[
                whole(rows, width),
                whole(rows, width),
                whole(1, width),
                whole(out_rows // 2, width),
                whole(out_rows // 2, width),
                whole(width // 2, own_width),
                whole(width // 2, own_width),
                whole(2, HEAD_SIZE),
                whole(rows, width),
            ],
            scratch_shapes=[pltpu.VMEM((rows, width), jnp.float32)] + attend_back_scratch(rows),
        ),
        out_shape=[
            wide,
            low(rows, width),
            jax.ShapeDtypeStruct((1, width), jnp.float32),
            low(out_rows // 2, width),
            low(out_rows // 2, width),
            low(width // 2, own_width),
            low(width // 2, own_width),
            jax.ShapeDtypeStruct((2, HEAD_SIZE), jnp.float32),
            wide,
        ],
        compiler_params=pltpu.CompilerParams(vmem_limit_bytes=46 * 1024 * 1024),
        cost_estimate=SMALL,
        name="back",
    )(device.reshape(1), residual, gain, cotangent, grad_gate, grad_up, *weight_args[:2], turned_out, *operands)


def ffn_out_body(residual_ref, hidden_ref, down_ref, mixed_ref, sum_ref, down_weight_ref):
    @pl.when(pl.program_id(0) == 0)
    def _():
        sum_ref[...] = residual_ref[...]

    gather_down(down_ref, down_weight_ref, residual_ref.shape[1])
    sum_ref[...] += jnp.dot(hidden_ref[...], down_weight_ref[...], preferred_element_type=jnp.float32)

    @pl.when(pl.program_id(0) == pl.num_programs(0) - 1)
    def _():
        mixed_ref[...] = sum_ref[...].astype(jnp.bfloat16)


def ffn_out(residual, hidden, weights, shard):
    rows, width = residual.shape
    tiles = 8
    tile = weights.shape[2] // tiles
    whole = pl.BlockSpec((rows, width), lambda j: (0, 0))
    weight_args, weight_specs = ffn_operands(weights, shard, width, tiles, lambda j: j)
    return pl.pallas_call(
        ffn_out_body,
        grid=(tiles,),
        in_specs=[whole, pl.BlockSpec((rows, tile), lambda j: (0, j)), weight_specs[2]],
        out_specs=whole,
        out_shape=jax.ShapeDtypeStruct((rows, width), jnp.bfloat16),
        scratch_shapes=[pltpu.VMEM((rows, width), jnp.float32), pltpu.VMEM((tile, width), jnp.bfloat16)],
        compiler_params=pltpu.CompilerParams(vmem_limit_bytes=16 * 1024 * 1024),
        cost_estimate=SMALL,
        name="ffn_out",
    )(residual, hidden, weight_args[2])


def end_body(first_kept, first_came, second_kept, second_came, query_ref, key_ref, value_ref, *gain_refs):
    def part(kept, came, start, size):
        columns = slice(start, start + size)
        return kept[:, columns].astype(jnp.float32) + came[:, columns].astype(jnp.float32)

    group = 0
    for kept, came in ((first_kept, first_came), (second_kept, second_came)):
        for start in range(0, KEY_VALUE_HEADS // 2 * GROUP, GROUP):
            for ref, size in ((query_ref, 2 * HEAD_SIZE), (key_ref, HEAD_SIZE), (value_ref, HEAD_SIZE)):
                ref[:, group * size : (group + 1) * size] = part(kept, came, start, size)
                start += size
            group += 1
    gains = part(second_kept, second_came, KEY_VALUE_HEADS // 2 * GROUP, 128).T
    for index, ref in enumerate(gain_refs):
        ref[...] = gains[index : index + 1, : ref.shape[1]]


def end_projections(first, second, head_shard):
    rows = first[0].shape[0]
    query_width, key_width = QUERY_HEADS * HEAD_SIZE, KEY_VALUE_HEADS * HEAD_SIZE
    return pl.pallas_call(
        end_body,
        out_shape=[
            jax.ShapeDtypeStruct(shape, jnp.float32)
            for shape in (
                (rows, query_width), (rows, key_width), (rows, key_width), (1, rows), (1, rows), (1, head_shard),
                (1, head_shard),
            )
        ],
        cost_estimate=SMALL,
        name="end_projections",
    )(*first, *second)


def on_device(
    tokens,
    seq_lengths,
    seq_owner,
    g_attn,
    w_query,
    key_projection,
    value_projection,
    query_norm_gain,
    g_key,
    w_out,
    g_ffn,
    w_gate,
    w_up,
    w_down,
    cotangent,
):
    row_total_count = tokens.shape[0]
    fence = lax.optimization_barrier
    count = lax.axis_size("fsdp")
    device = lax.axis_index("fsdp")
    early = middle_bits(count, False)
    late = middle_bits(count, True)
    cut_bits = len(early) // 2
    shard = g_attn.shape[0]
    head_shard = query_norm_gain.shape[0]

    pieces = w_down.shape[0] // shard
    down_pieces = w_down.reshape(pieces, shard, -1).transpose(1, 0, 2).reshape(shard, -1)
    ffn_weights = lax.all_gather(jnp.concatenate([w_gate, w_up, down_pieces], axis=0), "fsdp", axis=0, tiled=False)
    projections = join(
        w_query, key_projection, value_projection, gain_columns(g_attn, g_ffn, query_norm_gain, g_key, shard)
    )
    top = gather_top(projections, count)
    top, w_out = fence((top, w_out))
    top = gather_top_rest(top, count)
    top, w_out = fence((top, w_out))
    first_part, second_part = lay_top_split(top, device, count, KEY_VALUE_HEADS // 2 * GROUP + 128)
    first_parts = gather_bits({0: first_part}, count, early[:cut_bits])
    second_parts = gather_bits({0: second_part}, count, late[:cut_bits])
    out_top = gather_top(w_out, count)
    first_parts, second_parts, out_top = fence((first_parts, second_parts, out_top))
    first_parts = gather_bits(first_parts, count, early[cut_bits:])
    second_parts = gather_bits(second_parts, count, late[cut_bits:])
    out_top = gather_top_rest(out_top, count)
    first_parts, second_parts, out_top = fence((first_parts, second_parts, out_top))
    first_parts = gather_bits(first_parts, count, [0])
    out_parts = gather_bits(lay_top(out_top, device, count), count, early[:cut_bits])
    first_parts, second_parts = fence((first_parts, second_parts))
    second_parts = gather_bits(second_parts, count, [0])
    first_weight = lay(first_parts, device, count)

    seq_id, token_position = layout(seq_lengths, seq_owner, device, row_total_count)
    first_row = (jnp.arange(row_total_count, dtype=jnp.int32) - token_position)[:, None]
    cosine, sine = rotation_factors(token_position)
    inputs = tokens.astype(jnp.float32)
    gain_block = first_weight[:, KEY_VALUE_HEADS // 2 * GROUP :].astype(jnp.float32)
    head_gains = gain_block.reshape(count, shard, 128)[:, :head_shard, 2:4].reshape(HEAD_SIZE, 2).T
    gain_one = gain_block[:, 0]
    gain_two = gain_block[:, 1]
    normed_low = norm_forward(inputs, gain_one)[0].astype(jnp.bfloat16)
    attended_first, *saved_first = attend(normed_low, first_weight, head_gains, cosine, sine, first_row)
    attended_first, second_parts, out_parts = fence((attended_first, second_parts, out_parts))
    out_parts = gather_bits(out_parts, count, early[cut_bits:])
    second_weight = lay(second_parts, device, count)
    attended_second, *saved_second = attend(normed_low, second_weight, head_gains, cosine, sine, first_row)
    stages = sum_bits(count)
    orders = {name: row_order(count, bits) for name, bits in stages.items()}
    turned = {
        name: turn(values, device, orders[name])
        for name, values in (
            ("out", (attended_first, attended_second)), ("first", (normed_low,)), ("second", (normed_low,))
        )
    }
    attended_first, attended_second, turned, out_parts = fence((attended_first, attended_second, turned, out_parts))
    out_parts = gather_bits(out_parts, count, [0])
    out_weight = lay(out_parts, device, count)
    half_width = out_weight.shape[0] // 2
    residual = (
        inputs
        + jnp.dot(attended_first, out_weight[:half_width], preferred_element_type=jnp.float32)
        + jnp.dot(attended_second, out_weight[half_width:], preferred_element_type=jnp.float32)
    )
    (
        hidden, grad_gate, grad_up, gate_kept, gate_sent, up_kept, up_sent, down_kept, down_sent
    ) = feed_forward(
        device, residual, gain_two[None], cotangent, ffn_weights, shard, orders["gate"], orders["up"]
    )

    live = dict(
        hidden=hidden, grad_gate=grad_gate, grad_up=grad_up, gate=gate_kept, up=up_kept, down=down_kept,
    )
    flying = {}

    def cut():
        live.update(fence(dict(live)))

    def fly(**sent):
        live.update({name + "_sent": value for name, value in sent.items()})
        cut()
        for name in sent:
            flying[name] = exchange(live.pop(name + "_sent"), count, 1 << stages[name].pop(0))

    def land(*names):
        live.update({name + "_came": flying.pop(name) for name in names})
        cut()

    def halve(*names):
        halves = fold(*[(live[name], live.pop(name + "_came")) for name in names])
        live.update({name: kept for name, (kept, _) in zip(names, halves)})
        fly(**{name: sent for name, (_, sent) in zip(names, halves)})

    def pass_on(*names):
        land(*names)
        halve(*names)

    def end(*names):
        land(*names)
        return [(live.pop(name), live.pop(name + "_came")) for name in names]

    def operands(name, saved, weight):
        return out_weight, *saved, head_gains, cosine, sine, first_row, turned[name], weight

    fly(down=down_sent, gate=gate_sent, up=up_sent)
    pass_on("down")
    pass_on("gate")
    pass_on("up")
    (
        live["grad_residual"], live["low"], live["grad_gain_two"], live["out"], live["out_sent"], live["first"],
        live["first_sent"], live["head_sums"], live["normed_sum"],
    ) = back(
        device, residual, gain_two[None], cotangent, live.pop("grad_gate"), live.pop("grad_up"), ffn_weights, shard,
        turned["out"], operands("first", saved_first, first_weight),
    )
    land("down", "gate", "up")
    fly(first=live["first_sent"], out=live["out_sent"])
    halve("down", "gate", "up")
    pass_on("first", "out")
    live["second"], live["second_sent"], live["grad_tokens"] = attend_back_last(
        device, live.pop("low"), operands("second", saved_second, second_weight), (live.pop("head_sums"), live.pop("normed_sum")), tokens,
        gain_one[None], live.pop("grad_residual"), live.pop("grad_gain_two"), orders["second"], shard, head_shard,
    )
    land("down", "gate", "up", "first", "out")
    fly(second=live["second_sent"])
    halve("down", "gate", "up")
    land("second")
    halve("first", "out", "second")
    live["mixed"] = ffn_out(residual, live.pop("hidden"), ffn_weights, shard)
    cut()
    mixed, grad_tokens = live.pop("mixed"), live.pop("grad_tokens")
    while stages["down"]:
        pass_on("down", "gate", "up")
        pass_on("first", "out", "second")
    sums = {name: sum_end(pair) for name, pair in zip(("down", "gate", "up"), end("down", "gate", "up"))}
    live.update(sums)
    while stages["out"]:
        pass_on("first", "out", "second")
    sum_down, sum_gate, sum_up = live.pop("down"), live.pop("gate"), live.pop("up")
    first, out = end("first", "out")
    pass_on_last = stages["second"]
    while pass_on_last:
        pass_on("second")
    (second,) = end("second")
    sum_out = sum_end(out)
    sum_query, sum_key, sum_value, *sum_gains = end_projections(first, second, head_shard)
    return (
        mixed,
        grad_tokens,
        sum_gains[0].reshape(-1),
        sum_query,
        sum_key,
        sum_value,
        sum_gains[2].reshape(-1),
        sum_gains[3].reshape(-1),
        sum_out,
        sum_gains[1].reshape(-1),
        sum_gate,
        sum_up,
        sum_down,
    )


def solution(mesh):
    return jax.shard_map(
        on_device,
        mesh=mesh,
        in_specs=(
            P("fsdp", None),
            P(),
            P(),
            P("fsdp"),
            P("fsdp", None),
            P("fsdp", None),
            P("fsdp", None),
            P("fsdp"),
            P("fsdp"),
            P("fsdp", None),
            P("fsdp"),
            P("fsdp", None),
            P("fsdp", None),
            P("fsdp", None),
            P("fsdp", None),
        ),
        out_specs=(
            P("fsdp", None),
            P("fsdp", None),
            P("fsdp"),
            P("fsdp", None),
            P("fsdp", None),
            P("fsdp", None),
            P("fsdp"),
            P("fsdp"),
            P("fsdp", None),
            P("fsdp"),
            P("fsdp", None),
            P("fsdp", None),
            P("fsdp", None),
        ),
        check_vma=False,
    )
```

time: 438 us -> 418 us (0.954)
  starting transfers between devices: 79.1 us -> 56.8 us
  Pallas kernels: 157 us -> 145 us
  waiting for transfers between devices: 139 us -> 147 us
  local copies, waits for them, and re-layouts: 32.8 us -> 38.5 us
    ppermute x52 -> x57, starting transfers between devices: 79 us -> 56.7 us  [exchange(): lax.ppermute(values, 'fsdp', [(source, source ^ mask) for source in range...]
    pallas_call x50 -> x19, Pallas kernels: 149 us -> 131 us  [the longest x1 35.1 us: back(): pl.pallas_call(back_body, grid_spec=pltpu.PrefetchScalarGridSpec(num_scal...]
    ppermute x52 -> x57, waiting for transfers between devices: 139 us -> 147 us  [exchange(): lax.ppermute(values, 'fsdp', [(source, source ^ mask) for source in range...]
    pallas_call x4, Pallas kernels: 5.49 us -> 12 us  [place(): pl.pallas_call(place_body, grid_spec=pltpu.PrefetchScalarGridSpec(num_sca...]
    unnamed x129 -> x153, local copies, waits for them, and re-layouts: 28.7 us -> 33.2 us
  transfers between devices with their start and end apart: 54 -> 58, of which waited for: 23 -> 33; matrix products, arithmetic and copies ran while one was open for 2% -> 3% of each run, Pallas kernels for 27% -> 25%
where the time goes in v4:
time: 418 us; the launch traced here: 414 us
  waiting for transfers between devices  147 us (35%)
  Pallas kernels  145 us (35%)
  starting transfers between devices  56.8 us (14%)
  local copies, waits for them, and re-layouts  38.5 us (9%)
  between operations  14.9 us (4%)
  other arithmetic  9.73 us (2%)
    ppermute x57, waiting for transfers between devices, exchange(): lax.ppermute(values, 'fsdp', [(source, source ^ mask) for source in range...  147 us
    ppermute x57, starting transfers between devices, exchange(): lax.ppermute(values, 'fsdp', [(source, source ^ mask) for source in range...  56.7 us
    pallas_call x1, Pallas kernels, back(): pl.pallas_call(back_body, grid_spec=pltpu.PrefetchScalarGridSpec(num_scal...  35.1 us
    unnamed x153, local copies, waits for them, and re-layouts  33.2 us
    pallas_call x1, Pallas kernels, feed_forward(): pl.pallas_call(functools.partial(feed_forward_body, gate_order=gate_order...  31.3 us
    pallas_call x11, Pallas kernels, fold(): pl.pallas_call(fold_body, grid=(steps,), in_specs=in_specs, out_specs=out...  18.5 us
    pallas_call x2, Pallas kernels, attend(): pl.pallas_call(attend_body, grid=(groups,), in_specs=[whole(rows, width),...  18 us
    pallas_call x1, Pallas kernels, attend_back_last(): pl.pallas_call(functools.partial(attend_back_body, order=order, shard=sha...  18 us
  transfers between devices with their start and end apart: 58, of which 33 were waited for; matrix products, arithmetic and copies ran while one was open for 3% of the time, Pallas kernels for 25%

profile of v4, /device:TPU:0, one launch (start us, length us, event | category | flops | bytes accessed | tf_op | source)
XLA Modules:
  0.0 413.8 jit_solution(131784334698023971)
XLA Ops:
  12.9 4.0 collective-permute-start.1
  18.6 16.3 %collective-permute-done.1 = bf16[32,4224]{1,0:T(8,128)(2,1)S(1)} collective-permute-done((bf16[32,4224]{1,0:T(8,128)(2,1)}, bf16[32,4224]{1,0:T(8,128)(2,1)S(1)}, u32[]{:S(2)}, u32[]{:S(2)}) %collective-permute-start.1) | collective-permute-done | bytes 270368 | tf_op jit(solution)/shard_map/ppermute | solution.py:61
  35.4 4.0 collective-permute-start.2
  39.4 8.8 %collective-permute-done.2 = bf16[32,4224]{1,0:T(8,128)(2,1)S(1)} collective-permute-done((bf16[32,4224]{1,0:T(8,128)(2,1)S(1)}, bf16[32,4224]{1,0:T(8,128)(2,1)S(1)}, u32[]{:S(2)}, u32[]{:S(2)}) %collective-permute-start.2) | collective-permute-done | bytes 270368 | tf_op jit(solution)/shard_map/ppermute | solution.py:61
  56.2 11.4 %collective-permute-done.6 = bf16[64,1024]{1,0:T(8,128)(2,1)S(1)} collective-permute-done((bf16[64,1024]{1,0:T(8,128)(2,1)S(1)}, bf16[64,1024]{1,0:T(8,128)(2,1)S(1)}, u32[]{:S(2)}, u32[]{:S(2)}) %collective-permute-start.6) | collective-permute-done | bytes 131104 | tf_op jit(solution)/shard_map/ppermute | solution.py:61
  68.9 3.1 collective-permute-done.4.refs_4_
  72.0 4.3 %collective-permute-done.3.refs_2_ = bf16[4,32,2176]{2,1,0:T(8,128)(2,1)S(1)} collective-permute-done((bf16[4,32,2176]{2,1,0:T(8,128)(2,1)S(1)}, bf16[4,32,2176]{2,1,0:T(8,128)(2,1)S(1)}, u32[]{:S(2)}, u32[]{:S(2)}) %collective-permute-start.3) | collective-permute-done | bytes 557088 | tf_op jit(solution)/shard_map/ppermute | solution.py:61
  83.5 2.2 collective-permute-done.11
  85.6 7.1 %collective-permute-done.9.refs_2_ = bf16[4,32,2048]{2,1,0:T(8,128)(2,1)} collective-permute-done((bf16[4,32,2048]{2,1,0:T(8,128)(2,1)S(1)}, bf16[4,32,2048]{2,1,0:T(8,128)(2,1)}, u32[]{:S(2)}, u32[]{:S(2)}) %collective-permute-start.9) | collective-permute-done | bytes 524320 | tf_op jit(solution)/shard_map/ppermute | solution.py:61
  92.8 12.2 %collective-permute-done.10.refs_6_ = bf16[4,32,2048]{2,1,0:T(8,128)(2,1)} collective-permute-done((bf16[4,32,2048]{2,1,0:T(8,128)(2,1)}, bf16[4,32,2048]{2,1,0:T(8,128)(2,1)}, u32[]{:S(2)}, u32[]{:S(2)}) %collective-permute-start.10) | collective-permute-done | bytes 524320 | tf_op jit(solution)/shard_map/ppermute | solution.py:61
  104.9 2.5 collective-permute-done.8.refs_6_
  115.9 4.1 place.4
  122.0 2.3 copy-done
  124.2 9.1 %attend.2 = (bf16[384,1024]{1,0:T(8,128)(2,1)S(1)}, bf16[384,1024]{1,0:T(8,128)(2,1)S(1)}, bf16[384,512]{1,0:T(8,128)(2,1)S(1)}, bf16[384,512]{1,0:T(8,128)(2,1)...) custom-call(bf16[384,1024]{1,0:T(8,128)(2,1)S(1)} %fusion.2.normed_ref.refs_0_, bf16[1024,2176]{1,0:T(8,128)(2,1)S(1)} %bitcast.55, ...), custom_call_target="tpu_custom_call" | custom-call | flops 1 | bytes 1 | tf_op jit(solution)/shard_map/attend/pallas_call | solution.py:372
  136.1 4.2 %collective-permute-done.20.refs_2_ = bf16[4,64,1024]{2,1,0:T(8,128)(2,1)} collective-permute-done((bf16[4,64,1024]{2,1,0:T(8,128)(2,1)S(1)}, bf16[4,64,1024]{2,1,0:T(8,128)(2,1)}, u32[]{:S(2)}, u32[]{:S(2)}) %collective-permute-start.20) | collective-permute-done | bytes 524320 | tf_op jit(solution)/shard_map/ppermute | solution.py:61
  140.4 2.6 collective-permute-start.21
  145.5 4.1 place.6
  149.7 2.3 copy-done.1
  152.0 9.0 %attend.3 = (bf16[384,1024]{1,0:T(8,128)(2,1)S(1)}, bf16[384,1024]{1,0:T(8,128)(2,1)S(1)}, bf16[384,512]{1,0:T(8,128)(2,1)S(1)}, bf16[384,512]{1,0:T(8,128)(2,1)...) custom-call(bf16[384,1024]{1,0:T(8,128)(2,1)S(1)} %fusion.2.normed_ref.refs_0_, bf16[1024,2048]{1,0:T(8,128)(2,1)S(1)} %bitcast.57, ...), custom_call_target="tpu_custom_call" | custom-call | flops 1 | bytes 1 | tf_op jit(solution)/shard_map/attend/pallas_call | solution.py:372
  171.2 3.2 place.7
  174.4 2.7 fusion.8
  180.8 31.3 %feed_forward.1 = (bf16[384,3072]{1,0:T(8,128)(2,1)S(1)}, bf16[384,3072]{1,0:T(8,128)(2,1)S(1)}, bf16[384,3072]{1,0:T(8,128)(2,1)S(1)}, bf16[512,3072]{1,0:T(8,1...) custom-call(s32[1]{0:T(128)} %bitcast.device_ref, ...), custom_call_target="tpu_custom_call" | custom-call | flops 1 | bytes 1 | tf_op jit(solution)/shard_map/feed_forward/pallas_call | solution.py:680
  213.1 5.0 %collective-permute-done.27.refs_2_.refs_3_ = bf16[1536,1024]{1,0:T(8,128)(2,1)S(1)} collective-permute-done((bf16[1536,1024]{1,0:T(8,128)(2,1)}, bf16[1536,1024]{1,0:T(8,128)(2,1)S(1)}, u32[]{:S(2)}, u32[]{:S(2)}) %collective-permute-start.27) | collective-permute-done | bytes 3145760 | tf_op jit(solution)/shard_map/ppermute | solution.py:61
  220.0 1.9 fold.11
  223.7 1.9 fold.12
  227.1 1.9 fold.13
  230.2 35.1 %back.1 = (f32[384,1024]{1,0:T(8,128)S(1)}, bf16[384,1024]{1,0:T(8,128)(2,1)S(1)}, f32[1,1024]{1,0:T(1,128)S(1)}, bf16[1024,1024]{1,0:T(8,128)(2,1)}, bf16[1024,...) custom-call(s32[1]{0:T(128)} %bitcast.device_ref, ...), custom_call_target="tpu_custom_call" | custom-call | flops 1 | bytes 1 | tf_op jit(solution)/shard_map/back/pallas_call | solution.py:787
  266.8 2.2 fold.14
  270.8 2.9 collective-permute-done.34.refs_6_.refs_7_
  273.6 2.2 fold.15
  277.8 2.0 collective-permute-start.36
  284.6 18.0 %attend_back_last.1 = (bf16[512,2176]{1,0:T(8,128)(2,1)S(1)}, bf16[512,2176]{1,0:T(8,128)(2,1)S(1)}, bf16[384,1024]{1,0:T(8,128)(2,1)}) custom-call(s32[1]{0:T(128)} %bitcast.device_ref, bf16[384,1024]{1,0:T(8,128)(2,1)S(1)} %copy-done.46, bf16[2048,1024]{1,0:T(8,128)(2,1)} %bitcast.74, bf16[384,1024]{1,0:T(8,128)(2,1)S(1)} %copy-done.42, ...), custom_call_target="tpu_custom_call" | custom-call | flops 1 | bytes 1 | tf_op jit(solution)/shard_map/attend_back_last/pallas_call | solution.py:558
  304.0 15.7 %collective-permute-done.35.refs_2_.refs_3_ = bf16[384,1024]{1,0:T(8,128)(2,1)} collective-permute-done((bf16[384,1024]{1,0:T(8,128)(2,1)}, bf16[384,1024]{1,0:T(8,128)(2,1)}, u32[]{:S(2)}, u32[]{:S(2)}) %collective-permute-start.35) | collective-permute-done | bytes 786464 | tf_op jit(solution)/shard_map/ppermute | solution.py:61
  323.1 3.1 fold.16
  326.3 4.0 fold.17
  334.2 2.7 collective-permute-start.43
  336.9 14.5 %collective-permute-done.41.refs_2_.refs_3_ = bf16[192,1024]{1,0:T(8,128)(2,1)S(1)} collective-permute-done((bf16[192,1024]{1,0:T(8,128)(2,1)S(1)}, bf16[192,1024]{1,0:T(8,128)(2,1)S(1)}, u32[]{:S(2)}, u32[]{:S(2)}) %collective-permute-start.41) | collective-permute-done | bytes 393248 | tf_op jit(solution)/shard_map/ppermute | solution.py:61
  352.6 6.4 %ffn_out.1 = bf16[384,1024]{1,0:T(8,128)(2,1)} custom-call(f32[384,1024]{1,0:T(8,128)S(1)} %copy-done.3, bf16[384,3072]{1,0:T(8,128)(2,1)S(1)} %copy-done.27, bf16[32,96,3072]{2,1,0:T(8,128)(2,1)S(1)} %bitcast.52), custom_call_target="tpu_custom_call" | custom-call | flops 1 | bytes 1 | tf_op jit(solution)/shard_map/ffn_out/pallas_call | solution.py:845
  359.4 2.0 collective-permute-start.47
  364.5 2.8 collective-permute-done.47
  367.3 4.6 %collective-permute-done.48 = bf16[32,3072]{1,0:T(8,128)(2,1)S(1)} collective-permute-done((bf16[32,3072]{1,0:T(8,128)(2,1)S(1)}, bf16[32,3072]{1,0:T(8,128)(2,1)S(1)}, u32[]{:S(2)}, u32[]{:S(2)}) %collective-permute-start.48) | collective-permute-done | bytes 196640 | tf_op jit(solution)/shard_map/ppermute | solution.py:61
  378.9 6.8 %collective-permute-done.52.refs_10_.refs_11_ = bf16[128,2176]{1,0:T(8,128)(2,1)S(1)} collective-permute-done((bf16[128,2176]{1,0:T(8,128)(2,1)S(1)}, bf16[128,2176]{1,0:T(8,128)(2,1)S(1)}, u32[]{:S(2)}, u32[]{:S(2)}) %collective-permute-start.52) | collective-permute-done | bytes 557088 | tf_op jit(solution)/shard_map/ppermute | solution.py:61
  387.5 2.2 collective-permute-start.53
  390.4 5.2 %collective-permute-done.53.first_came = bf16[32,2048]{1,0:T(8,128)(2,1)S(1)} collective-permute-done((bf16[32,2048]{1,0:T(8,128)(2,1)S(1)}, bf16[32,2048]{1,0:T(8,128)(2,1)S(1)}, u32[]{:S(2)}, u32[]{:S(2)}) %collective-permute-start.53) | collective-permute-done | bytes 131104 | tf_op jit(solution)/shard_map/ppermute | solution.py:61
  395.6 2.5 collective-permute-done.54
  398.2 2.4 collective-permute-start.56
  401.3 3.1 collective-permute-done.56.second_came
  405.1 1.9 end_projections.1
  (279 shorter events, 95.4 us)
Async XLA Ops:
  7.2 171.9 %all-gather.3.cloned.1.call-start = ((), (), s32[]{:S(2)}) async-start(), calls=%async_computation | async-start | bytes 19464192 | tf_op jit(solution)/shard_map/all_gather | solution.py:921
  12.9 21.9 %collective-permute-start.1 = (bf16[32,4224]{1,0:T(8,128)(2,1)}, bf16[32,4224]{1,0:T(8,128)(2,1)S(1)}, u32[]{:S(2)}, u32[]{:S(2)}) collective-permute-start(bf16[32,4224]{1,0:T(8,128)(2,1)} %join.1), channel_id=1, source_target_pairs={{0,16},{1,17},{2,18},{3,19},{4,20},{5,21},{6,22},{7,23},{8,24},{9,... | collective-permute-start | bytes 811016 | tf_op jit(solution)/shard_map/ppermute | solution.py:61
  17.0 18.4 %collective-permute-start = (bf16[32,4224]{1,0:T(8,128)(2,1)}, bf16[32,4224]{1,0:T(8,128)(2,1)S(1)}, u32[]{:S(2)}, u32[]{:S(2)}) collective-permute-start(bf16[32,4224]{1,0:T(8,128)(2,1)} %join.1), channel_id=1, source_target_pairs={{0,8},{1,9},{2,10},{3,11},{4,12},{5,13},{6,14},{7,15},{8,0},{9,1},... | collective-permute-start | bytes 811016 | tf_op jit(solution)/shard_map/ppermute | solution.py:61
  35.4 12.8 %collective-permute-start.2 = (bf16[32,4224]{1,0:T(8,128)(2,1)S(1)}, bf16[32,4224]{1,0:T(8,128)(2,1)S(1)}, u32[]{:S(2)}, u32[]{:S(2)}) collective-permute-start(bf16[32,4224]{1,0:T(8,128)(2,1)S(1)} %collective-permute-done.1), channel_id=1, source_target_pairs={{0,8},{1,9},{2,10},{3,11},{4,12},{5,13},{6,14},{7,15},{8,0},{9,1},... | collective-permute-start | bytes 811016 | tf_op jit(solution)/shard_map/ppermute | solution.py:61
  49.6 26.6 %collective-permute-start.3 = (bf16[4,32,2176]{2,1,0:T(8,128)(2,1)S(1)}, bf16[4,32,2176]{2,1,0:T(8,128)(2,1)S(1)}, u32[]{:S(2)}, u32[]{:S(2)}) collective-permute-start(bf16[4,32,2176]{2,1,0:T(8,128)(2,1)S(1)} %get-tuple-element.425.refs_0_), channel_id=1, source_target_pairs={{0,2},{1,3},{2,0},{3,1},{4,6},{5,7},{6,4},{7,5},{8,10},{9,11},{10,... | collective-permute-start | bytes 1671176 | tf_op jit(solution)/shard_map/ppermute | solution.py:61
  51.2 20.8 %collective-permute-start.4 = (bf16[4,32,2048]{2,1,0:T(8,128)(2,1)S(1)}, bf16[4,32,2048]{2,1,0:T(8,128)(2,1)}, u32[]{:S(2)}, u32[]{:S(2)}) collective-permute-start(bf16[4,32,2048]{2,1,0:T(8,128)(2,1)S(1)} %get-tuple-element.443.refs_0_), channel_id=1, source_target_pairs={{0,4},{1,5},{2,6},{3,7},{4,0},{5,1},{6,2},{7,3},{8,12},{9,13},{10,... | collective-permute-start | bytes 1572872 | tf_op jit(solution)/shard_map/ppermute | solution.py:61
  52.7 14.8 %collective-permute-start.6 = (bf16[64,1024]{1,0:T(8,128)(2,1)S(1)}, bf16[64,1024]{1,0:T(8,128)(2,1)S(1)}, u32[]{:S(2)}, u32[]{:S(2)}) collective-permute-start(bf16[64,1024]{1,0:T(8,128)(2,1)S(1)} %copy-done.55), channel_id=1, source_target_pairs={{0,16},{1,17},{2,18},{3,19},{4,20},{5,21},{6,22},{7,23},{8,24},{9,... | collective-permute-start | bytes 393224 | tf_op jit(solution)/shard_map/ppermute | solution.py:61
  54.4 14.4 %collective-permute-start.5 = (bf16[64,1024]{1,0:T(8,128)(2,1)S(1)}, bf16[64,1024]{1,0:T(8,128)(2,1)S(1)}, u32[]{:S(2)}, u32[]{:S(2)}) collective-permute-start(bf16[64,1024]{1,0:T(8,128)(2,1)S(1)} %copy-done.55), channel_id=1, source_target_pairs={{0,8},{1,9},{2,10},{3,11},{4,12},{5,13},{6,14},{7,15},{8,0},{9,1},... | collective-permute-start | bytes 393224 | tf_op jit(solution)/shard_map/ppermute | solution.py:61
  76.2 16.6 %collective-permute-start.9 = (bf16[4,32,2048]{2,1,0:T(8,128)(2,1)S(1)}, bf16[4,32,2048]{2,1,0:T(8,128)(2,1)}, u32[]{:S(2)}, u32[]{:S(2)}) collective-permute-start(bf16[4,32,2048]{2,1,0:T(8,128)(2,1)S(1)} %get-tuple-element.443.refs_0_), channel_id=1, source_target_pairs={{0,2},{1,3},{2,0},{3,1},{4,6},{5,7},{6,4},{7,5},{8,10},{9,11},{10,... | collective-permute-start | bytes 1572872 | tf_op jit(solution)/shard_map/ppermute | solution.py:61
  78.1 26.8 %collective-permute-start.10 = (bf16[4,32,2048]{2,1,0:T(8,128)(2,1)}, bf16[4,32,2048]{2,1,0:T(8,128)(2,1)}, u32[]{:S(2)}, u32[]{:S(2)}) collective-permute-start(bf16[4,32,2048]{2,1,0:T(8,128)(2,1)} %collective-permute-done.4.refs_4_), channel_id=1, source_target_pairs={{0,2},{1,3},{2,0},{3,1},{4,6},{5,7},{6,4},{7,5},{8,10},{9,11},{10,... | collective-permute-start | bytes 1572872 | tf_op jit(solution)/shard_map/ppermute | solution.py:61
  78.2 26.7 %collective-permute-start.7 = (bf16[4,32,2176]{2,1,0:T(8,128)(2,1)S(1)}, bf16[4,32,2176]{2,1,0:T(8,128)(2,1)}, u32[]{:S(2)}, u32[]{:S(2)}) collective-permute-start(bf16[4,32,2176]{2,1,0:T(8,128)(2,1)S(1)} %get-tuple-element.425.refs_0_), channel_id=1, source_target_pairs={{0,4},{1,5},{2,6},{3,7},{4,0},{5,1},{6,2},{7,3},{8,12},{9,13},{10,... | collective-permute-start | bytes 1671176 | tf_op jit(solution)/shard_map/ppermute | solution.py:61
  79.9 27.5 %collective-permute-start.8 = (bf16[4,32,2176]{2,1,0:T(8,128)(2,1)S(1)}, bf16[4,32,2176]{2,1,0:T(8,128)(2,1)}, u32[]{:S(2)}, u32[]{:S(2)}) collective-permute-start(bf16[4,32,2176]{2,1,0:T(8,128)(2,1)S(1)} %collective-permute-done.3.refs_2_), channel_id=1, source_target_pairs={{0,4},{1,5},{2,6},{3,7},{4,0},{5,1},{6,2},{7,3},{8,12},{9,13},{10,... | collective-permute-start | bytes 1671176 | tf_op jit(solution)/shard_map/ppermute | solution.py:61
  107.5 7.3 %collective-permute-start.12 = (bf16[4,32,2176]{2,1,0:T(8,128)(2,1)S(1)}, bf16[4,32,2176]{2,1,0:T(8,128)(2,1)}, u32[]{:S(2)}, u32[]{:S(2)}) collective-permute-start(bf16[4,32,2176]{2,1,0:T(8,128)(2,1)S(1)} %get-tuple-element.425.refs_0_), channel_id=1, source_target_pairs={{0,1},{1,0},{2,3},{3,2},{4,5},{5,4},{6,7},{7,6},{8,9},{9,8},{10,11... | collective-permute-start | bytes 1671176 | tf_op jit(solution)/shard_map/ppermute | solution.py:61
  107.5 7.3 %collective-permute-start.13 = (bf16[4,32,2176]{2,1,0:T(8,128)(2,1)S(1)}, bf16[4,32,2176]{2,1,0:T(8,128)(2,1)}, u32[]{:S(2)}, u32[]{:S(2)}) collective-permute-start(bf16[4,32,2176]{2,1,0:T(8,128)(2,1)S(1)} %collective-permute-done.3.refs_2_), channel_id=1, source_target_pairs={{0,1},{1,0},{2,3},{3,2},{4,5},{5,4},{6,7},{7,6},{8,9},{9,8},{10,11... | collective-permute-start | bytes 1671176 | tf_op jit(solution)/shard_map/ppermute | solution.py:61
  108.0 6.8 %collective-permute-start.14 = (bf16[4,32,2176]{2,1,0:T(8,128)(2,1)}, bf16[4,32,2176]{2,1,0:T(8,128)(2,1)}, u32[]{:S(2)}, u32[]{:S(2)}) collective-permute-start(bf16[4,32,2176]{2,1,0:T(8,128)(2,1)} %collective-permute-done.7.refs_4_), channel_id=1, source_target_pairs={{0,1},{1,0},{2,3},{3,2},{4,5},{5,4},{6,7},{7,6},{8,9},{9,8},{10,11... | collective-permute-start | bytes 1671176 | tf_op jit(solution)/shard_map/ppermute | solution.py:61
  108.0 6.8 %collective-permute-start.15 = (bf16[4,32,2176]{2,1,0:T(8,128)(2,1)}, bf16[4,32,2176]{2,1,0:T(8,128)(2,1)}, u32[]{:S(2)}, u32[]{:S(2)}) collective-permute-start(bf16[4,32,2176]{2,1,0:T(8,128)(2,1)} %collective-permute-done.8.refs_6_), channel_id=1, source_target_pairs={{0,1},{1,0},{2,3},{3,2},{4,5},{5,4},{6,7},{7,6},{8,9},{9,8},{10,11... | collective-permute-start | bytes 1671176 | tf_op jit(solution)/shard_map/ppermute | solution.py:61
  114.5 25.8 %collective-permute-start.20 = (bf16[4,64,1024]{2,1,0:T(8,128)(2,1)S(1)}, bf16[4,64,1024]{2,1,0:T(8,128)(2,1)}, u32[]{:S(2)}, u32[]{:S(2)}) collective-permute-start(bf16[4,64,1024]{2,1,0:T(8,128)(2,1)S(1)} %bitcast.58), channel_id=1, source_target_pairs={{0,2},{1,3},{2,0},{3,1},{4,6},{5,7},{6,4},{7,5},{8,10},{9,11},{10,... | collective-permute-start | bytes 1572872 | tf_op jit(solution)/shard_map/ppermute | solution.py:61
  114.8 25.5 %collective-permute-start.16 = (bf16[4,32,2048]{2,1,0:T(8,128)(2,1)S(1)}, bf16[4,32,2048]{2,1,0:T(8,128)(2,1)}, u32[]{:S(2)}, u32[]{:S(2)}) collective-permute-start(bf16[4,32,2048]{2,1,0:T(8,128)(2,1)S(1)} %get-tuple-element.443.refs_0_), channel_id=1, source_target_pairs={{0,1},{1,0},{2,3},{3,2},{4,5},{5,4},{6,7},{7,6},{8,9},{9,8},{10,11... | collective-permute-start | bytes 1572872 | tf_op jit(solution)/shard_map/ppermute | solution.py:61
  114.9 25.5 %collective-permute-start.17 = (bf16[4,32,2048]{2,1,0:T(8,128)(2,1)}, bf16[4,32,2048]{2,1,0:T(8,128)(2,1)}, u32[]{:S(2)}, u32[]{:S(2)}) collective-permute-start(bf16[4,32,2048]{2,1,0:T(8,128)(2,1)} %collective-permute-done.9.refs_2_), channel_id=1, source_target_pairs={{0,1},{1,0},{2,3},{3,2},{4,5},{5,4},{6,7},{7,6},{8,9},{9,8},{10,11... | collective-permute-start | bytes 1572872 | tf_op jit(solution)/shard_map/ppermute | solution.py:61
  115.4 25.0 %collective-permute-start.18 = (bf16[4,32,2048]{2,1,0:T(8,128)(2,1)}, bf16[4,32,2048]{2,1,0:T(8,128)(2,1)}, u32[]{:S(2)}, u32[]{:S(2)}) collective-permute-start(bf16[4,32,2048]{2,1,0:T(8,128)(2,1)} %collective-permute-done.4.refs_4_), channel_id=1, source_target_pairs={{0,1},{1,0},{2,3},{3,2},{4,5},{5,4},{6,7},{7,6},{8,9},{9,8},{10,11... | collective-permute-start | bytes 1572872 | tf_op jit(solution)/shard_map/ppermute | solution.py:61
  115.5 24.9 %collective-permute-start.19 = (bf16[4,32,2048]{2,1,0:T(8,128)(2,1)}, bf16[4,32,2048]{2,1,0:T(8,128)(2,1)}, u32[]{:S(2)}, u32[]{:S(2)}) collective-permute-start(bf16[4,32,2048]{2,1,0:T(8,128)(2,1)} %collective-permute-done.10.refs_6_), channel_id=1, source_target_pairs={{0,1},{1,0},{2,3},{3,2},{4,5},{5,4},{6,7},{7,6},{8,9},{9,8},{10,11... | collective-permute-start | bytes 1572872 | tf_op jit(solution)/shard_map/ppermute | solution.py:61
  140.4 24.4 %collective-permute-start.21 = (bf16[4,64,1024]{2,1,0:T(8,128)(2,1)S(1)}, bf16[4,64,1024]{2,1,0:T(8,128)(2,1)S(1)}, u32[]{:S(2)}, u32[]{:S(2)}) collective-permute-start(bf16[4,64,1024]{2,1,0:T(8,128)(2,1)S(1)} %bitcast.59), channel_id=1, source_target_pairs={{0,4},{1,5},{2,6},{3,7},{4,0},{5,1},{6,2},{7,3},{8,12},{9,13},{10,... | collective-permute-start | bytes 1572872 | tf_op jit(solution)/shard_map/ppermute | solution.py:61
  143.0 22.5 %collective-permute-start.22 = (bf16[4,64,1024]{2,1,0:T(8,128)(2,1)}, bf16[4,64,1024]{2,1,0:T(8,128)(2,1)S(1)}, u32[]{:S(2)}, u32[]{:S(2)}) collective-permute-start(bf16[4,64,1024]{2,1,0:T(8,128)(2,1)} %collective-permute-done.20.refs_2_), channel_id=1, source_target_pairs={{0,4},{1,5},{2,6},{3,7},{4,0},{5,1},{6,2},{7,3},{8,12},{9,13},{10,... | collective-permute-start | bytes 1572872 | tf_op jit(solution)/shard_map/ppermute | solution.py:61
  212.6 11.1 %collective-permute-start.28 = (bf16[512,3072]{1,0:T(8,128)(2,1)}, bf16[512,3072]{1,0:T(8,128)(2,1)S(1)}, u32[]{:S(2)}, u32[]{:S(2)}) collective-permute-start(bf16[512,3072]{1,0:T(8,128)(2,1)} %get-tuple-element.487), channel_id=1, source_target_pairs={{0,1},{1,0},{2,3},{3,2},{4,5},{5,4},{6,7},{7,6},{8,9},{9,8},{10,11... | collective-permute-start | bytes 9437192 | tf_op jit(solution)/shard_map/ppermute | solution.py:61
  212.7 14.4 %collective-permute-start.29 = (bf16[512,3072]{1,0:T(8,128)(2,1)}, bf16[512,3072]{1,0:T(8,128)(2,1)S(1)}, u32[]{:S(2)}, u32[]{:S(2)}) collective-permute-start(bf16[512,3072]{1,0:T(8,128)(2,1)} %get-tuple-element.507), channel_id=1, source_target_pairs={{0,1},{1,0},{2,3},{3,2},{4,5},{5,4},{6,7},{7,6},{8,9},{9,8},{10,11... | collective-permute-start | bytes 9437192 | tf_op jit(solution)/shard_map/ppermute | solution.py:61
  221.9 44.2 %collective-permute-start.30 = (bf16[768,1024]{1,0:T(8,128)(2,1)}, bf16[768,1024]{1,0:T(8,128)(2,1)S(1)}, u32[]{:S(2)}, u32[]{:S(2)}) collective-permute-start(bf16[768,1024]{1,0:T(8,128)(2,1)} %get-tuple-element.518), channel_id=1, source_target_pairs={{0,4},{1,5},{2,6},{3,7},{4,0},{5,1},{6,2},{7,3},{8,12},{9,13},{10,... | collective-permute-start | bytes 4718600 | tf_op jit(solution)/shard_map/ppermute | solution.py:61
  225.6 40.5 %collective-permute-start.31 = (bf16[256,3072]{1,0:T(8,128)(2,1)}, bf16[256,3072]{1,0:T(8,128)(2,1)S(1)}, u32[]{:S(2)}, u32[]{:S(2)}) collective-permute-start(bf16[256,3072]{1,0:T(8,128)(2,1)} %get-tuple-element.531), channel_id=1, source_target_pairs={{0,2},{1,3},{2,0},{3,1},{4,6},{5,7},{6,4},{7,5},{8,10},{9,11},{10,... | collective-permute-start | bytes 4718600 | tf_op jit(solution)/shard_map/ppermute | solution.py:61
  229.0 37.1 %collective-permute-start.32 = (bf16[256,3072]{1,0:T(8,128)(2,1)}, bf16[256,3072]{1,0:T(8,128)(2,1)S(1)}, u32[]{:S(2)}, u32[]{:S(2)}) collective-permute-start(bf16[256,3072]{1,0:T(8,128)(2,1)} %get-tuple-element.541), channel_id=1, source_target_pairs={{0,8},{1,9},{2,10},{3,11},{4,12},{5,13},{6,14},{7,15},{8,0},{9,1},... | collective-permute-start | bytes 4718600 | tf_op jit(solution)/shard_map/ppermute | solution.py:61
  266.6 7.0 %collective-permute-start.34 = (bf16[1024,1024]{1,0:T(8,128)(2,1)}, bf16[1024,1024]{1,0:T(8,128)(2,1)S(1)}, u32[]{:S(2)}, u32[]{:S(2)}) collective-permute-start(bf16[1024,1024]{1,0:T(8,128)(2,1)} %get-tuple-element.573), channel_id=1, source_target_pairs={{0,1},{1,0},{2,3},{3,2},{4,5},{5,4},{6,7},{7,6},{8,9},{9,8},{10,11... | collective-permute-start | bytes 6291464 | tf_op jit(solution)/shard_map/ppermute | solution.py:61
  277.8 42.6 %collective-permute-start.36 = (bf16[256,2048]{1,0:T(8,128)(2,1)}, bf16[256,2048]{1,0:T(8,128)(2,1)}, u32[]{:S(2)}, u32[]{:S(2)}) collective-permute-start(bf16[256,2048]{1,0:T(8,128)(2,1)} %get-tuple-element.595), channel_id=1, source_target_pairs={{0,8},{1,9},{2,10},{3,11},{4,12},{5,13},{6,14},{7,15},{8,0},{9,1},... | collective-permute-start | bytes 3145736 | tf_op jit(solution)/shard_map/ppermute | solution.py:61
  279.8 40.6 %collective-permute-start.38 = (bf16[512,1024]{1,0:T(8,128)(2,1)}, bf16[512,1024]{1,0:T(8,128)(2,1)}, u32[]{:S(2)}, u32[]{:S(2)}) collective-permute-start(bf16[512,1024]{1,0:T(8,128)(2,1)} %get-tuple-element.612), channel_id=1, source_target_pairs={{0,2},{1,3},{2,0},{3,1},{4,6},{5,7},{6,4},{7,5},{8,10},{9,11},{10,... | collective-permute-start | bytes 3145736 | tf_op jit(solution)/shard_map/ppermute | solution.py:61
  280.4 39.3 %collective-permute-start.35 = (bf16[384,1024]{1,0:T(8,128)(2,1)}, bf16[384,1024]{1,0:T(8,128)(2,1)}, u32[]{:S(2)}, u32[]{:S(2)}) collective-permute-start(bf16[384,1024]{1,0:T(8,128)(2,1)} %get-tuple-element.593), channel_id=1, source_target_pairs={{0,16},{1,17},{2,18},{3,19},{4,20},{5,21},{6,22},{7,23},{8,24},{9,... | collective-permute-start | bytes 2359304 | tf_op jit(solution)/shard_map/ppermute | solution.py:61
  280.4 39.3 %collective-permute-start.37 = (bf16[128,3072]{1,0:T(8,128)(2,1)}, bf16[128,3072]{1,0:T(8,128)(2,1)}, u32[]{:S(2)}, u32[]{:S(2)}) collective-permute-start(bf16[128,3072]{1,0:T(8,128)(2,1)} %get-tuple-element.597), channel_id=1, source_target_pairs={{0,4},{1,5},{2,6},{3,7},{4,0},{5,1},{6,2},{7,3},{8,12},{9,13},{10,... | collective-permute-start | bytes 2359304 | tf_op jit(solution)/shard_map/ppermute | solution.py:61
  281.6 38.1 %collective-permute-start.39 = (bf16[128,3072]{1,0:T(8,128)(2,1)}, bf16[128,3072]{1,0:T(8,128)(2,1)}, u32[]{:S(2)}, u32[]{:S(2)}) collective-permute-start(bf16[128,3072]{1,0:T(8,128)(2,1)} %get-tuple-element.616), channel_id=1, source_target_pairs={{0,4},{1,5},{2,6},{3,7},{4,0},{5,1},{6,2},{7,3},{8,12},{9,13},{10,... | collective-permute-start | bytes 2359304 | tf_op jit(solution)/shard_map/ppermute | solution.py:61
  330.3 33.6 %collective-permute-start.46 = (bf16[256,2176]{1,0:T(8,128)(2,1)S(1)}, bf16[256,2176]{1,0:T(8,128)(2,1)S(1)}, u32[]{:S(2)}, u32[]{:S(2)}) collective-permute-start(bf16[256,2176]{1,0:T(8,128)(2,1)S(1)} %get-tuple-element.705), channel_id=1, source_target_pairs={{0,2},{1,3},{2,0},{3,1},{4,6},{5,7},{6,4},{7,5},{8,10},{9,11},{10,... | collective-permute-start | bytes 3342344 | tf_op jit(solution)/shard_map/ppermute | solution.py:61
  331.0 20.4 %collective-permute-start.41 = (bf16[192,1024]{1,0:T(8,128)(2,1)S(1)}, bf16[192,1024]{1,0:T(8,128)(2,1)S(1)}, u32[]{:S(2)}, u32[]{:S(2)}) collective-permute-start(bf16[192,1024]{1,0:T(8,128)(2,1)S(1)} %get-tuple-element.675), channel_id=1, source_target_pairs={{0,8},{1,9},{2,10},{3,11},{4,12},{5,13},{6,14},{7,15},{8,0},{9,1},... | collective-permute-start | bytes 1179656 | tf_op jit(solution)/shard_map/ppermute | solution.py:61
  331.0 31.0 %collective-permute-start.44 = (bf16[128,2048]{1,0:T(8,128)(2,1)S(1)}, bf16[128,2048]{1,0:T(8,128)(2,1)S(1)}, u32[]{:S(2)}, u32[]{:S(2)}) collective-permute-start(bf16[128,2048]{1,0:T(8,128)(2,1)S(1)} %get-tuple-element.700), channel_id=1, source_target_pairs={{0,4},{1,5},{2,6},{3,7},{4,0},{5,1},{6,2},{7,3},{8,12},{9,13},{10,... | collective-permute-start | bytes 1572872 | tf_op jit(solution)/shard_map/ppermute | solution.py:61
  332.4 26.6 %collective-permute-start.42 = (bf16[64,3072]{1,0:T(8,128)(2,1)S(1)}, bf16[64,3072]{1,0:T(8,128)(2,1)S(1)}, u32[]{:S(2)}, u32[]{:S(2)}) collective-permute-start(bf16[64,3072]{1,0:T(8,128)(2,1)S(1)} %get-tuple-element.678), channel_id=1, source_target_pairs={{0,8},{1,9},{2,10},{3,11},{4,12},{5,13},{6,14},{7,15},{8,0},{9,1},... | collective-permute-start | bytes 1179656 | tf_op jit(solution)/shard_map/ppermute | solution.py:61
  334.2 24.9 %collective-permute-start.43 = (bf16[64,3072]{1,0:T(8,128)(2,1)S(1)}, bf16[64,3072]{1,0:T(8,128)(2,1)S(1)}, u32[]{:S(2)}, u32[]{:S(2)}) collective-permute-start(bf16[64,3072]{1,0:T(8,128)(2,1)S(1)} %get-tuple-element.682), channel_id=1, source_target_pairs={{0,16},{1,17},{2,18},{3,19},{4,20},{5,21},{6,22},{7,23},{8,24},{9,... | collective-permute-start | bytes 1179656 | tf_op jit(solution)/shard_map/ppermute | solution.py:61
  351.4 12.5 %collective-permute-start.45 = (bf16[256,1024]{1,0:T(8,128)(2,1)S(1)}, bf16[256,1024]{1,0:T(8,128)(2,1)S(1)}, u32[]{:S(2)}, u32[]{:S(2)}) collective-permute-start(bf16[256,1024]{1,0:T(8,128)(2,1)S(1)} %get-tuple-element.703), channel_id=1, source_target_pairs={{0,4},{1,5},{2,6},{3,7},{4,0},{5,1},{6,2},{7,3},{8,12},{9,13},{10,... | collective-permute-start | bytes 1572872 | tf_op jit(solution)/shard_map/ppermute | solution.py:61
  359.4 7.9 %collective-permute-start.47 = (bf16[96,1024]{1,0:T(8,128)(2,1)S(1)}, bf16[96,1024]{1,0:T(8,128)(2,1)S(1)}, u32[]{:S(2)}, u32[]{:S(2)}) collective-permute-start(bf16[96,1024]{1,0:T(8,128)(2,1)S(1)} %get-tuple-element.723), channel_id=1, source_target_pairs={{0,2},{1,3},{2,0},{3,1},{4,6},{5,7},{6,4},{7,5},{8,10},{9,11},{10,... | collective-permute-start | bytes 589832 | tf_op jit(solution)/shard_map/ppermute | solution.py:61
  361.3 10.5 %collective-permute-start.48 = (bf16[32,3072]{1,0:T(8,128)(2,1)S(1)}, bf16[32,3072]{1,0:T(8,128)(2,1)S(1)}, u32[]{:S(2)}, u32[]{:S(2)}) collective-permute-start(bf16[32,3072]{1,0:T(8,128)(2,1)S(1)} %get-tuple-element.726), channel_id=1, source_target_pairs={{0,16},{1,17},{2,18},{3,19},{4,20},{5,21},{6,22},{7,23},{8,24},{9,... | collective-permute-start | bytes 589832 | tf_op jit(solution)/shard_map/ppermute | solution.py:61
  362.0 9.8 %collective-permute-start.49 = (bf16[32,3072]{1,0:T(8,128)(2,1)S(1)}, bf16[32,3072]{1,0:T(8,128)(2,1)S(1)}, u32[]{:S(2)}, u32[]{:S(2)}) collective-permute-start(bf16[32,3072]{1,0:T(8,128)(2,1)S(1)} %get-tuple-element.730), channel_id=1, source_target_pairs={{0,2},{1,3},{2,0},{3,1},{4,6},{5,7},{6,4},{7,5},{8,10},{9,11},{10,... | collective-permute-start | bytes 589832 | tf_op jit(solution)/shard_map/ppermute | solution.py:61
  371.8 6.7 %collective-permute-start.50 = (bf16[64,2048]{1,0:T(8,128)(2,1)S(1)}, bf16[64,2048]{1,0:T(8,128)(2,1)S(1)}, u32[]{:S(2)}, u32[]{:S(2)}) collective-permute-start(bf16[64,2048]{1,0:T(8,128)(2,1)S(1)} %get-tuple-element.734), channel_id=1, source_target_pairs={{0,2},{1,3},{2,0},{3,1},{4,6},{5,7},{6,4},{7,5},{8,10},{9,11},{10,... | collective-permute-start | bytes 786440 | tf_op jit(solution)/shard_map/ppermute | solution.py:61
  373.3 12.4 %collective-permute-start.52 = (bf16[128,2176]{1,0:T(8,128)(2,1)S(1)}, bf16[128,2176]{1,0:T(8,128)(2,1)S(1)}, u32[]{:S(2)}, u32[]{:S(2)}) collective-permute-start(bf16[128,2176]{1,0:T(8,128)(2,1)S(1)} %get-tuple-element.740), channel_id=1, source_target_pairs={{0,4},{1,5},{2,6},{3,7},{4,0},{5,1},{6,2},{7,3},{8,12},{9,13},{10,... | collective-permute-start | bytes 1671176 | tf_op jit(solution)/shard_map/ppermute | solution.py:61
  386.0 12.1 %collective-permute-start.55 = (bf16[64,2176]{1,0:T(8,128)(2,1)S(1)}, bf16[64,2176]{1,0:T(8,128)(2,1)S(1)}, u32[]{:S(2)}, u32[]{:S(2)}) collective-permute-start(bf16[64,2176]{1,0:T(8,128)(2,1)S(1)} %get-tuple-element.766), channel_id=1, source_target_pairs={{0,8},{1,9},{2,10},{3,11},{4,12},{5,13},{6,14},{7,15},{8,0},{9,1},... | collective-permute-start | bytes 835592 | tf_op jit(solution)/shard_map/ppermute | solution.py:61
  387.5 8.1 %collective-permute-start.53 = (bf16[32,2048]{1,0:T(8,128)(2,1)S(1)}, bf16[32,2048]{1,0:T(8,128)(2,1)S(1)}, u32[]{:S(2)}, u32[]{:S(2)}) collective-permute-start(bf16[32,2048]{1,0:T(8,128)(2,1)S(1)} %get-tuple-element.759), channel_id=1, source_target_pairs={{0,16},{1,17},{2,18},{3,19},{4,20},{5,21},{6,22},{7,23},{8,24},{9,... | collective-permute-start | bytes 393224 | tf_op jit(solution)/shard_map/ppermute | solution.py:61
  389.7 8.3 %collective-permute-start.54 = (bf16[64,1024]{1,0:T(8,128)(2,1)S(1)}, bf16[64,1024]{1,0:T(8,128)(2,1)S(1)}, u32[]{:S(2)}, u32[]{:S(2)}) collective-permute-start(bf16[64,1024]{1,0:T(8,128)(2,1)S(1)} %get-tuple-element.761), channel_id=1, source_target_pairs={{0,16},{1,17},{2,18},{3,19},{4,20},{5,21},{6,22},{7,23},{8,24},{9,... | collective-permute-start | bytes 393224 | tf_op jit(solution)/shard_map/ppermute | solution.py:61
  (86 other events, 1042.4 us)
Sparse Core Ops, SparseCore 0:
  11.0 160.6 all-gather.2

commit v5 on v4

--- a/solution.py
+++ b/solution.py
@@ -18,6 +18,10 @@
 
 def far(shape, dtype):
     return pltpu.HBM(tuple(shape), dtype)
+
+
+def from_far(*values):
+    return [pltpu.with_memory_space_constraint(value, pltpu.HBM) for value in values]
 
 
 epsilon = 1e-06
@@ -119,7 +123,7 @@
             out_specs=pl.BlockSpec((columns, rows), lambda i, d: (0, 0)),
             scratch_shapes=[pltpu.VMEM((columns, rows), held)],
         ),
-        out_shape=jax.ShapeDtypeStruct((columns, rows), values[0].dtype),
+        out_shape=far((columns, rows), values[0].dtype),
         compiler_params=pltpu.CompilerParams(vmem_limit_bytes=16 * 1024 * 1024),
         cost_estimate=SMALL,
         name="turn",
@@ -237,7 +241,7 @@
 
 
 def lay_top(blocks, device, count):
-    return {0: place(blocks, device // (count // 4)).reshape((4,) + blocks[0].shape[1:])}
+    return {0: place(from_far(*blocks), device // (count // 4)).reshape((4,) + blocks[0].shape[1:])}
 
 
 def split_body(device_ref, *refs):
@@ -273,7 +277,7 @@
         compiler_params=pltpu.CompilerParams(vmem_limit_bytes=10 * 1024 * 1024),
         cost_estimate=SMALL,
         name="lay_top_split",
-    )((device // (count // 4)).reshape(1), *[block[0] for block in blocks])
+    )((device // (count // 4)).reshape(1), *from_far(*[block[0] for block in blocks]))
 
 
 def gather_bits(parts, count, bits):
@@ -329,10 +333,29 @@
 GROUP = 4 * HEAD_SIZE
 
 
-def attend_body(
-    normed_ref, weight_ref, gains_ref, cosine_ref, sine_ref, first_ref,
-    attended_ref, query_ref, key_ref, value_ref, raw_ref, total_ref,
-):
+def weight_parts(parts, device, count):
+    if parts[0].shape[1] % 16 == 0:
+        return [parts[mask] for mask in range(count // 4)]
+    weight = lay(parts, device, count)
+    return [weight[None]]
+
+
+def part_specs(parts, index):
+    top, rows, _ = parts[0].shape
+    return [pl.BlockSpec((top, rows, GROUP), lambda *j: (0, 0, index(*j))) for _ in parts]
+
+
+def join_parts(device_ref, part_refs, weight_ref):
+    inner = device_ref[0] & (len(part_refs) - 1)
+    for mask, ref in enumerate(part_refs):
+        weight_ref[:, inner ^ mask] = ref[...]
+    top, count, rows, columns = weight_ref.shape
+    return weight_ref[...].reshape(top * count * rows, columns)
+
+
+def attend_body(device_ref, *refs):
+    (*part_refs, normed_ref, gains_ref, cosine_ref, sine_ref, first_ref), out_refs = refs[:-7], refs[-7:]
+    attended_ref, query_ref, key_ref, value_ref, raw_ref, total_ref, weight_ref = out_refs
     cosine = cosine_ref[...]
     sine = sine_ref[...]
 
@@ -340,7 +363,8 @@
         scaled = unit_head(raw)[0] * gain
         return (scaled * cosine + swap_halves(scaled) * sine).astype(jnp.bfloat16)
 
-    raw = jnp.dot(normed_ref[...], weight_ref[...], preferred_element_type=jnp.float32)
+    weight = join_parts(device_ref, part_refs, weight_ref)
+    raw = jnp.dot(normed_ref[...], weight, preferred_element_type=jnp.float32)
     raw_ref[...] = raw[:, : 3 * HEAD_SIZE]
     for head in range(2):
         part = slice(head * HEAD_SIZE, (head + 1) * HEAD_SIZE)
@@ -362,51 +386,56 @@
         total_ref[0, block, 1:2] = log_total[step:]
 
 
-def attend(normed, weight, head_gains, cosine, sine, first_row):
+def attend(device, normed, parts, head_gains, cosine, sine, first_row):
     rows, width = normed.shape
     groups = KEY_VALUE_HEADS // 2
-    whole = lambda *shape: pl.BlockSpec(shape, lambda h: (0, 0))
-    columns = lambda size: pl.BlockSpec((rows, size), lambda h: (0, h))
-    low = lambda size: jax.ShapeDtypeStruct((rows, groups * size), jnp.bfloat16)
+    whole = lambda *shape: pl.BlockSpec(shape, lambda h, d: (0, 0))
+    columns = lambda size: pl.BlockSpec((rows, size), lambda h, d: (0, h))
+    low = lambda size: far((rows, groups * size), jnp.bfloat16)
     pair = 2 * HEAD_SIZE
     return pl.pallas_call(
         attend_body,
-        grid=(groups,),
-        in_specs=[
-            whole(rows, width),
-            pl.BlockSpec((width, GROUP), lambda h: (0, h)),
-            whole(2, HEAD_SIZE),
-            whole(rows, HEAD_SIZE),
-            whole(rows, HEAD_SIZE),
-            whole(rows, 1),
-        ],
-        out_specs=[
-            columns(pair),
-            columns(pair),
-            columns(HEAD_SIZE),
-            columns(HEAD_SIZE),
-            columns(3 * HEAD_SIZE),
-            pl.BlockSpec((1, rows, 2), lambda h: (h, 0, 0)),
-        ],
+        grid_spec=pltpu.PrefetchScalarGridSpec(
+            num_scalar_prefetch=1,
+            grid=(groups,),
+            in_specs=part_specs(parts, lambda h, d: h)
+            + [
+                whole(rows, width),
+                whole(2, HEAD_SIZE),
+                whole(rows, HEAD_SIZE),
+                whole(rows, HEAD_SIZE),
+                whole(rows, 1),
+            ],
+            out_specs=[
+                columns(pair),
+                columns(pair),
+                columns(HEAD_SIZE),
+                columns(HEAD_SIZE),
+                columns(3 * HEAD_SIZE),
+                pl.BlockSpec((1, rows, 2), lambda h, d: (h, 0, 0)),
+            ],
+            scratch_shapes=[pltpu.VMEM((parts[0].shape[0], len(parts), parts[0].shape[1], GROUP), jnp.bfloat16)],
+        ),
         out_shape=[
-            low(pair),
+            jax.ShapeDtypeStruct((rows, groups * pair), jnp.bfloat16),
             low(pair),
             low(HEAD_SIZE),
             low(HEAD_SIZE),
-            jax.ShapeDtypeStruct((rows, groups * 3 * HEAD_SIZE), jnp.float32),
-            jax.ShapeDtypeStruct((groups, rows, 2), jnp.float32),
+            far((rows, groups * 3 * HEAD_SIZE), jnp.float32),
+            far((groups, rows, 2), jnp.float32),
         ],
         compiler_params=pltpu.CompilerParams(vmem_limit_bytes=26 * 1024 * 1024),
         cost_estimate=SMALL,
         name="attend",
-    )(normed, weight, head_gains, cosine, sine, first_row)
+    )(device.reshape(1), *parts, normed, head_gains, cosine, sine, first_row)
 
 
 def attend_back_body(
     device_ref, residual_ref, wo_ref, query_ref, key_ref, value_ref, raw_ref, total_ref,
-    gains_ref, cosine_ref, sine_ref, first_ref, turned_ref, weight_ref, *refs,
-    order, shard, head_shard, last, head=None,
+    gains_ref, cosine_ref, sine_ref, first_ref, turned_ref, *refs,
+    order, shard, head_shard, last, parts, head=None,
 ):
+    part_refs, refs = refs[:parts], refs[parts:]
     if last:
         head_gains_in_ref, normed_in_ref = refs[:2]
         refs = refs[2:]
@@ -416,7 +445,7 @@
     else:
         kept_ref, sent_ref, head_gains_ref, normed_sum_ref = refs[:4]
         scratch = refs[4:]
-    grad_out_ref, query_sum_ref, key_sum_ref, value_sum_ref, grads_ref = scratch
+    grad_out_ref, query_sum_ref, key_sum_ref, value_sum_ref, grads_ref, weight_ref = scratch
     scale = 1.0 / math.sqrt(HEAD_SIZE)
     heads = KEY_VALUE_HEADS // 2
     if head is None:
@@ -473,7 +502,7 @@
     columns = pl.ds(pl.multiple_of(head * GROUP, GROUP), GROUP)
     kept_ref[:, columns] = product[:half]
     sent_ref[:, columns] = product[half:]
-    normed_sum_ref[...] += contract(grads, weight_ref[...], 1, 1)
+    normed_sum_ref[...] += contract(grads, join_parts(device_ref, part_refs, weight_ref), 1, 1)
 
     if not last:
         return
@@ -516,7 +545,7 @@
             target_ref[row % half : row % half + group * shard, end] = block
 
 
-def attend_back_specs(rows, width, part, head):
+def attend_back_specs(rows, width, part, head, parts):
     first = part * KEY_VALUE_HEADS // 2
     whole = lambda *shape: pl.BlockSpec(shape, lambda *j: (0, 0))
     columns = lambda height, size: pl.BlockSpec((height, size), lambda *j: (0, head(*j)))
@@ -533,11 +562,10 @@
         whole(rows, HEAD_SIZE),
         whole(rows, 1),
         whole(width, rows),
-        columns(width, GROUP),
-    ]
-
-
-def attend_back_scratch(rows):
+    ] + part_specs(parts, head)
+
+
+def attend_back_scratch(rows, parts):
     pair = 2 * HEAD_SIZE
     return [
         pltpu.VMEM((rows, pair), jnp.bfloat16),
@@ -545,23 +573,26 @@
         pltpu.VMEM((rows, HEAD_SIZE), jnp.float32),
         pltpu.VMEM((rows, HEAD_SIZE), jnp.float32),
         pltpu.VMEM((rows, GROUP), jnp.bfloat16),
+        pltpu.VMEM((parts[0].shape[0], len(parts), parts[0].shape[1], GROUP), jnp.bfloat16),
     ]
 
 
 def attend_back_last(
-    device, residual_low, operands, sums, tokens, gain, grad_residual, grad_gain_two, order, shard, head_shard
+    device, residual_low, operands, parts, sums, tokens, gain, grad_residual, grad_gain_two, order, shard, head_shard
 ):
     rows, width = residual_low.shape
     whole = lambda *shape: pl.BlockSpec(shape, lambda *j: (0, 0))
     own_width = KEY_VALUE_HEADS * 2 * HEAD_SIZE + 128
     half = jax.ShapeDtypeStruct((width // 2, own_width), jnp.bfloat16)
     return pl.pallas_call(
-        functools.partial(attend_back_body, order=order, shard=shard, head_shard=head_shard, last=True),
+        functools.partial(
+            attend_back_body, order=order, shard=shard, head_shard=head_shard, last=True, parts=len(parts)
+        ),
         grid_spec=pltpu.PrefetchScalarGridSpec(
             num_scalar_prefetch=1,
             grid=(KEY_VALUE_HEADS // 2,),
             in_specs=[whole(rows, width)]
-            + attend_back_specs(rows, width, 1, lambda h, d: h)
+            + attend_back_specs(rows, width, 1, lambda h, d: h, parts)
             + [whole(2, HEAD_SIZE), whole(rows, width)]
             + [whole(rows, width), whole(1, width), whole(rows, width), whole(1, width)],
             out_specs=[whole(width // 2, own_width), whole(width // 2, own_width), whole(rows, width)],
@@ -570,13 +601,56 @@
                 pltpu.VMEM((rows, width), jnp.float32),
                 pltpu.VMEM((width, 128), jnp.float32),
             ]
-            + attend_back_scratch(rows),
+            + attend_back_scratch(rows, parts),
         ),
         out_shape=[half, half, jax.ShapeDtypeStruct((rows, width), jnp.bfloat16)],
         compiler_params=pltpu.CompilerParams(vmem_limit_bytes=38 * 1024 * 1024),
         cost_estimate=SMALL,
         name="attend_back_last",
-    )(device.reshape(1), residual_low, *operands, *sums, tokens, gain, grad_residual, grad_gain_two)
+    )(
+        device.reshape(1), residual_low, *operands, *parts, sums[0], *from_far(sums[1], tokens), gain, *from_far(grad_residual),
+        grad_gain_two,
+    )
+
+
+def project_body(device_ref, *refs):
+    (*part_refs, tokens_ref, attended_ref), (residual_ref, weight_out_ref) = refs[:-2], refs[-2:]
+    inner = device_ref[0] & (len(part_refs) - 1)
+
+    @pl.when(pl.program_id(0) == 0)
+    def _():
+        residual_ref[...] = tokens_ref[...].astype(jnp.float32)
+
+    for mask, ref in enumerate(part_refs):
+        weight_out_ref[:, inner ^ mask] = ref[...]
+    top, count, rows, columns = weight_out_ref.shape
+    weight = weight_out_ref[...].reshape(top * count * rows, columns)
+    residual_ref[...] += jnp.dot(attended_ref[...], weight, preferred_element_type=jnp.float32)
+
+
+def project(device, parts, tokens, attended):
+    rows, width = tokens.shape
+    top, part_rows, _ = parts[0].shape
+    step_rows = len(parts) * part_rows
+    whole = pl.BlockSpec((rows, width), lambda j, d: (0, 0))
+    residual, weight = pl.pallas_call(
+        project_body,
+        grid_spec=pltpu.PrefetchScalarGridSpec(
+            num_scalar_prefetch=1,
+            grid=(top,),
+            in_specs=[pl.BlockSpec((1, part_rows, width), lambda j, d: (j, 0, 0)) for _ in parts]
+            + [whole, pl.BlockSpec((rows, step_rows), lambda j, d: (0, j))],
+            out_specs=[whole, pl.BlockSpec((1, len(parts), part_rows, width), lambda j, d: (j, 0, 0, 0))],
+        ),
+        out_shape=[
+            jax.ShapeDtypeStruct((rows, width), jnp.float32),
+            far((top, len(parts), part_rows, width), jnp.bfloat16),
+        ],
+        compiler_params=pltpu.CompilerParams(vmem_limit_bytes=20 * 1024 * 1024),
+        cost_estimate=SMALL,
+        name="project",
+    )(device.reshape(1), *parts, tokens, attended)
+    return residual, weight.reshape(top * step_rows, width)
 
 
 def gather_down(down_ref, down_weight_ref, width):
@@ -642,7 +716,7 @@
     low = device & (owners - 1)
     for target, core in ((down_kept_ref, 0), (down_sent_ref, 1)):
         blocks = [product_ref[low ^ (index | core)] for index in range(0, owners, 2)]
-        target[...] = jnp.concatenate(blocks, axis=0).astype(jnp.bfloat16)
+        target[...] = jnp.concatenate(blocks, axis=0).astype(jnp.bfloat16).reshape(target.shape)
 
 
 def ffn_operands(weights, shard, width, tiles, at):
@@ -666,18 +740,18 @@
 def feed_forward(device, residual, gain, cotangent, weights, shard, gate_order, up_order):
     rows, width = residual.shape
     count, _, hidden_width = weights.shape
-    tiles = 8
+    tiles = 4
     tile = hidden_width // tiles
     owners = count // tiles
     at = lambda j, d: j ^ (d[0] // owners)
-    back = lambda j: (j & 1) * 4 + j // 2
     whole = pl.BlockSpec((rows, width), lambda j, d: (0, 0))
     row = pl.BlockSpec((1, width), lambda j, d: (0, 0))
     low = lambda height, size: jax.ShapeDtypeStruct((height, size), jnp.bfloat16)
+    low4 = jax.ShapeDtypeStruct((2, tiles, tile // 4, width), jnp.bfloat16)
     weight_args, weight_specs = ffn_operands(weights, shard, width, tiles, at)
     columns = lambda height: pl.BlockSpec((height, tile), lambda j, d: (0, at(j, d)))
-    down_half = pl.BlockSpec((tile // 2, width), lambda j, d: (back(j), 0))
-    return pl.pallas_call(
+    down_half = pl.BlockSpec((2, 1, tile // 4, width), lambda j, d: (0, j, 0, 0))
+    *out, down_kept, down_sent = pl.pallas_call(
         functools.partial(feed_forward_body, gate_order=gate_order, up_order=up_order),
         grid_spec=pltpu.PrefetchScalarGridSpec(
             num_scalar_prefetch=1,
@@ -704,30 +778,31 @@
             ],
         ),
         out_shape=[
-            low(rows, hidden_width),
-            low(rows, hidden_width),
-            low(rows, hidden_width),
+            far((rows, hidden_width), jnp.bfloat16),
+            far((rows, hidden_width), jnp.bfloat16),
+            far((rows, hidden_width), jnp.bfloat16),
             low(width // 2, hidden_width),
             low(width // 2, hidden_width),
             low(width // 2, hidden_width),
             low(width // 2, hidden_width),
-            low(hidden_width // 2, width),
-            low(hidden_width // 2, width),
+            low4,
+            low4,
         ],
-        compiler_params=pltpu.CompilerParams(vmem_limit_bytes=40 * 1024 * 1024),
+        compiler_params=pltpu.CompilerParams(vmem_limit_bytes=56 * 1024 * 1024),
         cost_estimate=SMALL,
         name="feed_forward",
-    )(device.reshape(1), residual, gain, cotangent, *weight_args)
-
-
-FFN_STEPS = 8
-
-
-def back_body(device_ref, *refs):
+    )(device.reshape(1), residual, gain, *from_far(cotangent, *weight_args))
+    return *out, down_kept.reshape(-1, width), down_sent.reshape(-1, width)
+
+
+FFN_STEPS = 4
+
+
+def back_body(device_ref, *refs, parts):
     (
         residual_ref, gain_ref, cotangent_ref, grad_gate_ref, grad_up_ref, gate_ref, up_ref, turned_out_ref
     ), refs = refs[:8], refs[8:]
-    operands, refs = refs[:12], refs[12:]
+    operands, refs = refs[: 11 + parts], refs[11 + parts :]
     (
         grad_residual_ref, grad_low_ref, grad_gain_ref, out_kept_ref, out_sent_ref, kept_ref, sent_ref, head_gains_ref,
         normed_sum_ref, back_ref,
@@ -768,11 +843,11 @@
     def _():
         attend_back_body(
             device_ref, grad_low_ref, *operands, kept_ref, sent_ref, head_gains_ref, normed_sum_ref, *scratch,
-            order=None, shard=None, head_shard=None, last=False, head=step - FFN_STEPS,
+            order=None, shard=None, head_shard=None, last=False, parts=parts, head=step - FFN_STEPS,
         )
 
 
-def back(device, residual, gain, cotangent, grad_gate, grad_up, weights, shard, turned_out, operands):
+def back(device, residual, gain, cotangent, grad_gate, grad_up, weights, shard, turned_out, operands, parts):
     rows, width = residual.shape
     tile = weights.shape[2] // FFN_STEPS
     at = lambda j, d: jnp.minimum(j, FFN_STEPS - 1)
@@ -783,16 +858,16 @@
     out_rows = turned_out.shape[0]
     own_width = KEY_VALUE_HEADS * 2 * HEAD_SIZE
     low = lambda height, size: jax.ShapeDtypeStruct((height, size), jnp.bfloat16)
-    wide = jax.ShapeDtypeStruct((rows, width), jnp.float32)
+    wide = far((rows, width), jnp.float32)
     return pl.pallas_call(
-        back_body,
+        functools.partial(back_body, parts=len(parts)),
         grid_spec=pltpu.PrefetchScalarGridSpec(
             num_scalar_prefetch=1,
             grid=(FFN_STEPS + KEY_VALUE_HEADS // 2,),
             in_specs=[whole(rows, width), whole(1, width), whole(rows, width), columns, columns]
             + weight_specs[:2]
             + [whole(out_rows, rows)]
-            + attend_back_specs(rows, width, 0, head),
+            + attend_back_specs(rows, width, 0, head, parts),
             out_specs=[
                 whole(rows, width),
                 whole(rows, width),
@@ -804,7 +879,7 @@
                 whole(2, HEAD_SIZE),
                 whole(rows, width),
             ],
-            scratch_shapes=[pltpu.VMEM((rows, width), jnp.float32)] + attend_back_scratch(rows),
+            scratch_shapes=[pltpu.VMEM((rows, width), jnp.float32)] + attend_back_scratch(rows, parts),
         ),
         out_shape=[
             wide,
@@ -817,10 +892,12 @@
             jax.ShapeDtypeStruct((2, HEAD_SIZE), jnp.float32),
             wide,
         ],
-        compiler_params=pltpu.CompilerParams(vmem_limit_bytes=46 * 1024 * 1024),
+        compiler_params=pltpu.CompilerParams(vmem_limit_bytes=50 * 1024 * 1024),
         cost_estimate=SMALL,
         name="back",
-    )(device.reshape(1), residual, gain, cotangent, grad_gate, grad_up, *weight_args[:2], turned_out, *operands)
+    )(
+        device.reshape(1), residual, gain, *from_far(cotangent, grad_gate, grad_up, *weight_args[:2], turned_out), *operands, *parts
+    )
 
 
 def ffn_out_body(residual_ref, hidden_ref, down_ref, mixed_ref, sum_ref, down_weight_ref):
@@ -852,7 +929,7 @@
         compiler_params=pltpu.CompilerParams(vmem_limit_bytes=16 * 1024 * 1024),
         cost_estimate=SMALL,
         name="ffn_out",
-    )(residual, hidden, weight_args[2])
+    )(*from_far(residual, hidden, weight_args[2]))
 
 
 def end_body(first_kept, first_came, second_kept, second_came, query_ref, key_ref, value_ref, *gain_refs):
@@ -939,38 +1016,32 @@
     out_parts = gather_bits(lay_top(out_top, device, count), count, early[:cut_bits])
     first_parts, second_parts = fence((first_parts, second_parts))
     second_parts = gather_bits(second_parts, count, [0])
-    first_weight = lay(first_parts, device, count)
+    first_gains = lay({mask: part[..., -128:] for mask, part in first_parts.items()}, device, count)
+    first_weight = weight_parts(first_parts, device, count)
 
     seq_id, token_position = layout(seq_lengths, seq_owner, device, row_total_count)
     first_row = (jnp.arange(row_total_count, dtype=jnp.int32) - token_position)[:, None]
     cosine, sine = rotation_factors(token_position)
     inputs = tokens.astype(jnp.float32)
-    gain_block = first_weight[:, KEY_VALUE_HEADS // 2 * GROUP :].astype(jnp.float32)
+    gain_block = first_gains.astype(jnp.float32)
     head_gains = gain_block.reshape(count, shard, 128)[:, :head_shard, 2:4].reshape(HEAD_SIZE, 2).T
     gain_one = gain_block[:, 0]
     gain_two = gain_block[:, 1]
     normed_low = norm_forward(inputs, gain_one)[0].astype(jnp.bfloat16)
-    attended_first, *saved_first = attend(normed_low, first_weight, head_gains, cosine, sine, first_row)
+    attended_first, *saved_first = attend(device, normed_low, first_weight, head_gains, cosine, sine, first_row)
     attended_first, second_parts, out_parts = fence((attended_first, second_parts, out_parts))
     out_parts = gather_bits(out_parts, count, early[cut_bits:])
-    second_weight = lay(second_parts, device, count)
-    attended_second, *saved_second = attend(normed_low, second_weight, head_gains, cosine, sine, first_row)
+    second_weight = weight_parts(second_parts, device, count)
+    attended_second, *saved_second = attend(device, normed_low, second_weight, head_gains, cosine, sine, first_row)
     stages = sum_bits(count)
     orders = {name: row_order(count, bits) for name, bits in stages.items()}
-    turned = {
-        name: turn(values, device, orders[name])
-        for name, values in (
-            ("out", (attended_first, attended_second)), ("first", (normed_low,)), ("second", (normed_low,))
-        )
-    }
-    attended_first, attended_second, turned, out_parts = fence((attended_first, attended_second, turned, out_parts))
+    attended_first, attended_second, out_parts = fence((attended_first, attended_second, out_parts))
     out_parts = gather_bits(out_parts, count, [0])
-    out_weight = lay(out_parts, device, count)
-    half_width = out_weight.shape[0] // 2
-    residual = (
-        inputs
-        + jnp.dot(attended_first, out_weight[:half_width], preferred_element_type=jnp.float32)
-        + jnp.dot(attended_second, out_weight[half_width:], preferred_element_type=jnp.float32)
+    residual, out_weight = project(
+        device,
+        [out_parts[mask] for mask in range(count // 4)],
+        tokens,
+        jnp.concatenate([attended_first, attended_second], axis=1),
     )
     (
         hidden, grad_gate, grad_up, gate_kept, gate_sent, up_kept, up_sent, down_kept, down_sent
@@ -1009,39 +1080,48 @@
         land(*names)
         return [(live.pop(name), live.pop(name + "_came")) for name in names]
 
-    def operands(name, saved, weight):
-        return out_weight, *saved, head_gains, cosine, sine, first_row, turned[name], weight
-
+    def operands(name, saved):
+        return *from_far(out_weight, *saved), head_gains, cosine, sine, first_row, *from_far(turned[name])
+
+    live.update(attended_first=attended_first, attended_second=attended_second, normed=normed_low)
     fly(down=down_sent, gate=gate_sent, up=up_sent)
+    live["turned"] = dict(
+        out=turn((live.pop("attended_first"), live.pop("attended_second")), device, orders["out"]),
+        first=turn((live["normed"],), device, orders["first"]),
+        second=turn((live.pop("normed"),), device, orders["second"]),
+    )
     pass_on("down")
     pass_on("gate")
     pass_on("up")
+    turned = live.pop("turned")
     (
         live["grad_residual"], live["low"], live["grad_gain_two"], live["out"], live["out_sent"], live["first"],
         live["first_sent"], live["head_sums"], live["normed_sum"],
     ) = back(
         device, residual, gain_two[None], cotangent, live.pop("grad_gate"), live.pop("grad_up"), ffn_weights, shard,
-        turned["out"], operands("first", saved_first, first_weight),
+        turned["out"], operands("first", saved_first), first_weight,
     )
     land("down", "gate", "up")
     fly(first=live["first_sent"], out=live["out_sent"])
     halve("down", "gate", "up")
     pass_on("first", "out")
     live["second"], live["second_sent"], live["grad_tokens"] = attend_back_last(
-        device, live.pop("low"), operands("second", saved_second, second_weight), (live.pop("head_sums"), live.pop("normed_sum")), tokens,
+        device, live.pop("low"), operands("second", saved_second), second_weight, (live.pop("head_sums"), live.pop("normed_sum")), tokens,
         gain_one[None], live.pop("grad_residual"), live.pop("grad_gain_two"), orders["second"], shard, head_shard,
     )
-    land("down", "gate", "up", "first", "out")
+    land("down", "gate", "up")
+    land("first", "out")
     fly(second=live["second_sent"])
     halve("down", "gate", "up")
-    land("second")
-    halve("first", "out", "second")
+    pass_on("second")
+    halve("first", "out")
     live["mixed"] = ffn_out(residual, live.pop("hidden"), ffn_weights, shard)
     cut()
     mixed, grad_tokens = live.pop("mixed"), live.pop("grad_tokens")
     while stages["down"]:
         pass_on("down", "gate", "up")
-        pass_on("first", "out", "second")
+        pass_on("first", "out")
+        pass_on("second")
     sums = {name: sum_end(pair) for name, pair in zip(("down", "gate", "up"), end("down", "gate", "up"))}
     live.update(sums)
     while stages["out"]:

time: 418 us -> 402 us (0.962)
  local copies, waits for them, and re-layouts: 38.5 us -> 17.2 us
  waiting for transfers between devices: 147 us -> 159 us
    unnamed x153 -> x76, local copies, waits for them, and re-layouts: 33.2 us -> 9.55 us
    ppermute x57, waiting for transfers between devices: 147 us -> 159 us  [exchange(): lax.ppermute(values, 'fsdp', [(source, source ^ mask) for source in range...]
    pallas_call x4 -> x2, Pallas kernels: 12 us -> 2.8 us  [place(): pl.pallas_call(place_body, grid_spec=pltpu.PrefetchScalarGridSpec(num_sca...]
    pallas_call x3 -> x4, Pallas kernels: 53.1 us -> 61.9 us  [the longest x1 34.2 us: back(): pl.pallas_call(functools.partial(back_body, parts=len(parts)), grid_spec=...]
    pallas_call x11 -> x13, Pallas kernels: 18.5 us -> 12.1 us  [fold(): pl.pallas_call(fold_body, grid=(steps,), in_specs=in_specs, out_specs=out...]
    pallas_call x1, Pallas kernels: 31.3 us -> 27 us  [feed_forward(): pl.pallas_call(functools.partial(feed_forward_body, gate_order=gate_order...]
  transfers between devices with their start and end apart: 58 -> 58, of which waited for: 33 -> 32; matrix products, arithmetic and copies ran while one was open for 3% -> 4% of each run, Pallas kernels for 25% -> 28%
where the time goes in v5:
time: 402 us; the launch traced here: 401 us
  waiting for transfers between devices  159 us (40%)
  Pallas kernels  144 us (36%)
  starting transfers between devices  56 us (14%)
  local copies, waits for them, and re-layouts  17.2 us (4%)
  between operations  14.6 us (4%)
  other arithmetic  10.9 us (3%)
    ppermute x57, waiting for transfers between devices, exchange(): lax.ppermute(values, 'fsdp', [(source, source ^ mask) for source in range...  159 us
    ppermute x57, starting transfers between devices, exchange(): lax.ppermute(values, 'fsdp', [(source, source ^ mask) for source in range...  56 us
    pallas_call x1, Pallas kernels, back(): pl.pallas_call(functools.partial(back_body, parts=len(parts)), grid_spec=...  34.2 us
    pallas_call x1, Pallas kernels, feed_forward(): pl.pallas_call(functools.partial(feed_forward_body, gate_order=gate_order...  27 us
    pallas_call x2, Pallas kernels, attend(): pl.pallas_call(attend_body, grid_spec=pltpu.PrefetchScalarGridSpec(num_sc...  21.9 us
    pallas_call x1, Pallas kernels, attend_back_last(): pl.pallas_call(functools.partial(attend_back_body, order=order, shard=sha...  20 us
    pallas_call x13, Pallas kernels, fold(): pl.pallas_call(fold_body, grid=(steps,), in_specs=in_specs, out_specs=out...  12.1 us
    pallas_call x1, Pallas kernels, ffn_out(): pl.pallas_call(ffn_out_body, grid=(tiles,), in_specs=[whole, pl.BlockSpec...  9.64 us
  transfers between devices with their start and end apart: 58, of which 32 were waited for; matrix products, arithmetic and copies ran while one was open for 4% of the time, Pallas kernels for 28%

profile of v5, /device:TPU:0, one launch (start us, length us, event | category | flops | bytes accessed | tf_op | source)
XLA Modules:
  0.0 401.3 jit_solution(13826387394187881883)
XLA Ops:
  8.5 2.0 pad_maximum_fusion.1
  12.9 3.0 collective-permute-start
  16.0 2.6 collective-permute-start.1
  18.6 13.4 %collective-permute-done = bf16[32,4224]{1,0:T(8,128)(2,1)S(1)} collective-permute-done((bf16[32,4224]{1,0:T(8,128)(2,1)}, bf16[32,4224]{1,0:T(8,128)(2,1)S(1)}, u32[]{:S(2)}, u32[]{:S(2)}) %collective-permute-start) | collective-permute-done | bytes 270368 | tf_op jit(solution)/shard_map/ppermute | solution.py:65
  33.5 2.2 collective-permute-start.2
  35.7 11.6 %collective-permute-done.2 = bf16[32,4224]{1,0:T(8,128)(2,1)S(1)} collective-permute-done((bf16[32,4224]{1,0:T(8,128)(2,1)S(1)}, bf16[32,4224]{1,0:T(8,128)(2,1)S(1)}, u32[]{:S(2)}, u32[]{:S(2)}) %collective-permute-start.2) | collective-permute-done | bytes 270368 | tf_op jit(solution)/shard_map/ppermute | solution.py:65
  48.1 2.2 lay_top_split.1
  54.6 2.5 collective-permute-start.6
  57.2 9.8 %collective-permute-done.5 = bf16[64,1024]{1,0:T(8,128)(2,1)S(1)} collective-permute-done((bf16[64,1024]{1,0:T(8,128)(2,1)S(1)}, bf16[64,1024]{1,0:T(8,128)(2,1)S(1)}, u32[]{:S(2)}, u32[]{:S(2)}) %collective-permute-start.5) | collective-permute-done | bytes 131104 | tf_op jit(solution)/shard_map/ppermute | solution.py:65
  67.0 3.1 collective-permute-done.6
  70.1 3.1 collective-permute-done.4.refs_4_
  73.2 2.2 collective-permute-done.3.refs_2_.refs_21_
  77.4 2.0 collective-permute-start.10
  82.1 2.7 collective-permute-done.11
  84.8 8.9 %collective-permute-done.10.refs_6_ = bf16[4,32,2048]{2,1,0:T(8,128)(2,1)} collective-permute-done((bf16[4,32,2048]{2,1,0:T(8,128)(2,1)}, bf16[4,32,2048]{2,1,0:T(8,128)(2,1)}, u32[]{:S(2)}, u32[]{:S(2)}) %collective-permute-start.10) | collective-permute-done | bytes 524320 | tf_op jit(solution)/shard_map/ppermute | solution.py:65
  93.7 11.2 %collective-permute-done.9.refs_2_ = bf16[4,32,2048]{2,1,0:T(8,128)(2,1)} collective-permute-done((bf16[4,32,2048]{2,1,0:T(8,128)(2,1)}, bf16[4,32,2048]{2,1,0:T(8,128)(2,1)}, u32[]{:S(2)}, u32[]{:S(2)}) %collective-permute-start.9) | collective-permute-done | bytes 524320 | tf_op jit(solution)/shard_map/ppermute | solution.py:65
  107.6 1.9 place.3
  109.5 2.6 collective-permute-start.20
  123.7 11.0 %attend.2 = (bf16[384,1024]{1,0:T(8,128)(2,1)S(1)}, bf16[384,1024]{1,0:T(8,128)(2,1)}, bf16[384,512]{1,0:T(8,128)(2,1)}, bf16[384,512]{1,0:T(8,128)(2,1)}, f32[384,1536]{1,0:T(8,128)}, /*index=5*/f32[4,384,2]{2,1,0:T(8,128)}) custom-call(s32[1]{0:T(128)} %bitcast.device_ref, bf16[4,32,2176]{2,1,0:T(8,128)(2,1)S(1)} %get-tuple-element.479.refs_0_.refs_19_, ...), custom_call_target="tpu_custom_call" | custom-call | flops 1 | bytes 1 | tf_op jit(solution)/shard_map/attend/pallas_call | solution.py:396
  138.3 10.9 %attend.3 = (bf16[384,1024]{1,0:T(8,128)(2,1)S(1)}, bf16[384,1024]{1,0:T(8,128)(2,1)}, bf16[384,512]{1,0:T(8,128)(2,1)}, bf16[384,512]{1,0:T(8,128)(2,1)}, f32[384,1536]{1,0:T(8,128)}, /*index=5*/f32[4,384,2]{2,1,0:T(8,128)}) custom-call(s32[1]{0:T(128)} %bitcast.device_ref, bf16[4,32,2048]{2,1,0:T(8,128)(2,1)} %get-tuple-element.497.refs_0_, ...), custom_call_target="tpu_custom_call" | custom-call | flops 1 | bytes 1 | tf_op jit(solution)/shard_map/attend/pallas_call | solution.py:396
  151.4 9.7 %collective-permute-done.22.refs_6_ = bf16[4,64,1024]{2,1,0:T(8,128)(2,1)} collective-permute-done((bf16[4,64,1024]{2,1,0:T(8,128)(2,1)}, bf16[4,64,1024]{2,1,0:T(8,128)(2,1)}, u32[]{:S(2)}, u32[]{:S(2)}) %collective-permute-start.22) | collective-permute-done | bytes 524320 | tf_op jit(solution)/shard_map/ppermute | solution.py:65
  162.2 1.8 copy.57
  166.7 5.8 %project.1 = (f32[384,1024]{1,0:T(8,128)S(1)}, bf16[4,8,64,1024]{3,2,1,0:T(8,128)(2,1)}) custom-call(s32[1]{0:T(128)} %bitcast.device_ref, bf16[4,64,1024]{2,1,0:T(8,128)(2,1)} %bitcast.23.refs_0_, bf16[4,64,1024]{2,1,0:T(8,128)(2,1)} %collective-permute-done.23.refs_1_, bf16[4,64,1024]{2,1,0:T(8,128)(2,1)} %collective-permute-done.20.refs_2_, ...), custom_call_target="tpu_custom_call" | custom-call | flops 1 | bytes 1 | tf_op jit(solution)/shard_map/project/pallas_call | solution.py:636
  173.7 27.0 %feed_forward.1 = (bf16[384,3072]{1,0:T(8,128)(2,1)}, bf16[384,3072]{1,0:T(8,128)(2,1)}, bf16[384,3072]{1,0:T(8,128)(2,1)}, bf16[512,3072]{1,0:T(8,128)(2,1)}, b...) custom-call(s32[1]{0:T(128)} %bitcast.device_ref, ...), custom_call_target="tpu_custom_call" | custom-call | flops 1 | bytes 1 | tf_op jit(solution)/shard_map/feed_forward/pallas_call | solution.py:754
  206.7 1.9 fold.13
  208.6 2.6 collective-permute-done.28.refs_2_.refs_3_
  211.2 1.9 fold.14
  213.1 2.6 collective-permute-done.29.refs_2_.refs_3_
  215.6 1.9 fold.15
  217.6 1.8 collective-permute-start.31
  220.8 34.2 %back.1 = (f32[384,1024]{1,0:T(8,128)}, bf16[384,1024]{1,0:T(8,128)(2,1)}, f32[1,1024]{1,0:T(1,128)S(1)}, bf16[1024,1024]{1,0:T(8,128)(2,1)}, bf16[1024,1024]{1,...) custom-call(s32[1]{0:T(128)} %bitcast.device_ref, ...), custom_call_target="tpu_custom_call" | custom-call | flops 1 | bytes 1 | tf_op jit(solution)/shard_map/back/pallas_call | solution.py:862
  256.3 2.3 fold.16
  260.2 3.0 collective-permute-done.34.refs_6_.refs_7_
  266.4 2.3 collective-permute-start.35
  270.7 20.0 %attend_back_last.1 = (bf16[512,2176]{1,0:T(8,128)(2,1)S(1)}, bf16[512,2176]{1,0:T(8,128)(2,1)S(1)}, bf16[384,1024]{1,0:T(8,128)(2,1)}) custom-call(s32[1]{0:T(128)} %bitcast.device_ref, bf16[384,1024]{1,0:T(8,128)(2,1)S(1)} %copy-done.17, bf16[2048,1024]{1,0:T(8,128)(2,1)} %bitcast.61, bf16[384,1024]{1,0:T(8,128)(2,1)} %get-tuple-element.672.query_ref, ...), custom_call_target="tpu_custom_call" | custom-call | flops 1 | bytes 1 | tf_op jit(solution)/shard_map/attend_back_last/pallas_call | solution.py:587
  290.8 14.9 %collective-permute-done.35.refs_2_.refs_3_ = bf16[384,1024]{1,0:T(8,128)(2,1)S(1)} collective-permute-done((bf16[384,1024]{1,0:T(8,128)(2,1)}, bf16[384,1024]{1,0:T(8,128)(2,1)S(1)}, u32[]{:S(2)}, u32[]{:S(2)}) %collective-permute-start.35) | collective-permute-done | bytes 786464 | tf_op jit(solution)/shard_map/ppermute | solution.py:65
  307.0 3.7 collective-permute-done.40.refs_2_.refs_3_
  311.7 3.9 collective-permute-start.41
  318.3 15.6 %collective-permute-done.41.refs_2_.refs_3_ = bf16[192,1024]{1,0:T(8,128)(2,1)S(1)} collective-permute-done((bf16[192,1024]{1,0:T(8,128)(2,1)S(1)}, bf16[192,1024]{1,0:T(8,128)(2,1)S(1)}, u32[]{:S(2)}, u32[]{:S(2)}) %collective-permute-start.41) | collective-permute-done | bytes 393248 | tf_op jit(solution)/shard_map/ppermute | solution.py:65
  335.5 9.6 %ffn_out.1 = bf16[384,1024]{1,0:T(8,128)(2,1)} custom-call(f32[384,1024]{1,0:T(8,128)} %copy-done, bf16[384,3072]{1,0:T(8,128)(2,1)} %get-tuple-element.764.hidden_ref, bf16[32,96,3072]{2,1,0:T(8,128)(2,1)} %bitcast.59), custom_call_target="tpu_custom_call" | custom-call | flops 1 | bytes 1 | tf_op jit(solution)/shard_map/ffn_out/pallas_call | solution.py:922
  349.3 2.3 collective-permute-start.51
  353.4 2.5 collective-permute-done.48
  360.5 8.9 %collective-permute-done.52.refs_10_.refs_11_ = bf16[128,2176]{1,0:T(8,128)(2,1)S(1)} collective-permute-done((bf16[128,2176]{1,0:T(8,128)(2,1)S(1)}, bf16[128,2176]{1,0:T(8,128)(2,1)S(1)}, u32[]{:S(2)}, u32[]{:S(2)}) %collective-permute-start.52) | collective-permute-done | bytes 557088 | tf_op jit(solution)/shard_map/ppermute | solution.py:65
  369.8 2.5 collective-permute-start.53
  372.8 5.4 %collective-permute-done.53.first_came = bf16[32,2048]{1,0:T(8,128)(2,1)S(1)} collective-permute-done((bf16[32,2048]{1,0:T(8,128)(2,1)S(1)}, bf16[32,2048]{1,0:T(8,128)(2,1)S(1)}, u32[]{:S(2)}, u32[]{:S(2)}) %collective-permute-start.53) | collective-permute-done | bytes 131104 | tf_op jit(solution)/shard_map/ppermute | solution.py:65
  378.2 6.3 %collective-permute-done.54 = bf16[64,1024]{1,0:T(8,128)(2,1)S(1)} collective-permute-done((bf16[64,1024]{1,0:T(8,128)(2,1)S(1)}, bf16[64,1024]{1,0:T(8,128)(2,1)S(1)}, u32[]{:S(2)}, u32[]{:S(2)}) %collective-permute-start.54) | collective-permute-done | bytes 131104 | tf_op jit(solution)/shard_map/ppermute | solution.py:65
  386.0 5.9 %collective-permute-done.56.second_came = bf16[32,2176]{1,0:T(8,128)(2,1)S(1)} collective-permute-done((bf16[32,2176]{1,0:T(8,128)(2,1)S(1)}, bf16[32,2176]{1,0:T(8,128)(2,1)S(1)}, u32[]{:S(2)}, u32[]{:S(2)}) %collective-permute-start.56) | collective-permute-done | bytes 139296 | tf_op jit(solution)/shard_map/ppermute | solution.py:65
  392.5 1.9 end_projections.1
  (208 shorter events, 75.5 us)
Async XLA Ops:
  7.2 166.5 %all-gather.3.cloned.1.call-start = ((), (), s32[]{:S(2)}) async-start(), calls=%async_computation | async-start | bytes 19464192 | tf_op jit(solution)/shard_map/all_gather | solution.py:998
  12.9 19.0 %collective-permute-start = (bf16[32,4224]{1,0:T(8,128)(2,1)}, bf16[32,4224]{1,0:T(8,128)(2,1)S(1)}, u32[]{:S(2)}, u32[]{:S(2)}) collective-permute-start(bf16[32,4224]{1,0:T(8,128)(2,1)} %join.1), channel_id=1, source_target_pairs={{0,8},{1,9},{2,10},{3,11},{4,12},{5,13},{6,14},{7,15},{8,0},{9,1},... | collective-permute-start | bytes 811016 | tf_op jit(solution)/shard_map/ppermute | solution.py:65
  16.0 17.5 %collective-permute-start.1 = (bf16[32,4224]{1,0:T(8,128)(2,1)}, bf16[32,4224]{1,0:T(8,128)(2,1)S(1)}, u32[]{:S(2)}, u32[]{:S(2)}) collective-permute-start(bf16[32,4224]{1,0:T(8,128)(2,1)} %join.1), channel_id=1, source_target_pairs={{0,16},{1,17},{2,18},{3,19},{4,20},{5,21},{6,22},{7,23},{8,24},{9,... | collective-permute-start | bytes 811016 | tf_op jit(solution)/shard_map/ppermute | solution.py:65
  33.5 13.9 %collective-permute-start.2 = (bf16[32,4224]{1,0:T(8,128)(2,1)S(1)}, bf16[32,4224]{1,0:T(8,128)(2,1)S(1)}, u32[]{:S(2)}, u32[]{:S(2)}) collective-permute-start(bf16[32,4224]{1,0:T(8,128)(2,1)S(1)} %collective-permute-done.1), channel_id=1, source_target_pairs={{0,8},{1,9},{2,10},{3,11},{4,12},{5,13},{6,14},{7,15},{8,0},{9,1},... | collective-permute-start | bytes 811016 | tf_op jit(solution)/shard_map/ppermute | solution.py:65
  50.2 25.1 %collective-permute-start.3 = (bf16[4,32,2176]{2,1,0:T(8,128)(2,1)S(1)}, bf16[4,32,2176]{2,1,0:T(8,128)(2,1)S(1)}, u32[]{:S(2)}, u32[]{:S(2)}) collective-permute-start(bf16[4,32,2176]{2,1,0:T(8,128)(2,1)S(1)} %get-tuple-element.479.refs_0_.refs_19_), channel_id=1, source_target_pairs={{0,2},{1,3},{2,0},{3,1},{4,6},{5,7},{6,4},{7,5},{8,10},{9,11},{10,... | collective-permute-start | bytes 1671176 | tf_op jit(solution)/shard_map/ppermute | solution.py:65
  51.8 21.4 %collective-permute-start.4 = (bf16[4,32,2048]{2,1,0:T(8,128)(2,1)}, bf16[4,32,2048]{2,1,0:T(8,128)(2,1)}, u32[]{:S(2)}, u32[]{:S(2)}) collective-permute-start(bf16[4,32,2048]{2,1,0:T(8,128)(2,1)} %get-tuple-element.497.refs_0_), channel_id=1, source_target_pairs={{0,4},{1,5},{2,6},{3,7},{4,0},{5,1},{6,2},{7,3},{8,12},{9,13},{10,... | collective-permute-start | bytes 1572872 | tf_op jit(solution)/shard_map/ppermute | solution.py:65
  53.3 13.7 %collective-permute-start.5 = (bf16[64,1024]{1,0:T(8,128)(2,1)S(1)}, bf16[64,1024]{1,0:T(8,128)(2,1)S(1)}, u32[]{:S(2)}, u32[]{:S(2)}) collective-permute-start(bf16[64,1024]{1,0:T(8,128)(2,1)S(1)} %copy-done.26), channel_id=1, source_target_pairs={{0,8},{1,9},{2,10},{3,11},{4,12},{5,13},{6,14},{7,15},{8,0},{9,1},... | collective-permute-start | bytes 393224 | tf_op jit(solution)/shard_map/ppermute | solution.py:65
  54.6 15.5 %collective-permute-start.6 = (bf16[64,1024]{1,0:T(8,128)(2,1)S(1)}, bf16[64,1024]{1,0:T(8,128)(2,1)S(1)}, u32[]{:S(2)}, u32[]{:S(2)}) collective-permute-start(bf16[64,1024]{1,0:T(8,128)(2,1)S(1)} %copy-done.26), channel_id=1, source_target_pairs={{0,16},{1,17},{2,18},{3,19},{4,20},{5,21},{6,22},{7,23},{8,24},{9,... | collective-permute-start | bytes 393224 | tf_op jit(solution)/shard_map/ppermute | solution.py:65
  75.3 29.5 %collective-permute-start.7 = (bf16[4,32,2176]{2,1,0:T(8,128)(2,1)S(1)}, bf16[4,32,2176]{2,1,0:T(8,128)(2,1)S(1)}, u32[]{:S(2)}, u32[]{:S(2)}) collective-permute-start(bf16[4,32,2176]{2,1,0:T(8,128)(2,1)S(1)} %get-tuple-element.479.refs_0_.refs_19_), channel_id=1, source_target_pairs={{0,4},{1,5},{2,6},{3,7},{4,0},{5,1},{6,2},{7,3},{8,12},{9,13},{10,... | collective-permute-start | bytes 1671176 | tf_op jit(solution)/shard_map/ppermute | solution.py:65
  76.8 28.0 %collective-permute-start.8 = (bf16[4,32,2176]{2,1,0:T(8,128)(2,1)S(1)}, bf16[4,32,2176]{2,1,0:T(8,128)(2,1)}, u32[]{:S(2)}, u32[]{:S(2)}) collective-permute-start(bf16[4,32,2176]{2,1,0:T(8,128)(2,1)S(1)} %collective-permute-done.3.refs_2_.refs_21_), channel_id=1, source_target_pairs={{0,4},{1,5},{2,6},{3,7},{4,0},{5,1},{6,2},{7,3},{8,12},{9,13},{10,... | collective-permute-start | bytes 1671176 | tf_op jit(solution)/shard_map/ppermute | solution.py:65
  77.4 16.3 %collective-permute-start.10 = (bf16[4,32,2048]{2,1,0:T(8,128)(2,1)}, bf16[4,32,2048]{2,1,0:T(8,128)(2,1)}, u32[]{:S(2)}, u32[]{:S(2)}) collective-permute-start(bf16[4,32,2048]{2,1,0:T(8,128)(2,1)} %collective-permute-done.4.refs_4_), channel_id=1, source_target_pairs={{0,2},{1,3},{2,0},{3,1},{4,6},{5,7},{6,4},{7,5},{8,10},{9,11},{10,... | collective-permute-start | bytes 1572872 | tf_op jit(solution)/shard_map/ppermute | solution.py:65
  79.4 25.5 %collective-permute-start.9 = (bf16[4,32,2048]{2,1,0:T(8,128)(2,1)}, bf16[4,32,2048]{2,1,0:T(8,128)(2,1)}, u32[]{:S(2)}, u32[]{:S(2)}) collective-permute-start(bf16[4,32,2048]{2,1,0:T(8,128)(2,1)} %get-tuple-element.497.refs_0_), channel_id=1, source_target_pairs={{0,2},{1,3},{2,0},{3,1},{4,6},{5,7},{6,4},{7,5},{8,10},{9,11},{10,... | collective-permute-start | bytes 1572872 | tf_op jit(solution)/shard_map/ppermute | solution.py:65
  104.9 7.2 %collective-permute-start.12 = (bf16[4,32,2176]{2,1,0:T(8,128)(2,1)S(1)}, bf16[4,32,2176]{2,1,0:T(8,128)(2,1)}, u32[]{:S(2)}, u32[]{:S(2)}) collective-permute-start(bf16[4,32,2176]{2,1,0:T(8,128)(2,1)S(1)} %get-tuple-element.479.refs_0_.refs_19_), channel_id=1, source_target_pairs={{0,1},{1,0},{2,3},{3,2},{4,5},{5,4},{6,7},{7,6},{8,9},{9,8},{10,11... | collective-permute-start | bytes 1671176 | tf_op jit(solution)/shard_map/ppermute | solution.py:65
  105.0 7.1 %collective-permute-start.13 = (bf16[4,32,2176]{2,1,0:T(8,128)(2,1)S(1)}, bf16[4,32,2176]{2,1,0:T(8,128)(2,1)}, u32[]{:S(2)}, u32[]{:S(2)}) collective-permute-start(bf16[4,32,2176]{2,1,0:T(8,128)(2,1)S(1)} %collective-permute-done.3.refs_2_.refs_21_), channel_id=1, source_target_pairs={{0,1},{1,0},{2,3},{3,2},{4,5},{5,4},{6,7},{7,6},{8,9},{9,8},{10,11... | collective-permute-start | bytes 1671176 | tf_op jit(solution)/shard_map/ppermute | solution.py:65
  109.5 26.6 %collective-permute-start.20 = (bf16[4,64,1024]{2,1,0:T(8,128)(2,1)}, bf16[4,64,1024]{2,1,0:T(8,128)(2,1)}, u32[]{:S(2)}, u32[]{:S(2)}) collective-permute-start(bf16[4,64,1024]{2,1,0:T(8,128)(2,1)} %bitcast.23.refs_0_), channel_id=1, source_target_pairs={{0,2},{1,3},{2,0},{3,1},{4,6},{5,7},{6,4},{7,5},{8,10},{9,11},{10,... | collective-permute-start | bytes 1572872 | tf_op jit(solution)/shard_map/ppermute | solution.py:65
  115.9 20.2 %collective-permute-start.16 = (bf16[4,32,2048]{2,1,0:T(8,128)(2,1)}, bf16[4,32,2048]{2,1,0:T(8,128)(2,1)}, u32[]{:S(2)}, u32[]{:S(2)}) collective-permute-start(bf16[4,32,2048]{2,1,0:T(8,128)(2,1)} %get-tuple-element.497.refs_0_), channel_id=1, source_target_pairs={{0,1},{1,0},{2,3},{3,2},{4,5},{5,4},{6,7},{7,6},{8,9},{9,8},{10,11... | collective-permute-start | bytes 1572872 | tf_op jit(solution)/shard_map/ppermute | solution.py:65
  115.9 20.2 %collective-permute-start.17 = (bf16[4,32,2048]{2,1,0:T(8,128)(2,1)}, bf16[4,32,2048]{2,1,0:T(8,128)(2,1)}, u32[]{:S(2)}, u32[]{:S(2)}) collective-permute-start(bf16[4,32,2048]{2,1,0:T(8,128)(2,1)} %collective-permute-done.9.refs_2_), channel_id=1, source_target_pairs={{0,1},{1,0},{2,3},{3,2},{4,5},{5,4},{6,7},{7,6},{8,9},{9,8},{10,11... | collective-permute-start | bytes 1572872 | tf_op jit(solution)/shard_map/ppermute | solution.py:65
  116.5 19.7 %collective-permute-start.18 = (bf16[4,32,2048]{2,1,0:T(8,128)(2,1)}, bf16[4,32,2048]{2,1,0:T(8,128)(2,1)}, u32[]{:S(2)}, u32[]{:S(2)}) collective-permute-start(bf16[4,32,2048]{2,1,0:T(8,128)(2,1)} %collective-permute-done.4.refs_4_), channel_id=1, source_target_pairs={{0,1},{1,0},{2,3},{3,2},{4,5},{5,4},{6,7},{7,6},{8,9},{9,8},{10,11... | collective-permute-start | bytes 1572872 | tf_op jit(solution)/shard_map/ppermute | solution.py:65
  116.5 19.7 %collective-permute-start.19 = (bf16[4,32,2048]{2,1,0:T(8,128)(2,1)}, bf16[4,32,2048]{2,1,0:T(8,128)(2,1)}, u32[]{:S(2)}, u32[]{:S(2)}) collective-permute-start(bf16[4,32,2048]{2,1,0:T(8,128)(2,1)} %collective-permute-done.10.refs_6_), channel_id=1, source_target_pairs={{0,1},{1,0},{2,3},{3,2},{4,5},{5,4},{6,7},{7,6},{8,9},{9,8},{10,11... | collective-permute-start | bytes 1572872 | tf_op jit(solution)/shard_map/ppermute | solution.py:65
  136.2 15.2 %collective-permute-start.21 = (bf16[4,64,1024]{2,1,0:T(8,128)(2,1)}, bf16[4,64,1024]{2,1,0:T(8,128)(2,1)}, u32[]{:S(2)}, u32[]{:S(2)}) collective-permute-start(bf16[4,64,1024]{2,1,0:T(8,128)(2,1)} %bitcast.23.refs_0_), channel_id=1, source_target_pairs={{0,4},{1,5},{2,6},{3,7},{4,0},{5,1},{6,2},{7,3},{8,12},{9,13},{10,... | collective-permute-start | bytes 1572872 | tf_op jit(solution)/shard_map/ppermute | solution.py:65
  137.1 24.0 %collective-permute-start.22 = (bf16[4,64,1024]{2,1,0:T(8,128)(2,1)}, bf16[4,64,1024]{2,1,0:T(8,128)(2,1)}, u32[]{:S(2)}, u32[]{:S(2)}) collective-permute-start(bf16[4,64,1024]{2,1,0:T(8,128)(2,1)} %collective-permute-done.20.refs_2_), channel_id=1, source_target_pairs={{0,4},{1,5},{2,6},{3,7},{4,0},{5,1},{6,2},{7,3},{8,12},{9,13},{10,... | collective-permute-start | bytes 1572872 | tf_op jit(solution)/shard_map/ppermute | solution.py:65
  201.0 10.1 %collective-permute-start.28 = (bf16[512,3072]{1,0:T(8,128)(2,1)}, bf16[512,3072]{1,0:T(8,128)(2,1)S(1)}, u32[]{:S(2)}, u32[]{:S(2)}) collective-permute-start(bf16[512,3072]{1,0:T(8,128)(2,1)} %get-tuple-element.548), channel_id=1, source_target_pairs={{0,1},{1,0},{2,3},{3,2},{4,5},{5,4},{6,7},{7,6},{8,9},{9,8},{10,11... | collective-permute-start | bytes 9437192 | tf_op jit(solution)/shard_map/ppermute | solution.py:65
  201.3 14.4 %collective-permute-start.29 = (bf16[512,3072]{1,0:T(8,128)(2,1)}, bf16[512,3072]{1,0:T(8,128)(2,1)S(1)}, u32[]{:S(2)}, u32[]{:S(2)}) collective-permute-start(bf16[512,3072]{1,0:T(8,128)(2,1)} %get-tuple-element.577), channel_id=1, source_target_pairs={{0,1},{1,0},{2,3},{3,2},{4,5},{5,4},{6,7},{7,6},{8,9},{9,8},{10,11... | collective-permute-start | bytes 9437192 | tf_op jit(solution)/shard_map/ppermute | solution.py:65
  217.6 37.4 %collective-permute-start.32 = (bf16[256,3072]{1,0:T(8,128)(2,1)}, bf16[256,3072]{1,0:T(8,128)(2,1)S(1)}, u32[]{:S(2)}, u32[]{:S(2)}) collective-permute-start(bf16[256,3072]{1,0:T(8,128)(2,1)} %get-tuple-element.615), channel_id=1, source_target_pairs={{0,8},{1,9},{2,10},{3,11},{4,12},{5,13},{6,14},{7,15},{8,0},{9,1},... | collective-permute-start | bytes 4718600 | tf_op jit(solution)/shard_map/ppermute | solution.py:65
  217.6 37.3 %collective-permute-start.31 = (bf16[256,3072]{1,0:T(8,128)(2,1)}, bf16[256,3072]{1,0:T(8,128)(2,1)S(1)}, u32[]{:S(2)}, u32[]{:S(2)}) collective-permute-start(bf16[256,3072]{1,0:T(8,128)(2,1)} %get-tuple-element.605), channel_id=1, source_target_pairs={{0,2},{1,3},{2,0},{3,1},{4,6},{5,7},{6,4},{7,5},{8,10},{9,11},{10,... | collective-permute-start | bytes 4718600 | tf_op jit(solution)/shard_map/ppermute | solution.py:65
  219.5 36.4 %collective-permute-start.30 = (bf16[768,1024]{1,0:T(8,128)(2,1)}, bf16[768,1024]{1,0:T(8,128)(2,1)S(1)}, u32[]{:S(2)}, u32[]{:S(2)}) collective-permute-start(bf16[768,1024]{1,0:T(8,128)(2,1)} %get-tuple-element.591), channel_id=1, source_target_pairs={{0,4},{1,5},{2,6},{3,7},{4,0},{5,1},{6,2},{7,3},{8,12},{9,13},{10,... | collective-permute-start | bytes 4718600 | tf_op jit(solution)/shard_map/ppermute | solution.py:65
  255.8 7.4 %collective-permute-start.34 = (bf16[1024,1024]{1,0:T(8,128)(2,1)}, bf16[1024,1024]{1,0:T(8,128)(2,1)S(1)}, u32[]{:S(2)}, u32[]{:S(2)}) collective-permute-start(bf16[1024,1024]{1,0:T(8,128)(2,1)} %get-tuple-element.647), channel_id=1, source_target_pairs={{0,1},{1,0},{2,3},{3,2},{4,5},{5,4},{6,7},{7,6},{8,9},{9,8},{10,11... | collective-permute-start | bytes 6291464 | tf_op jit(solution)/shard_map/ppermute | solution.py:65
  264.2 42.1 %collective-permute-start.38 = (bf16[256,2048]{1,0:T(8,128)(2,1)S(1)}, bf16[256,2048]{1,0:T(8,128)(2,1)S(1)}, u32[]{:S(2)}, u32[]{:S(2)}) collective-permute-start(bf16[256,2048]{1,0:T(8,128)(2,1)S(1)} %get-tuple-element.692), channel_id=1, source_target_pairs={{0,8},{1,9},{2,10},{3,11},{4,12},{5,13},{6,14},{7,15},{8,0},{9,1},... | collective-permute-start | bytes 3145736 | tf_op jit(solution)/shard_map/ppermute | solution.py:65
  266.0 40.3 %collective-permute-start.39 = (bf16[512,1024]{1,0:T(8,128)(2,1)S(1)}, bf16[512,1024]{1,0:T(8,128)(2,1)S(1)}, u32[]{:S(2)}, u32[]{:S(2)}) collective-permute-start(bf16[512,1024]{1,0:T(8,128)(2,1)S(1)} %get-tuple-element.698), channel_id=1, source_target_pairs={{0,2},{1,3},{2,0},{3,1},{4,6},{5,7},{6,4},{7,5},{8,10},{9,11},{10,... | collective-permute-start | bytes 3145736 | tf_op jit(solution)/shard_map/ppermute | solution.py:65
  266.4 39.3 %collective-permute-start.35 = (bf16[384,1024]{1,0:T(8,128)(2,1)}, bf16[384,1024]{1,0:T(8,128)(2,1)S(1)}, u32[]{:S(2)}, u32[]{:S(2)}) collective-permute-start(bf16[384,1024]{1,0:T(8,128)(2,1)} %get-tuple-element.667), channel_id=1, source_target_pairs={{0,16},{1,17},{2,18},{3,19},{4,20},{5,21},{6,22},{7,23},{8,24},{9,... | collective-permute-start | bytes 2359304 | tf_op jit(solution)/shard_map/ppermute | solution.py:65
  268.7 37.0 %collective-permute-start.36 = (bf16[128,3072]{1,0:T(8,128)(2,1)}, bf16[128,3072]{1,0:T(8,128)(2,1)S(1)}, u32[]{:S(2)}, u32[]{:S(2)}) collective-permute-start(bf16[128,3072]{1,0:T(8,128)(2,1)} %get-tuple-element.670), channel_id=1, source_target_pairs={{0,4},{1,5},{2,6},{3,7},{4,0},{5,1},{6,2},{7,3},{8,12},{9,13},{10,... | collective-permute-start | bytes 2359304 | tf_op jit(solution)/shard_map/ppermute | solution.py:65
  270.3 35.5 %collective-permute-start.37 = (bf16[128,3072]{1,0:T(8,128)(2,1)}, bf16[128,3072]{1,0:T(8,128)(2,1)S(1)}, u32[]{:S(2)}, u32[]{:S(2)}) collective-permute-start(bf16[128,3072]{1,0:T(8,128)(2,1)} %get-tuple-element.688), channel_id=1, source_target_pairs={{0,4},{1,5},{2,6},{3,7},{4,0},{5,1},{6,2},{7,3},{8,12},{9,13},{10,... | collective-permute-start | bytes 2359304 | tf_op jit(solution)/shard_map/ppermute | solution.py:65
  311.3 38.1 %collective-permute-start.46 = (bf16[256,2176]{1,0:T(8,128)(2,1)S(1)}, bf16[256,2176]{1,0:T(8,128)(2,1)S(1)}, u32[]{:S(2)}, u32[]{:S(2)}) collective-permute-start(bf16[256,2176]{1,0:T(8,128)(2,1)S(1)} %get-tuple-element.819), channel_id=1, source_target_pairs={{0,2},{1,3},{2,0},{3,1},{4,6},{5,7},{6,4},{7,5},{8,10},{9,11},{10,... | collective-permute-start | bytes 3342344 | tf_op jit(solution)/shard_map/ppermute | solution.py:65
  311.7 22.2 %collective-permute-start.41 = (bf16[192,1024]{1,0:T(8,128)(2,1)S(1)}, bf16[192,1024]{1,0:T(8,128)(2,1)S(1)}, u32[]{:S(2)}, u32[]{:S(2)}) collective-permute-start(bf16[192,1024]{1,0:T(8,128)(2,1)S(1)} %get-tuple-element.771), channel_id=1, source_target_pairs={{0,8},{1,9},{2,10},{3,11},{4,12},{5,13},{6,14},{7,15},{8,0},{9,1},... | collective-permute-start | bytes 1179656 | tf_op jit(solution)/shard_map/ppermute | solution.py:65
  316.1 30.8 %collective-permute-start.44 = (bf16[128,2048]{1,0:T(8,128)(2,1)S(1)}, bf16[128,2048]{1,0:T(8,128)(2,1)S(1)}, u32[]{:S(2)}, u32[]{:S(2)}) collective-permute-start(bf16[128,2048]{1,0:T(8,128)(2,1)S(1)} %get-tuple-element.796), channel_id=1, source_target_pairs={{0,4},{1,5},{2,6},{3,7},{4,0},{5,1},{6,2},{7,3},{8,12},{9,13},{10,... | collective-permute-start | bytes 1572872 | tf_op jit(solution)/shard_map/ppermute | solution.py:65
  317.7 27.4 %collective-permute-start.42 = (bf16[64,3072]{1,0:T(8,128)(2,1)S(1)}, bf16[64,3072]{1,0:T(8,128)(2,1)S(1)}, u32[]{:S(2)}, u32[]{:S(2)}) collective-permute-start(bf16[64,3072]{1,0:T(8,128)(2,1)S(1)} %get-tuple-element.774), channel_id=1, source_target_pairs={{0,8},{1,9},{2,10},{3,11},{4,12},{5,13},{6,14},{7,15},{8,0},{9,1},... | collective-permute-start | bytes 1179656 | tf_op jit(solution)/shard_map/ppermute | solution.py:65
  317.7 27.4 %collective-permute-start.43 = (bf16[64,3072]{1,0:T(8,128)(2,1)S(1)}, bf16[64,3072]{1,0:T(8,128)(2,1)S(1)}, u32[]{:S(2)}, u32[]{:S(2)}) collective-permute-start(bf16[64,3072]{1,0:T(8,128)(2,1)S(1)} %get-tuple-element.778), channel_id=1, source_target_pairs={{0,16},{1,17},{2,18},{3,19},{4,20},{5,21},{6,22},{7,23},{8,24},{9,... | collective-permute-start | bytes 1179656 | tf_op jit(solution)/shard_map/ppermute | solution.py:65
  333.9 13.6 %collective-permute-start.45 = (bf16[256,1024]{1,0:T(8,128)(2,1)S(1)}, bf16[256,1024]{1,0:T(8,128)(2,1)S(1)}, u32[]{:S(2)}, u32[]{:S(2)}) collective-permute-start(bf16[256,1024]{1,0:T(8,128)(2,1)S(1)} %get-tuple-element.799), channel_id=1, source_target_pairs={{0,4},{1,5},{2,6},{3,7},{4,0},{5,1},{6,2},{7,3},{8,12},{9,13},{10,... | collective-permute-start | bytes 1572872 | tf_op jit(solution)/shard_map/ppermute | solution.py:65
  345.5 7.9 %collective-permute-start.47 = (bf16[96,1024]{1,0:T(8,128)(2,1)S(1)}, bf16[96,1024]{1,0:T(8,128)(2,1)S(1)}, u32[]{:S(2)}, u32[]{:S(2)}) collective-permute-start(bf16[96,1024]{1,0:T(8,128)(2,1)S(1)} %get-tuple-element.831), channel_id=1, source_target_pairs={{0,2},{1,3},{2,0},{3,1},{4,6},{5,7},{6,4},{7,5},{8,10},{9,11},{10,... | collective-permute-start | bytes 589832 | tf_op jit(solution)/shard_map/ppermute | solution.py:65
  346.9 9.0 %collective-permute-start.48 = (bf16[32,3072]{1,0:T(8,128)(2,1)S(1)}, bf16[32,3072]{1,0:T(8,128)(2,1)S(1)}, u32[]{:S(2)}, u32[]{:S(2)}) collective-permute-start(bf16[32,3072]{1,0:T(8,128)(2,1)S(1)} %get-tuple-element.834), channel_id=1, source_target_pairs={{0,16},{1,17},{2,18},{3,19},{4,20},{5,21},{6,22},{7,23},{8,24},{9,... | collective-permute-start | bytes 589832 | tf_op jit(solution)/shard_map/ppermute | solution.py:65
  346.9 10.7 %collective-permute-start.49 = (bf16[32,3072]{1,0:T(8,128)(2,1)S(1)}, bf16[32,3072]{1,0:T(8,128)(2,1)S(1)}, u32[]{:S(2)}, u32[]{:S(2)}) collective-permute-start(bf16[32,3072]{1,0:T(8,128)(2,1)S(1)} %get-tuple-element.838), channel_id=1, source_target_pairs={{0,2},{1,3},{2,0},{3,1},{4,6},{5,7},{6,4},{7,5},{8,10},{9,11},{10,... | collective-permute-start | bytes 589832 | tf_op jit(solution)/shard_map/ppermute | solution.py:65
  347.9 12.6 %collective-permute-start.50 = (bf16[64,2048]{1,0:T(8,128)(2,1)S(1)}, bf16[64,2048]{1,0:T(8,128)(2,1)S(1)}, u32[]{:S(2)}, u32[]{:S(2)}) collective-permute-start(bf16[64,2048]{1,0:T(8,128)(2,1)S(1)} %get-tuple-element.842), channel_id=1, source_target_pairs={{0,2},{1,3},{2,0},{3,1},{4,6},{5,7},{6,4},{7,5},{8,10},{9,11},{10,... | collective-permute-start | bytes 786440 | tf_op jit(solution)/shard_map/ppermute | solution.py:65
  349.3 11.1 %collective-permute-start.51 = (bf16[128,1024]{1,0:T(8,128)(2,1)S(1)}, bf16[128,1024]{1,0:T(8,128)(2,1)S(1)}, u32[]{:S(2)}, u32[]{:S(2)}) collective-permute-start(bf16[128,1024]{1,0:T(8,128)(2,1)S(1)} %get-tuple-element.846), channel_id=1, source_target_pairs={{0,8},{1,9},{2,10},{3,11},{4,12},{5,13},{6,14},{7,15},{8,0},{9,1},... | collective-permute-start | bytes 786440 | tf_op jit(solution)/shard_map/ppermute | solution.py:65
  357.6 11.8 %collective-permute-start.52 = (bf16[128,2176]{1,0:T(8,128)(2,1)S(1)}, bf16[128,2176]{1,0:T(8,128)(2,1)S(1)}, u32[]{:S(2)}, u32[]{:S(2)}) collective-permute-start(bf16[128,2176]{1,0:T(8,128)(2,1)S(1)} %get-tuple-element.848), channel_id=1, source_target_pairs={{0,4},{1,5},{2,6},{3,7},{4,0},{5,1},{6,2},{7,3},{8,12},{9,13},{10,... | collective-permute-start | bytes 1671176 | tf_op jit(solution)/shard_map/ppermute | solution.py:65
  369.7 14.8 %collective-permute-start.55 = (bf16[64,2176]{1,0:T(8,128)(2,1)S(1)}, bf16[64,2176]{1,0:T(8,128)(2,1)S(1)}, u32[]{:S(2)}, u32[]{:S(2)}) collective-permute-start(bf16[64,2176]{1,0:T(8,128)(2,1)S(1)} %get-tuple-element.874), channel_id=1, source_target_pairs={{0,8},{1,9},{2,10},{3,11},{4,12},{5,13},{6,14},{7,15},{8,0},{9,1},... | collective-permute-start | bytes 835592 | tf_op jit(solution)/shard_map/ppermute | solution.py:65
  369.8 8.4 %collective-permute-start.53 = (bf16[32,2048]{1,0:T(8,128)(2,1)S(1)}, bf16[32,2048]{1,0:T(8,128)(2,1)S(1)}, u32[]{:S(2)}, u32[]{:S(2)}) collective-permute-start(bf16[32,2048]{1,0:T(8,128)(2,1)S(1)} %get-tuple-element.867), channel_id=1, source_target_pairs={{0,16},{1,17},{2,18},{3,19},{4,20},{5,21},{6,22},{7,23},{8,24},{9,... | collective-permute-start | bytes 393224 | tf_op jit(solution)/shard_map/ppermute | solution.py:65
  372.3 12.2 %collective-permute-start.54 = (bf16[64,1024]{1,0:T(8,128)(2,1)S(1)}, bf16[64,1024]{1,0:T(8,128)(2,1)S(1)}, u32[]{:S(2)}, u32[]{:S(2)}) collective-permute-start(bf16[64,1024]{1,0:T(8,128)(2,1)S(1)} %get-tuple-element.869), channel_id=1, source_target_pairs={{0,16},{1,17},{2,18},{3,19},{4,20},{5,21},{6,22},{7,23},{8,24},{9,... | collective-permute-start | bytes 393224 | tf_op jit(solution)/shard_map/ppermute | solution.py:65
  385.2 6.6 %collective-permute-start.56 = (bf16[32,2176]{1,0:T(8,128)(2,1)S(1)}, bf16[32,2176]{1,0:T(8,128)(2,1)S(1)}, u32[]{:S(2)}, u32[]{:S(2)}) collective-permute-start(bf16[32,2176]{1,0:T(8,128)(2,1)S(1)} %get-tuple-element.878), channel_id=1, source_target_pairs={{0,16},{1,17},{2,18},{3,19},{4,20},{5,21},{6,22},{7,23},{8,24},{9,... | collective-permute-start | bytes 417800 | tf_op jit(solution)/shard_map/ppermute | solution.py:65
  (46 other events, 629.7 us)
Sparse Core Ops, SparseCore 0:
  11.0 160.5 all-gather.2

commit v6 on v5

--- a/solution.py
+++ b/solution.py
@@ -130,43 +130,53 @@
     )(device.reshape(1), *values)
 
 
-def fold_body(*refs):
-    pairs = len(refs) // 6
-
+def fold_body(*refs, pairs, merged):
     def add(first, second):
         return (first[...].astype(jnp.float32) + second[...].astype(jnp.float32)).astype(jnp.bfloat16)
 
+    out_refs = refs[4 * pairs :]
+    start = 0
     for index in range(pairs):
         kept_first, kept_second, came_first, came_second = refs[4 * index : 4 * index + 4]
-        kept_ref, sent_ref = refs[4 * pairs + 2 * index : 4 * pairs + 2 * index + 2]
-        sent_ref[...] = add(kept_second, came_second)
-        kept_ref[...] = add(kept_first, came_first)
-
-
-def fold(*pairs):
-    halves = [kept.shape[0] // 2 for kept, _ in pairs]
+        sent = add(kept_second, came_second)
+        if merged:
+            out_refs[pairs][:, start : start + sent.shape[1]] = sent
+            start += sent.shape[1]
+        else:
+            out_refs[pairs + index][...] = sent
+        out_refs[index][...] = add(kept_first, came_first)
+
+
+def fold(*pairs, merged=False):
+    halves = [kept.shape[0] // 2 for kept, *_ in pairs]
     steps = next(n for n in (4, 2, 1) if n == 1 or all(rows % (16 * n) == 0 for rows in halves))
     in_specs, out_specs, out_shape, operands = [], [], [], []
-    for rows, (kept, came) in zip(halves, pairs):
+    for rows, (kept, came, place) in zip(halves, pairs):
         columns = kept.shape[1]
-        first = pl.BlockSpec((rows // steps, columns), lambda i: (i, 0))
-        second = pl.BlockSpec((rows // steps, columns), lambda i: (i + steps, 0))
-        in_specs += [first, second, first, second]
+        spec = lambda shift, place=0, rows=rows, columns=columns: pl.BlockSpec(
+            (rows // steps, columns), lambda i: (i + shift, place)
+        )
+        in_specs += [spec(0), spec(steps), spec(0, place), spec(steps, place)]
         operands += [kept, kept, came, came]
-        out_specs += [first, first]
-        out_shape += [jax.ShapeDtypeStruct((rows, columns), jnp.bfloat16)] * 2
-    block_bytes = sum(6 * 2 * (rows // steps) * kept.shape[1] for rows, (kept, _) in zip(halves, pairs))
-    out = pl.pallas_call(
-        fold_body,
+        out_specs += [spec(0)]
+        out_shape += [jax.ShapeDtypeStruct((rows, columns), jnp.bfloat16)]
+    if merged:
+        columns = sum(kept.shape[1] for kept, *_ in pairs)
+        sent_specs = [pl.BlockSpec((halves[0] // steps, columns), lambda i: (i, 0))]
+        sent_shape = [jax.ShapeDtypeStruct((halves[0], columns), jnp.bfloat16)]
+    else:
+        sent_specs, sent_shape = list(out_specs), list(out_shape)
+    block_bytes = sum(6 * 2 * (rows // steps) * kept.shape[1] for rows, (kept, *_) in zip(halves, pairs))
+    return pl.pallas_call(
+        functools.partial(fold_body, pairs=len(pairs), merged=merged),
         grid=(steps,),
         in_specs=in_specs,
-        out_specs=out_specs,
-        out_shape=out_shape,
+        out_specs=out_specs + sent_specs,
+        out_shape=out_shape + sent_shape,
         compiler_params=pltpu.CompilerParams(vmem_limit_bytes=2 * block_bytes + 6 * 1024 * 1024),
         cost_estimate=SMALL,
         name="fold",
     )(*operands)
-    return [out[2 * index : 2 * index + 2] for index in range(len(pairs))]
 
 
 def sum_end(pair):
@@ -213,6 +223,30 @@
 
 def gather_top_rest(blocks, count):
     return [block[None] for block in blocks + [exchange(blocks[2], count, count // 4)]]
+
+
+def stack_body(gate_ref, up_ref, down_ref, out_ref):
+    rows = gate_ref.shape[0]
+    width = down_ref.shape[1]
+    out_ref[:rows, :] = gate_ref[...]
+    out_ref[rows : 2 * rows, :] = up_ref[...]
+    for piece in range(down_ref.shape[0] // rows):
+        columns = slice(piece * width, (piece + 1) * width)
+        out_ref[2 * rows :, columns] = down_ref[piece * rows : (piece + 1) * rows, :]
+
+
+def stack(w_gate, w_up, w_down):
+    rows, columns = w_gate.shape
+    pieces = w_down.shape[0] // rows
+    if rows % 16:
+        down = w_down.reshape(pieces, rows, -1).transpose(1, 0, 2).reshape(rows, -1)
+        return jnp.concatenate([w_gate, w_up, down], axis=0)
+    return pl.pallas_call(
+        stack_body,
+        out_shape=jax.ShapeDtypeStruct((3 * rows, columns), w_gate.dtype),
+        cost_estimate=SMALL,
+        name="stack",
+    )(w_gate, w_up, w_down)
 
 
 def join_body(query_ref, key_ref, value_ref, gains_ref, out_ref):
@@ -439,9 +473,10 @@
     if last:
         head_gains_in_ref, normed_in_ref = refs[:2]
         refs = refs[2:]
-        tokens_ref, gain_ref, grad_residual_ref, gain_two_ref, kept_ref, sent_ref, tokens_out_ref = refs[:7]
-        head_gains_ref, normed_sum_ref, lines_ref = refs[7:10]
-        scratch = refs[10:]
+        tokens_ref, gain_ref, grad_residual_ref, gain_two_ref, hidden_ref, down_ref, ffn_in_ref = refs[:7]
+        kept_ref, sent_ref, tokens_out_ref, mixed_ref = refs[7:11]
+        head_gains_ref, normed_sum_ref, lines_ref, mixed_sum_ref, down_weight_ref = refs[11:16]
+        scratch = refs[16:]
     else:
         kept_ref, sent_ref, head_gains_ref, normed_sum_ref = refs[:4]
         scratch = refs[4:]
@@ -455,6 +490,19 @@
     def _():
         head_gains_ref[...] = head_gains_in_ref[...] if last else jnp.zeros_like(head_gains_ref)
         normed_sum_ref[...] = normed_in_ref[...] if last else jnp.zeros_like(normed_sum_ref)
+
+    if last:
+        gather_down(down_ref, down_weight_ref, down_weight_ref.shape[1])
+
+        @pl.when(head == 0)
+        def _():
+            mixed_sum_ref[...] = ffn_in_ref[...]
+
+        mixed_sum_ref[...] += jnp.dot(hidden_ref[...], down_weight_ref[...], preferred_element_type=jnp.float32)
+
+        @pl.when(head == heads - 1)
+        def _():
+            mixed_ref[...] = mixed_sum_ref[...].astype(jnp.bfloat16)
 
     grad_out_ref[...] = contract(residual_ref[...], wo_ref[...], 1, 1).astype(jnp.bfloat16)
     key_sum_ref[...] = jnp.zeros_like(key_sum_ref)
@@ -578,12 +626,17 @@
 
 
 def attend_back_last(
-    device, residual_low, operands, parts, sums, tokens, gain, grad_residual, grad_gain_two, order, shard, head_shard
+    device, residual_low, operands, parts, sums, tokens, gain, grad_residual, grad_gain_two, ffn_in, hidden, weights,
+    order, shard, head_shard,
 ):
     rows, width = residual_low.shape
     whole = lambda *shape: pl.BlockSpec(shape, lambda *j: (0, 0))
     own_width = KEY_VALUE_HEADS * 2 * HEAD_SIZE + 128
     half = jax.ShapeDtypeStruct((width // 2, own_width), jnp.bfloat16)
+    low = jax.ShapeDtypeStruct((rows, width), jnp.bfloat16)
+    tiles = KEY_VALUE_HEADS // 2
+    tile = weights.shape[2] // tiles
+    weight_args, weight_specs = ffn_operands(weights, shard, width, tiles, lambda h, d: h)
     return pl.pallas_call(
         functools.partial(
             attend_back_body, order=order, shard=shard, head_shard=head_shard, last=True, parts=len(parts)
@@ -594,22 +647,27 @@
             in_specs=[whole(rows, width)]
             + attend_back_specs(rows, width, 1, lambda h, d: h, parts)
             + [whole(2, HEAD_SIZE), whole(rows, width)]
-            + [whole(rows, width), whole(1, width), whole(rows, width), whole(1, width)],
-            out_specs=[whole(width // 2, own_width), whole(width // 2, own_width), whole(rows, width)],
+            + [whole(rows, width), whole(1, width), whole(rows, width), whole(1, width)]
+            + [pl.BlockSpec((rows, tile), lambda h, d: (0, h)), weight_specs[2], whole(rows, width)],
+            out_specs=[
+                whole(width // 2, own_width), whole(width // 2, own_width), whole(rows, width), whole(rows, width)
+            ],
             scratch_shapes=[
                 pltpu.VMEM((2, HEAD_SIZE), jnp.float32),
                 pltpu.VMEM((rows, width), jnp.float32),
                 pltpu.VMEM((width, 128), jnp.float32),
+                pltpu.VMEM((rows, width), jnp.float32),
+                pltpu.VMEM((tile, width), jnp.bfloat16),
             ]
             + attend_back_scratch(rows, parts),
         ),
-        out_shape=[half, half, jax.ShapeDtypeStruct((rows, width), jnp.bfloat16)],
-        compiler_params=pltpu.CompilerParams(vmem_limit_bytes=38 * 1024 * 1024),
+        out_shape=[half, half, low, low],
+        compiler_params=pltpu.CompilerParams(vmem_limit_bytes=46 * 1024 * 1024),
         cost_estimate=SMALL,
         name="attend_back_last",
     )(
         device.reshape(1), residual_low, *operands, *parts, sums[0], *from_far(sums[1], tokens), gain, *from_far(grad_residual),
-        grad_gain_two,
+        grad_gain_two, *from_far(hidden, weight_args[2], ffn_in),
     )
 
 
@@ -900,38 +958,6 @@
     )
 
 
-def ffn_out_body(residual_ref, hidden_ref, down_ref, mixed_ref, sum_ref, down_weight_ref):
-    @pl.when(pl.program_id(0) == 0)
-    def _():
-        sum_ref[...] = residual_ref[...]
-
-    gather_down(down_ref, down_weight_ref, residual_ref.shape[1])
-    sum_ref[...] += jnp.dot(hidden_ref[...], down_weight_ref[...], preferred_element_type=jnp.float32)
-
-    @pl.when(pl.program_id(0) == pl.num_programs(0) - 1)
-    def _():
-        mixed_ref[...] = sum_ref[...].astype(jnp.bfloat16)
-
-
-def ffn_out(residual, hidden, weights, shard):
-    rows, width = residual.shape
-    tiles = 8
-    tile = weights.shape[2] // tiles
-    whole = pl.BlockSpec((rows, width), lambda j: (0, 0))
-    weight_args, weight_specs = ffn_operands(weights, shard, width, tiles, lambda j: j)
-    return pl.pallas_call(
-        ffn_out_body,
-        grid=(tiles,),
-        in_specs=[whole, pl.BlockSpec((rows, tile), lambda j: (0, j)), weight_specs[2]],
-        out_specs=whole,
-        out_shape=jax.ShapeDtypeStruct((rows, width), jnp.bfloat16),
-        scratch_shapes=[pltpu.VMEM((rows, width), jnp.float32), pltpu.VMEM((tile, width), jnp.bfloat16)],
-        compiler_params=pltpu.CompilerParams(vmem_limit_bytes=16 * 1024 * 1024),
-        cost_estimate=SMALL,
-        name="ffn_out",
-    )(*from_far(residual, hidden, weight_args[2]))
-
-
 def end_body(first_kept, first_came, second_kept, second_came, query_ref, key_ref, value_ref, *gain_refs):
     def part(kept, came, start, size):
         columns = slice(start, start + size)
@@ -993,9 +1019,7 @@
     shard = g_attn.shape[0]
     head_shard = query_norm_gain.shape[0]
 
-    pieces = w_down.shape[0] // shard
-    down_pieces = w_down.reshape(pieces, shard, -1).transpose(1, 0, 2).reshape(shard, -1)
-    ffn_weights = lax.all_gather(jnp.concatenate([w_gate, w_up, down_pieces], axis=0), "fsdp", axis=0, tiled=False)
+    ffn_weights = lax.all_gather(stack(w_gate, w_up, w_down), "fsdp", axis=0, tiled=False)
     projections = join(
         w_query, key_projection, value_projection, gain_columns(g_attn, g_ffn, query_norm_gain, g_key, shard)
     )
@@ -1066,19 +1090,12 @@
     def land(*names):
         live.update({name + "_came": flying.pop(name) for name in names})
         cut()
-
-    def halve(*names):
-        halves = fold(*[(live[name], live.pop(name + "_came")) for name in names])
-        live.update({name: kept for name, (kept, _) in zip(names, halves)})
-        fly(**{name: sent for name, (_, sent) in zip(names, halves)})
-
-    def pass_on(*names):
-        land(*names)
-        halve(*names)
-
-    def end(*names):
-        land(*names)
-        return [(live.pop(name), live.pop(name + "_came")) for name in names]
+        flying.update({name: live.pop(name + "_came") for name in names})
+
+    def relay(*names, places=(0, 0, 0, 0, 0, 0)):
+        for name, place in zip(names, places):
+            live[name], sent = fold((live[name], flying[name], place))
+            flying[name] = exchange(sent, count, 1 << stages[name].pop(0))
 
     def operands(name, saved):
         return *from_far(out_weight, *saved), head_gains, cosine, sine, first_row, *from_far(turned[name])
@@ -1090,9 +1107,9 @@
         first=turn((live["normed"],), device, orders["first"]),
         second=turn((live.pop("normed"),), device, orders["second"]),
     )
-    pass_on("down")
-    pass_on("gate")
-    pass_on("up")
+    cut()
+    relay("down", "gate", "up")
+    cut()
     turned = live.pop("turned")
     (
         live["grad_residual"], live["low"], live["grad_gain_two"], live["out"], live["out_sent"], live["first"],
@@ -1103,36 +1120,40 @@
     )
     land("down", "gate", "up")
     fly(first=live["first_sent"], out=live["out_sent"])
-    halve("down", "gate", "up")
-    pass_on("first", "out")
-    live["second"], live["second_sent"], live["grad_tokens"] = attend_back_last(
-        device, live.pop("low"), operands("second", saved_second), second_weight, (live.pop("head_sums"), live.pop("normed_sum")), tokens,
-        gain_one[None], live.pop("grad_residual"), live.pop("grad_gain_two"), orders["second"], shard, head_shard,
-    )
-    land("down", "gate", "up")
+    relay("down")
+    live["gate"], live["up"], sent = fold(
+        (live["gate"], flying["gate"], 0), (live["up"], flying["up"], 0), merged=True
+    )
+    stages["gate"].pop(0)
+    flying["both"] = exchange(sent, count, 1 << stages["up"].pop(0))
+    relay("first", "out")
+    cut()
+    live["second"], live["second_sent"], live["grad_tokens"], live["mixed"] = attend_back_last(
+        device, live.pop("low"), operands("second", saved_second), second_weight,
+        (live.pop("head_sums"), live.pop("normed_sum")), tokens, gain_one[None], live.pop("grad_residual"),
+        live.pop("grad_gain_two"), residual, live.pop("hidden"), ffn_weights, orders["second"], shard, head_shard,
+    )
+    land("down", "both")
     land("first", "out")
     fly(second=live["second_sent"])
-    halve("down", "gate", "up")
-    pass_on("second")
-    halve("first", "out")
-    live["mixed"] = ffn_out(residual, live.pop("hidden"), ffn_weights, shard)
+    relay("second")
+    both = flying.pop("both")
+    flying.update(gate=both, up=both)
+    mixed, grad_tokens = live.pop("mixed"), live.pop("grad_tokens")
+    relay("down", "gate", "up", places=(0, 0, 1))
+    relay("first", "out")
+    relay("down", "gate", "up")
+    relay("second")
     cut()
-    mixed, grad_tokens = live.pop("mixed"), live.pop("grad_tokens")
-    while stages["down"]:
-        pass_on("down", "gate", "up")
-        pass_on("first", "out")
-        pass_on("second")
-    sums = {name: sum_end(pair) for name, pair in zip(("down", "gate", "up"), end("down", "gate", "up"))}
-    live.update(sums)
-    while stages["out"]:
-        pass_on("first", "out", "second")
-    sum_down, sum_gate, sum_up = live.pop("down"), live.pop("gate"), live.pop("up")
-    first, out = end("first", "out")
-    pass_on_last = stages["second"]
-    while pass_on_last:
-        pass_on("second")
-    (second,) = end("second")
-    sum_out = sum_end(out)
+    relay("first", "out", "second")
+    cut()
+    while any(stages.values()):
+        for name in ("second", "first", "out", "down", "gate", "up"):
+            if stages[name]:
+                relay(name)
+    pairs = {name: (live.pop(name), flying.pop(name)) for name in stages}
+    sum_down, sum_gate, sum_up, sum_out = (sum_end(pairs[name]) for name in ("down", "gate", "up", "out"))
+    first, second = pairs["first"], pairs["second"]
     sum_query, sum_key, sum_value, *sum_gains = end_projections(first, second, head_shard)
     return (
         mixed,

time: 402 us -> 390 us (0.970)
  waiting for transfers between devices: 159 us -> 142 us
  starting transfers between devices: 56 us -> 64 us
    ppermute x57 -> x56, waiting for transfers between devices: 159 us -> 142 us  [exchange(): lax.ppermute(values, 'fsdp', [(source, source ^ mask) for source in range...]
    ppermute x57 -> x56, starting transfers between devices: 56 us -> 64 us  [exchange(): lax.ppermute(values, 'fsdp', [(source, source ^ mask) for source in range...]
    pallas_call x1, Pallas kernels: 20 us -> 26.3 us  [attend_back_last(): pl.pallas_call(functools.partial(attend_back_body, order=order, shard=sha...]
    pallas_call x14 -> x24, Pallas kernels: 21.8 us -> 16 us  [the longest x23 14 us: fold(): pl.pallas_call(functools.partial(fold_body, pairs=len(pairs), merged=merg...]
    unnamed x76 -> x79, local copies, waits for them, and re-layouts: 9.55 us -> 8.58 us
  transfers between devices with their start and end apart: 58 -> 57, of which waited for: 32 -> 32; matrix products, arithmetic and copies ran while one was open for 4% -> 5% of each run, Pallas kernels for 28% -> 29%
where the time goes in v6:
time: 390 us; the launch traced here: 389 us
  Pallas kernels  144 us (37%)
  waiting for transfers between devices  142 us (36%)
  starting transfers between devices  64 us (16%)
  local copies, waits for them, and re-layouts  15.2 us (4%)
  between operations  14.7 us (4%)
  other arithmetic  8.94 us (2%)
    ppermute x56, waiting for transfers between devices, exchange(): lax.ppermute(values, 'fsdp', [(source, source ^ mask) for source in range...  142 us
    ppermute x56, starting transfers between devices, exchange(): lax.ppermute(values, 'fsdp', [(source, source ^ mask) for source in range...  64 us
    pallas_call x1, Pallas kernels, back(): pl.pallas_call(functools.partial(back_body, parts=len(parts)), grid_spec=...  33.9 us
    pallas_call x1, Pallas kernels, feed_forward(): pl.pallas_call(functools.partial(feed_forward_body, gate_order=gate_order...  27.1 us
    pallas_call x1, Pallas kernels, attend_back_last(): pl.pallas_call(functools.partial(attend_back_body, order=order, shard=sha...  26.3 us
    pallas_call x2, Pallas kernels, attend(): pl.pallas_call(attend_body, grid_spec=pltpu.PrefetchScalarGridSpec(num_sc...  21.9 us
    pallas_call x23, Pallas kernels, fold(): pl.pallas_call(functools.partial(fold_body, pairs=len(pairs), merged=merg...  14 us
    unnamed x79, local copies, waits for them, and re-layouts  8.58 us
  transfers between devices with their start and end apart: 57, of which 32 were waited for; matrix products, arithmetic and copies ran while one was open for 5% of the time, Pallas kernels for 29%

profile of v6, /device:TPU:0, one launch (start us, length us, event | category | flops | bytes accessed | tf_op | source)
XLA Modules:
  0.0 388.7 jit_solution(6131631123547524285)
XLA Ops:
  7.3 2.0 stack.1
  11.8 3.0 collective-permute-start
  14.9 2.6 collective-permute-start.1
  17.5 12.3 %collective-permute-done = bf16[32,4224]{1,0:T(8,128)(2,1)S(1)} collective-permute-done((bf16[32,4224]{1,0:T(8,128)(2,1)}, bf16[32,4224]{1,0:T(8,128)(2,1)S(1)}, u32[]{:S(2)}, u32[]{:S(2)}) %collective-permute-start) | collective-permute-done | bytes 270368 | tf_op jit(solution)/shard_map/ppermute | solution.py:65
  31.4 2.9 collective-permute-start.2
  34.4 12.0 %collective-permute-done.2 = bf16[32,4224]{1,0:T(8,128)(2,1)S(1)} collective-permute-done((bf16[32,4224]{1,0:T(8,128)(2,1)S(1)}, bf16[32,4224]{1,0:T(8,128)(2,1)S(1)}, u32[]{:S(2)}, u32[]{:S(2)}) %collective-permute-start.2) | collective-permute-done | bytes 270368 | tf_op jit(solution)/shard_map/ppermute | solution.py:65
  47.0 2.2 lay_top_split.1
  53.5 2.5 collective-permute-start.6
  56.1 8.5 %collective-permute-done.5 = bf16[64,1024]{1,0:T(8,128)(2,1)S(1)} collective-permute-done((bf16[64,1024]{1,0:T(8,128)(2,1)S(1)}, bf16[64,1024]{1,0:T(8,128)(2,1)S(1)}, u32[]{:S(2)}, u32[]{:S(2)}) %collective-permute-start.5) | collective-permute-done | bytes 131104 | tf_op jit(solution)/shard_map/ppermute | solution.py:65
  64.6 4.4 %collective-permute-done.6 = bf16[64,1024]{1,0:T(8,128)(2,1)S(1)} collective-permute-done((bf16[64,1024]{1,0:T(8,128)(2,1)S(1)}, bf16[64,1024]{1,0:T(8,128)(2,1)S(1)}, u32[]{:S(2)}, u32[]{:S(2)}) %collective-permute-start.6) | collective-permute-done | bytes 131104 | tf_op jit(solution)/shard_map/ppermute | solution.py:65
  69.0 3.1 collective-permute-done.4.refs_4_
  72.1 1.9 collective-permute-done.3.refs_2_.refs_21_
  76.0 2.5 collective-permute-start.10
  81.1 2.8 collective-permute-done.11
  83.9 8.8 %collective-permute-done.10.refs_6_ = bf16[4,32,2048]{2,1,0:T(8,128)(2,1)} collective-permute-done((bf16[4,32,2048]{2,1,0:T(8,128)(2,1)}, bf16[4,32,2048]{2,1,0:T(8,128)(2,1)}, u32[]{:S(2)}, u32[]{:S(2)}) %collective-permute-start.10) | collective-permute-done | bytes 524320 | tf_op jit(solution)/shard_map/ppermute | solution.py:65
  92.7 10.5 %collective-permute-done.9.refs_2_ = bf16[4,32,2048]{2,1,0:T(8,128)(2,1)} collective-permute-done((bf16[4,32,2048]{2,1,0:T(8,128)(2,1)}, bf16[4,32,2048]{2,1,0:T(8,128)(2,1)}, u32[]{:S(2)}, u32[]{:S(2)}) %collective-permute-start.9) | collective-permute-done | bytes 524320 | tf_op jit(solution)/shard_map/ppermute | solution.py:65
  105.8 1.9 place.3
  107.8 2.5 collective-permute-start.20
  122.0 11.0 %attend.2 = (bf16[384,1024]{1,0:T(8,128)(2,1)S(1)}, bf16[384,1024]{1,0:T(8,128)(2,1)}, bf16[384,512]{1,0:T(8,128)(2,1)}, bf16[384,512]{1,0:T(8,128)(2,1)}, f32[384,1536]{1,0:T(8,128)}, /*index=5*/f32[4,384,2]{2,1,0:T(8,128)}) custom-call(s32[1]{0:T(128)} %bitcast.device_ref, bf16[4,32,2176]{2,1,0:T(8,128)(2,1)S(1)} %get-tuple-element.301.refs_0_.refs_19_, ...), custom_call_target="tpu_custom_call" | custom-call | flops 1 | bytes 1 | tf_op jit(solution)/shard_map/attend/pallas_call | solution.py:430
  136.5 10.9 %attend.3 = (bf16[384,1024]{1,0:T(8,128)(2,1)S(1)}, bf16[384,1024]{1,0:T(8,128)(2,1)}, bf16[384,512]{1,0:T(8,128)(2,1)}, bf16[384,512]{1,0:T(8,128)(2,1)}, f32[384,1536]{1,0:T(8,128)}, /*index=5*/f32[4,384,2]{2,1,0:T(8,128)}) custom-call(s32[1]{0:T(128)} %bitcast.device_ref, bf16[4,32,2048]{2,1,0:T(8,128)(2,1)} %get-tuple-element.319.refs_0_, ...), custom_call_target="tpu_custom_call" | custom-call | flops 1 | bytes 1 | tf_op jit(solution)/shard_map/attend/pallas_call | solution.py:430
  149.7 9.7 %collective-permute-done.22.refs_6_ = bf16[4,64,1024]{2,1,0:T(8,128)(2,1)} collective-permute-done((bf16[4,64,1024]{2,1,0:T(8,128)(2,1)}, bf16[4,64,1024]{2,1,0:T(8,128)(2,1)}, u32[]{:S(2)}, u32[]{:S(2)}) %collective-permute-start.22) | collective-permute-done | bytes 524320 | tf_op jit(solution)/shard_map/ppermute | solution.py:65
  160.4 1.8 copy.53
  164.9 6.2 %project.1 = (f32[384,1024]{1,0:T(8,128)S(1)}, bf16[4,8,64,1024]{3,2,1,0:T(8,128)(2,1)}) custom-call(s32[1]{0:T(128)} %bitcast.device_ref, bf16[4,64,1024]{2,1,0:T(8,128)(2,1)} %bitcast.23.refs_0_, bf16[4,64,1024]{2,1,0:T(8,128)(2,1)} %collective-permute-done.23.refs_1_, bf16[4,64,1024]{2,1,0:T(8,128)(2,1)} %collective-permute-done.20.refs_2_, ...), custom_call_target="tpu_custom_call" | custom-call | flops 1 | bytes 1 | tf_op jit(solution)/shard_map/project/pallas_call | solution.py:694
  172.3 27.1 %feed_forward.1 = (bf16[384,3072]{1,0:T(8,128)(2,1)}, bf16[384,3072]{1,0:T(8,128)(2,1)}, bf16[384,3072]{1,0:T(8,128)(2,1)}, bf16[512,3072]{1,0:T(8,128)(2,1)}, b...) custom-call(s32[1]{0:T(128)} %bitcast.device_ref, ...), custom_call_target="tpu_custom_call" | custom-call | flops 1 | bytes 1 | tf_op jit(solution)/shard_map/feed_forward/pallas_call | solution.py:812
  205.3 1.9 fold.25
  207.4 2.4 collective-permute-done.28.refs_2_.refs_3_
  209.8 1.9 fold.24
  211.7 1.9 collective-permute-start.31
  214.3 1.9 fold.23
  216.8 33.9 %back.1 = (f32[384,1024]{1,0:T(8,128)}, bf16[384,1024]{1,0:T(8,128)(2,1)}, f32[1,1024]{1,0:T(1,128)S(1)}, bf16[1024,1024]{1,0:T(8,128)(2,1)}, bf16[1024,1024]{1,...) custom-call(s32[1]{0:T(128)} %bitcast.device_ref, ...), custom_call_target="tpu_custom_call" | custom-call | flops 1 | bytes 1 | tf_op jit(solution)/shard_map/back/pallas_call | solution.py:920
  250.8 2.3 collective-permute-done.30.refs_2_.refs_3_
  255.1 2.4 collective-permute-done.35.refs_2_.refs_3_
  263.8 2.9 collective-permute-start.36
  266.6 26.3 %attend_back_last.1 = (bf16[512,2176]{1,0:T(8,128)(2,1)S(1)}, bf16[512,2176]{1,0:T(8,128)(2,1)}, bf16[384,1024]{1,0:T(8,128)(2,1)}, bf16[384,1024]{1,0:T(8,128)(2,1)}) custom-call(s32[1]{0:T(128)} %bitcast.device_ref, bf16[384,1024]{1,0:T(8,128)(2,1)S(1)} %copy-done.19, bf16[2048,1024]{1,0:T(8,128)(2,1)} %bitcast.57, ...), custom_call_target="tpu_custom_call" | custom-call | flops 1 | bytes 1 | tf_op jit(solution)/shard_map/attend_back_last/pallas_call | solution.py:640
  293.0 9.3 %collective-permute-done.36.refs_2_.refs_3_ = bf16[384,1024]{1,0:T(8,128)(2,1)S(1)} collective-permute-done((bf16[384,1024]{1,0:T(8,128)(2,1)}, bf16[384,1024]{1,0:T(8,128)(2,1)S(1)}, u32[]{:S(2)}, u32[]{:S(2)}) %collective-permute-start.36) | collective-permute-done | bytes 786464 | tf_op jit(solution)/shard_map/ppermute | solution.py:65
  302.3 2.1 collective-permute-done.37.refs_2_.refs_3_
  304.4 4.6 %collective-permute-done.41.refs_2_.refs_3_ = bf16[512,2176]{1,0:T(8,128)(2,1)S(1)} collective-permute-done((bf16[512,2176]{1,0:T(8,128)(2,1)}, bf16[512,2176]{1,0:T(8,128)(2,1)S(1)}, u32[]{:S(2)}, u32[]{:S(2)}) %collective-permute-start.41) | collective-permute-done | bytes 2228256 | tf_op jit(solution)/shard_map/ppermute | solution.py:65
  316.2 2.1 collective-permute-start.40
  318.5 17.7 %collective-permute-done.42.refs_2_.refs_3_ = bf16[256,2176]{1,0:T(8,128)(2,1)S(1)} collective-permute-done((bf16[256,2176]{1,0:T(8,128)(2,1)S(1)}, bf16[256,2176]{1,0:T(8,128)(2,1)S(1)}, u32[]{:S(2)}, u32[]{:S(2)}) %collective-permute-start.42) | collective-permute-done | bytes 1114144 | tf_op jit(solution)/shard_map/ppermute | solution.py:65
  340.1 6.4 %collective-permute-done.39.refs_2_.refs_3_ = bf16[192,1024]{1,0:T(8,128)(2,1)S(1)} collective-permute-done((bf16[192,1024]{1,0:T(8,128)(2,1)S(1)}, bf16[192,1024]{1,0:T(8,128)(2,1)S(1)}, u32[]{:S(2)}, u32[]{:S(2)}) %collective-permute-start.39) | collective-permute-done | bytes 393248 | tf_op jit(solution)/shard_map/ppermute | solution.py:65
  348.8 1.8 collective-permute-start.47
  354.6 3.6 collective-permute-start.52
  359.2 2.3 collective-permute-done.54
  361.5 2.3 collective-permute-start.48
  364.6 2.1 collective-permute-done.53
  371.9 1.9 collective-permute-done.52
  374.5 3.3 collective-permute-done.48.first_came
  380.0 1.9 end_projections.1
  (217 shorter events, 81.4 us)
Async XLA Ops:
  7.3 165.0 %all-gather.3.cloned.1.call-start = ((), (), s32[]{:S(2)}) async-start(), calls=%async_computation | async-start | bytes 19464192 | tf_op jit(solution)/shard_map/all_gather | solution.py:1022
  11.8 18.0 %collective-permute-start = (bf16[32,4224]{1,0:T(8,128)(2,1)}, bf16[32,4224]{1,0:T(8,128)(2,1)S(1)}, u32[]{:S(2)}, u32[]{:S(2)}) collective-permute-start(bf16[32,4224]{1,0:T(8,128)(2,1)} %join.1), channel_id=1, source_target_pairs={{0,8},{1,9},{2,10},{3,11},{4,12},{5,13},{6,14},{7,15},{8,0},{9,1},... | collective-permute-start | bytes 811016 | tf_op jit(solution)/shard_map/ppermute | solution.py:65
  14.9 16.6 %collective-permute-start.1 = (bf16[32,4224]{1,0:T(8,128)(2,1)}, bf16[32,4224]{1,0:T(8,128)(2,1)S(1)}, u32[]{:S(2)}, u32[]{:S(2)}) collective-permute-start(bf16[32,4224]{1,0:T(8,128)(2,1)} %join.1), channel_id=1, source_target_pairs={{0,16},{1,17},{2,18},{3,19},{4,20},{5,21},{6,22},{7,23},{8,24},{9,... | collective-permute-start | bytes 811016 | tf_op jit(solution)/shard_map/ppermute | solution.py:65
  31.4 14.9 %collective-permute-start.2 = (bf16[32,4224]{1,0:T(8,128)(2,1)S(1)}, bf16[32,4224]{1,0:T(8,128)(2,1)S(1)}, u32[]{:S(2)}, u32[]{:S(2)}) collective-permute-start(bf16[32,4224]{1,0:T(8,128)(2,1)S(1)} %collective-permute-done.1), channel_id=1, source_target_pairs={{0,8},{1,9},{2,10},{3,11},{4,12},{5,13},{6,14},{7,15},{8,0},{9,1},... | collective-permute-start | bytes 811016 | tf_op jit(solution)/shard_map/ppermute | solution.py:65
  49.2 24.8 %collective-permute-start.3 = (bf16[4,32,2176]{2,1,0:T(8,128)(2,1)S(1)}, bf16[4,32,2176]{2,1,0:T(8,128)(2,1)S(1)}, u32[]{:S(2)}, u32[]{:S(2)}) collective-permute-start(bf16[4,32,2176]{2,1,0:T(8,128)(2,1)S(1)} %get-tuple-element.301.refs_0_.refs_19_), channel_id=1, source_target_pairs={{0,2},{1,3},{2,0},{3,1},{4,6},{5,7},{6,4},{7,5},{8,10},{9,11},{10,... | collective-permute-start | bytes 1671176 | tf_op jit(solution)/shard_map/ppermute | solution.py:65
  50.7 21.3 %collective-permute-start.4 = (bf16[4,32,2048]{2,1,0:T(8,128)(2,1)}, bf16[4,32,2048]{2,1,0:T(8,128)(2,1)}, u32[]{:S(2)}, u32[]{:S(2)}) collective-permute-start(bf16[4,32,2048]{2,1,0:T(8,128)(2,1)} %get-tuple-element.319.refs_0_), channel_id=1, source_target_pairs={{0,4},{1,5},{2,6},{3,7},{4,0},{5,1},{6,2},{7,3},{8,12},{9,13},{10,... | collective-permute-start | bytes 1572872 | tf_op jit(solution)/shard_map/ppermute | solution.py:65
  52.2 12.4 %collective-permute-start.5 = (bf16[64,1024]{1,0:T(8,128)(2,1)S(1)}, bf16[64,1024]{1,0:T(8,128)(2,1)S(1)}, u32[]{:S(2)}, u32[]{:S(2)}) collective-permute-start(bf16[64,1024]{1,0:T(8,128)(2,1)S(1)} %copy-done.28), channel_id=1, source_target_pairs={{0,8},{1,9},{2,10},{3,11},{4,12},{5,13},{6,14},{7,15},{8,0},{9,1},... | collective-permute-start | bytes 393224 | tf_op jit(solution)/shard_map/ppermute | solution.py:65
  53.5 15.4 %collective-permute-start.6 = (bf16[64,1024]{1,0:T(8,128)(2,1)S(1)}, bf16[64,1024]{1,0:T(8,128)(2,1)S(1)}, u32[]{:S(2)}, u32[]{:S(2)}) collective-permute-start(bf16[64,1024]{1,0:T(8,128)(2,1)S(1)} %copy-done.28), channel_id=1, source_target_pairs={{0,16},{1,17},{2,18},{3,19},{4,20},{5,21},{6,22},{7,23},{8,24},{9,... | collective-permute-start | bytes 393224 | tf_op jit(solution)/shard_map/ppermute | solution.py:65
  74.0 29.2 %collective-permute-start.7 = (bf16[4,32,2176]{2,1,0:T(8,128)(2,1)S(1)}, bf16[4,32,2176]{2,1,0:T(8,128)(2,1)S(1)}, u32[]{:S(2)}, u32[]{:S(2)}) collective-permute-start(bf16[4,32,2176]{2,1,0:T(8,128)(2,1)S(1)} %get-tuple-element.301.refs_0_.refs_19_), channel_id=1, source_target_pairs={{0,4},{1,5},{2,6},{3,7},{4,0},{5,1},{6,2},{7,3},{8,12},{9,13},{10,... | collective-permute-start | bytes 1671176 | tf_op jit(solution)/shard_map/ppermute | solution.py:65
  75.3 27.8 %collective-permute-start.8 = (bf16[4,32,2176]{2,1,0:T(8,128)(2,1)S(1)}, bf16[4,32,2176]{2,1,0:T(8,128)(2,1)}, u32[]{:S(2)}, u32[]{:S(2)}) collective-permute-start(bf16[4,32,2176]{2,1,0:T(8,128)(2,1)S(1)} %collective-permute-done.3.refs_2_.refs_21_), channel_id=1, source_target_pairs={{0,4},{1,5},{2,6},{3,7},{4,0},{5,1},{6,2},{7,3},{8,12},{9,13},{10,... | collective-permute-start | bytes 1671176 | tf_op jit(solution)/shard_map/ppermute | solution.py:65
  76.0 16.7 %collective-permute-start.10 = (bf16[4,32,2048]{2,1,0:T(8,128)(2,1)}, bf16[4,32,2048]{2,1,0:T(8,128)(2,1)}, u32[]{:S(2)}, u32[]{:S(2)}) collective-permute-start(bf16[4,32,2048]{2,1,0:T(8,128)(2,1)} %collective-permute-done.4.refs_4_), channel_id=1, source_target_pairs={{0,2},{1,3},{2,0},{3,1},{4,6},{5,7},{6,4},{7,5},{8,10},{9,11},{10,... | collective-permute-start | bytes 1572872 | tf_op jit(solution)/shard_map/ppermute | solution.py:65
  78.5 24.6 %collective-permute-start.9 = (bf16[4,32,2048]{2,1,0:T(8,128)(2,1)}, bf16[4,32,2048]{2,1,0:T(8,128)(2,1)}, u32[]{:S(2)}, u32[]{:S(2)}) collective-permute-start(bf16[4,32,2048]{2,1,0:T(8,128)(2,1)} %get-tuple-element.319.refs_0_), channel_id=1, source_target_pairs={{0,2},{1,3},{2,0},{3,1},{4,6},{5,7},{6,4},{7,5},{8,10},{9,11},{10,... | collective-permute-start | bytes 1572872 | tf_op jit(solution)/shard_map/ppermute | solution.py:65
  103.2 7.2 %collective-permute-start.12 = (bf16[4,32,2176]{2,1,0:T(8,128)(2,1)S(1)}, bf16[4,32,2176]{2,1,0:T(8,128)(2,1)}, u32[]{:S(2)}, u32[]{:S(2)}) collective-permute-start(bf16[4,32,2176]{2,1,0:T(8,128)(2,1)S(1)} %get-tuple-element.301.refs_0_.refs_19_), channel_id=1, source_target_pairs={{0,1},{1,0},{2,3},{3,2},{4,5},{5,4},{6,7},{7,6},{8,9},{9,8},{10,11... | collective-permute-start | bytes 1671176 | tf_op jit(solution)/shard_map/ppermute | solution.py:65
  103.2 7.1 %collective-permute-start.13 = (bf16[4,32,2176]{2,1,0:T(8,128)(2,1)S(1)}, bf16[4,32,2176]{2,1,0:T(8,128)(2,1)}, u32[]{:S(2)}, u32[]{:S(2)}) collective-permute-start(bf16[4,32,2176]{2,1,0:T(8,128)(2,1)S(1)} %collective-permute-done.3.refs_2_.refs_21_), channel_id=1, source_target_pairs={{0,1},{1,0},{2,3},{3,2},{4,5},{5,4},{6,7},{7,6},{8,9},{9,8},{10,11... | collective-permute-start | bytes 1671176 | tf_op jit(solution)/shard_map/ppermute | solution.py:65
  103.7 6.6 %collective-permute-start.14 = (bf16[4,32,2176]{2,1,0:T(8,128)(2,1)S(1)}, bf16[4,32,2176]{2,1,0:T(8,128)(2,1)}, u32[]{:S(2)}, u32[]{:S(2)}) collective-permute-start(bf16[4,32,2176]{2,1,0:T(8,128)(2,1)S(1)} %collective-permute-done.7.refs_4_.refs_23_), channel_id=1, source_target_pairs={{0,1},{1,0},{2,3},{3,2},{4,5},{5,4},{6,7},{7,6},{8,9},{9,8},{10,11... | collective-permute-start | bytes 1671176 | tf_op jit(solution)/shard_map/ppermute | solution.py:65
  107.8 26.6 %collective-permute-start.20 = (bf16[4,64,1024]{2,1,0:T(8,128)(2,1)}, bf16[4,64,1024]{2,1,0:T(8,128)(2,1)}, u32[]{:S(2)}, u32[]{:S(2)}) collective-permute-start(bf16[4,64,1024]{2,1,0:T(8,128)(2,1)} %bitcast.23.refs_0_), channel_id=1, source_target_pairs={{0,2},{1,3},{2,0},{3,1},{4,6},{5,7},{6,4},{7,5},{8,10},{9,11},{10,... | collective-permute-start | bytes 1572872 | tf_op jit(solution)/shard_map/ppermute | solution.py:65
  114.2 20.2 %collective-permute-start.16 = (bf16[4,32,2048]{2,1,0:T(8,128)(2,1)}, bf16[4,32,2048]{2,1,0:T(8,128)(2,1)}, u32[]{:S(2)}, u32[]{:S(2)}) collective-permute-start(bf16[4,32,2048]{2,1,0:T(8,128)(2,1)} %get-tuple-element.319.refs_0_), channel_id=1, source_target_pairs={{0,1},{1,0},{2,3},{3,2},{4,5},{5,4},{6,7},{7,6},{8,9},{9,8},{10,11... | collective-permute-start | bytes 1572872 | tf_op jit(solution)/shard_map/ppermute | solution.py:65
  114.2 20.2 %collective-permute-start.17 = (bf16[4,32,2048]{2,1,0:T(8,128)(2,1)}, bf16[4,32,2048]{2,1,0:T(8,128)(2,1)}, u32[]{:S(2)}, u32[]{:S(2)}) collective-permute-start(bf16[4,32,2048]{2,1,0:T(8,128)(2,1)} %collective-permute-done.9.refs_2_), channel_id=1, source_target_pairs={{0,1},{1,0},{2,3},{3,2},{4,5},{5,4},{6,7},{7,6},{8,9},{9,8},{10,11... | collective-permute-start | bytes 1572872 | tf_op jit(solution)/shard_map/ppermute | solution.py:65
  114.7 19.7 %collective-permute-start.18 = (bf16[4,32,2048]{2,1,0:T(8,128)(2,1)}, bf16[4,32,2048]{2,1,0:T(8,128)(2,1)}, u32[]{:S(2)}, u32[]{:S(2)}) collective-permute-start(bf16[4,32,2048]{2,1,0:T(8,128)(2,1)} %collective-permute-done.4.refs_4_), channel_id=1, source_target_pairs={{0,1},{1,0},{2,3},{3,2},{4,5},{5,4},{6,7},{7,6},{8,9},{9,8},{10,11... | collective-permute-start | bytes 1572872 | tf_op jit(solution)/shard_map/ppermute | solution.py:65
  114.7 19.7 %collective-permute-start.19 = (bf16[4,32,2048]{2,1,0:T(8,128)(2,1)}, bf16[4,32,2048]{2,1,0:T(8,128)(2,1)}, u32[]{:S(2)}, u32[]{:S(2)}) collective-permute-start(bf16[4,32,2048]{2,1,0:T(8,128)(2,1)} %collective-permute-done.10.refs_6_), channel_id=1, source_target_pairs={{0,1},{1,0},{2,3},{3,2},{4,5},{5,4},{6,7},{7,6},{8,9},{9,8},{10,11... | collective-permute-start | bytes 1572872 | tf_op jit(solution)/shard_map/ppermute | solution.py:65
  134.4 15.2 %collective-permute-start.21 = (bf16[4,64,1024]{2,1,0:T(8,128)(2,1)}, bf16[4,64,1024]{2,1,0:T(8,128)(2,1)}, u32[]{:S(2)}, u32[]{:S(2)}) collective-permute-start(bf16[4,64,1024]{2,1,0:T(8,128)(2,1)} %bitcast.23.refs_0_), channel_id=1, source_target_pairs={{0,4},{1,5},{2,6},{3,7},{4,0},{5,1},{6,2},{7,3},{8,12},{9,13},{10,... | collective-permute-start | bytes 1572872 | tf_op jit(solution)/shard_map/ppermute | solution.py:65
  135.4 24.0 %collective-permute-start.22 = (bf16[4,64,1024]{2,1,0:T(8,128)(2,1)}, bf16[4,64,1024]{2,1,0:T(8,128)(2,1)}, u32[]{:S(2)}, u32[]{:S(2)}) collective-permute-start(bf16[4,64,1024]{2,1,0:T(8,128)(2,1)} %collective-permute-done.20.refs_2_), channel_id=1, source_target_pairs={{0,4},{1,5},{2,6},{3,7},{4,0},{5,1},{6,2},{7,3},{8,12},{9,13},{10,... | collective-permute-start | bytes 1572872 | tf_op jit(solution)/shard_map/ppermute | solution.py:65
  199.8 10.1 %collective-permute-start.28 = (bf16[512,3072]{1,0:T(8,128)(2,1)}, bf16[512,3072]{1,0:T(8,128)(2,1)S(1)}, u32[]{:S(2)}, u32[]{:S(2)}) collective-permute-start(bf16[512,3072]{1,0:T(8,128)(2,1)} %get-tuple-element.359), channel_id=1, source_target_pairs={{0,1},{1,0},{2,3},{3,2},{4,5},{5,4},{6,7},{7,6},{8,9},{9,8},{10,11... | collective-permute-start | bytes 9437192 | tf_op jit(solution)/shard_map/ppermute | solution.py:65
  200.0 14.4 %collective-permute-start.27 = (bf16[1536,1024]{1,0:T(8,128)(2,1)}, bf16[1536,1024]{1,0:T(8,128)(2,1)S(1)}, u32[]{:S(2)}, u32[]{:S(2)}) collective-permute-start(bf16[1536,1024]{1,0:T(8,128)(2,1)} %bitcast.65), channel_id=1, source_target_pairs={{0,1},{1,0},{2,3},{3,2},{4,5},{5,4},{6,7},{7,6},{8,9},{9,8},{10,11... | collective-permute-start | bytes 9437192 | tf_op jit(solution)/shard_map/ppermute | solution.py:65
  207.3 43.5 %collective-permute-start.32 = (bf16[256,3072]{1,0:T(8,128)(2,1)}, bf16[256,3072]{1,0:T(8,128)(2,1)S(1)}, u32[]{:S(2)}, u32[]{:S(2)}) collective-permute-start(bf16[256,3072]{1,0:T(8,128)(2,1)} %get-tuple-element.395), channel_id=1, source_target_pairs={{0,8},{1,9},{2,10},{3,11},{4,12},{5,13},{6,14},{7,15},{8,0},{9,1},... | collective-permute-start | bytes 4718600 | tf_op jit(solution)/shard_map/ppermute | solution.py:65
  211.7 39.0 %collective-permute-start.31 = (bf16[256,3072]{1,0:T(8,128)(2,1)}, bf16[256,3072]{1,0:T(8,128)(2,1)S(1)}, u32[]{:S(2)}, u32[]{:S(2)}) collective-permute-start(bf16[256,3072]{1,0:T(8,128)(2,1)} %get-tuple-element.385), channel_id=1, source_target_pairs={{0,2},{1,3},{2,0},{3,1},{4,6},{5,7},{6,4},{7,5},{8,10},{9,11},{10,... | collective-permute-start | bytes 4718600 | tf_op jit(solution)/shard_map/ppermute | solution.py:65
  216.3 36.8 %collective-permute-start.30 = (bf16[768,1024]{1,0:T(8,128)(2,1)}, bf16[768,1024]{1,0:T(8,128)(2,1)S(1)}, u32[]{:S(2)}, u32[]{:S(2)}) collective-permute-start(bf16[768,1024]{1,0:T(8,128)(2,1)} %get-tuple-element.371), channel_id=1, source_target_pairs={{0,4},{1,5},{2,6},{3,7},{4,0},{5,1},{6,2},{7,3},{8,12},{9,13},{10,... | collective-permute-start | bytes 4718600 | tf_op jit(solution)/shard_map/ppermute | solution.py:65
  253.1 7.4 %collective-permute-start.34 = (bf16[512,2048]{1,0:T(8,128)(2,1)}, bf16[512,2048]{1,0:T(8,128)(2,1)S(1)}, u32[]{:S(2)}, u32[]{:S(2)}) collective-permute-start(bf16[512,2048]{1,0:T(8,128)(2,1)} %get-tuple-element.418), channel_id=1, source_target_pairs={{0,1},{1,0},{2,3},{3,2},{4,5},{5,4},{6,7},{7,6},{8,9},{9,8},{10,11... | collective-permute-start | bytes 6291464 | tf_op jit(solution)/shard_map/ppermute | solution.py:65
  254.4 47.9 %collective-permute-start.33 = (bf16[128,6144]{1,0:T(8,128)(2,1)S(1)}, bf16[128,6144]{1,0:T(8,128)(2,1)S(1)}, u32[]{:S(2)}, u32[]{:S(2)}) collective-permute-start(bf16[128,6144]{1,0:T(8,128)(2,1)S(1)} %get-tuple-element.413), channel_id=1, source_target_pairs={{0,4},{1,5},{2,6},{3,7},{4,0},{5,1},{6,2},{7,3},{8,12},{9,13},{10,... | collective-permute-start | bytes 4718600 | tf_op jit(solution)/shard_map/ppermute | solution.py:65
  258.0 44.3 %collective-permute-start.38 = (bf16[512,1024]{1,0:T(8,128)(2,1)S(1)}, bf16[512,1024]{1,0:T(8,128)(2,1)S(1)}, u32[]{:S(2)}, u32[]{:S(2)}) collective-permute-start(bf16[512,1024]{1,0:T(8,128)(2,1)S(1)} %get-tuple-element.460), channel_id=1, source_target_pairs={{0,2},{1,3},{2,0},{3,1},{4,6},{5,7},{6,4},{7,5},{8,10},{9,11},{10,... | collective-permute-start | bytes 3145736 | tf_op jit(solution)/shard_map/ppermute | solution.py:65
  262.1 42.3 %collective-permute-start.37 = (bf16[256,2048]{1,0:T(8,128)(2,1)}, bf16[256,2048]{1,0:T(8,128)(2,1)S(1)}, u32[]{:S(2)}, u32[]{:S(2)}) collective-permute-start(bf16[256,2048]{1,0:T(8,128)(2,1)} %get-tuple-element.455), channel_id=1, source_target_pairs={{0,8},{1,9},{2,10},{3,11},{4,12},{5,13},{6,14},{7,15},{8,0},{9,1},... | collective-permute-start | bytes 3145736 | tf_op jit(solution)/shard_map/ppermute | solution.py:65
  263.8 38.5 %collective-permute-start.36 = (bf16[384,1024]{1,0:T(8,128)(2,1)}, bf16[384,1024]{1,0:T(8,128)(2,1)S(1)}, u32[]{:S(2)}, u32[]{:S(2)}) collective-permute-start(bf16[384,1024]{1,0:T(8,128)(2,1)} %get-tuple-element.432), channel_id=1, source_target_pairs={{0,16},{1,17},{2,18},{3,19},{4,20},{5,21},{6,22},{7,23},{8,24},{9,... | collective-permute-start | bytes 2359304 | tf_op jit(solution)/shard_map/ppermute | solution.py:65
  309.5 26.7 %collective-permute-start.42 = (bf16[256,2176]{1,0:T(8,128)(2,1)S(1)}, bf16[256,2176]{1,0:T(8,128)(2,1)S(1)}, u32[]{:S(2)}, u32[]{:S(2)}) collective-permute-start(bf16[256,2176]{1,0:T(8,128)(2,1)S(1)} %get-tuple-element.494), channel_id=1, source_target_pairs={{0,2},{1,3},{2,0},{3,1},{4,6},{5,7},{6,4},{7,5},{8,10},{9,11},{10,... | collective-permute-start | bytes 3342344 | tf_op jit(solution)/shard_map/ppermute | solution.py:65
  311.7 26.5 %collective-permute-start.43 = (bf16[64,3072]{1,0:T(8,128)(2,1)S(1)}, bf16[64,3072]{1,0:T(8,128)(2,1)S(1)}, u32[]{:S(2)}, u32[]{:S(2)}) collective-permute-start(bf16[64,3072]{1,0:T(8,128)(2,1)S(1)} %get-tuple-element.498), channel_id=1, source_target_pairs={{0,16},{1,17},{2,18},{3,19},{4,20},{5,21},{6,22},{7,23},{8,24},{9,... | collective-permute-start | bytes 1179656 | tf_op jit(solution)/shard_map/ppermute | solution.py:65
  313.3 33.3 %collective-permute-start.45 = (bf16[256,1024]{1,0:T(8,128)(2,1)S(1)}, bf16[256,1024]{1,0:T(8,128)(2,1)S(1)}, u32[]{:S(2)}, u32[]{:S(2)}) collective-permute-start(bf16[256,1024]{1,0:T(8,128)(2,1)S(1)} %get-tuple-element.506), channel_id=1, source_target_pairs={{0,4},{1,5},{2,6},{3,7},{4,0},{5,1},{6,2},{7,3},{8,12},{9,13},{10,... | collective-permute-start | bytes 1572872 | tf_op jit(solution)/shard_map/ppermute | solution.py:65
  315.0 33.6 %collective-permute-start.44 = (bf16[128,2048]{1,0:T(8,128)(2,1)S(1)}, bf16[128,2048]{1,0:T(8,128)(2,1)S(1)}, u32[]{:S(2)}, u32[]{:S(2)}) collective-permute-start(bf16[128,2048]{1,0:T(8,128)(2,1)S(1)} %get-tuple-element.502), channel_id=1, source_target_pairs={{0,4},{1,5},{2,6},{3,7},{4,0},{5,1},{6,2},{7,3},{8,12},{9,13},{10,... | collective-permute-start | bytes 1572872 | tf_op jit(solution)/shard_map/ppermute | solution.py:65
  316.2 23.8 %collective-permute-start.40 = (bf16[64,3072]{1,0:T(8,128)(2,1)S(1)}, bf16[64,3072]{1,0:T(8,128)(2,1)S(1)}, u32[]{:S(2)}, u32[]{:S(2)}) collective-permute-start(bf16[64,3072]{1,0:T(8,128)(2,1)S(1)} %get-tuple-element.486), channel_id=1, source_target_pairs={{0,8},{1,9},{2,10},{3,11},{4,12},{5,13},{6,14},{7,15},{8,0},{9,1},... | collective-permute-start | bytes 1179656 | tf_op jit(solution)/shard_map/ppermute | solution.py:65
  336.2 10.3 %collective-permute-start.39 = (bf16[192,1024]{1,0:T(8,128)(2,1)S(1)}, bf16[192,1024]{1,0:T(8,128)(2,1)S(1)}, u32[]{:S(2)}, u32[]{:S(2)}) collective-permute-start(bf16[192,1024]{1,0:T(8,128)(2,1)S(1)} %get-tuple-element.478), channel_id=1, source_target_pairs={{0,8},{1,9},{2,10},{3,11},{4,12},{5,13},{6,14},{7,15},{8,0},{9,1},... | collective-permute-start | bytes 1179656 | tf_op jit(solution)/shard_map/ppermute | solution.py:65
  338.2 14.4 %collective-permute-start.46 = (bf16[128,2176]{1,0:T(8,128)(2,1)S(1)}, bf16[128,2176]{1,0:T(8,128)(2,1)S(1)}, u32[]{:S(2)}, u32[]{:S(2)}) collective-permute-start(bf16[128,2176]{1,0:T(8,128)(2,1)S(1)} %get-tuple-element.509), channel_id=1, source_target_pairs={{0,4},{1,5},{2,6},{3,7},{4,0},{5,1},{6,2},{7,3},{8,12},{9,13},{10,... | collective-permute-start | bytes 1671176 | tf_op jit(solution)/shard_map/ppermute | solution.py:65
  346.9 7.6 %collective-permute-start.51 = (bf16[128,1024]{1,0:T(8,128)(2,1)S(1)}, bf16[128,1024]{1,0:T(8,128)(2,1)S(1)}, u32[]{:S(2)}, u32[]{:S(2)}) collective-permute-start(bf16[128,1024]{1,0:T(8,128)(2,1)S(1)} %get-tuple-element.527), channel_id=1, source_target_pairs={{0,8},{1,9},{2,10},{3,11},{4,12},{5,13},{6,14},{7,15},{8,0},{9,1},... | collective-permute-start | bytes 786440 | tf_op jit(solution)/shard_map/ppermute | solution.py:65
  348.8 9.5 %collective-permute-start.47 = (bf16[64,2048]{1,0:T(8,128)(2,1)S(1)}, bf16[64,2048]{1,0:T(8,128)(2,1)S(1)}, u32[]{:S(2)}, u32[]{:S(2)}) collective-permute-start(bf16[64,2048]{1,0:T(8,128)(2,1)S(1)} %get-tuple-element.513), channel_id=1, source_target_pairs={{0,2},{1,3},{2,0},{3,1},{4,6},{5,7},{6,4},{7,5},{8,10},{9,11},{10,... | collective-permute-start | bytes 786440 | tf_op jit(solution)/shard_map/ppermute | solution.py:65
  350.6 10.9 %collective-permute-start.54 = (bf16[32,3072]{1,0:T(8,128)(2,1)S(1)}, bf16[32,3072]{1,0:T(8,128)(2,1)S(1)}, u32[]{:S(2)}, u32[]{:S(2)}) collective-permute-start(bf16[32,3072]{1,0:T(8,128)(2,1)S(1)} %get-tuple-element.534), channel_id=1, source_target_pairs={{0,2},{1,3},{2,0},{3,1},{4,6},{5,7},{6,4},{7,5},{8,10},{9,11},{10,... | collective-permute-start | bytes 589832 | tf_op jit(solution)/shard_map/ppermute | solution.py:65
  350.9 16.6 %collective-permute-start.55 = (bf16[96,1024]{1,0:T(8,128)(2,1)S(1)}, bf16[96,1024]{1,0:T(8,128)(2,1)S(1)}, u32[]{:S(2)}, u32[]{:S(2)}) collective-permute-start(bf16[96,1024]{1,0:T(8,128)(2,1)S(1)} %get-tuple-element.536), channel_id=1, source_target_pairs={{0,2},{1,3},{2,0},{3,1},{4,6},{5,7},{6,4},{7,5},{8,10},{9,11},{10,... | collective-permute-start | bytes 589832 | tf_op jit(solution)/shard_map/ppermute | solution.py:65
  352.6 14.1 %collective-permute-start.53 = (bf16[32,3072]{1,0:T(8,128)(2,1)S(1)}, bf16[32,3072]{1,0:T(8,128)(2,1)S(1)}, u32[]{:S(2)}, u32[]{:S(2)}) collective-permute-start(bf16[32,3072]{1,0:T(8,128)(2,1)S(1)} %get-tuple-element.532), channel_id=1, source_target_pairs={{0,16},{1,17},{2,18},{3,19},{4,20},{5,21},{6,22},{7,23},{8,24},{9,... | collective-permute-start | bytes 589832 | tf_op jit(solution)/shard_map/ppermute | solution.py:65
  354.6 19.1 %collective-permute-start.52 = (bf16[64,1024]{1,0:T(8,128)(2,1)S(1)}, bf16[64,1024]{1,0:T(8,128)(2,1)S(1)}, u32[]{:S(2)}, u32[]{:S(2)}) collective-permute-start(bf16[64,1024]{1,0:T(8,128)(2,1)S(1)} %get-tuple-element.529), channel_id=1, source_target_pairs={{0,16},{1,17},{2,18},{3,19},{4,20},{5,21},{6,22},{7,23},{8,24},{9,... | collective-permute-start | bytes 393224 | tf_op jit(solution)/shard_map/ppermute | solution.py:65
  358.2 11.4 %collective-permute-start.49 = (bf16[64,2176]{1,0:T(8,128)(2,1)S(1)}, bf16[64,2176]{1,0:T(8,128)(2,1)S(1)}, u32[]{:S(2)}, u32[]{:S(2)}) collective-permute-start(bf16[64,2176]{1,0:T(8,128)(2,1)S(1)} %get-tuple-element.517), channel_id=1, source_target_pairs={{0,8},{1,9},{2,10},{3,11},{4,12},{5,13},{6,14},{7,15},{8,0},{9,1},... | collective-permute-start | bytes 835592 | tf_op jit(solution)/shard_map/ppermute | solution.py:65
  361.5 16.4 %collective-permute-start.48 = (bf16[32,2048]{1,0:T(8,128)(2,1)S(1)}, bf16[32,2048]{1,0:T(8,128)(2,1)S(1)}, u32[]{:S(2)}, u32[]{:S(2)}) collective-permute-start(bf16[32,2048]{1,0:T(8,128)(2,1)S(1)} %get-tuple-element.515), channel_id=1, source_target_pairs={{0,16},{1,17},{2,18},{3,19},{4,20},{5,21},{6,22},{7,23},{8,24},{9,... | collective-permute-start | bytes 393224 | tf_op jit(solution)/shard_map/ppermute | solution.py:65
  370.5 8.9 %collective-permute-start.50 = (bf16[32,2176]{1,0:T(8,128)(2,1)S(1)}, bf16[32,2176]{1,0:T(8,128)(2,1)S(1)}, u32[]{:S(2)}, u32[]{:S(2)}) collective-permute-start(bf16[32,2176]{1,0:T(8,128)(2,1)S(1)} %get-tuple-element.519), channel_id=1, source_target_pairs={{0,16},{1,17},{2,18},{3,19},{4,20},{5,21},{6,22},{7,23},{8,24},{9,... | collective-permute-start | bytes 417800 | tf_op jit(solution)/shard_map/ppermute | solution.py:65
  (47 other events, 565.5 us)
Sparse Core Ops, SparseCore 0:
  11.0 159.5 all-gather.2

commit v7 on v6

--- a/solution.py
+++ b/solution.py
@@ -149,7 +149,7 @@
 
 def fold(*pairs, merged=False):
     halves = [kept.shape[0] // 2 for kept, *_ in pairs]
-    steps = next(n for n in (4, 2, 1) if n == 1 or all(rows % (16 * n) == 0 for rows in halves))
+    steps = next(n for n in (2, 1) if n == 1 or all(rows % (16 * n) == 0 for rows in halves))
     in_specs, out_specs, out_shape, operands = [], [], [], []
     for rows, (kept, came, place) in zip(halves, pairs):
         columns = kept.shape[1]
@@ -385,6 +385,50 @@
         weight_ref[:, inner ^ mask] = ref[...]
     top, count, rows, columns = weight_ref.shape
     return weight_ref[...].reshape(top * count * rows, columns)
+
+
+def prepare_body(device_ref, *refs, shard, head_shard):
+    (*part_refs, tokens_ref), (normed_ref, first_gain_ref, second_gain_ref, head_gains_ref, gains_ref) = refs[:-5], refs[-5:]
+    lines = join_parts(device_ref, part_refs, gains_ref).astype(jnp.float32).T
+    gain = lines[0:1, :]
+    first_gain_ref[...] = gain
+    second_gain_ref[...] = lines[1:2, :]
+    width = lines.shape[1]
+    source = lax.broadcasted_iota(jnp.int32, (width, HEAD_SIZE), 0)
+    target = lax.broadcasted_iota(jnp.int32, (width, HEAD_SIZE), 1)
+    pick = jnp.where(target // head_shard * shard + target % head_shard == source, 1.0, 0.0)
+    head_gains_ref[...] = jnp.dot(
+        lines[2:4, :], pick, precision=lax.Precision.HIGHEST, preferred_element_type=jnp.float32
+    )
+    unit, _ = unit_head(tokens_ref[...].astype(jnp.float32))
+    normed_ref[...] = (unit * gain).astype(jnp.bfloat16)
+
+
+def prepare(device, parts, tokens, shard, head_shard):
+    rows, width = tokens.shape
+    top, part_rows, columns = parts[0].shape
+    whole = lambda *shape: pl.BlockSpec(shape, lambda i, d: (0, 0))
+    line = jax.ShapeDtypeStruct((1, width), jnp.float32)
+    return pl.pallas_call(
+        functools.partial(prepare_body, shard=shard, head_shard=head_shard),
+        grid_spec=pltpu.PrefetchScalarGridSpec(
+            num_scalar_prefetch=1,
+            grid=(1,),
+            in_specs=[pl.BlockSpec((top, part_rows, 128), lambda i, d: (0, 0, columns // 128 - 1)) for _ in parts]
+            + [whole(rows, width)],
+            out_specs=[whole(rows, width), whole(1, width), whole(1, width), whole(2, HEAD_SIZE)],
+            scratch_shapes=[pltpu.VMEM((top, len(parts), part_rows, 128), jnp.bfloat16)],
+        ),
+        out_shape=[
+            jax.ShapeDtypeStruct((rows, width), jnp.bfloat16),
+            line,
+            line,
+            jax.ShapeDtypeStruct((2, HEAD_SIZE), jnp.float32),
+        ],
+        compiler_params=pltpu.CompilerParams(vmem_limit_bytes=16 * 1024 * 1024),
+        cost_estimate=SMALL,
+        name="prepare",
+    )(device.reshape(1), *parts, tokens)
 
 
 def attend_body(device_ref, *refs):
@@ -671,8 +715,8 @@
     )
 
 
-def project_body(device_ref, *refs):
-    (*part_refs, tokens_ref, attended_ref), (residual_ref, weight_out_ref) = refs[:-2], refs[-2:]
+def project_body(device_ref, *refs, top_steps):
+    (*part_refs, tokens_ref, first_ref, second_ref), (residual_ref, weight_out_ref) = refs[:-2], refs[-2:]
     inner = device_ref[0] & (len(part_refs) - 1)
 
     @pl.when(pl.program_id(0) == 0)
@@ -683,31 +727,39 @@
         weight_out_ref[:, inner ^ mask] = ref[...]
     top, count, rows, columns = weight_out_ref.shape
     weight = weight_out_ref[...].reshape(top * count * rows, columns)
-    residual_ref[...] += jnp.dot(attended_ref[...], weight, preferred_element_type=jnp.float32)
-
-
-def project(device, parts, tokens, attended):
+    for ref, part in ((first_ref, 0), (second_ref, 1)):
+
+        @pl.when(pl.program_id(0) // (top_steps // 2) == part)
+        def _():
+            residual_ref[...] += jnp.dot(ref[...], weight, preferred_element_type=jnp.float32)
+
+
+def project(device, parts, tokens, first, second):
     rows, width = tokens.shape
     top, part_rows, _ = parts[0].shape
     step_rows = len(parts) * part_rows
     whole = pl.BlockSpec((rows, width), lambda j, d: (0, 0))
     residual, weight = pl.pallas_call(
-        project_body,
+        functools.partial(project_body, top_steps=top),
         grid_spec=pltpu.PrefetchScalarGridSpec(
             num_scalar_prefetch=1,
             grid=(top,),
             in_specs=[pl.BlockSpec((1, part_rows, width), lambda j, d: (j, 0, 0)) for _ in parts]
-            + [whole, pl.BlockSpec((rows, step_rows), lambda j, d: (0, j))],
+            + [
+                whole,
+                pl.BlockSpec((rows, step_rows), lambda j, d: (0, jnp.minimum(j, top // 2 - 1))),
+                pl.BlockSpec((rows, step_rows), lambda j, d: (0, jnp.maximum(j - top // 2, 0))),
+            ],
             out_specs=[whole, pl.BlockSpec((1, len(parts), part_rows, width), lambda j, d: (j, 0, 0, 0))],
         ),
         out_shape=[
-            jax.ShapeDtypeStruct((rows, width), jnp.float32),
+            far((rows, width), jnp.float32),
             far((top, len(parts), part_rows, width), jnp.bfloat16),
         ],
         compiler_params=pltpu.CompilerParams(vmem_limit_bytes=20 * 1024 * 1024),
         cost_estimate=SMALL,
         name="project",
-    )(device.reshape(1), *parts, tokens, attended)
+    )(device.reshape(1), *parts, tokens, first, second)
     return residual, weight.reshape(top * step_rows, width)
 
 
@@ -1031,7 +1083,12 @@
     first_parts = gather_bits({0: first_part}, count, early[:cut_bits])
     second_parts = gather_bits({0: second_part}, count, late[:cut_bits])
     out_top = gather_top(w_out, count)
-    first_parts, second_parts, out_top = fence((first_parts, second_parts, out_top))
+    seq_id, token_position = layout(seq_lengths, seq_owner, device, row_total_count)
+    first_row = (jnp.arange(row_total_count, dtype=jnp.int32) - token_position)[:, None]
+    cosine, sine = rotation_factors(token_position)
+    first_parts, second_parts, out_top, first_row, cosine, sine = fence(
+        (first_parts, second_parts, out_top, first_row, cosine, sine)
+    )
     first_parts = gather_bits(first_parts, count, early[cut_bits:])
     second_parts = gather_bits(second_parts, count, late[cut_bits:])
     out_top = gather_top_rest(out_top, count)
@@ -1040,18 +1097,9 @@
     out_parts = gather_bits(lay_top(out_top, device, count), count, early[:cut_bits])
     first_parts, second_parts = fence((first_parts, second_parts))
     second_parts = gather_bits(second_parts, count, [0])
-    first_gains = lay({mask: part[..., -128:] for mask, part in first_parts.items()}, device, count)
     first_weight = weight_parts(first_parts, device, count)
 
-    seq_id, token_position = layout(seq_lengths, seq_owner, device, row_total_count)
-    first_row = (jnp.arange(row_total_count, dtype=jnp.int32) - token_position)[:, None]
-    cosine, sine = rotation_factors(token_position)
-    inputs = tokens.astype(jnp.float32)
-    gain_block = first_gains.astype(jnp.float32)
-    head_gains = gain_block.reshape(count, shard, 128)[:, :head_shard, 2:4].reshape(HEAD_SIZE, 2).T
-    gain_one = gain_block[:, 0]
-    gain_two = gain_block[:, 1]
-    normed_low = norm_forward(inputs, gain_one)[0].astype(jnp.bfloat16)
+    normed_low, gain_one, gain_two, head_gains = prepare(device, first_weight, tokens, shard, head_shard)
     attended_first, *saved_first = attend(device, normed_low, first_weight, head_gains, cosine, sine, first_row)
     attended_first, second_parts, out_parts = fence((attended_first, second_parts, out_parts))
     out_parts = gather_bits(out_parts, count, early[cut_bits:])
@@ -1065,12 +1113,13 @@
         device,
         [out_parts[mask] for mask in range(count // 4)],
         tokens,
-        jnp.concatenate([attended_first, attended_second], axis=1),
+        attended_first,
+        attended_second,
     )
     (
         hidden, grad_gate, grad_up, gate_kept, gate_sent, up_kept, up_sent, down_kept, down_sent
     ) = feed_forward(
-        device, residual, gain_two[None], cotangent, ffn_weights, shard, orders["gate"], orders["up"]
+        device, residual, gain_two, cotangent, ffn_weights, shard, orders["gate"], orders["up"]
     )
 
     live = dict(
@@ -1108,14 +1157,14 @@
         second=turn((live.pop("normed"),), device, orders["second"]),
     )
     cut()
-    relay("down", "gate", "up")
+    relay("up", "gate", "down")
     cut()
     turned = live.pop("turned")
     (
         live["grad_residual"], live["low"], live["grad_gain_two"], live["out"], live["out_sent"], live["first"],
         live["first_sent"], live["head_sums"], live["normed_sum"],
     ) = back(
-        device, residual, gain_two[None], cotangent, live.pop("grad_gate"), live.pop("grad_up"), ffn_weights, shard,
+        device, residual, gain_two, cotangent, live.pop("grad_gate"), live.pop("grad_up"), ffn_weights, shard,
         turned["out"], operands("first", saved_first), first_weight,
     )
     land("down", "gate", "up")
@@ -1130,7 +1179,7 @@
     cut()
     live["second"], live["second_sent"], live["grad_tokens"], live["mixed"] = attend_back_last(
         device, live.pop("low"), operands("second", saved_second), second_weight,
-        (live.pop("head_sums"), live.pop("normed_sum")), tokens, gain_one[None], live.pop("grad_residual"),
+        (live.pop("head_sums"), live.pop("normed_sum")), tokens, gain_one, live.pop("grad_residual"),
         live.pop("grad_gain_two"), residual, live.pop("hidden"), ffn_weights, orders["second"], shard, head_shard,
     )
     land("down", "both")

time: 390 us -> 387 us (level)
  waiting for transfers between devices: 142 us -> 163 us
  local copies, waits for them, and re-layouts: 15.2 us -> 5.8 us
  starting transfers between devices: 64 us -> 58 us
  Pallas kernels: 144 us -> 139 us
    ppermute x56, waiting for transfers between devices: 142 us -> 163 us  [exchange(): lax.ppermute(values, 'fsdp', [(source, source ^ mask) for source in range...]
    ppermute x56, starting transfers between devices: 64 us -> 57.9 us  [exchange(): lax.ppermute(values, 'fsdp', [(source, source ^ mask) for source in range...]
    slice x10 -> x0, local copies, waits for them, and re-layouts: 5.78 us -> none  [the longest x8 3.83 us: on_device(): part[..., -128:]]
    unnamed x79 -> x126, local copies, waits for them, and re-layouts: 8.58 us -> 4.41 us
  transfers between devices with their start and end apart: 57 -> 57, of which waited for: 32 -> 39; matrix products, arithmetic and copies ran while one was open for 5% -> 2% of each run, Pallas kernels for 29% -> 28%
where the time goes in v7:
time: 387 us; the launch traced here: 386 us
  waiting for transfers between devices  163 us (42%)
  Pallas kernels  139 us (36%)
  starting transfers between devices  58 us (15%)
  between operations  14.8 us (4%)
  local copies, waits for them, and re-layouts  5.8 us (1%)
  other arithmetic  5.16 us (1%)
    ppermute x56, waiting for transfers between devices, exchange(): lax.ppermute(values, 'fsdp', [(source, source ^ mask) for source in range...  163 us
    ppermute x56, starting transfers between devices, exchange(): lax.ppermute(values, 'fsdp', [(source, source ^ mask) for source in range...  57.9 us
    pallas_call x1, Pallas kernels, back(): pl.pallas_call(functools.partial(back_body, parts=len(parts)), grid_spec=...  34.2 us
    pallas_call x1, Pallas kernels, feed_forward(): pl.pallas_call(functools.partial(feed_forward_body, gate_order=gate_order...  27 us
    pallas_call x1, Pallas kernels, attend_back_last(): pl.pallas_call(functools.partial(attend_back_body, order=order, shard=sha...  26.3 us
    pallas_call x2, Pallas kernels, attend(): pl.pallas_call(attend_body, grid_spec=pltpu.PrefetchScalarGridSpec(num_sc...  20.9 us
    pallas_call x23, Pallas kernels, fold(): pl.pallas_call(functools.partial(fold_body, pairs=len(pairs), merged=merg...  12.9 us
  transfers between devices with their start and end apart: 57, of which 39 were waited for; matrix products, arithmetic and copies ran while one was open for 2% of the time, Pallas kernels for 28%

profile of v7, /device:TPU:0, one launch (start us, length us, event | category | flops | bytes accessed | tf_op | source)
XLA Modules:
  0.0 386.3 jit_solution(12211346104337452365)
XLA Ops:
  7.3 2.0 stack.1
  11.4 1.7 join.1
  13.1 3.0 collective-permute-start
  16.1 2.6 collective-permute-start.1
  18.9 13.2 %collective-permute-done = bf16[32,4224]{1,0:T(8,128)(2,1)S(1)} collective-permute-done((bf16[32,4224]{1,0:T(8,128)(2,1)}, bf16[32,4224]{1,0:T(8,128)(2,1)S(1)}, u32[]{:S(2)}, u32[]{:S(2)}) %collective-permute-start) | collective-permute-done | bytes 270368 | tf_op jit(solution)/shard_map/ppermute | solution.py:65
  32.1 1.8 collective-permute-done.1
  33.9 2.0 collective-permute-start.2
  36.1 11.4 %collective-permute-done.2 = bf16[32,4224]{1,0:T(8,128)(2,1)S(1)} collective-permute-done((bf16[32,4224]{1,0:T(8,128)(2,1)S(1)}, bf16[32,4224]{1,0:T(8,128)(2,1)S(1)}, u32[]{:S(2)}, u32[]{:S(2)}) %collective-permute-start.2) | collective-permute-done | bytes 270368 | tf_op jit(solution)/shard_map/ppermute | solution.py:65
  54.8 2.5 collective-permute-start.6
  57.7 10.1 %collective-permute-done.5 = bf16[64,1024]{1,0:T(8,128)(2,1)S(1)} collective-permute-done((bf16[64,1024]{1,0:T(8,128)(2,1)S(1)}, bf16[64,1024]{1,0:T(8,128)(2,1)S(1)}, u32[]{:S(2)}, u32[]{:S(2)}) %collective-permute-start.5) | collective-permute-done | bytes 131104 | tf_op jit(solution)/shard_map/ppermute | solution.py:65
  67.8 2.3 collective-permute-done.6
  70.2 1.9 collective-permute-done.4.refs_4_
  72.1 2.3 collective-permute-done.3.refs_2_.refs_21_
  76.5 2.5 collective-permute-start.10
  79.6 4.4 %collective-permute-done.11 = bf16[64,1024]{1,0:T(8,128)(2,1)S(1)} collective-permute-done((bf16[64,1024]{1,0:T(8,128)(2,1)S(1)}, bf16[64,1024]{1,0:T(8,128)(2,1)S(1)}, u32[]{:S(2)}, u32[]{:S(2)}) %collective-permute-start.11) | collective-permute-done | bytes 131104 | tf_op jit(solution)/shard_map/ppermute | solution.py:65
  84.0 8.9 %collective-permute-done.10.refs_6_ = bf16[4,32,2048]{2,1,0:T(8,128)(2,1)S(1)} collective-permute-done((bf16[4,32,2048]{2,1,0:T(8,128)(2,1)S(1)}, bf16[4,32,2048]{2,1,0:T(8,128)(2,1)S(1)}, u32[]{:S(2)}, u32[]{:S(2)}) %collective-permute-start.10) | collective-permute-done | bytes 524320 | tf_op jit(solution)/shard_map/ppermute | solution.py:65
  92.9 10.3 %collective-permute-done.9.refs_2_ = bf16[4,32,2048]{2,1,0:T(8,128)(2,1)S(1)} collective-permute-done((bf16[4,32,2048]{2,1,0:T(8,128)(2,1)S(1)}, bf16[4,32,2048]{2,1,0:T(8,128)(2,1)S(1)}, u32[]{:S(2)}, u32[]{:S(2)}) %collective-permute-start.9) | collective-permute-done | bytes 524320 | tf_op jit(solution)/shard_map/ppermute | solution.py:65
  105.4 2.5 collective-permute-start.20
  112.3 11.0 %attend.2 = (bf16[384,1024]{1,0:T(8,128)(2,1)S(1)}, bf16[384,1024]{1,0:T(8,128)(2,1)}, bf16[384,512]{1,0:T(8,128)(2,1)}, bf16[384,512]{1,0:T(8,128)(2,1)}, f32[384,1536]{1,0:T(8,128)}, /*index=5*/f32[4,384,2]{2,1,0:T(8,128)}) custom-call(s32[1]{0:T(128)} %bitcast.device_ref, bf16[4,32,2176]{2,1,0:T(8,128)(2,1)S(1)} %get-tuple-element.308.refs_0_.refs_19_, ...), custom_call_target="tpu_custom_call" | custom-call | flops 1 | bytes 1 | tf_op jit(solution)/shard_map/attend/pallas_call | solution.py:474
  123.3 8.4 %collective-permute-done.20.refs_2_ = bf16[4,64,1024]{2,1,0:T(8,128)(2,1)S(1)} collective-permute-done((bf16[4,64,1024]{2,1,0:T(8,128)(2,1)S(1)}, bf16[4,64,1024]{2,1,0:T(8,128)(2,1)S(1)}, u32[]{:S(2)}, u32[]{:S(2)}) %collective-permute-start.20) | collective-permute-done | bytes 524320 | tf_op jit(solution)/shard_map/ppermute | solution.py:65
  133.9 10.0 %attend.3 = (bf16[384,1024]{1,0:T(8,128)(2,1)S(1)}, bf16[384,1024]{1,0:T(8,128)(2,1)}, bf16[384,512]{1,0:T(8,128)(2,1)}, bf16[384,512]{1,0:T(8,128)(2,1)}, f32[384,1536]{1,0:T(8,128)}, /*index=5*/f32[4,384,2]{2,1,0:T(8,128)}) custom-call(s32[1]{0:T(128)} %bitcast.device_ref, bf16[4,32,2048]{2,1,0:T(8,128)(2,1)S(1)} %get-tuple-element.331.refs_0_, ...), custom_call_target="tpu_custom_call" | custom-call | flops 1 | bytes 1 | tf_op jit(solution)/shard_map/attend/pallas_call | solution.py:474
  143.9 4.3 %collective-permute-done.21.refs_4_ = bf16[4,64,1024]{2,1,0:T(8,128)(2,1)S(1)} collective-permute-done((bf16[4,64,1024]{2,1,0:T(8,128)(2,1)S(1)}, bf16[4,64,1024]{2,1,0:T(8,128)(2,1)S(1)}, u32[]{:S(2)}, u32[]{:S(2)}) %collective-permute-start.21) | collective-permute-done | bytes 524320 | tf_op jit(solution)/shard_map/ppermute | solution.py:65
  148.2 10.8 %collective-permute-done.22.refs_6_ = bf16[4,64,1024]{2,1,0:T(8,128)(2,1)S(1)} collective-permute-done((bf16[4,64,1024]{2,1,0:T(8,128)(2,1)S(1)}, bf16[4,64,1024]{2,1,0:T(8,128)(2,1)S(1)}, u32[]{:S(2)}, u32[]{:S(2)}) %collective-permute-start.22) | collective-permute-done | bytes 524320 | tf_op jit(solution)/shard_map/ppermute | solution.py:65
  164.6 5.0 %project.1 = (f32[384,1024]{1,0:T(8,128)}, bf16[4,8,64,1024]{3,2,1,0:T(8,128)(2,1)}) custom-call(s32[1]{0:T(128)} %bitcast.device_ref, bf16[4,64,1024]{2,1,0:T(8,128)(2,1)S(1)} %bitcast.34, bf16[4,64,1024]{2,1,0:T(8,128)(2,1)S(1)} %collective-permute-done.23.refs_1_, bf16[4,64,1024]{2,1,0:T(8,128)(2,1)S(1)} %collective-permute-done.20.refs_2_, ...), custom_call_target="tpu_custom_call" | custom-call | flops 1 | bytes 1 | tf_op jit(solution)/shard_map/project/pallas_call | solution.py:742
  171.1 27.0 %feed_forward.1 = (bf16[384,3072]{1,0:T(8,128)(2,1)}, bf16[384,3072]{1,0:T(8,128)(2,1)}, bf16[384,3072]{1,0:T(8,128)(2,1)}, bf16[512,3072]{1,0:T(8,128)(2,1)}, b...) custom-call(s32[1]{0:T(128)} %bitcast.device_ref, ...), custom_call_target="tpu_custom_call" | custom-call | flops 1 | bytes 1 | tf_op jit(solution)/shard_map/feed_forward/pallas_call | solution.py:864
  201.3 1.8 turn.4.refs_7_
  206.0 2.6 collective-permute-done.28.refs_2_.refs_3_
  210.9 2.1 collective-permute-done.27.refs_2_.refs_3_
  216.1 34.2 %back.1 = (f32[384,1024]{1,0:T(8,128)}, bf16[384,1024]{1,0:T(8,128)(2,1)}, f32[1,1024]{1,0:T(1,128)S(1)}, bf16[1024,1024]{1,0:T(8,128)(2,1)}, bf16[1024,1024]{1,...) custom-call(s32[1]{0:T(128)} %bitcast.device_ref, ...), custom_call_target="tpu_custom_call" | custom-call | flops 1 | bytes 1 | tf_op jit(solution)/shard_map/back/pallas_call | solution.py:972
  261.6 2.4 collective-permute-start.36
  264.1 26.3 %attend_back_last.1 = (bf16[512,2176]{1,0:T(8,128)(2,1)S(1)}, bf16[512,2176]{1,0:T(8,128)(2,1)}, bf16[384,1024]{1,0:T(8,128)(2,1)}, bf16[384,1024]{1,0:T(8,128)(2,1)}) custom-call(s32[1]{0:T(128)} %bitcast.device_ref, bf16[384,1024]{1,0:T(8,128)(2,1)S(1)} %copy-done.47, bf16[2048,1024]{1,0:T(8,128)(2,1)} %bitcast.42, ...), custom_call_target="tpu_custom_call" | custom-call | flops 1 | bytes 1 | tf_op jit(solution)/shard_map/attend_back_last/pallas_call | solution.py:684
  290.5 10.0 %collective-permute-done.36.refs_2_.refs_3_ = bf16[384,1024]{1,0:T(8,128)(2,1)S(1)} collective-permute-done((bf16[384,1024]{1,0:T(8,128)(2,1)}, bf16[384,1024]{1,0:T(8,128)(2,1)S(1)}, u32[]{:S(2)}, u32[]{:S(2)}) %collective-permute-start.36) | collective-permute-done | bytes 786464 | tf_op jit(solution)/shard_map/ppermute | solution.py:65
  300.5 1.9 collective-permute-done.37.refs_2_.refs_3_
  302.3 4.6 %collective-permute-done.41.refs_2_.refs_3_ = bf16[512,2176]{1,0:T(8,128)(2,1)S(1)} collective-permute-done((bf16[512,2176]{1,0:T(8,128)(2,1)}, bf16[512,2176]{1,0:T(8,128)(2,1)S(1)}, u32[]{:S(2)}, u32[]{:S(2)}) %collective-permute-start.41) | collective-permute-done | bytes 2228256 | tf_op jit(solution)/shard_map/ppermute | solution.py:65
  308.6 2.1 collective-permute-start.43
  313.7 1.9 collective-permute-start.40
  315.8 18.3 %collective-permute-done.42.refs_2_.refs_3_ = bf16[256,2176]{1,0:T(8,128)(2,1)S(1)} collective-permute-done((bf16[256,2176]{1,0:T(8,128)(2,1)S(1)}, bf16[256,2176]{1,0:T(8,128)(2,1)S(1)}, u32[]{:S(2)}, u32[]{:S(2)}) %collective-permute-start.42) | collective-permute-done | bytes 1114144 | tf_op jit(solution)/shard_map/ppermute | solution.py:65
  334.1 1.7 collective-permute-start.39
  337.8 6.6 %collective-permute-done.39.refs_2_.refs_3_ = bf16[192,1024]{1,0:T(8,128)(2,1)S(1)} collective-permute-done((bf16[192,1024]{1,0:T(8,128)(2,1)S(1)}, bf16[192,1024]{1,0:T(8,128)(2,1)S(1)}, u32[]{:S(2)}, u32[]{:S(2)}) %collective-permute-start.39) | collective-permute-done | bytes 393248 | tf_op jit(solution)/shard_map/ppermute | solution.py:65
  344.8 1.8 collective-permute-start.51
  352.1 2.1 collective-permute-start.52
  354.2 1.7 collective-permute-done.47.refs_2_.refs_3_
  357.7 1.7 collective-permute-done.54
  361.4 2.9 collective-permute-done.53
  368.2 2.7 collective-permute-done.52
  371.6 3.6 collective-permute-done.48.first_came
  375.2 1.7 collective-permute-done.50.second_came
  377.6 1.9 end_projections.1
  (248 shorter events, 72.8 us)
Async XLA Ops:
  7.2 163.8 %all-gather.3.cloned.1.call-start = ((), (), s32[]{:S(2)}) async-start(), calls=%async_computation | async-start | bytes 19464192 | tf_op jit(solution)/shard_map/all_gather | solution.py:1074
  13.1 19.0 %collective-permute-start = (bf16[32,4224]{1,0:T(8,128)(2,1)}, bf16[32,4224]{1,0:T(8,128)(2,1)S(1)}, u32[]{:S(2)}, u32[]{:S(2)}) collective-permute-start(bf16[32,4224]{1,0:T(8,128)(2,1)} %join.1), channel_id=1, source_target_pairs={{0,8},{1,9},{2,10},{3,11},{4,12},{5,13},{6,14},{7,15},{8,0},{9,1},... | collective-permute-start | bytes 811016 | tf_op jit(solution)/shard_map/ppermute | solution.py:65
  16.1 17.8 %collective-permute-start.1 = (bf16[32,4224]{1,0:T(8,128)(2,1)}, bf16[32,4224]{1,0:T(8,128)(2,1)S(1)}, u32[]{:S(2)}, u32[]{:S(2)}) collective-permute-start(bf16[32,4224]{1,0:T(8,128)(2,1)} %join.1), channel_id=1, source_target_pairs={{0,16},{1,17},{2,18},{3,19},{4,20},{5,21},{6,22},{7,23},{8,24},{9,... | collective-permute-start | bytes 811016 | tf_op jit(solution)/shard_map/ppermute | solution.py:65
  33.9 13.5 %collective-permute-start.2 = (bf16[32,4224]{1,0:T(8,128)(2,1)S(1)}, bf16[32,4224]{1,0:T(8,128)(2,1)S(1)}, u32[]{:S(2)}, u32[]{:S(2)}) collective-permute-start(bf16[32,4224]{1,0:T(8,128)(2,1)S(1)} %collective-permute-done.1), channel_id=1, source_target_pairs={{0,8},{1,9},{2,10},{3,11},{4,12},{5,13},{6,14},{7,15},{8,0},{9,1},... | collective-permute-start | bytes 811016 | tf_op jit(solution)/shard_map/ppermute | solution.py:65
  49.5 24.9 %collective-permute-start.3 = (bf16[4,32,2176]{2,1,0:T(8,128)(2,1)S(1)}, bf16[4,32,2176]{2,1,0:T(8,128)(2,1)S(1)}, u32[]{:S(2)}, u32[]{:S(2)}) collective-permute-start(bf16[4,32,2176]{2,1,0:T(8,128)(2,1)S(1)} %get-tuple-element.308.refs_0_.refs_19_), channel_id=1, source_target_pairs={{0,2},{1,3},{2,0},{3,1},{4,6},{5,7},{6,4},{7,5},{8,10},{9,11},{10,... | collective-permute-start | bytes 1671176 | tf_op jit(solution)/shard_map/ppermute | solution.py:65
  51.1 21.0 %collective-permute-start.4 = (bf16[4,32,2048]{2,1,0:T(8,128)(2,1)S(1)}, bf16[4,32,2048]{2,1,0:T(8,128)(2,1)S(1)}, u32[]{:S(2)}, u32[]{:S(2)}) collective-permute-start(bf16[4,32,2048]{2,1,0:T(8,128)(2,1)S(1)} %get-tuple-element.331.refs_0_), channel_id=1, source_target_pairs={{0,4},{1,5},{2,6},{3,7},{4,0},{5,1},{6,2},{7,3},{8,12},{9,13},{10,... | collective-permute-start | bytes 1572872 | tf_op jit(solution)/shard_map/ppermute | solution.py:65
  53.5 14.4 %collective-permute-start.5 = (bf16[64,1024]{1,0:T(8,128)(2,1)S(1)}, bf16[64,1024]{1,0:T(8,128)(2,1)S(1)}, u32[]{:S(2)}, u32[]{:S(2)}) collective-permute-start(bf16[64,1024]{1,0:T(8,128)(2,1)S(1)} %copy-done.57), channel_id=1, source_target_pairs={{0,8},{1,9},{2,10},{3,11},{4,12},{5,13},{6,14},{7,15},{8,0},{9,1},... | collective-permute-start | bytes 393224 | tf_op jit(solution)/shard_map/ppermute | solution.py:65
  54.8 15.3 %collective-permute-start.6 = (bf16[64,1024]{1,0:T(8,128)(2,1)S(1)}, bf16[64,1024]{1,0:T(8,128)(2,1)S(1)}, u32[]{:S(2)}, u32[]{:S(2)}) collective-permute-start(bf16[64,1024]{1,0:T(8,128)(2,1)S(1)} %copy-done.57), channel_id=1, source_target_pairs={{0,16},{1,17},{2,18},{3,19},{4,20},{5,21},{6,22},{7,23},{8,24},{9,... | collective-permute-start | bytes 393224 | tf_op jit(solution)/shard_map/ppermute | solution.py:65
  74.4 28.7 %collective-permute-start.7 = (bf16[4,32,2176]{2,1,0:T(8,128)(2,1)S(1)}, bf16[4,32,2176]{2,1,0:T(8,128)(2,1)S(1)}, u32[]{:S(2)}, u32[]{:S(2)}) collective-permute-start(bf16[4,32,2176]{2,1,0:T(8,128)(2,1)S(1)} %get-tuple-element.308.refs_0_.refs_19_), channel_id=1, source_target_pairs={{0,4},{1,5},{2,6},{3,7},{4,0},{5,1},{6,2},{7,3},{8,12},{9,13},{10,... | collective-permute-start | bytes 1671176 | tf_op jit(solution)/shard_map/ppermute | solution.py:65
  76.0 27.2 %collective-permute-start.8 = (bf16[4,32,2176]{2,1,0:T(8,128)(2,1)S(1)}, bf16[4,32,2176]{2,1,0:T(8,128)(2,1)S(1)}, u32[]{:S(2)}, u32[]{:S(2)}) collective-permute-start(bf16[4,32,2176]{2,1,0:T(8,128)(2,1)S(1)} %collective-permute-done.3.refs_2_.refs_21_), channel_id=1, source_target_pairs={{0,4},{1,5},{2,6},{3,7},{4,0},{5,1},{6,2},{7,3},{8,12},{9,13},{10,... | collective-permute-start | bytes 1671176 | tf_op jit(solution)/shard_map/ppermute | solution.py:65
  76.5 16.4 %collective-permute-start.10 = (bf16[4,32,2048]{2,1,0:T(8,128)(2,1)S(1)}, bf16[4,32,2048]{2,1,0:T(8,128)(2,1)S(1)}, u32[]{:S(2)}, u32[]{:S(2)}) collective-permute-start(bf16[4,32,2048]{2,1,0:T(8,128)(2,1)S(1)} %collective-permute-done.4.refs_4_), channel_id=1, source_target_pairs={{0,2},{1,3},{2,0},{3,1},{4,6},{5,7},{6,4},{7,5},{8,10},{9,11},{10,... | collective-permute-start | bytes 1572872 | tf_op jit(solution)/shard_map/ppermute | solution.py:65
  78.9 24.2 %collective-permute-start.9 = (bf16[4,32,2048]{2,1,0:T(8,128)(2,1)S(1)}, bf16[4,32,2048]{2,1,0:T(8,128)(2,1)S(1)}, u32[]{:S(2)}, u32[]{:S(2)}) collective-permute-start(bf16[4,32,2048]{2,1,0:T(8,128)(2,1)S(1)} %get-tuple-element.331.refs_0_), channel_id=1, source_target_pairs={{0,2},{1,3},{2,0},{3,1},{4,6},{5,7},{6,4},{7,5},{8,10},{9,11},{10,... | collective-permute-start | bytes 1572872 | tf_op jit(solution)/shard_map/ppermute | solution.py:65
  103.8 5.3 %collective-permute-start.14 = (bf16[4,32,2176]{2,1,0:T(8,128)(2,1)S(1)}, bf16[4,32,2176]{2,1,0:T(8,128)(2,1)S(1)}, u32[]{:S(2)}, u32[]{:S(2)}) collective-permute-start(bf16[4,32,2176]{2,1,0:T(8,128)(2,1)S(1)} %collective-permute-done.7.refs_4_.refs_23_), channel_id=1, source_target_pairs={{0,1},{1,0},{2,3},{3,2},{4,5},{5,4},{6,7},{7,6},{8,9},{9,8},{10,11... | collective-permute-start | bytes 1671176 | tf_op jit(solution)/shard_map/ppermute | solution.py:65
  103.8 6.1 %collective-permute-start.15 = (bf16[4,32,2176]{2,1,0:T(8,128)(2,1)S(1)}, bf16[4,32,2176]{2,1,0:T(8,128)(2,1)S(1)}, u32[]{:S(2)}, u32[]{:S(2)}) collective-permute-start(bf16[4,32,2176]{2,1,0:T(8,128)(2,1)S(1)} %collective-permute-done.8.refs_6_.refs_25_), channel_id=1, source_target_pairs={{0,1},{1,0},{2,3},{3,2},{4,5},{5,4},{6,7},{7,6},{8,9},{9,8},{10,11... | collective-permute-start | bytes 1671176 | tf_op jit(solution)/shard_map/ppermute | solution.py:65
  105.4 26.3 %collective-permute-start.20 = (bf16[4,64,1024]{2,1,0:T(8,128)(2,1)S(1)}, bf16[4,64,1024]{2,1,0:T(8,128)(2,1)S(1)}, u32[]{:S(2)}, u32[]{:S(2)}) collective-permute-start(bf16[4,64,1024]{2,1,0:T(8,128)(2,1)S(1)} %bitcast.31), channel_id=1, source_target_pairs={{0,2},{1,3},{2,0},{3,1},{4,6},{5,7},{6,4},{7,5},{8,10},{9,11},{10,... | collective-permute-start | bytes 1572872 | tf_op jit(solution)/shard_map/ppermute | solution.py:65
  110.0 21.8 %collective-permute-start.16 = (bf16[4,32,2048]{2,1,0:T(8,128)(2,1)S(1)}, bf16[4,32,2048]{2,1,0:T(8,128)(2,1)S(1)}, u32[]{:S(2)}, u32[]{:S(2)}) collective-permute-start(bf16[4,32,2048]{2,1,0:T(8,128)(2,1)S(1)} %get-tuple-element.331.refs_0_), channel_id=1, source_target_pairs={{0,1},{1,0},{2,3},{3,2},{4,5},{5,4},{6,7},{7,6},{8,9},{9,8},{10,11... | collective-permute-start | bytes 1572872 | tf_op jit(solution)/shard_map/ppermute | solution.py:65
  110.1 21.7 %collective-permute-start.17 = (bf16[4,32,2048]{2,1,0:T(8,128)(2,1)S(1)}, bf16[4,32,2048]{2,1,0:T(8,128)(2,1)S(1)}, u32[]{:S(2)}, u32[]{:S(2)}) collective-permute-start(bf16[4,32,2048]{2,1,0:T(8,128)(2,1)S(1)} %collective-permute-done.9.refs_2_), channel_id=1, source_target_pairs={{0,1},{1,0},{2,3},{3,2},{4,5},{5,4},{6,7},{7,6},{8,9},{9,8},{10,11... | collective-permute-start | bytes 1572872 | tf_op jit(solution)/shard_map/ppermute | solution.py:65
  110.5 21.3 %collective-permute-start.18 = (bf16[4,32,2048]{2,1,0:T(8,128)(2,1)S(1)}, bf16[4,32,2048]{2,1,0:T(8,128)(2,1)S(1)}, u32[]{:S(2)}, u32[]{:S(2)}) collective-permute-start(bf16[4,32,2048]{2,1,0:T(8,128)(2,1)S(1)} %collective-permute-done.4.refs_4_), channel_id=1, source_target_pairs={{0,1},{1,0},{2,3},{3,2},{4,5},{5,4},{6,7},{7,6},{8,9},{9,8},{10,11... | collective-permute-start | bytes 1572872 | tf_op jit(solution)/shard_map/ppermute | solution.py:65
  110.6 21.2 %collective-permute-start.19 = (bf16[4,32,2048]{2,1,0:T(8,128)(2,1)S(1)}, bf16[4,32,2048]{2,1,0:T(8,128)(2,1)S(1)}, u32[]{:S(2)}, u32[]{:S(2)}) collective-permute-start(bf16[4,32,2048]{2,1,0:T(8,128)(2,1)S(1)} %collective-permute-done.10.refs_6_), channel_id=1, source_target_pairs={{0,1},{1,0},{2,3},{3,2},{4,5},{5,4},{6,7},{7,6},{8,9},{9,8},{10,11... | collective-permute-start | bytes 1572872 | tf_op jit(solution)/shard_map/ppermute | solution.py:65
  131.8 16.4 %collective-permute-start.21 = (bf16[4,64,1024]{2,1,0:T(8,128)(2,1)S(1)}, bf16[4,64,1024]{2,1,0:T(8,128)(2,1)S(1)}, u32[]{:S(2)}, u32[]{:S(2)}) collective-permute-start(bf16[4,64,1024]{2,1,0:T(8,128)(2,1)S(1)} %bitcast.32), channel_id=1, source_target_pairs={{0,4},{1,5},{2,6},{3,7},{4,0},{5,1},{6,2},{7,3},{8,12},{9,13},{10,... | collective-permute-start | bytes 1572872 | tf_op jit(solution)/shard_map/ppermute | solution.py:65
  133.2 25.8 %collective-permute-start.22 = (bf16[4,64,1024]{2,1,0:T(8,128)(2,1)S(1)}, bf16[4,64,1024]{2,1,0:T(8,128)(2,1)S(1)}, u32[]{:S(2)}, u32[]{:S(2)}) collective-permute-start(bf16[4,64,1024]{2,1,0:T(8,128)(2,1)S(1)} %collective-permute-done.20.refs_2_), channel_id=1, source_target_pairs={{0,4},{1,5},{2,6},{3,7},{4,0},{5,1},{6,2},{7,3},{8,12},{9,13},{10,... | collective-permute-start | bytes 1572872 | tf_op jit(solution)/shard_map/ppermute | solution.py:65
  198.1 5.9 %collective-permute-start.29 = (bf16[512,3072]{1,0:T(8,128)(2,1)}, bf16[512,3072]{1,0:T(8,128)(2,1)S(1)}, u32[]{:S(2)}, u32[]{:S(2)}) collective-permute-start(bf16[512,3072]{1,0:T(8,128)(2,1)} %get-tuple-element.381), channel_id=1, source_target_pairs={{0,1},{1,0},{2,3},{3,2},{4,5},{5,4},{6,7},{7,6},{8,9},{9,8},{10,11... | collective-permute-start | bytes 9437192 | tf_op jit(solution)/shard_map/ppermute | solution.py:65
  198.4 10.1 %collective-permute-start.28 = (bf16[512,3072]{1,0:T(8,128)(2,1)}, bf16[512,3072]{1,0:T(8,128)(2,1)S(1)}, u32[]{:S(2)}, u32[]{:S(2)}) collective-permute-start(bf16[512,3072]{1,0:T(8,128)(2,1)} %get-tuple-element.372), channel_id=1, source_target_pairs={{0,1},{1,0},{2,3},{3,2},{4,5},{5,4},{6,7},{7,6},{8,9},{9,8},{10,11... | collective-permute-start | bytes 9437192 | tf_op jit(solution)/shard_map/ppermute | solution.py:65
  198.7 14.4 %collective-permute-start.27 = (bf16[1536,1024]{1,0:T(8,128)(2,1)}, bf16[1536,1024]{1,0:T(8,128)(2,1)S(1)}, u32[]{:S(2)}, u32[]{:S(2)}) collective-permute-start(bf16[1536,1024]{1,0:T(8,128)(2,1)} %bitcast.49), channel_id=1, source_target_pairs={{0,1},{1,0},{2,3},{3,2},{4,5},{5,4},{6,7},{7,6},{8,9},{9,8},{10,11... | collective-permute-start | bytes 9437192 | tf_op jit(solution)/shard_map/ppermute | solution.py:65
  205.6 44.7 %collective-permute-start.32 = (bf16[256,3072]{1,0:T(8,128)(2,1)}, bf16[256,3072]{1,0:T(8,128)(2,1)S(1)}, u32[]{:S(2)}, u32[]{:S(2)}) collective-permute-start(bf16[256,3072]{1,0:T(8,128)(2,1)} %get-tuple-element.408), channel_id=1, source_target_pairs={{0,8},{1,9},{2,10},{3,11},{4,12},{5,13},{6,14},{7,15},{8,0},{9,1},... | collective-permute-start | bytes 4718600 | tf_op jit(solution)/shard_map/ppermute | solution.py:65
  210.1 40.2 %collective-permute-start.31 = (bf16[256,3072]{1,0:T(8,128)(2,1)}, bf16[256,3072]{1,0:T(8,128)(2,1)S(1)}, u32[]{:S(2)}, u32[]{:S(2)}) collective-permute-start(bf16[256,3072]{1,0:T(8,128)(2,1)} %get-tuple-element.398), channel_id=1, source_target_pairs={{0,2},{1,3},{2,0},{3,1},{4,6},{5,7},{6,4},{7,5},{8,10},{9,11},{10,... | collective-permute-start | bytes 4718600 | tf_op jit(solution)/shard_map/ppermute | solution.py:65
  214.6 36.8 %collective-permute-start.30 = (bf16[768,1024]{1,0:T(8,128)(2,1)}, bf16[768,1024]{1,0:T(8,128)(2,1)S(1)}, u32[]{:S(2)}, u32[]{:S(2)}) collective-permute-start(bf16[768,1024]{1,0:T(8,128)(2,1)} %get-tuple-element.384), channel_id=1, source_target_pairs={{0,4},{1,5},{2,6},{3,7},{4,0},{5,1},{6,2},{7,3},{8,12},{9,13},{10,... | collective-permute-start | bytes 4718600 | tf_op jit(solution)/shard_map/ppermute | solution.py:65
  251.3 7.4 %collective-permute-start.34 = (bf16[512,2048]{1,0:T(8,128)(2,1)}, bf16[512,2048]{1,0:T(8,128)(2,1)S(1)}, u32[]{:S(2)}, u32[]{:S(2)}) collective-permute-start(bf16[512,2048]{1,0:T(8,128)(2,1)} %get-tuple-element.431), channel_id=1, source_target_pairs={{0,1},{1,0},{2,3},{3,2},{4,5},{5,4},{6,7},{7,6},{8,9},{9,8},{10,11... | collective-permute-start | bytes 6291464 | tf_op jit(solution)/shard_map/ppermute | solution.py:65
  253.4 47.1 %collective-permute-start.33 = (bf16[128,6144]{1,0:T(8,128)(2,1)}, bf16[128,6144]{1,0:T(8,128)(2,1)S(1)}, u32[]{:S(2)}, u32[]{:S(2)}) collective-permute-start(bf16[128,6144]{1,0:T(8,128)(2,1)} %get-tuple-element.426), channel_id=1, source_target_pairs={{0,4},{1,5},{2,6},{3,7},{4,0},{5,1},{6,2},{7,3},{8,12},{9,13},{10,... | collective-permute-start | bytes 4718600 | tf_op jit(solution)/shard_map/ppermute | solution.py:65
  256.9 43.5 %collective-permute-start.38 = (bf16[512,1024]{1,0:T(8,128)(2,1)}, bf16[512,1024]{1,0:T(8,128)(2,1)S(1)}, u32[]{:S(2)}, u32[]{:S(2)}) collective-permute-start(bf16[512,1024]{1,0:T(8,128)(2,1)} %get-tuple-element.474), channel_id=1, source_target_pairs={{0,2},{1,3},{2,0},{3,1},{4,6},{5,7},{6,4},{7,5},{8,10},{9,11},{10,... | collective-permute-start | bytes 3145736 | tf_op jit(solution)/shard_map/ppermute | solution.py:65
  260.0 42.3 %collective-permute-start.37 = (bf16[256,2048]{1,0:T(8,128)(2,1)}, bf16[256,2048]{1,0:T(8,128)(2,1)S(1)}, u32[]{:S(2)}, u32[]{:S(2)}) collective-permute-start(bf16[256,2048]{1,0:T(8,128)(2,1)} %get-tuple-element.469), channel_id=1, source_target_pairs={{0,8},{1,9},{2,10},{3,11},{4,12},{5,13},{6,14},{7,15},{8,0},{9,1},... | collective-permute-start | bytes 3145736 | tf_op jit(solution)/shard_map/ppermute | solution.py:65
  261.6 38.8 %collective-permute-start.36 = (bf16[384,1024]{1,0:T(8,128)(2,1)}, bf16[384,1024]{1,0:T(8,128)(2,1)S(1)}, u32[]{:S(2)}, u32[]{:S(2)}) collective-permute-start(bf16[384,1024]{1,0:T(8,128)(2,1)} %get-tuple-element.445), channel_id=1, source_target_pairs={{0,16},{1,17},{2,18},{3,19},{4,20},{5,21},{6,22},{7,23},{8,24},{9,... | collective-permute-start | bytes 2359304 | tf_op jit(solution)/shard_map/ppermute | solution.py:65
  307.4 26.7 %collective-permute-start.42 = (bf16[256,2176]{1,0:T(8,128)(2,1)S(1)}, bf16[256,2176]{1,0:T(8,128)(2,1)S(1)}, u32[]{:S(2)}, u32[]{:S(2)}) collective-permute-start(bf16[256,2176]{1,0:T(8,128)(2,1)S(1)} %get-tuple-element.508), channel_id=1, source_target_pairs={{0,2},{1,3},{2,0},{3,1},{4,6},{5,7},{6,4},{7,5},{8,10},{9,11},{10,... | collective-permute-start | bytes 3342344 | tf_op jit(solution)/shard_map/ppermute | solution.py:65
  308.6 27.5 %collective-permute-start.43 = (bf16[64,3072]{1,0:T(8,128)(2,1)S(1)}, bf16[64,3072]{1,0:T(8,128)(2,1)S(1)}, u32[]{:S(2)}, u32[]{:S(2)}) collective-permute-start(bf16[64,3072]{1,0:T(8,128)(2,1)S(1)} %get-tuple-element.512), channel_id=1, source_target_pairs={{0,16},{1,17},{2,18},{3,19},{4,20},{5,21},{6,22},{7,23},{8,24},{9,... | collective-permute-start | bytes 1179656 | tf_op jit(solution)/shard_map/ppermute | solution.py:65
  310.9 33.7 %collective-permute-start.45 = (bf16[256,1024]{1,0:T(8,128)(2,1)S(1)}, bf16[256,1024]{1,0:T(8,128)(2,1)S(1)}, u32[]{:S(2)}, u32[]{:S(2)}) collective-permute-start(bf16[256,1024]{1,0:T(8,128)(2,1)S(1)} %get-tuple-element.520), channel_id=1, source_target_pairs={{0,4},{1,5},{2,6},{3,7},{4,0},{5,1},{6,2},{7,3},{8,12},{9,13},{10,... | collective-permute-start | bytes 1572872 | tf_op jit(solution)/shard_map/ppermute | solution.py:65
  312.5 34.0 %collective-permute-start.44 = (bf16[128,2048]{1,0:T(8,128)(2,1)S(1)}, bf16[128,2048]{1,0:T(8,128)(2,1)S(1)}, u32[]{:S(2)}, u32[]{:S(2)}) collective-permute-start(bf16[128,2048]{1,0:T(8,128)(2,1)S(1)} %get-tuple-element.516), channel_id=1, source_target_pairs={{0,4},{1,5},{2,6},{3,7},{4,0},{5,1},{6,2},{7,3},{8,12},{9,13},{10,... | collective-permute-start | bytes 1572872 | tf_op jit(solution)/shard_map/ppermute | solution.py:65
  313.7 24.0 %collective-permute-start.40 = (bf16[64,3072]{1,0:T(8,128)(2,1)S(1)}, bf16[64,3072]{1,0:T(8,128)(2,1)S(1)}, u32[]{:S(2)}, u32[]{:S(2)}) collective-permute-start(bf16[64,3072]{1,0:T(8,128)(2,1)S(1)} %get-tuple-element.500), channel_id=1, source_target_pairs={{0,8},{1,9},{2,10},{3,11},{4,12},{5,13},{6,14},{7,15},{8,0},{9,1},... | collective-permute-start | bytes 1179656 | tf_op jit(solution)/shard_map/ppermute | solution.py:65
  334.1 10.3 %collective-permute-start.39 = (bf16[192,1024]{1,0:T(8,128)(2,1)S(1)}, bf16[192,1024]{1,0:T(8,128)(2,1)S(1)}, u32[]{:S(2)}, u32[]{:S(2)}) collective-permute-start(bf16[192,1024]{1,0:T(8,128)(2,1)S(1)} %get-tuple-element.492), channel_id=1, source_target_pairs={{0,8},{1,9},{2,10},{3,11},{4,12},{5,13},{6,14},{7,15},{8,0},{9,1},... | collective-permute-start | bytes 1179656 | tf_op jit(solution)/shard_map/ppermute | solution.py:65
  336.1 14.1 %collective-permute-start.46 = (bf16[128,2176]{1,0:T(8,128)(2,1)S(1)}, bf16[128,2176]{1,0:T(8,128)(2,1)S(1)}, u32[]{:S(2)}, u32[]{:S(2)}) collective-permute-start(bf16[128,2176]{1,0:T(8,128)(2,1)S(1)} %get-tuple-element.523), channel_id=1, source_target_pairs={{0,4},{1,5},{2,6},{3,7},{4,0},{5,1},{6,2},{7,3},{8,12},{9,13},{10,... | collective-permute-start | bytes 1671176 | tf_op jit(solution)/shard_map/ppermute | solution.py:65
  344.8 7.3 %collective-permute-start.51 = (bf16[128,1024]{1,0:T(8,128)(2,1)S(1)}, bf16[128,1024]{1,0:T(8,128)(2,1)S(1)}, u32[]{:S(2)}, u32[]{:S(2)}) collective-permute-start(bf16[128,1024]{1,0:T(8,128)(2,1)S(1)} %get-tuple-element.541), channel_id=1, source_target_pairs={{0,8},{1,9},{2,10},{3,11},{4,12},{5,13},{6,14},{7,15},{8,0},{9,1},... | collective-permute-start | bytes 786440 | tf_op jit(solution)/shard_map/ppermute | solution.py:65
  346.7 9.3 %collective-permute-start.47 = (bf16[64,2048]{1,0:T(8,128)(2,1)S(1)}, bf16[64,2048]{1,0:T(8,128)(2,1)S(1)}, u32[]{:S(2)}, u32[]{:S(2)}) collective-permute-start(bf16[64,2048]{1,0:T(8,128)(2,1)S(1)} %get-tuple-element.527), channel_id=1, source_target_pairs={{0,2},{1,3},{2,0},{3,1},{4,6},{5,7},{6,4},{7,5},{8,10},{9,11},{10,... | collective-permute-start | bytes 786440 | tf_op jit(solution)/shard_map/ppermute | solution.py:65
  348.2 11.2 %collective-permute-start.54 = (bf16[32,3072]{1,0:T(8,128)(2,1)S(1)}, bf16[32,3072]{1,0:T(8,128)(2,1)S(1)}, u32[]{:S(2)}, u32[]{:S(2)}) collective-permute-start(bf16[32,3072]{1,0:T(8,128)(2,1)S(1)} %get-tuple-element.548), channel_id=1, source_target_pairs={{0,2},{1,3},{2,0},{3,1},{4,6},{5,7},{6,4},{7,5},{8,10},{9,11},{10,... | collective-permute-start | bytes 589832 | tf_op jit(solution)/shard_map/ppermute | solution.py:65
  348.8 16.3 %collective-permute-start.55 = (bf16[96,1024]{1,0:T(8,128)(2,1)S(1)}, bf16[96,1024]{1,0:T(8,128)(2,1)S(1)}, u32[]{:S(2)}, u32[]{:S(2)}) collective-permute-start(bf16[96,1024]{1,0:T(8,128)(2,1)S(1)} %get-tuple-element.550), channel_id=1, source_target_pairs={{0,2},{1,3},{2,0},{3,1},{4,6},{5,7},{6,4},{7,5},{8,10},{9,11},{10,... | collective-permute-start | bytes 589832 | tf_op jit(solution)/shard_map/ppermute | solution.py:65
  350.2 14.1 %collective-permute-start.53 = (bf16[32,3072]{1,0:T(8,128)(2,1)S(1)}, bf16[32,3072]{1,0:T(8,128)(2,1)S(1)}, u32[]{:S(2)}, u32[]{:S(2)}) collective-permute-start(bf16[32,3072]{1,0:T(8,128)(2,1)S(1)} %get-tuple-element.546), channel_id=1, source_target_pairs={{0,16},{1,17},{2,18},{3,19},{4,20},{5,21},{6,22},{7,23},{8,24},{9,... | collective-permute-start | bytes 589832 | tf_op jit(solution)/shard_map/ppermute | solution.py:65
  352.1 18.8 %collective-permute-start.52 = (bf16[64,1024]{1,0:T(8,128)(2,1)S(1)}, bf16[64,1024]{1,0:T(8,128)(2,1)S(1)}, u32[]{:S(2)}, u32[]{:S(2)}) collective-permute-start(bf16[64,1024]{1,0:T(8,128)(2,1)S(1)} %get-tuple-element.543), channel_id=1, source_target_pairs={{0,16},{1,17},{2,18},{3,19},{4,20},{5,21},{6,22},{7,23},{8,24},{9,... | collective-permute-start | bytes 393224 | tf_op jit(solution)/shard_map/ppermute | solution.py:65
  356.0 11.4 %collective-permute-start.49 = (bf16[64,2176]{1,0:T(8,128)(2,1)S(1)}, bf16[64,2176]{1,0:T(8,128)(2,1)S(1)}, u32[]{:S(2)}, u32[]{:S(2)}) collective-permute-start(bf16[64,2176]{1,0:T(8,128)(2,1)S(1)} %get-tuple-element.531), channel_id=1, source_target_pairs={{0,8},{1,9},{2,10},{3,11},{4,12},{5,13},{6,14},{7,15},{8,0},{9,1},... | collective-permute-start | bytes 835592 | tf_op jit(solution)/shard_map/ppermute | solution.py:65
  359.4 15.8 %collective-permute-start.48 = (bf16[32,2048]{1,0:T(8,128)(2,1)S(1)}, bf16[32,2048]{1,0:T(8,128)(2,1)S(1)}, u32[]{:S(2)}, u32[]{:S(2)}) collective-permute-start(bf16[32,2048]{1,0:T(8,128)(2,1)S(1)} %get-tuple-element.529), channel_id=1, source_target_pairs={{0,16},{1,17},{2,18},{3,19},{4,20},{5,21},{6,22},{7,23},{8,24},{9,... | collective-permute-start | bytes 393224 | tf_op jit(solution)/shard_map/ppermute | solution.py:65
  368.2 8.7 %collective-permute-start.50 = (bf16[32,2176]{1,0:T(8,128)(2,1)S(1)}, bf16[32,2176]{1,0:T(8,128)(2,1)S(1)}, u32[]{:S(2)}, u32[]{:S(2)}) collective-permute-start(bf16[32,2176]{1,0:T(8,128)(2,1)S(1)} %get-tuple-element.533), channel_id=1, source_target_pairs={{0,16},{1,17},{2,18},{3,19},{4,20},{5,21},{6,22},{7,23},{8,24},{9,... | collective-permute-start | bytes 417800 | tf_op jit(solution)/shard_map/ppermute | solution.py:65
  (72 other events, 1038.2 us)
Sparse Core Ops, SparseCore 0:
  10.9 160.0 all-gather.2

commit v8 on v7

--- a/solution.py
+++ b/solution.py
@@ -774,8 +774,8 @@
 
 def feed_forward_body(
     device_ref, residual_ref, gain_ref, cotangent_ref, gate_ref, up_ref, down_ref,
-    hidden_ref, grad_gate_ref, grad_up_ref, gate_kept_ref, gate_sent_ref, up_kept_ref, up_sent_ref,
-    down_kept_ref, down_sent_ref, normed_ref, down_weight_ref, turned_ref, for_gate_ref, for_up_ref, product_ref,
+    hidden_ref, grad_gate_ref, grad_up_ref, gate_kept_ref, gate_sent_ref, for_up_ref,
+    down_kept_ref, down_sent_ref, normed_ref, down_weight_ref, turned_ref, for_gate_ref, product_ref,
     *, gate_order, up_order,
 ):
     device = device_ref[0]
@@ -813,14 +813,10 @@
     grad_up = (grad_hidden * silu).astype(jnp.bfloat16)
     grad_up_ref[...] = grad_up
 
-    for ordered_ref, grad, kept_ref, sent_ref in (
-        (for_gate_ref, grad_gate, gate_kept_ref, gate_sent_ref),
-        (for_up_ref, grad_up, up_kept_ref, up_sent_ref),
-    ):
-        product = jnp.dot(ordered_ref[...], grad, preferred_element_type=jnp.float32).astype(jnp.bfloat16)
-        half = product.shape[0] // 2
-        kept_ref[...] = product[:half]
-        sent_ref[...] = product[half:]
+    product = jnp.dot(for_gate_ref[...], grad_gate, preferred_element_type=jnp.float32).astype(jnp.bfloat16)
+    half = product.shape[0] // 2
+    gate_kept_ref[...] = product[:half]
+    gate_sent_ref[...] = product[half:]
     product_ref[...] = contract(hidden, cotangent, 0, 0).reshape(product_ref.shape)
     owners = product_ref.shape[0]
     low = device & (owners - 1)
@@ -873,8 +869,7 @@
                 columns(rows),
                 columns(width // 2),
                 columns(width // 2),
-                columns(width // 2),
-                columns(width // 2),
+                pl.BlockSpec((width, rows), lambda j, d: (0, 0)),
                 down_half,
                 down_half,
             ],
@@ -882,7 +877,6 @@
                 pltpu.VMEM((rows, width), jnp.bfloat16),
                 pltpu.VMEM((tile, width), jnp.bfloat16),
                 pltpu.VMEM((width, rows), jnp.bfloat16 if shard % 16 == 0 else jnp.float32),
-                pltpu.VMEM((width, rows), jnp.bfloat16),
                 pltpu.VMEM((width, rows), jnp.bfloat16),
                 pltpu.VMEM((owners, tile // owners, width), jnp.float32),
             ],
@@ -893,8 +887,7 @@
             far((rows, hidden_width), jnp.bfloat16),
             low(width // 2, hidden_width),
             low(width // 2, hidden_width),
-            low(width // 2, hidden_width),
-            low(width // 2, hidden_width),
+            low(width, rows),
             low4,
             low4,
         ],
@@ -903,6 +896,30 @@
         name="feed_forward",
     )(device.reshape(1), residual, gain, *from_far(cotangent, *weight_args))
     return *out, down_kept.reshape(-1, width), down_sent.reshape(-1, width)
+
+
+def product_body(left_ref, right_ref, kept_ref, sent_ref):
+    product = jnp.dot(left_ref[...], right_ref[...], preferred_element_type=jnp.float32).astype(jnp.bfloat16)
+    half = product.shape[0] // 2
+    kept_ref[...] = product[:half]
+    sent_ref[...] = product[half:]
+
+
+def product_halves(left, right):
+    rows, depth = left.shape
+    columns = right.shape[1]
+    tile = min(columns, 768)
+    half = jax.ShapeDtypeStruct((rows // 2, columns), jnp.bfloat16)
+    return pl.pallas_call(
+        product_body,
+        grid=(columns // tile,),
+        in_specs=[pl.BlockSpec((rows, depth), lambda j: (0, 0)), pl.BlockSpec((depth, tile), lambda j: (0, j))],
+        out_specs=[pl.BlockSpec((rows // 2, tile), lambda j: (0, j))] * 2,
+        out_shape=[half, half],
+        compiler_params=pltpu.CompilerParams(vmem_limit_bytes=20 * 1024 * 1024),
+        cost_estimate=SMALL,
+        name="product_halves",
+    )(left, right)
 
 
 FFN_STEPS = 4
@@ -1107,7 +1124,12 @@
     attended_second, *saved_second = attend(device, normed_low, second_weight, head_gains, cosine, sine, first_row)
     stages = sum_bits(count)
     orders = {name: row_order(count, bits) for name, bits in stages.items()}
-    attended_first, attended_second, out_parts = fence((attended_first, attended_second, out_parts))
+    turned = dict(
+        out=turn((attended_first, attended_second), device, orders["out"]),
+        first=turn((normed_low,), device, orders["first"]),
+        second=turn((normed_low,), device, orders["second"]),
+    )
+    attended_first, attended_second, out_parts, turned = fence((attended_first, attended_second, out_parts, turned))
     out_parts = gather_bits(out_parts, count, [0])
     residual, out_weight = project(
         device,
@@ -1117,13 +1139,13 @@
         attended_second,
     )
     (
-        hidden, grad_gate, grad_up, gate_kept, gate_sent, up_kept, up_sent, down_kept, down_sent
+        hidden, grad_gate, grad_up, gate_kept, gate_sent, turned_up, down_kept, down_sent
     ) = feed_forward(
         device, residual, gain_two, cotangent, ffn_weights, shard, orders["gate"], orders["up"]
     )
 
     live = dict(
-        hidden=hidden, grad_gate=grad_gate, grad_up=grad_up, gate=gate_kept, up=up_kept, down=down_kept,
+        hidden=hidden, grad_gate=grad_gate, grad_up=grad_up, gate=gate_kept, down=down_kept, turned_up=turned_up,
     )
     flying = {}
 
@@ -1149,15 +1171,11 @@
     def operands(name, saved):
         return *from_far(out_weight, *saved), head_gains, cosine, sine, first_row, *from_far(turned[name])
 
-    live.update(attended_first=attended_first, attended_second=attended_second, normed=normed_low)
-    fly(down=down_sent, gate=gate_sent, up=up_sent)
-    live["turned"] = dict(
-        out=turn((live.pop("attended_first"), live.pop("attended_second")), device, orders["out"]),
-        first=turn((live["normed"],), device, orders["first"]),
-        second=turn((live.pop("normed"),), device, orders["second"]),
-    )
-    cut()
-    relay("up", "gate", "down")
+    live["turned"] = turned
+    fly(down=down_sent, gate=gate_sent)
+    live["up"], up_sent = product_halves(live.pop("turned_up"), live["grad_up"])
+    fly(up=up_sent)
+    relay("down", "gate", "up")
     cut()
     turned = live.pop("turned")
     (
@@ -1189,12 +1207,11 @@
     both = flying.pop("both")
     flying.update(gate=both, up=both)
     mixed, grad_tokens = live.pop("mixed"), live.pop("grad_tokens")
-    relay("down", "gate", "up", places=(0, 0, 1))
+    relay("up", "gate", places=(1, 0))
     relay("first", "out")
-    relay("down", "gate", "up")
+    relay("up", "gate")
     relay("second")
-    cut()
-    relay("first", "out", "second")
+    relay("down")
     cut()
     while any(stages.values()):
         for name in ("second", "first", "out", "down", "gate", "up"):

time: 387 us -> 388 us (level)
    pallas_call x0 -> x1, Pallas kernels: none -> 4.61 us  [product_halves(): pl.pallas_call(product_body, grid=(columns // tile,), in_specs=[pl.BlockS...]
  transfers between devices with their start and end apart: 57 -> 57, of which waited for: 39 -> 31; matrix products, arithmetic and copies ran while one was open for 2% -> 2% of each run, Pallas kernels for 28% -> 29%
where the time goes in v8:
time: 388 us; the launch traced here: 384 us
  waiting for transfers between devices  160 us (41%)
  Pallas kernels  140 us (36%)
  starting transfers between devices  55.7 us (14%)
  between operations  15.1 us (4%)
  local copies, waits for them, and re-layouts  8.15 us (2%)
  other arithmetic  5.16 us (1%)
    ppermute x56, waiting for transfers between devices, exchange(): lax.ppermute(values, 'fsdp', [(source, source ^ mask) for source in range...  160 us
    ppermute x56, starting transfers between devices, exchange(): lax.ppermute(values, 'fsdp', [(source, source ^ mask) for source in range...  55.6 us
    pallas_call x1, Pallas kernels, back(): pl.pallas_call(functools.partial(back_body, parts=len(parts)), grid_spec=...  34.1 us
    pallas_call x1, Pallas kernels, attend_back_last(): pl.pallas_call(functools.partial(attend_back_body, order=order, shard=sha...  26.2 us
    pallas_call x1, Pallas kernels, feed_forward(): pl.pallas_call(functools.partial(feed_forward_body, gate_order=gate_order...  23.3 us
    pallas_call x2, Pallas kernels, attend(): pl.pallas_call(attend_body, grid_spec=pltpu.PrefetchScalarGridSpec(num_sc...  21.2 us
    pallas_call x23, Pallas kernels, fold(): pl.pallas_call(functools.partial(fold_body, pairs=len(pairs), merged=merg...  13 us
  transfers between devices with their start and end apart: 57, of which 31 were waited for; matrix products, arithmetic and copies ran while one was open for 2% of the time, Pallas kernels for 29%

profile of v8, /device:TPU:0, one launch (start us, length us, event | category | flops | bytes accessed | tf_op | source)
XLA Modules:
  0.0 384.4 jit_solution(2447457312785459822)
XLA Ops:
  7.3 2.0 stack.1
  11.4 1.7 join.1
  13.0 4.0 %collective-permute-start.1 = (bf16[32,4224]{1,0:T(8,128)(2,1)}, bf16[32,4224]{1,0:T(8,128)(2,1)S(1)}, u32[]{:S(2)}, u32[]{:S(2)}) collective-permute-start(bf16[32,4224]{1,0:T(8,128)(2,1)} %join.1), channel_id=1, source_target_pairs={{0,16},{1,17},{2,18},{3,19},{4,20},{5,21},{6,22},{7,23},{8,24},{9,... | collective-permute-start | bytes 811016 | tf_op jit(solution)/shard_map/ppermute | solution.py:65
  17.1 1.6 collective-permute-start
  18.9 16.1 %collective-permute-done.1 = bf16[32,4224]{1,0:T(8,128)(2,1)S(1)} collective-permute-done((bf16[32,4224]{1,0:T(8,128)(2,1)}, bf16[32,4224]{1,0:T(8,128)(2,1)S(1)}, u32[]{:S(2)}, u32[]{:S(2)}) %collective-permute-start.1) | collective-permute-done | bytes 270368 | tf_op jit(solution)/shard_map/ppermute | solution.py:65
  35.6 4.0 %collective-permute-start.2 = (bf16[32,4224]{1,0:T(8,128)(2,1)S(1)}, bf16[32,4224]{1,0:T(8,128)(2,1)S(1)}, u32[]{:S(2)}, u32[]{:S(2)}) collective-permute-start(bf16[32,4224]{1,0:T(8,128)(2,1)S(1)} %collective-permute-done.1), channel_id=1, source_target_pairs={{0,8},{1,9},{2,10},{3,11},{4,12},{5,13},{6,14},{7,15},{8,0},{9,1},... | collective-permute-start | bytes 811016 | tf_op jit(solution)/shard_map/ppermute | solution.py:65
  39.7 8.5 %collective-permute-done.2 = bf16[32,4224]{1,0:T(8,128)(2,1)S(1)} collective-permute-done((bf16[32,4224]{1,0:T(8,128)(2,1)S(1)}, bf16[32,4224]{1,0:T(8,128)(2,1)S(1)}, u32[]{:S(2)}, u32[]{:S(2)}) %collective-permute-start.2) | collective-permute-done | bytes 270368 | tf_op jit(solution)/shard_map/ppermute | solution.py:65
  50.4 1.6 collective-permute-start.4
  54.3 1.9 collective-permute-start.6
  56.2 1.7 collective-permute-start.5
  58.3 11.3 %collective-permute-done.6 = bf16[64,1024]{1,0:T(8,128)(2,1)S(1)} collective-permute-done((bf16[64,1024]{1,0:T(8,128)(2,1)S(1)}, bf16[64,1024]{1,0:T(8,128)(2,1)S(1)}, u32[]{:S(2)}, u32[]{:S(2)}) %collective-permute-start.6) | collective-permute-done | bytes 131104 | tf_op jit(solution)/shard_map/ppermute | solution.py:65
  70.3 1.6 collective-permute-done.4.refs_4_
  71.9 7.1 %collective-permute-done.3.refs_2_.refs_21_ = bf16[4,32,2176]{2,1,0:T(8,128)(2,1)S(1)} collective-permute-done((bf16[4,32,2176]{2,1,0:T(8,128)(2,1)S(1)}, bf16[4,32,2176]{2,1,0:T(8,128)(2,1)S(1)}, u32[]{:S(2)}, u32[]{:S(2)}) %collective-permute-start.3) | collective-permute-done | bytes 557088 | tf_op jit(solution)/shard_map/ppermute | solution.py:65
  79.3 1.6 collective-permute-start.8
  84.3 9.9 %collective-permute-done.11 = bf16[64,1024]{1,0:T(8,128)(2,1)S(1)} collective-permute-done((bf16[64,1024]{1,0:T(8,128)(2,1)S(1)}, bf16[64,1024]{1,0:T(8,128)(2,1)S(1)}, u32[]{:S(2)}, u32[]{:S(2)}) %collective-permute-start.11) | collective-permute-done | bytes 131104 | tf_op jit(solution)/shard_map/ppermute | solution.py:65
  94.2 1.6 collective-permute-done.9.refs_2_
  95.8 14.0 %collective-permute-done.10.refs_6_ = bf16[4,32,2048]{2,1,0:T(8,128)(2,1)S(1)} collective-permute-done((bf16[4,32,2048]{2,1,0:T(8,128)(2,1)S(1)}, bf16[4,32,2048]{2,1,0:T(8,128)(2,1)S(1)}, u32[]{:S(2)}, u32[]{:S(2)}) %collective-permute-start.10) | collective-permute-done | bytes 524320 | tf_op jit(solution)/shard_map/ppermute | solution.py:65
  112.1 2.5 collective-permute-start.20
  117.2 11.2 %attend.2 = (bf16[384,1024]{1,0:T(8,128)(2,1)S(1)}, bf16[384,1024]{1,0:T(8,128)(2,1)}, bf16[384,512]{1,0:T(8,128)(2,1)}, bf16[384,512]{1,0:T(8,128)(2,1)}, f32[384,1536]{1,0:T(8,128)}, /*index=5*/f32[4,384,2]{2,1,0:T(8,128)}) custom-call(s32[1]{0:T(128)} %bitcast.device_ref, bf16[4,32,2176]{2,1,0:T(8,128)(2,1)S(1)} %get-tuple-element.306.refs_0_.refs_19_, ...), custom_call_target="tpu_custom_call" | custom-call | flops 1 | bytes 1 | tf_op jit(solution)/shard_map/attend/pallas_call | solution.py:474
  128.4 10.0 %collective-permute-done.20.refs_2_ = bf16[4,64,1024]{2,1,0:T(8,128)(2,1)S(1)} collective-permute-done((bf16[4,64,1024]{2,1,0:T(8,128)(2,1)S(1)}, bf16[4,64,1024]{2,1,0:T(8,128)(2,1)S(1)}, u32[]{:S(2)}, u32[]{:S(2)}) %collective-permute-start.20) | collective-permute-done | bytes 524320 | tf_op jit(solution)/shard_map/ppermute | solution.py:65
  138.6 2.0 collective-permute-start.22
  143.0 10.0 %attend.3 = (bf16[384,1024]{1,0:T(8,128)(2,1)S(1)}, bf16[384,1024]{1,0:T(8,128)(2,1)}, bf16[384,512]{1,0:T(8,128)(2,1)}, bf16[384,512]{1,0:T(8,128)(2,1)}, f32[384,1536]{1,0:T(8,128)}, /*index=5*/f32[4,384,2]{2,1,0:T(8,128)}) custom-call(s32[1]{0:T(128)} %bitcast.device_ref, bf16[4,32,2048]{2,1,0:T(8,128)(2,1)S(1)} %get-tuple-element.329.refs_0_, ...), custom_call_target="tpu_custom_call" | custom-call | flops 1 | bytes 1 | tf_op jit(solution)/shard_map/attend/pallas_call | solution.py:474
  153.0 1.8 turn.4.refs_7_
  154.8 8.4 %collective-permute-done.22.refs_6_ = bf16[4,64,1024]{2,1,0:T(8,128)(2,1)S(1)} collective-permute-done((bf16[4,64,1024]{2,1,0:T(8,128)(2,1)S(1)}, bf16[4,64,1024]{2,1,0:T(8,128)(2,1)S(1)}, u32[]{:S(2)}, u32[]{:S(2)}) %collective-permute-start.22) | collective-permute-done | bytes 524320 | tf_op jit(solution)/shard_map/ppermute | solution.py:65
  168.8 5.0 %project.1 = (f32[384,1024]{1,0:T(8,128)}, bf16[4,8,64,1024]{3,2,1,0:T(8,128)(2,1)}) custom-call(s32[1]{0:T(128)} %bitcast.device_ref, bf16[4,64,1024]{2,1,0:T(8,128)(2,1)S(1)} %bitcast.34, bf16[4,64,1024]{2,1,0:T(8,128)(2,1)S(1)} %collective-permute-done.23.refs_1_, bf16[4,64,1024]{2,1,0:T(8,128)(2,1)S(1)} %collective-permute-done.20.refs_2_, ...), custom_call_target="tpu_custom_call" | custom-call | flops 1 | bytes 1 | tf_op jit(solution)/shard_map/project/pallas_call | solution.py:742
  173.8 23.3 %feed_forward.1 = (bf16[384,3072]{1,0:T(8,128)(2,1)}, bf16[384,3072]{1,0:T(8,128)(2,1)}, bf16[384,3072]{1,0:T(8,128)(2,1)}, bf16[512,3072]{1,0:T(8,128)(2,1)}, b...) custom-call(s32[1]{0:T(128)} %bitcast.device_ref, ...), custom_call_target="tpu_custom_call" | custom-call | flops 1 | bytes 1 | tf_op jit(solution)/shard_map/feed_forward/pallas_call | solution.py:860
  197.6 2.0 copy-done.2
  200.7 4.6 %product_halves.1 = (bf16[512,3072]{1,0:T(8,128)(2,1)S(1)}, bf16[512,3072]{1,0:T(8,128)(2,1)S(1)}) custom-call(bf16[1024,384]{1,0:T(8,128)(2,1)S(1)} %copy-done.43, bf16[384,3072]{1,0:T(8,128)(2,1)S(1)} %copy-done.2), custom_call_target="tpu_custom_call" | custom-call | flops 1 | bytes 1 | tf_op jit(solution)/shard_map/product_halves/pallas_call | solution.py:913
  205.5 2.0 collective-permute-done.28.refs_2_.refs_3_
  207.5 1.6 fold.24
  214.9 34.1 %back.1 = (f32[384,1024]{1,0:T(8,128)}, bf16[384,1024]{1,0:T(8,128)(2,1)}, f32[1,1024]{1,0:T(1,128)S(1)}, bf16[1024,1024]{1,0:T(8,128)(2,1)}, bf16[1024,1024]{1,...) custom-call(s32[1]{0:T(128)} %bitcast.device_ref, ...), custom_call_target="tpu_custom_call" | custom-call | flops 1 | bytes 1 | tf_op jit(solution)/shard_map/back/pallas_call | solution.py:989
  252.2 1.7 collective-permute-start.33
  261.8 26.2 %attend_back_last.1 = (bf16[512,2176]{1,0:T(8,128)(2,1)S(1)}, bf16[512,2176]{1,0:T(8,128)(2,1)}, bf16[384,1024]{1,0:T(8,128)(2,1)}, bf16[384,1024]{1,0:T(8,128)(2,1)}) custom-call(s32[1]{0:T(128)} %bitcast.device_ref, bf16[384,1024]{1,0:T(8,128)(2,1)S(1)} %copy-done.44, bf16[2048,1024]{1,0:T(8,128)(2,1)} %bitcast.42, ...), custom_call_target="tpu_custom_call" | custom-call | flops 1 | bytes 1 | tf_op jit(solution)/shard_map/attend_back_last/pallas_call | solution.py:684
  288.0 10.6 %collective-permute-done.36.refs_2_.refs_3_ = bf16[384,1024]{1,0:T(8,128)(2,1)S(1)} collective-permute-done((bf16[384,1024]{1,0:T(8,128)(2,1)}, bf16[384,1024]{1,0:T(8,128)(2,1)S(1)}, u32[]{:S(2)}, u32[]{:S(2)}) %collective-permute-start.36) | collective-permute-done | bytes 786464 | tf_op jit(solution)/shard_map/ppermute | solution.py:65
  298.7 4.5 %collective-permute-done.40.refs_2_.refs_3_ = bf16[512,2176]{1,0:T(8,128)(2,1)S(1)} collective-permute-done((bf16[512,2176]{1,0:T(8,128)(2,1)}, bf16[512,2176]{1,0:T(8,128)(2,1)S(1)}, u32[]{:S(2)}, u32[]{:S(2)}) %collective-permute-start.40) | collective-permute-done | bytes 2228256 | tf_op jit(solution)/shard_map/ppermute | solution.py:65
  307.4 1.6 collective-permute-start.49
  310.0 14.2 %collective-permute-done.39.refs_2_.refs_3_ = bf16[64,3072]{1,0:T(8,128)(2,1)S(1)} collective-permute-done((bf16[64,3072]{1,0:T(8,128)(2,1)S(1)}, bf16[64,3072]{1,0:T(8,128)(2,1)S(1)}, u32[]{:S(2)}, u32[]{:S(2)}) %collective-permute-start.39) | collective-permute-done | bytes 393248 | tf_op jit(solution)/shard_map/ppermute | solution.py:65
  325.7 4.7 %collective-permute-done.41.refs_2_.refs_3_ = bf16[256,2176]{1,0:T(8,128)(2,1)S(1)} collective-permute-done((bf16[256,2176]{1,0:T(8,128)(2,1)S(1)}, bf16[256,2176]{1,0:T(8,128)(2,1)S(1)}, u32[]{:S(2)}, u32[]{:S(2)}) %collective-permute-start.41) | collective-permute-done | bytes 1114144 | tf_op jit(solution)/shard_map/ppermute | solution.py:65
  331.5 6.9 %collective-permute-done.54.refs_2_.refs_3_ = bf16[192,1024]{1,0:T(8,128)(2,1)S(1)} collective-permute-done((bf16[192,1024]{1,0:T(8,128)(2,1)S(1)}, bf16[192,1024]{1,0:T(8,128)(2,1)S(1)}, u32[]{:S(2)}, u32[]{:S(2)}) %collective-permute-start.54) | collective-permute-done | bytes 393248 | tf_op jit(solution)/shard_map/ppermute | solution.py:65
  341.1 1.6 collective-permute-start.46
  343.5 10.5 %collective-permute-done.46.refs_2_.refs_3_ = bf16[128,2176]{1,0:T(8,128)(2,1)S(1)} collective-permute-done((bf16[128,2176]{1,0:T(8,128)(2,1)S(1)}, bf16[128,2176]{1,0:T(8,128)(2,1)S(1)}, u32[]{:S(2)}, u32[]{:S(2)}) %collective-permute-start.46) | collective-permute-done | bytes 557088 | tf_op jit(solution)/shard_map/ppermute | solution.py:65
  354.1 1.8 collective-permute-start.47
  359.3 2.0 collective-permute-start.45
  361.3 1.8 collective-permute-done.47.refs_2_.refs_3_
  363.9 2.9 collective-permute-start.48
  366.9 2.8 collective-permute-done.51
  370.4 2.9 collective-permute-done.45.first_came
  375.4 1.9 end_projections.1
  (243 shorter events, 62.0 us)
Async XLA Ops:
  7.2 166.5 %all-gather.3.cloned.1.call-start = ((), (), s32[]{:S(2)}) async-start(), calls=%async_computation | async-start | bytes 19464192 | tf_op jit(solution)/shard_map/all_gather | solution.py:1091
  13.0 21.9 %collective-permute-start.1 = (bf16[32,4224]{1,0:T(8,128)(2,1)}, bf16[32,4224]{1,0:T(8,128)(2,1)S(1)}, u32[]{:S(2)}, u32[]{:S(2)}) collective-permute-start(bf16[32,4224]{1,0:T(8,128)(2,1)} %join.1), channel_id=1, source_target_pairs={{0,16},{1,17},{2,18},{3,19},{4,20},{5,21},{6,22},{7,23},{8,24},{9,... | collective-permute-start | bytes 811016 | tf_op jit(solution)/shard_map/ppermute | solution.py:65
  17.1 18.5 %collective-permute-start = (bf16[32,4224]{1,0:T(8,128)(2,1)}, bf16[32,4224]{1,0:T(8,128)(2,1)S(1)}, u32[]{:S(2)}, u32[]{:S(2)}) collective-permute-start(bf16[32,4224]{1,0:T(8,128)(2,1)} %join.1), channel_id=1, source_target_pairs={{0,8},{1,9},{2,10},{3,11},{4,12},{5,13},{6,14},{7,15},{8,0},{9,1},... | collective-permute-start | bytes 811016 | tf_op jit(solution)/shard_map/ppermute | solution.py:65
  35.6 12.7 %collective-permute-start.2 = (bf16[32,4224]{1,0:T(8,128)(2,1)S(1)}, bf16[32,4224]{1,0:T(8,128)(2,1)S(1)}, u32[]{:S(2)}, u32[]{:S(2)}) collective-permute-start(bf16[32,4224]{1,0:T(8,128)(2,1)S(1)} %collective-permute-done.1), channel_id=1, source_target_pairs={{0,8},{1,9},{2,10},{3,11},{4,12},{5,13},{6,14},{7,15},{8,0},{9,1},... | collective-permute-start | bytes 811016 | tf_op jit(solution)/shard_map/ppermute | solution.py:65
  50.4 21.4 %collective-permute-start.4 = (bf16[4,32,2048]{2,1,0:T(8,128)(2,1)S(1)}, bf16[4,32,2048]{2,1,0:T(8,128)(2,1)S(1)}, u32[]{:S(2)}, u32[]{:S(2)}) collective-permute-start(bf16[4,32,2048]{2,1,0:T(8,128)(2,1)S(1)} %get-tuple-element.329.refs_0_), channel_id=1, source_target_pairs={{0,4},{1,5},{2,6},{3,7},{4,0},{5,1},{6,2},{7,3},{8,12},{9,13},{10,... | collective-permute-start | bytes 1572872 | tf_op jit(solution)/shard_map/ppermute | solution.py:65
  52.0 26.9 %collective-permute-start.3 = (bf16[4,32,2176]{2,1,0:T(8,128)(2,1)S(1)}, bf16[4,32,2176]{2,1,0:T(8,128)(2,1)S(1)}, u32[]{:S(2)}, u32[]{:S(2)}) collective-permute-start(bf16[4,32,2176]{2,1,0:T(8,128)(2,1)S(1)} %get-tuple-element.306.refs_0_.refs_19_), channel_id=1, source_target_pairs={{0,2},{1,3},{2,0},{3,1},{4,6},{5,7},{6,4},{7,5},{8,10},{9,11},{10,... | collective-permute-start | bytes 1671176 | tf_op jit(solution)/shard_map/ppermute | solution.py:65
  54.3 15.2 %collective-permute-start.6 = (bf16[64,1024]{1,0:T(8,128)(2,1)S(1)}, bf16[64,1024]{1,0:T(8,128)(2,1)S(1)}, u32[]{:S(2)}, u32[]{:S(2)}) collective-permute-start(bf16[64,1024]{1,0:T(8,128)(2,1)S(1)} %copy-done.54), channel_id=1, source_target_pairs={{0,16},{1,17},{2,18},{3,19},{4,20},{5,21},{6,22},{7,23},{8,24},{9,... | collective-permute-start | bytes 393224 | tf_op jit(solution)/shard_map/ppermute | solution.py:65
  56.2 14.1 %collective-permute-start.5 = (bf16[64,1024]{1,0:T(8,128)(2,1)S(1)}, bf16[64,1024]{1,0:T(8,128)(2,1)S(1)}, u32[]{:S(2)}, u32[]{:S(2)}) collective-permute-start(bf16[64,1024]{1,0:T(8,128)(2,1)S(1)} %copy-done.54), channel_id=1, source_target_pairs={{0,8},{1,9},{2,10},{3,11},{4,12},{5,13},{6,14},{7,15},{8,0},{9,1},... | collective-permute-start | bytes 393224 | tf_op jit(solution)/shard_map/ppermute | solution.py:65
  78.9 30.9 %collective-permute-start.7 = (bf16[4,32,2176]{2,1,0:T(8,128)(2,1)S(1)}, bf16[4,32,2176]{2,1,0:T(8,128)(2,1)S(1)}, u32[]{:S(2)}, u32[]{:S(2)}) collective-permute-start(bf16[4,32,2176]{2,1,0:T(8,128)(2,1)S(1)} %get-tuple-element.306.refs_0_.refs_19_), channel_id=1, source_target_pairs={{0,4},{1,5},{2,6},{3,7},{4,0},{5,1},{6,2},{7,3},{8,12},{9,13},{10,... | collective-permute-start | bytes 1671176 | tf_op jit(solution)/shard_map/ppermute | solution.py:65
  79.3 30.5 %collective-permute-start.8 = (bf16[4,32,2176]{2,1,0:T(8,128)(2,1)S(1)}, bf16[4,32,2176]{2,1,0:T(8,128)(2,1)S(1)}, u32[]{:S(2)}, u32[]{:S(2)}) collective-permute-start(bf16[4,32,2176]{2,1,0:T(8,128)(2,1)S(1)} %collective-permute-done.3.refs_2_.refs_21_), channel_id=1, source_target_pairs={{0,4},{1,5},{2,6},{3,7},{4,0},{5,1},{6,2},{7,3},{8,12},{9,13},{10,... | collective-permute-start | bytes 1671176 | tf_op jit(solution)/shard_map/ppermute | solution.py:65
  81.0 14.9 %collective-permute-start.9 = (bf16[4,32,2048]{2,1,0:T(8,128)(2,1)S(1)}, bf16[4,32,2048]{2,1,0:T(8,128)(2,1)S(1)}, u32[]{:S(2)}, u32[]{:S(2)}) collective-permute-start(bf16[4,32,2048]{2,1,0:T(8,128)(2,1)S(1)} %get-tuple-element.329.refs_0_), channel_id=1, source_target_pairs={{0,2},{1,3},{2,0},{3,1},{4,6},{5,7},{6,4},{7,5},{8,10},{9,11},{10,... | collective-permute-start | bytes 1572872 | tf_op jit(solution)/shard_map/ppermute | solution.py:65
  82.5 27.4 %collective-permute-start.10 = (bf16[4,32,2048]{2,1,0:T(8,128)(2,1)S(1)}, bf16[4,32,2048]{2,1,0:T(8,128)(2,1)S(1)}, u32[]{:S(2)}, u32[]{:S(2)}) collective-permute-start(bf16[4,32,2048]{2,1,0:T(8,128)(2,1)S(1)} %collective-permute-done.4.refs_4_), channel_id=1, source_target_pairs={{0,2},{1,3},{2,0},{3,1},{4,6},{5,7},{6,4},{7,5},{8,10},{9,11},{10,... | collective-permute-start | bytes 1572872 | tf_op jit(solution)/shard_map/ppermute | solution.py:65
  83.0 11.2 %collective-permute-start.11 = (bf16[64,1024]{1,0:T(8,128)(2,1)S(1)}, bf16[64,1024]{1,0:T(8,128)(2,1)S(1)}, u32[]{:S(2)}, u32[]{:S(2)}) collective-permute-start(bf16[64,1024]{1,0:T(8,128)(2,1)S(1)} %collective-permute-done.6), channel_id=1, source_target_pairs={{0,8},{1,9},{2,10},{3,11},{4,12},{5,13},{6,14},{7,15},{8,0},{9,1},... | collective-permute-start | bytes 393224 | tf_op jit(solution)/shard_map/ppermute | solution.py:65
  112.1 26.3 %collective-permute-start.20 = (bf16[4,64,1024]{2,1,0:T(8,128)(2,1)S(1)}, bf16[4,64,1024]{2,1,0:T(8,128)(2,1)S(1)}, u32[]{:S(2)}, u32[]{:S(2)}) collective-permute-start(bf16[4,64,1024]{2,1,0:T(8,128)(2,1)S(1)} %bitcast.31), channel_id=1, source_target_pairs={{0,2},{1,3},{2,0},{3,1},{4,6},{5,7},{6,4},{7,5},{8,10},{9,11},{10,... | collective-permute-start | bytes 1572872 | tf_op jit(solution)/shard_map/ppermute | solution.py:65
  114.7 23.7 %collective-permute-start.16 = (bf16[4,32,2048]{2,1,0:T(8,128)(2,1)S(1)}, bf16[4,32,2048]{2,1,0:T(8,128)(2,1)S(1)}, u32[]{:S(2)}, u32[]{:S(2)}) collective-permute-start(bf16[4,32,2048]{2,1,0:T(8,128)(2,1)S(1)} %get-tuple-element.329.refs_0_), channel_id=1, source_target_pairs={{0,1},{1,0},{2,3},{3,2},{4,5},{5,4},{6,7},{7,6},{8,9},{9,8},{10,11... | collective-permute-start | bytes 1572872 | tf_op jit(solution)/shard_map/ppermute | solution.py:65
  114.8 23.6 %collective-permute-start.17 = (bf16[4,32,2048]{2,1,0:T(8,128)(2,1)S(1)}, bf16[4,32,2048]{2,1,0:T(8,128)(2,1)S(1)}, u32[]{:S(2)}, u32[]{:S(2)}) collective-permute-start(bf16[4,32,2048]{2,1,0:T(8,128)(2,1)S(1)} %collective-permute-done.9.refs_2_), channel_id=1, source_target_pairs={{0,1},{1,0},{2,3},{3,2},{4,5},{5,4},{6,7},{7,6},{8,9},{9,8},{10,11... | collective-permute-start | bytes 1572872 | tf_op jit(solution)/shard_map/ppermute | solution.py:65
  115.3 23.2 %collective-permute-start.18 = (bf16[4,32,2048]{2,1,0:T(8,128)(2,1)S(1)}, bf16[4,32,2048]{2,1,0:T(8,128)(2,1)S(1)}, u32[]{:S(2)}, u32[]{:S(2)}) collective-permute-start(bf16[4,32,2048]{2,1,0:T(8,128)(2,1)S(1)} %collective-permute-done.4.refs_4_), channel_id=1, source_target_pairs={{0,1},{1,0},{2,3},{3,2},{4,5},{5,4},{6,7},{7,6},{8,9},{9,8},{10,11... | collective-permute-start | bytes 1572872 | tf_op jit(solution)/shard_map/ppermute | solution.py:65
  115.4 23.1 %collective-permute-start.19 = (bf16[4,32,2048]{2,1,0:T(8,128)(2,1)S(1)}, bf16[4,32,2048]{2,1,0:T(8,128)(2,1)S(1)}, u32[]{:S(2)}, u32[]{:S(2)}) collective-permute-start(bf16[4,32,2048]{2,1,0:T(8,128)(2,1)S(1)} %collective-permute-done.10.refs_6_), channel_id=1, source_target_pairs={{0,1},{1,0},{2,3},{3,2},{4,5},{5,4},{6,7},{7,6},{8,9},{9,8},{10,11... | collective-permute-start | bytes 1572872 | tf_op jit(solution)/shard_map/ppermute | solution.py:65
  138.5 16.3 %collective-permute-start.21 = (bf16[4,64,1024]{2,1,0:T(8,128)(2,1)S(1)}, bf16[4,64,1024]{2,1,0:T(8,128)(2,1)S(1)}, u32[]{:S(2)}, u32[]{:S(2)}) collective-permute-start(bf16[4,64,1024]{2,1,0:T(8,128)(2,1)S(1)} %bitcast.32), channel_id=1, source_target_pairs={{0,4},{1,5},{2,6},{3,7},{4,0},{5,1},{6,2},{7,3},{8,12},{9,13},{10,... | collective-permute-start | bytes 1572872 | tf_op jit(solution)/shard_map/ppermute | solution.py:65
  138.6 24.7 %collective-permute-start.22 = (bf16[4,64,1024]{2,1,0:T(8,128)(2,1)S(1)}, bf16[4,64,1024]{2,1,0:T(8,128)(2,1)S(1)}, u32[]{:S(2)}, u32[]{:S(2)}) collective-permute-start(bf16[4,64,1024]{2,1,0:T(8,128)(2,1)S(1)} %collective-permute-done.20.refs_2_), channel_id=1, source_target_pairs={{0,4},{1,5},{2,6},{3,7},{4,0},{5,1},{6,2},{7,3},{8,12},{9,13},{10,... | collective-permute-start | bytes 1572872 | tf_op jit(solution)/shard_map/ppermute | solution.py:65
  163.7 5.1 %collective-permute-start.26 = (bf16[4,64,1024]{2,1,0:T(8,128)(2,1)S(1)}, bf16[4,64,1024]{2,1,0:T(8,128)(2,1)S(1)}, u32[]{:S(2)}, u32[]{:S(2)}) collective-permute-start(bf16[4,64,1024]{2,1,0:T(8,128)(2,1)S(1)} %collective-permute-done.22.refs_6_), channel_id=1, source_target_pairs={{0,1},{1,0},{2,3},{3,2},{4,5},{5,4},{6,7},{7,6},{8,9},{9,8},{10,11... | collective-permute-start | bytes 1572872 | tf_op jit(solution)/shard_map/ppermute | solution.py:65
  197.1 13.5 %collective-permute-start.27 = (bf16[1536,1024]{1,0:T(8,128)(2,1)}, bf16[1536,1024]{1,0:T(8,128)(2,1)S(1)}, u32[]{:S(2)}, u32[]{:S(2)}) collective-permute-start(bf16[1536,1024]{1,0:T(8,128)(2,1)} %bitcast.49), channel_id=1, source_target_pairs={{0,1},{1,0},{2,3},{3,2},{4,5},{5,4},{6,7},{7,6},{8,9},{9,8},{10,11... | collective-permute-start | bytes 9437192 | tf_op jit(solution)/shard_map/ppermute | solution.py:65
  197.3 10.2 %collective-permute-start.28 = (bf16[512,3072]{1,0:T(8,128)(2,1)}, bf16[512,3072]{1,0:T(8,128)(2,1)S(1)}, u32[]{:S(2)}, u32[]{:S(2)}) collective-permute-start(bf16[512,3072]{1,0:T(8,128)(2,1)} %get-tuple-element.374), channel_id=1, source_target_pairs={{0,1},{1,0},{2,3},{3,2},{4,5},{5,4},{6,7},{7,6},{8,9},{9,8},{10,11... | collective-permute-start | bytes 9437192 | tf_op jit(solution)/shard_map/ppermute | solution.py:65
  205.3 6.9 %collective-permute-start.29 = (bf16[512,3072]{1,0:T(8,128)(2,1)S(1)}, bf16[512,3072]{1,0:T(8,128)(2,1)S(1)}, u32[]{:S(2)}, u32[]{:S(2)}) collective-permute-start(bf16[512,3072]{1,0:T(8,128)(2,1)S(1)} %get-tuple-element.383), channel_id=1, source_target_pairs={{0,1},{1,0},{2,3},{3,2},{4,5},{5,4},{6,7},{7,6},{8,9},{9,8},{10,11... | collective-permute-start | bytes 9437192 | tf_op jit(solution)/shard_map/ppermute | solution.py:65
  209.1 39.9 %collective-permute-start.31 = (bf16[256,3072]{1,0:T(8,128)(2,1)}, bf16[256,3072]{1,0:T(8,128)(2,1)S(1)}, u32[]{:S(2)}, u32[]{:S(2)}) collective-permute-start(bf16[256,3072]{1,0:T(8,128)(2,1)} %get-tuple-element.400), channel_id=1, source_target_pairs={{0,2},{1,3},{2,0},{3,1},{4,6},{5,7},{6,4},{7,5},{8,10},{9,11},{10,... | collective-permute-start | bytes 4718600 | tf_op jit(solution)/shard_map/ppermute | solution.py:65
  212.1 36.8 %collective-permute-start.30 = (bf16[768,1024]{1,0:T(8,128)(2,1)}, bf16[768,1024]{1,0:T(8,128)(2,1)S(1)}, u32[]{:S(2)}, u32[]{:S(2)}) collective-permute-start(bf16[768,1024]{1,0:T(8,128)(2,1)} %get-tuple-element.386), channel_id=1, source_target_pairs={{0,4},{1,5},{2,6},{3,7},{4,0},{5,1},{6,2},{7,3},{8,12},{9,13},{10,... | collective-permute-start | bytes 4718600 | tf_op jit(solution)/shard_map/ppermute | solution.py:65
  213.8 36.4 %collective-permute-start.32 = (bf16[256,3072]{1,0:T(8,128)(2,1)}, bf16[256,3072]{1,0:T(8,128)(2,1)S(1)}, u32[]{:S(2)}, u32[]{:S(2)}) collective-permute-start(bf16[256,3072]{1,0:T(8,128)(2,1)} %get-tuple-element.410), channel_id=1, source_target_pairs={{0,8},{1,9},{2,10},{3,11},{4,12},{5,13},{6,14},{7,15},{8,0},{9,1},... | collective-permute-start | bytes 4718600 | tf_op jit(solution)/shard_map/ppermute | solution.py:65
  250.2 7.4 %collective-permute-start.35 = (bf16[1024,1024]{1,0:T(8,128)(2,1)}, bf16[1024,1024]{1,0:T(8,128)(2,1)S(1)}, u32[]{:S(2)}, u32[]{:S(2)}) collective-permute-start(bf16[1024,1024]{1,0:T(8,128)(2,1)} %get-tuple-element.443), channel_id=1, source_target_pairs={{0,1},{1,0},{2,3},{3,2},{4,5},{5,4},{6,7},{7,6},{8,9},{9,8},{10,11... | collective-permute-start | bytes 6291464 | tf_op jit(solution)/shard_map/ppermute | solution.py:65
  252.2 46.4 %collective-permute-start.33 = (bf16[128,6144]{1,0:T(8,128)(2,1)}, bf16[128,6144]{1,0:T(8,128)(2,1)S(1)}, u32[]{:S(2)}, u32[]{:S(2)}) collective-permute-start(bf16[128,6144]{1,0:T(8,128)(2,1)} %get-tuple-element.428), channel_id=1, source_target_pairs={{0,4},{1,5},{2,6},{3,7},{4,0},{5,1},{6,2},{7,3},{8,12},{9,13},{10,... | collective-permute-start | bytes 4718600 | tf_op jit(solution)/shard_map/ppermute | solution.py:65
  255.8 42.8 %collective-permute-start.37 = (bf16[256,2048]{1,0:T(8,128)(2,1)}, bf16[256,2048]{1,0:T(8,128)(2,1)S(1)}, u32[]{:S(2)}, u32[]{:S(2)}) collective-permute-start(bf16[256,2048]{1,0:T(8,128)(2,1)} %get-tuple-element.471), channel_id=1, source_target_pairs={{0,8},{1,9},{2,10},{3,11},{4,12},{5,13},{6,14},{7,15},{8,0},{9,1},... | collective-permute-start | bytes 3145736 | tf_op jit(solution)/shard_map/ppermute | solution.py:65
  258.9 39.7 %collective-permute-start.38 = (bf16[512,1024]{1,0:T(8,128)(2,1)}, bf16[512,1024]{1,0:T(8,128)(2,1)S(1)}, u32[]{:S(2)}, u32[]{:S(2)}) collective-permute-start(bf16[512,1024]{1,0:T(8,128)(2,1)} %get-tuple-element.476), channel_id=1, source_target_pairs={{0,2},{1,3},{2,0},{3,1},{4,6},{5,7},{6,4},{7,5},{8,10},{9,11},{10,... | collective-permute-start | bytes 3145736 | tf_op jit(solution)/shard_map/ppermute | solution.py:65
  261.3 37.3 %collective-permute-start.36 = (bf16[384,1024]{1,0:T(8,128)(2,1)}, bf16[384,1024]{1,0:T(8,128)(2,1)S(1)}, u32[]{:S(2)}, u32[]{:S(2)}) collective-permute-start(bf16[384,1024]{1,0:T(8,128)(2,1)} %get-tuple-element.447), channel_id=1, source_target_pairs={{0,16},{1,17},{2,18},{3,19},{4,20},{5,21},{6,22},{7,23},{8,24},{9,... | collective-permute-start | bytes 2359304 | tf_op jit(solution)/shard_map/ppermute | solution.py:65
  303.8 26.7 %collective-permute-start.41 = (bf16[256,2176]{1,0:T(8,128)(2,1)S(1)}, bf16[256,2176]{1,0:T(8,128)(2,1)S(1)}, u32[]{:S(2)}, u32[]{:S(2)}) collective-permute-start(bf16[256,2176]{1,0:T(8,128)(2,1)S(1)} %get-tuple-element.508), channel_id=1, source_target_pairs={{0,2},{1,3},{2,0},{3,1},{4,6},{5,7},{6,4},{7,5},{8,10},{9,11},{10,... | collective-permute-start | bytes 3342344 | tf_op jit(solution)/shard_map/ppermute | solution.py:65
  304.9 19.3 %collective-permute-start.39 = (bf16[64,3072]{1,0:T(8,128)(2,1)S(1)}, bf16[64,3072]{1,0:T(8,128)(2,1)S(1)}, u32[]{:S(2)}, u32[]{:S(2)}) collective-permute-start(bf16[64,3072]{1,0:T(8,128)(2,1)S(1)} %get-tuple-element.500), channel_id=1, source_target_pairs={{0,8},{1,9},{2,10},{3,11},{4,12},{5,13},{6,14},{7,15},{8,0},{9,1},... | collective-permute-start | bytes 1179656 | tf_op jit(solution)/shard_map/ppermute | solution.py:65
  305.6 19.1 %collective-permute-start.42 = (bf16[64,3072]{1,0:T(8,128)(2,1)S(1)}, bf16[64,3072]{1,0:T(8,128)(2,1)S(1)}, u32[]{:S(2)}, u32[]{:S(2)}) collective-permute-start(bf16[64,3072]{1,0:T(8,128)(2,1)S(1)} %get-tuple-element.512), channel_id=1, source_target_pairs={{0,16},{1,17},{2,18},{3,19},{4,20},{5,21},{6,22},{7,23},{8,24},{9,... | collective-permute-start | bytes 1179656 | tf_op jit(solution)/shard_map/ppermute | solution.py:65
  307.4 32.0 %collective-permute-start.49 = (bf16[256,1024]{1,0:T(8,128)(2,1)S(1)}, bf16[256,1024]{1,0:T(8,128)(2,1)S(1)}, u32[]{:S(2)}, u32[]{:S(2)}) collective-permute-start(bf16[256,1024]{1,0:T(8,128)(2,1)S(1)} %get-tuple-element.533), channel_id=1, source_target_pairs={{0,4},{1,5},{2,6},{3,7},{4,0},{5,1},{6,2},{7,3},{8,12},{9,13},{10,... | collective-permute-start | bytes 1572872 | tf_op jit(solution)/shard_map/ppermute | solution.py:65
  309.3 30.3 %collective-permute-start.43 = (bf16[128,2048]{1,0:T(8,128)(2,1)S(1)}, bf16[128,2048]{1,0:T(8,128)(2,1)S(1)}, u32[]{:S(2)}, u32[]{:S(2)}) collective-permute-start(bf16[128,2048]{1,0:T(8,128)(2,1)S(1)} %get-tuple-element.515), channel_id=1, source_target_pairs={{0,4},{1,5},{2,6},{3,7},{4,0},{5,1},{6,2},{7,3},{8,12},{9,13},{10,... | collective-permute-start | bytes 1572872 | tf_op jit(solution)/shard_map/ppermute | solution.py:65
  324.2 14.2 %collective-permute-start.54 = (bf16[192,1024]{1,0:T(8,128)(2,1)S(1)}, bf16[192,1024]{1,0:T(8,128)(2,1)S(1)}, u32[]{:S(2)}, u32[]{:S(2)}) collective-permute-start(bf16[192,1024]{1,0:T(8,128)(2,1)S(1)} %get-tuple-element.544), channel_id=1, source_target_pairs={{0,8},{1,9},{2,10},{3,11},{4,12},{5,13},{6,14},{7,15},{8,0},{9,1},... | collective-permute-start | bytes 1179656 | tf_op jit(solution)/shard_map/ppermute | solution.py:65
  324.7 16.4 %collective-permute-start.52 = (bf16[32,3072]{1,0:T(8,128)(2,1)S(1)}, bf16[32,3072]{1,0:T(8,128)(2,1)S(1)}, u32[]{:S(2)}, u32[]{:S(2)}) collective-permute-start(bf16[32,3072]{1,0:T(8,128)(2,1)S(1)} %get-tuple-element.540), channel_id=1, source_target_pairs={{0,16},{1,17},{2,18},{3,19},{4,20},{5,21},{6,22},{7,23},{8,24},{9,... | collective-permute-start | bytes 589832 | tf_op jit(solution)/shard_map/ppermute | solution.py:65
  330.4 25.4 %collective-permute-start.53 = (bf16[32,3072]{1,0:T(8,128)(2,1)S(1)}, bf16[32,3072]{1,0:T(8,128)(2,1)S(1)}, u32[]{:S(2)}, u32[]{:S(2)}) collective-permute-start(bf16[32,3072]{1,0:T(8,128)(2,1)S(1)} %get-tuple-element.542), channel_id=1, source_target_pairs={{0,2},{1,3},{2,0},{3,1},{4,6},{5,7},{6,4},{7,5},{8,10},{9,11},{10,... | collective-permute-start | bytes 589832 | tf_op jit(solution)/shard_map/ppermute | solution.py:65
  338.5 19.3 %collective-permute-start.55 = (bf16[96,1024]{1,0:T(8,128)(2,1)S(1)}, bf16[96,1024]{1,0:T(8,128)(2,1)S(1)}, u32[]{:S(2)}, u32[]{:S(2)}) collective-permute-start(bf16[96,1024]{1,0:T(8,128)(2,1)S(1)} %get-tuple-element.546), channel_id=1, source_target_pairs={{0,2},{1,3},{2,0},{3,1},{4,6},{5,7},{6,4},{7,5},{8,10},{9,11},{10,... | collective-permute-start | bytes 589832 | tf_op jit(solution)/shard_map/ppermute | solution.py:65
  339.5 17.1 %collective-permute-start.50 = (bf16[128,1024]{1,0:T(8,128)(2,1)S(1)}, bf16[128,1024]{1,0:T(8,128)(2,1)S(1)}, u32[]{:S(2)}, u32[]{:S(2)}) collective-permute-start(bf16[128,1024]{1,0:T(8,128)(2,1)S(1)} %get-tuple-element.535), channel_id=1, source_target_pairs={{0,8},{1,9},{2,10},{3,11},{4,12},{5,13},{6,14},{7,15},{8,0},{9,1},... | collective-permute-start | bytes 786440 | tf_op jit(solution)/shard_map/ppermute | solution.py:65
  339.8 18.8 %collective-permute-start.44 = (bf16[64,2048]{1,0:T(8,128)(2,1)S(1)}, bf16[64,2048]{1,0:T(8,128)(2,1)S(1)}, u32[]{:S(2)}, u32[]{:S(2)}) collective-permute-start(bf16[64,2048]{1,0:T(8,128)(2,1)S(1)} %get-tuple-element.517), channel_id=1, source_target_pairs={{0,2},{1,3},{2,0},{3,1},{4,6},{5,7},{6,4},{7,5},{8,10},{9,11},{10,... | collective-permute-start | bytes 786440 | tf_op jit(solution)/shard_map/ppermute | solution.py:65
  341.1 12.8 %collective-permute-start.46 = (bf16[128,2176]{1,0:T(8,128)(2,1)S(1)}, bf16[128,2176]{1,0:T(8,128)(2,1)S(1)}, u32[]{:S(2)}, u32[]{:S(2)}) collective-permute-start(bf16[128,2176]{1,0:T(8,128)(2,1)S(1)} %get-tuple-element.521), channel_id=1, source_target_pairs={{0,4},{1,5},{2,6},{3,7},{4,0},{5,1},{6,2},{7,3},{8,12},{9,13},{10,... | collective-permute-start | bytes 1671176 | tf_op jit(solution)/shard_map/ppermute | solution.py:65
  354.1 9.0 %collective-permute-start.47 = (bf16[64,2176]{1,0:T(8,128)(2,1)S(1)}, bf16[64,2176]{1,0:T(8,128)(2,1)S(1)}, u32[]{:S(2)}, u32[]{:S(2)}) collective-permute-start(bf16[64,2176]{1,0:T(8,128)(2,1)S(1)} %get-tuple-element.523), channel_id=1, source_target_pairs={{0,8},{1,9},{2,10},{3,11},{4,12},{5,13},{6,14},{7,15},{8,0},{9,1},... | collective-permute-start | bytes 835592 | tf_op jit(solution)/shard_map/ppermute | solution.py:65
  356.8 12.9 %collective-permute-start.51 = (bf16[64,1024]{1,0:T(8,128)(2,1)S(1)}, bf16[64,1024]{1,0:T(8,128)(2,1)S(1)}, u32[]{:S(2)}, u32[]{:S(2)}) collective-permute-start(bf16[64,1024]{1,0:T(8,128)(2,1)S(1)} %get-tuple-element.537), channel_id=1, source_target_pairs={{0,16},{1,17},{2,18},{3,19},{4,20},{5,21},{6,22},{7,23},{8,24},{9,... | collective-permute-start | bytes 393224 | tf_op jit(solution)/shard_map/ppermute | solution.py:65
  359.3 13.9 %collective-permute-start.45 = (bf16[32,2048]{1,0:T(8,128)(2,1)S(1)}, bf16[32,2048]{1,0:T(8,128)(2,1)S(1)}, u32[]{:S(2)}, u32[]{:S(2)}) collective-permute-start(bf16[32,2048]{1,0:T(8,128)(2,1)S(1)} %get-tuple-element.519), channel_id=1, source_target_pairs={{0,16},{1,17},{2,18},{3,19},{4,20},{5,21},{6,22},{7,23},{8,24},{9,... | collective-permute-start | bytes 393224 | tf_op jit(solution)/shard_map/ppermute | solution.py:65
  363.9 10.9 %collective-permute-start.48 = (bf16[32,2176]{1,0:T(8,128)(2,1)S(1)}, bf16[32,2176]{1,0:T(8,128)(2,1)S(1)}, u32[]{:S(2)}, u32[]{:S(2)}) collective-permute-start(bf16[32,2176]{1,0:T(8,128)(2,1)S(1)} %get-tuple-element.525), channel_id=1, source_target_pairs={{0,16},{1,17},{2,18},{3,19},{4,20},{5,21},{6,22},{7,23},{8,24},{9,... | collective-permute-start | bytes 417800 | tf_op jit(solution)/shard_map/ppermute | solution.py:65
  (69 other events, 1009.5 us)
Sparse Core Ops, SparseCore 0:
  10.9 161.1 all-gather.2

commit v9 on v8

--- a/solution.py
+++ b/solution.py
@@ -1213,6 +1213,9 @@
     relay("second")
     relay("down")
     cut()
+    relay("first", "out")
+    cut()
+    relay("second")
     while any(stages.values()):
         for name in ("second", "first", "out", "down", "gate", "up"):
             if stages[name]:

time: 388 us -> 388 us (level)
  transfers between devices with their start and end apart: 57 -> 57, of which waited for: 31 -> 32; matrix products, arithmetic and copies ran while one was open for 2% -> 2% of each run, Pallas kernels for 29% -> 29%
where the time goes in v9:
time: 388 us; the launch traced here: 384 us
  waiting for transfers between devices  160 us (41%)
  Pallas kernels  140 us (36%)
  starting transfers between devices  55.5 us (14%)
  between operations  15.1 us (4%)
  local copies, waits for them, and re-layouts  8.15 us (2%)
  other arithmetic  5.16 us (1%)
    ppermute x56, waiting for transfers between devices, exchange(): lax.ppermute(values, 'fsdp', [(source, source ^ mask) for source in range...  160 us
    ppermute x56, starting transfers between devices, exchange(): lax.ppermute(values, 'fsdp', [(source, source ^ mask) for source in range...  55.5 us
    pallas_call x1, Pallas kernels, back(): pl.pallas_call(functools.partial(back_body, parts=len(parts)), grid_spec=...  34.1 us
    pallas_call x1, Pallas kernels, attend_back_last(): pl.pallas_call(functools.partial(attend_back_body, order=order, shard=sha...  26.2 us
    pallas_call x1, Pallas kernels, feed_forward(): pl.pallas_call(functools.partial(feed_forward_body, gate_order=gate_order...  23.3 us
    pallas_call x2, Pallas kernels, attend(): pl.pallas_call(attend_body, grid_spec=pltpu.PrefetchScalarGridSpec(num_sc...  21.2 us
    pallas_call x23, Pallas kernels, fold(): pl.pallas_call(functools.partial(fold_body, pairs=len(pairs), merged=merg...  13 us
  transfers between devices with their start and end apart: 57, of which 32 were waited for; matrix products, arithmetic and copies ran while one was open for 2% of the time, Pallas kernels for 29%

profile of v9, /device:TPU:0, one launch (start us, length us, event | category | flops | bytes accessed | tf_op | source)
XLA Modules:
  0.0 383.9 jit_solution(4650993360061032716)
XLA Ops:
  7.3 2.0 stack.1
  11.4 1.7 join.1
  13.0 4.0 %collective-permute-start.1 = (bf16[32,4224]{1,0:T(8,128)(2,1)}, bf16[32,4224]{1,0:T(8,128)(2,1)S(1)}, u32[]{:S(2)}, u32[]{:S(2)}) collective-permute-start(bf16[32,4224]{1,0:T(8,128)(2,1)} %join.1), channel_id=1, source_target_pairs={{0,16},{1,17},{2,18},{3,19},{4,20},{5,21},{6,22},{7,23},{8,24},{9,... | collective-permute-start | bytes 811016 | tf_op jit(solution)/shard_map/ppermute | solution.py:65
  17.1 1.6 collective-permute-start
  18.9 16.1 %collective-permute-done.1 = bf16[32,4224]{1,0:T(8,128)(2,1)S(1)} collective-permute-done((bf16[32,4224]{1,0:T(8,128)(2,1)}, bf16[32,4224]{1,0:T(8,128)(2,1)S(1)}, u32[]{:S(2)}, u32[]{:S(2)}) %collective-permute-start.1) | collective-permute-done | bytes 270368 | tf_op jit(solution)/shard_map/ppermute | solution.py:65
  35.6 4.0 %collective-permute-start.2 = (bf16[32,4224]{1,0:T(8,128)(2,1)S(1)}, bf16[32,4224]{1,0:T(8,128)(2,1)S(1)}, u32[]{:S(2)}, u32[]{:S(2)}) collective-permute-start(bf16[32,4224]{1,0:T(8,128)(2,1)S(1)} %collective-permute-done.1), channel_id=1, source_target_pairs={{0,8},{1,9},{2,10},{3,11},{4,12},{5,13},{6,14},{7,15},{8,0},{9,1},... | collective-permute-start | bytes 811016 | tf_op jit(solution)/shard_map/ppermute | solution.py:65
  39.7 8.5 %collective-permute-done.2 = bf16[32,4224]{1,0:T(8,128)(2,1)S(1)} collective-permute-done((bf16[32,4224]{1,0:T(8,128)(2,1)S(1)}, bf16[32,4224]{1,0:T(8,128)(2,1)S(1)}, u32[]{:S(2)}, u32[]{:S(2)}) %collective-permute-start.2) | collective-permute-done | bytes 270368 | tf_op jit(solution)/shard_map/ppermute | solution.py:65
  50.4 1.6 collective-permute-start.4
  54.3 1.9 collective-permute-start.6
  56.2 1.7 collective-permute-start.5
  58.3 11.3 %collective-permute-done.6 = bf16[64,1024]{1,0:T(8,128)(2,1)S(1)} collective-permute-done((bf16[64,1024]{1,0:T(8,128)(2,1)S(1)}, bf16[64,1024]{1,0:T(8,128)(2,1)S(1)}, u32[]{:S(2)}, u32[]{:S(2)}) %collective-permute-start.6) | collective-permute-done | bytes 131104 | tf_op jit(solution)/shard_map/ppermute | solution.py:65
  70.3 1.6 collective-permute-done.4.refs_4_
  71.9 7.1 %collective-permute-done.3.refs_2_.refs_21_ = bf16[4,32,2176]{2,1,0:T(8,128)(2,1)S(1)} collective-permute-done((bf16[4,32,2176]{2,1,0:T(8,128)(2,1)S(1)}, bf16[4,32,2176]{2,1,0:T(8,128)(2,1)S(1)}, u32[]{:S(2)}, u32[]{:S(2)}) %collective-permute-start.3) | collective-permute-done | bytes 557088 | tf_op jit(solution)/shard_map/ppermute | solution.py:65
  79.3 1.6 collective-permute-start.8
  84.3 9.9 %collective-permute-done.11 = bf16[64,1024]{1,0:T(8,128)(2,1)S(1)} collective-permute-done((bf16[64,1024]{1,0:T(8,128)(2,1)S(1)}, bf16[64,1024]{1,0:T(8,128)(2,1)S(1)}, u32[]{:S(2)}, u32[]{:S(2)}) %collective-permute-start.11) | collective-permute-done | bytes 131104 | tf_op jit(solution)/shard_map/ppermute | solution.py:65
  94.2 1.6 collective-permute-done.9.refs_2_
  95.8 14.0 %collective-permute-done.10.refs_6_ = bf16[4,32,2048]{2,1,0:T(8,128)(2,1)S(1)} collective-permute-done((bf16[4,32,2048]{2,1,0:T(8,128)(2,1)S(1)}, bf16[4,32,2048]{2,1,0:T(8,128)(2,1)S(1)}, u32[]{:S(2)}, u32[]{:S(2)}) %collective-permute-start.10) | collective-permute-done | bytes 524320 | tf_op jit(solution)/shard_map/ppermute | solution.py:65
  112.1 2.5 collective-permute-start.20
  117.2 11.2 %attend.2 = (bf16[384,1024]{1,0:T(8,128)(2,1)S(1)}, bf16[384,1024]{1,0:T(8,128)(2,1)}, bf16[384,512]{1,0:T(8,128)(2,1)}, bf16[384,512]{1,0:T(8,128)(2,1)}, f32[384,1536]{1,0:T(8,128)}, /*index=5*/f32[4,384,2]{2,1,0:T(8,128)}) custom-call(s32[1]{0:T(128)} %bitcast.device_ref, bf16[4,32,2176]{2,1,0:T(8,128)(2,1)S(1)} %get-tuple-element.312.refs_0_.refs_19_, ...), custom_call_target="tpu_custom_call" | custom-call | flops 1 | bytes 1 | tf_op jit(solution)/shard_map/attend/pallas_call | solution.py:474
  128.4 10.0 %collective-permute-done.20.refs_2_ = bf16[4,64,1024]{2,1,0:T(8,128)(2,1)S(1)} collective-permute-done((bf16[4,64,1024]{2,1,0:T(8,128)(2,1)S(1)}, bf16[4,64,1024]{2,1,0:T(8,128)(2,1)S(1)}, u32[]{:S(2)}, u32[]{:S(2)}) %collective-permute-start.20) | collective-permute-done | bytes 524320 | tf_op jit(solution)/shard_map/ppermute | solution.py:65
  138.6 2.0 collective-permute-start.22
  143.0 10.0 %attend.3 = (bf16[384,1024]{1,0:T(8,128)(2,1)S(1)}, bf16[384,1024]{1,0:T(8,128)(2,1)}, bf16[384,512]{1,0:T(8,128)(2,1)}, bf16[384,512]{1,0:T(8,128)(2,1)}, f32[384,1536]{1,0:T(8,128)}, /*index=5*/f32[4,384,2]{2,1,0:T(8,128)}) custom-call(s32[1]{0:T(128)} %bitcast.device_ref, bf16[4,32,2048]{2,1,0:T(8,128)(2,1)S(1)} %get-tuple-element.335.refs_0_, ...), custom_call_target="tpu_custom_call" | custom-call | flops 1 | bytes 1 | tf_op jit(solution)/shard_map/attend/pallas_call | solution.py:474
  153.0 1.8 turn.4.refs_7_
  154.8 8.4 %collective-permute-done.22.refs_6_ = bf16[4,64,1024]{2,1,0:T(8,128)(2,1)S(1)} collective-permute-done((bf16[4,64,1024]{2,1,0:T(8,128)(2,1)S(1)}, bf16[4,64,1024]{2,1,0:T(8,128)(2,1)S(1)}, u32[]{:S(2)}, u32[]{:S(2)}) %collective-permute-start.22) | collective-permute-done | bytes 524320 | tf_op jit(solution)/shard_map/ppermute | solution.py:65
  168.8 5.0 %project.1 = (f32[384,1024]{1,0:T(8,128)}, bf16[4,8,64,1024]{3,2,1,0:T(8,128)(2,1)}) custom-call(s32[1]{0:T(128)} %bitcast.device_ref, bf16[4,64,1024]{2,1,0:T(8,128)(2,1)S(1)} %bitcast.34, bf16[4,64,1024]{2,1,0:T(8,128)(2,1)S(1)} %collective-permute-done.23.refs_1_, bf16[4,64,1024]{2,1,0:T(8,128)(2,1)S(1)} %collective-permute-done.20.refs_2_, ...), custom_call_target="tpu_custom_call" | custom-call | flops 1 | bytes 1 | tf_op jit(solution)/shard_map/project/pallas_call | solution.py:742
  173.8 23.3 %feed_forward.1 = (bf16[384,3072]{1,0:T(8,128)(2,1)}, bf16[384,3072]{1,0:T(8,128)(2,1)}, bf16[384,3072]{1,0:T(8,128)(2,1)}, bf16[512,3072]{1,0:T(8,128)(2,1)}, b...) custom-call(s32[1]{0:T(128)} %bitcast.device_ref, ...), custom_call_target="tpu_custom_call" | custom-call | flops 1 | bytes 1 | tf_op jit(solution)/shard_map/feed_forward/pallas_call | solution.py:860
  197.6 2.0 copy-done.2
  200.7 4.6 %product_halves.1 = (bf16[512,3072]{1,0:T(8,128)(2,1)S(1)}, bf16[512,3072]{1,0:T(8,128)(2,1)S(1)}) custom-call(bf16[1024,384]{1,0:T(8,128)(2,1)S(1)} %copy-done.43, bf16[384,3072]{1,0:T(8,128)(2,1)S(1)} %copy-done.2), custom_call_target="tpu_custom_call" | custom-call | flops 1 | bytes 1 | tf_op jit(solution)/shard_map/product_halves/pallas_call | solution.py:913
  205.5 2.0 collective-permute-done.28.refs_2_.refs_3_
  207.5 1.6 fold.24
  214.9 34.1 %back.1 = (f32[384,1024]{1,0:T(8,128)}, bf16[384,1024]{1,0:T(8,128)(2,1)}, f32[1,1024]{1,0:T(1,128)S(1)}, bf16[1024,1024]{1,0:T(8,128)(2,1)}, bf16[1024,1024]{1,...) custom-call(s32[1]{0:T(128)} %bitcast.device_ref, ...), custom_call_target="tpu_custom_call" | custom-call | flops 1 | bytes 1 | tf_op jit(solution)/shard_map/back/pallas_call | solution.py:989
  252.2 1.7 collective-permute-start.33
  261.8 26.2 %attend_back_last.1 = (bf16[512,2176]{1,0:T(8,128)(2,1)S(1)}, bf16[512,2176]{1,0:T(8,128)(2,1)}, bf16[384,1024]{1,0:T(8,128)(2,1)}, bf16[384,1024]{1,0:T(8,128)(2,1)}) custom-call(s32[1]{0:T(128)} %bitcast.device_ref, bf16[384,1024]{1,0:T(8,128)(2,1)S(1)} %copy-done.44, bf16[2048,1024]{1,0:T(8,128)(2,1)} %bitcast.42, ...), custom_call_target="tpu_custom_call" | custom-call | flops 1 | bytes 1 | tf_op jit(solution)/shard_map/attend_back_last/pallas_call | solution.py:684
  288.0 10.6 %collective-permute-done.36.refs_2_.refs_3_ = bf16[384,1024]{1,0:T(8,128)(2,1)S(1)} collective-permute-done((bf16[384,1024]{1,0:T(8,128)(2,1)}, bf16[384,1024]{1,0:T(8,128)(2,1)S(1)}, u32[]{:S(2)}, u32[]{:S(2)}) %collective-permute-start.36) | collective-permute-done | bytes 786464 | tf_op jit(solution)/shard_map/ppermute | solution.py:65
  298.7 4.5 %collective-permute-done.40.refs_2_.refs_3_ = bf16[512,2176]{1,0:T(8,128)(2,1)S(1)} collective-permute-done((bf16[512,2176]{1,0:T(8,128)(2,1)}, bf16[512,2176]{1,0:T(8,128)(2,1)S(1)}, u32[]{:S(2)}, u32[]{:S(2)}) %collective-permute-start.40) | collective-permute-done | bytes 2228256 | tf_op jit(solution)/shard_map/ppermute | solution.py:65
  307.4 1.6 collective-permute-start.43
  310.0 14.2 %collective-permute-done.39.refs_2_.refs_3_ = bf16[64,3072]{1,0:T(8,128)(2,1)S(1)} collective-permute-done((bf16[64,3072]{1,0:T(8,128)(2,1)S(1)}, bf16[64,3072]{1,0:T(8,128)(2,1)S(1)}, u32[]{:S(2)}, u32[]{:S(2)}) %collective-permute-start.39) | collective-permute-done | bytes 393248 | tf_op jit(solution)/shard_map/ppermute | solution.py:65
  325.7 4.7 %collective-permute-done.41.refs_2_.refs_3_ = bf16[256,2176]{1,0:T(8,128)(2,1)S(1)} collective-permute-done((bf16[256,2176]{1,0:T(8,128)(2,1)S(1)}, bf16[256,2176]{1,0:T(8,128)(2,1)S(1)}, u32[]{:S(2)}, u32[]{:S(2)}) %collective-permute-start.41) | collective-permute-done | bytes 1114144 | tf_op jit(solution)/shard_map/ppermute | solution.py:65
  332.2 6.2 %collective-permute-done.54.refs_2_.refs_3_ = bf16[192,1024]{1,0:T(8,128)(2,1)S(1)} collective-permute-done((bf16[192,1024]{1,0:T(8,128)(2,1)S(1)}, bf16[192,1024]{1,0:T(8,128)(2,1)S(1)}, u32[]{:S(2)}, u32[]{:S(2)}) %collective-permute-start.54) | collective-permute-done | bytes 393248 | tf_op jit(solution)/shard_map/ppermute | solution.py:65
  340.6 1.6 collective-permute-start.47
  343.0 10.5 %collective-permute-done.47.refs_2_.refs_3_ = bf16[128,2176]{1,0:T(8,128)(2,1)S(1)} collective-permute-done((bf16[128,2176]{1,0:T(8,128)(2,1)S(1)}, bf16[128,2176]{1,0:T(8,128)(2,1)S(1)}, u32[]{:S(2)}, u32[]{:S(2)}) %collective-permute-start.47) | collective-permute-done | bytes 557088 | tf_op jit(solution)/shard_map/ppermute | solution.py:65
  353.6 1.8 collective-permute-start.48
  358.8 2.0 collective-permute-start.46
  360.9 1.9 collective-permute-done.48.refs_2_.refs_3_
  363.5 2.9 collective-permute-start.49
  366.4 2.8 collective-permute-done.51
  369.9 2.9 collective-permute-done.46.first_came
  374.9 1.9 end_projections.1
  (243 shorter events, 62.2 us)
Async XLA Ops:
  7.2 166.5 %all-gather.3.cloned.1.call-start = ((), (), s32[]{:S(2)}) async-start(), calls=%async_computation | async-start | bytes 19464192 | tf_op jit(solution)/shard_map/all_gather | solution.py:1091
  13.0 21.9 %collective-permute-start.1 = (bf16[32,4224]{1,0:T(8,128)(2,1)}, bf16[32,4224]{1,0:T(8,128)(2,1)S(1)}, u32[]{:S(2)}, u32[]{:S(2)}) collective-permute-start(bf16[32,4224]{1,0:T(8,128)(2,1)} %join.1), channel_id=1, source_target_pairs={{0,16},{1,17},{2,18},{3,19},{4,20},{5,21},{6,22},{7,23},{8,24},{9,... | collective-permute-start | bytes 811016 | tf_op jit(solution)/shard_map/ppermute | solution.py:65
  17.1 18.5 %collective-permute-start = (bf16[32,4224]{1,0:T(8,128)(2,1)}, bf16[32,4224]{1,0:T(8,128)(2,1)S(1)}, u32[]{:S(2)}, u32[]{:S(2)}) collective-permute-start(bf16[32,4224]{1,0:T(8,128)(2,1)} %join.1), channel_id=1, source_target_pairs={{0,8},{1,9},{2,10},{3,11},{4,12},{5,13},{6,14},{7,15},{8,0},{9,1},... | collective-permute-start | bytes 811016 | tf_op jit(solution)/shard_map/ppermute | solution.py:65
  35.6 12.7 %collective-permute-start.2 = (bf16[32,4224]{1,0:T(8,128)(2,1)S(1)}, bf16[32,4224]{1,0:T(8,128)(2,1)S(1)}, u32[]{:S(2)}, u32[]{:S(2)}) collective-permute-start(bf16[32,4224]{1,0:T(8,128)(2,1)S(1)} %collective-permute-done.1), channel_id=1, source_target_pairs={{0,8},{1,9},{2,10},{3,11},{4,12},{5,13},{6,14},{7,15},{8,0},{9,1},... | collective-permute-start | bytes 811016 | tf_op jit(solution)/shard_map/ppermute | solution.py:65
  50.4 21.4 %collective-permute-start.4 = (bf16[4,32,2048]{2,1,0:T(8,128)(2,1)S(1)}, bf16[4,32,2048]{2,1,0:T(8,128)(2,1)S(1)}, u32[]{:S(2)}, u32[]{:S(2)}) collective-permute-start(bf16[4,32,2048]{2,1,0:T(8,128)(2,1)S(1)} %get-tuple-element.335.refs_0_), channel_id=1, source_target_pairs={{0,4},{1,5},{2,6},{3,7},{4,0},{5,1},{6,2},{7,3},{8,12},{9,13},{10,... | collective-permute-start | bytes 1572872 | tf_op jit(solution)/shard_map/ppermute | solution.py:65
  52.0 26.9 %collective-permute-start.3 = (bf16[4,32,2176]{2,1,0:T(8,128)(2,1)S(1)}, bf16[4,32,2176]{2,1,0:T(8,128)(2,1)S(1)}, u32[]{:S(2)}, u32[]{:S(2)}) collective-permute-start(bf16[4,32,2176]{2,1,0:T(8,128)(2,1)S(1)} %get-tuple-element.312.refs_0_.refs_19_), channel_id=1, source_target_pairs={{0,2},{1,3},{2,0},{3,1},{4,6},{5,7},{6,4},{7,5},{8,10},{9,11},{10,... | collective-permute-start | bytes 1671176 | tf_op jit(solution)/shard_map/ppermute | solution.py:65
  54.3 15.2 %collective-permute-start.6 = (bf16[64,1024]{1,0:T(8,128)(2,1)S(1)}, bf16[64,1024]{1,0:T(8,128)(2,1)S(1)}, u32[]{:S(2)}, u32[]{:S(2)}) collective-permute-start(bf16[64,1024]{1,0:T(8,128)(2,1)S(1)} %copy-done.54), channel_id=1, source_target_pairs={{0,16},{1,17},{2,18},{3,19},{4,20},{5,21},{6,22},{7,23},{8,24},{9,... | collective-permute-start | bytes 393224 | tf_op jit(solution)/shard_map/ppermute | solution.py:65
  56.2 14.1 %collective-permute-start.5 = (bf16[64,1024]{1,0:T(8,128)(2,1)S(1)}, bf16[64,1024]{1,0:T(8,128)(2,1)S(1)}, u32[]{:S(2)}, u32[]{:S(2)}) collective-permute-start(bf16[64,1024]{1,0:T(8,128)(2,1)S(1)} %copy-done.54), channel_id=1, source_target_pairs={{0,8},{1,9},{2,10},{3,11},{4,12},{5,13},{6,14},{7,15},{8,0},{9,1},... | collective-permute-start | bytes 393224 | tf_op jit(solution)/shard_map/ppermute | solution.py:65
  78.9 30.9 %collective-permute-start.7 = (bf16[4,32,2176]{2,1,0:T(8,128)(2,1)S(1)}, bf16[4,32,2176]{2,1,0:T(8,128)(2,1)S(1)}, u32[]{:S(2)}, u32[]{:S(2)}) collective-permute-start(bf16[4,32,2176]{2,1,0:T(8,128)(2,1)S(1)} %get-tuple-element.312.refs_0_.refs_19_), channel_id=1, source_target_pairs={{0,4},{1,5},{2,6},{3,7},{4,0},{5,1},{6,2},{7,3},{8,12},{9,13},{10,... | collective-permute-start | bytes 1671176 | tf_op jit(solution)/shard_map/ppermute | solution.py:65
  79.3 30.5 %collective-permute-start.8 = (bf16[4,32,2176]{2,1,0:T(8,128)(2,1)S(1)}, bf16[4,32,2176]{2,1,0:T(8,128)(2,1)S(1)}, u32[]{:S(2)}, u32[]{:S(2)}) collective-permute-start(bf16[4,32,2176]{2,1,0:T(8,128)(2,1)S(1)} %collective-permute-done.3.refs_2_.refs_21_), channel_id=1, source_target_pairs={{0,4},{1,5},{2,6},{3,7},{4,0},{5,1},{6,2},{7,3},{8,12},{9,13},{10,... | collective-permute-start | bytes 1671176 | tf_op jit(solution)/shard_map/ppermute | solution.py:65
  81.0 14.9 %collective-permute-start.9 = (bf16[4,32,2048]{2,1,0:T(8,128)(2,1)S(1)}, bf16[4,32,2048]{2,1,0:T(8,128)(2,1)S(1)}, u32[]{:S(2)}, u32[]{:S(2)}) collective-permute-start(bf16[4,32,2048]{2,1,0:T(8,128)(2,1)S(1)} %get-tuple-element.335.refs_0_), channel_id=1, source_target_pairs={{0,2},{1,3},{2,0},{3,1},{4,6},{5,7},{6,4},{7,5},{8,10},{9,11},{10,... | collective-permute-start | bytes 1572872 | tf_op jit(solution)/shard_map/ppermute | solution.py:65
  82.5 27.4 %collective-permute-start.10 = (bf16[4,32,2048]{2,1,0:T(8,128)(2,1)S(1)}, bf16[4,32,2048]{2,1,0:T(8,128)(2,1)S(1)}, u32[]{:S(2)}, u32[]{:S(2)}) collective-permute-start(bf16[4,32,2048]{2,1,0:T(8,128)(2,1)S(1)} %collective-permute-done.4.refs_4_), channel_id=1, source_target_pairs={{0,2},{1,3},{2,0},{3,1},{4,6},{5,7},{6,4},{7,5},{8,10},{9,11},{10,... | collective-permute-start | bytes 1572872 | tf_op jit(solution)/shard_map/ppermute | solution.py:65
  83.0 11.2 %collective-permute-start.11 = (bf16[64,1024]{1,0:T(8,128)(2,1)S(1)}, bf16[64,1024]{1,0:T(8,128)(2,1)S(1)}, u32[]{:S(2)}, u32[]{:S(2)}) collective-permute-start(bf16[64,1024]{1,0:T(8,128)(2,1)S(1)} %collective-permute-done.6), channel_id=1, source_target_pairs={{0,8},{1,9},{2,10},{3,11},{4,12},{5,13},{6,14},{7,15},{8,0},{9,1},... | collective-permute-start | bytes 393224 | tf_op jit(solution)/shard_map/ppermute | solution.py:65
  112.1 26.3 %collective-permute-start.20 = (bf16[4,64,1024]{2,1,0:T(8,128)(2,1)S(1)}, bf16[4,64,1024]{2,1,0:T(8,128)(2,1)S(1)}, u32[]{:S(2)}, u32[]{:S(2)}) collective-permute-start(bf16[4,64,1024]{2,1,0:T(8,128)(2,1)S(1)} %bitcast.31), channel_id=1, source_target_pairs={{0,2},{1,3},{2,0},{3,1},{4,6},{5,7},{6,4},{7,5},{8,10},{9,11},{10,... | collective-permute-start | bytes 1572872 | tf_op jit(solution)/shard_map/ppermute | solution.py:65
  114.7 23.7 %collective-permute-start.16 = (bf16[4,32,2048]{2,1,0:T(8,128)(2,1)S(1)}, bf16[4,32,2048]{2,1,0:T(8,128)(2,1)S(1)}, u32[]{:S(2)}, u32[]{:S(2)}) collective-permute-start(bf16[4,32,2048]{2,1,0:T(8,128)(2,1)S(1)} %get-tuple-element.335.refs_0_), channel_id=1, source_target_pairs={{0,1},{1,0},{2,3},{3,2},{4,5},{5,4},{6,7},{7,6},{8,9},{9,8},{10,11... | collective-permute-start | bytes 1572872 | tf_op jit(solution)/shard_map/ppermute | solution.py:65
  114.8 23.6 %collective-permute-start.17 = (bf16[4,32,2048]{2,1,0:T(8,128)(2,1)S(1)}, bf16[4,32,2048]{2,1,0:T(8,128)(2,1)S(1)}, u32[]{:S(2)}, u32[]{:S(2)}) collective-permute-start(bf16[4,32,2048]{2,1,0:T(8,128)(2,1)S(1)} %collective-permute-done.9.refs_2_), channel_id=1, source_target_pairs={{0,1},{1,0},{2,3},{3,2},{4,5},{5,4},{6,7},{7,6},{8,9},{9,8},{10,11... | collective-permute-start | bytes 1572872 | tf_op jit(solution)/shard_map/ppermute | solution.py:65
  115.3 23.2 %collective-permute-start.18 = (bf16[4,32,2048]{2,1,0:T(8,128)(2,1)S(1)}, bf16[4,32,2048]{2,1,0:T(8,128)(2,1)S(1)}, u32[]{:S(2)}, u32[]{:S(2)}) collective-permute-start(bf16[4,32,2048]{2,1,0:T(8,128)(2,1)S(1)} %collective-permute-done.4.refs_4_), channel_id=1, source_target_pairs={{0,1},{1,0},{2,3},{3,2},{4,5},{5,4},{6,7},{7,6},{8,9},{9,8},{10,11... | collective-permute-start | bytes 1572872 | tf_op jit(solution)/shard_map/ppermute | solution.py:65
  115.4 23.1 %collective-permute-start.19 = (bf16[4,32,2048]{2,1,0:T(8,128)(2,1)S(1)}, bf16[4,32,2048]{2,1,0:T(8,128)(2,1)S(1)}, u32[]{:S(2)}, u32[]{:S(2)}) collective-permute-start(bf16[4,32,2048]{2,1,0:T(8,128)(2,1)S(1)} %collective-permute-done.10.refs_6_), channel_id=1, source_target_pairs={{0,1},{1,0},{2,3},{3,2},{4,5},{5,4},{6,7},{7,6},{8,9},{9,8},{10,11... | collective-permute-start | bytes 1572872 | tf_op jit(solution)/shard_map/ppermute | solution.py:65
  138.5 16.3 %collective-permute-start.21 = (bf16[4,64,1024]{2,1,0:T(8,128)(2,1)S(1)}, bf16[4,64,1024]{2,1,0:T(8,128)(2,1)S(1)}, u32[]{:S(2)}, u32[]{:S(2)}) collective-permute-start(bf16[4,64,1024]{2,1,0:T(8,128)(2,1)S(1)} %bitcast.32), channel_id=1, source_target_pairs={{0,4},{1,5},{2,6},{3,7},{4,0},{5,1},{6,2},{7,3},{8,12},{9,13},{10,... | collective-permute-start | bytes 1572872 | tf_op jit(solution)/shard_map/ppermute | solution.py:65
  138.6 24.7 %collective-permute-start.22 = (bf16[4,64,1024]{2,1,0:T(8,128)(2,1)S(1)}, bf16[4,64,1024]{2,1,0:T(8,128)(2,1)S(1)}, u32[]{:S(2)}, u32[]{:S(2)}) collective-permute-start(bf16[4,64,1024]{2,1,0:T(8,128)(2,1)S(1)} %collective-permute-done.20.refs_2_), channel_id=1, source_target_pairs={{0,4},{1,5},{2,6},{3,7},{4,0},{5,1},{6,2},{7,3},{8,12},{9,13},{10,... | collective-permute-start | bytes 1572872 | tf_op jit(solution)/shard_map/ppermute | solution.py:65
  163.7 5.1 %collective-permute-start.26 = (bf16[4,64,1024]{2,1,0:T(8,128)(2,1)S(1)}, bf16[4,64,1024]{2,1,0:T(8,128)(2,1)S(1)}, u32[]{:S(2)}, u32[]{:S(2)}) collective-permute-start(bf16[4,64,1024]{2,1,0:T(8,128)(2,1)S(1)} %collective-permute-done.22.refs_6_), channel_id=1, source_target_pairs={{0,1},{1,0},{2,3},{3,2},{4,5},{5,4},{6,7},{7,6},{8,9},{9,8},{10,11... | collective-permute-start | bytes 1572872 | tf_op jit(solution)/shard_map/ppermute | solution.py:65
  197.1 13.5 %collective-permute-start.27 = (bf16[1536,1024]{1,0:T(8,128)(2,1)}, bf16[1536,1024]{1,0:T(8,128)(2,1)S(1)}, u32[]{:S(2)}, u32[]{:S(2)}) collective-permute-start(bf16[1536,1024]{1,0:T(8,128)(2,1)} %bitcast.49), channel_id=1, source_target_pairs={{0,1},{1,0},{2,3},{3,2},{4,5},{5,4},{6,7},{7,6},{8,9},{9,8},{10,11... | collective-permute-start | bytes 9437192 | tf_op jit(solution)/shard_map/ppermute | solution.py:65
  197.3 10.2 %collective-permute-start.28 = (bf16[512,3072]{1,0:T(8,128)(2,1)}, bf16[512,3072]{1,0:T(8,128)(2,1)S(1)}, u32[]{:S(2)}, u32[]{:S(2)}) collective-permute-start(bf16[512,3072]{1,0:T(8,128)(2,1)} %get-tuple-element.380), channel_id=1, source_target_pairs={{0,1},{1,0},{2,3},{3,2},{4,5},{5,4},{6,7},{7,6},{8,9},{9,8},{10,11... | collective-permute-start | bytes 9437192 | tf_op jit(solution)/shard_map/ppermute | solution.py:65
  205.3 6.9 %collective-permute-start.29 = (bf16[512,3072]{1,0:T(8,128)(2,1)S(1)}, bf16[512,3072]{1,0:T(8,128)(2,1)S(1)}, u32[]{:S(2)}, u32[]{:S(2)}) collective-permute-start(bf16[512,3072]{1,0:T(8,128)(2,1)S(1)} %get-tuple-element.389), channel_id=1, source_target_pairs={{0,1},{1,0},{2,3},{3,2},{4,5},{5,4},{6,7},{7,6},{8,9},{9,8},{10,11... | collective-permute-start | bytes 9437192 | tf_op jit(solution)/shard_map/ppermute | solution.py:65
  209.1 39.9 %collective-permute-start.31 = (bf16[256,3072]{1,0:T(8,128)(2,1)}, bf16[256,3072]{1,0:T(8,128)(2,1)S(1)}, u32[]{:S(2)}, u32[]{:S(2)}) collective-permute-start(bf16[256,3072]{1,0:T(8,128)(2,1)} %get-tuple-element.406), channel_id=1, source_target_pairs={{0,2},{1,3},{2,0},{3,1},{4,6},{5,7},{6,4},{7,5},{8,10},{9,11},{10,... | collective-permute-start | bytes 4718600 | tf_op jit(solution)/shard_map/ppermute | solution.py:65
  212.1 36.8 %collective-permute-start.30 = (bf16[768,1024]{1,0:T(8,128)(2,1)}, bf16[768,1024]{1,0:T(8,128)(2,1)S(1)}, u32[]{:S(2)}, u32[]{:S(2)}) collective-permute-start(bf16[768,1024]{1,0:T(8,128)(2,1)} %get-tuple-element.392), channel_id=1, source_target_pairs={{0,4},{1,5},{2,6},{3,7},{4,0},{5,1},{6,2},{7,3},{8,12},{9,13},{10,... | collective-permute-start | bytes 4718600 | tf_op jit(solution)/shard_map/ppermute | solution.py:65
  213.8 36.4 %collective-permute-start.32 = (bf16[256,3072]{1,0:T(8,128)(2,1)}, bf16[256,3072]{1,0:T(8,128)(2,1)S(1)}, u32[]{:S(2)}, u32[]{:S(2)}) collective-permute-start(bf16[256,3072]{1,0:T(8,128)(2,1)} %get-tuple-element.416), channel_id=1, source_target_pairs={{0,8},{1,9},{2,10},{3,11},{4,12},{5,13},{6,14},{7,15},{8,0},{9,1},... | collective-permute-start | bytes 4718600 | tf_op jit(solution)/shard_map/ppermute | solution.py:65
  250.2 7.4 %collective-permute-start.35 = (bf16[1024,1024]{1,0:T(8,128)(2,1)}, bf16[1024,1024]{1,0:T(8,128)(2,1)S(1)}, u32[]{:S(2)}, u32[]{:S(2)}) collective-permute-start(bf16[1024,1024]{1,0:T(8,128)(2,1)} %get-tuple-element.449), channel_id=1, source_target_pairs={{0,1},{1,0},{2,3},{3,2},{4,5},{5,4},{6,7},{7,6},{8,9},{9,8},{10,11... | collective-permute-start | bytes 6291464 | tf_op jit(solution)/shard_map/ppermute | solution.py:65
  252.2 46.4 %collective-permute-start.33 = (bf16[128,6144]{1,0:T(8,128)(2,1)}, bf16[128,6144]{1,0:T(8,128)(2,1)S(1)}, u32[]{:S(2)}, u32[]{:S(2)}) collective-permute-start(bf16[128,6144]{1,0:T(8,128)(2,1)} %get-tuple-element.434), channel_id=1, source_target_pairs={{0,4},{1,5},{2,6},{3,7},{4,0},{5,1},{6,2},{7,3},{8,12},{9,13},{10,... | collective-permute-start | bytes 4718600 | tf_op jit(solution)/shard_map/ppermute | solution.py:65
  255.8 42.8 %collective-permute-start.37 = (bf16[256,2048]{1,0:T(8,128)(2,1)}, bf16[256,2048]{1,0:T(8,128)(2,1)S(1)}, u32[]{:S(2)}, u32[]{:S(2)}) collective-permute-start(bf16[256,2048]{1,0:T(8,128)(2,1)} %get-tuple-element.477), channel_id=1, source_target_pairs={{0,8},{1,9},{2,10},{3,11},{4,12},{5,13},{6,14},{7,15},{8,0},{9,1},... | collective-permute-start | bytes 3145736 | tf_op jit(solution)/shard_map/ppermute | solution.py:65
  258.9 39.7 %collective-permute-start.38 = (bf16[512,1024]{1,0:T(8,128)(2,1)}, bf16[512,1024]{1,0:T(8,128)(2,1)S(1)}, u32[]{:S(2)}, u32[]{:S(2)}) collective-permute-start(bf16[512,1024]{1,0:T(8,128)(2,1)} %get-tuple-element.482), channel_id=1, source_target_pairs={{0,2},{1,3},{2,0},{3,1},{4,6},{5,7},{6,4},{7,5},{8,10},{9,11},{10,... | collective-permute-start | bytes 3145736 | tf_op jit(solution)/shard_map/ppermute | solution.py:65
  261.3 37.3 %collective-permute-start.36 = (bf16[384,1024]{1,0:T(8,128)(2,1)}, bf16[384,1024]{1,0:T(8,128)(2,1)S(1)}, u32[]{:S(2)}, u32[]{:S(2)}) collective-permute-start(bf16[384,1024]{1,0:T(8,128)(2,1)} %get-tuple-element.453), channel_id=1, source_target_pairs={{0,16},{1,17},{2,18},{3,19},{4,20},{5,21},{6,22},{7,23},{8,24},{9,... | collective-permute-start | bytes 2359304 | tf_op jit(solution)/shard_map/ppermute | solution.py:65
  303.8 26.7 %collective-permute-start.41 = (bf16[256,2176]{1,0:T(8,128)(2,1)S(1)}, bf16[256,2176]{1,0:T(8,128)(2,1)S(1)}, u32[]{:S(2)}, u32[]{:S(2)}) collective-permute-start(bf16[256,2176]{1,0:T(8,128)(2,1)S(1)} %get-tuple-element.514), channel_id=1, source_target_pairs={{0,2},{1,3},{2,0},{3,1},{4,6},{5,7},{6,4},{7,5},{8,10},{9,11},{10,... | collective-permute-start | bytes 3342344 | tf_op jit(solution)/shard_map/ppermute | solution.py:65
  304.9 19.3 %collective-permute-start.39 = (bf16[64,3072]{1,0:T(8,128)(2,1)S(1)}, bf16[64,3072]{1,0:T(8,128)(2,1)S(1)}, u32[]{:S(2)}, u32[]{:S(2)}) collective-permute-start(bf16[64,3072]{1,0:T(8,128)(2,1)S(1)} %get-tuple-element.506), channel_id=1, source_target_pairs={{0,8},{1,9},{2,10},{3,11},{4,12},{5,13},{6,14},{7,15},{8,0},{9,1},... | collective-permute-start | bytes 1179656 | tf_op jit(solution)/shard_map/ppermute | solution.py:65
  305.6 19.1 %collective-permute-start.42 = (bf16[64,3072]{1,0:T(8,128)(2,1)S(1)}, bf16[64,3072]{1,0:T(8,128)(2,1)S(1)}, u32[]{:S(2)}, u32[]{:S(2)}) collective-permute-start(bf16[64,3072]{1,0:T(8,128)(2,1)S(1)} %get-tuple-element.518), channel_id=1, source_target_pairs={{0,16},{1,17},{2,18},{3,19},{4,20},{5,21},{6,22},{7,23},{8,24},{9,... | collective-permute-start | bytes 1179656 | tf_op jit(solution)/shard_map/ppermute | solution.py:65
  307.4 24.1 %collective-permute-start.43 = (bf16[128,2048]{1,0:T(8,128)(2,1)S(1)}, bf16[128,2048]{1,0:T(8,128)(2,1)S(1)}, u32[]{:S(2)}, u32[]{:S(2)}) collective-permute-start(bf16[128,2048]{1,0:T(8,128)(2,1)S(1)} %get-tuple-element.522), channel_id=1, source_target_pairs={{0,4},{1,5},{2,6},{3,7},{4,0},{5,1},{6,2},{7,3},{8,12},{9,13},{10,... | collective-permute-start | bytes 1572872 | tf_op jit(solution)/shard_map/ppermute | solution.py:65
  309.3 22.8 %collective-permute-start.44 = (bf16[256,1024]{1,0:T(8,128)(2,1)S(1)}, bf16[256,1024]{1,0:T(8,128)(2,1)S(1)}, u32[]{:S(2)}, u32[]{:S(2)}) collective-permute-start(bf16[256,1024]{1,0:T(8,128)(2,1)S(1)} %get-tuple-element.526), channel_id=1, source_target_pairs={{0,4},{1,5},{2,6},{3,7},{4,0},{5,1},{6,2},{7,3},{8,12},{9,13},{10,... | collective-permute-start | bytes 1572872 | tf_op jit(solution)/shard_map/ppermute | solution.py:65
  324.2 14.2 %collective-permute-start.54 = (bf16[192,1024]{1,0:T(8,128)(2,1)S(1)}, bf16[192,1024]{1,0:T(8,128)(2,1)S(1)}, u32[]{:S(2)}, u32[]{:S(2)}) collective-permute-start(bf16[192,1024]{1,0:T(8,128)(2,1)S(1)} %get-tuple-element.556), channel_id=1, source_target_pairs={{0,8},{1,9},{2,10},{3,11},{4,12},{5,13},{6,14},{7,15},{8,0},{9,1},... | collective-permute-start | bytes 1179656 | tf_op jit(solution)/shard_map/ppermute | solution.py:65
  324.7 15.9 %collective-permute-start.52 = (bf16[32,3072]{1,0:T(8,128)(2,1)S(1)}, bf16[32,3072]{1,0:T(8,128)(2,1)S(1)}, u32[]{:S(2)}, u32[]{:S(2)}) collective-permute-start(bf16[32,3072]{1,0:T(8,128)(2,1)S(1)} %get-tuple-element.552), channel_id=1, source_target_pairs={{0,16},{1,17},{2,18},{3,19},{4,20},{5,21},{6,22},{7,23},{8,24},{9,... | collective-permute-start | bytes 589832 | tf_op jit(solution)/shard_map/ppermute | solution.py:65
  330.4 25.0 %collective-permute-start.53 = (bf16[32,3072]{1,0:T(8,128)(2,1)S(1)}, bf16[32,3072]{1,0:T(8,128)(2,1)S(1)}, u32[]{:S(2)}, u32[]{:S(2)}) collective-permute-start(bf16[32,3072]{1,0:T(8,128)(2,1)S(1)} %get-tuple-element.554), channel_id=1, source_target_pairs={{0,2},{1,3},{2,0},{3,1},{4,6},{5,7},{6,4},{7,5},{8,10},{9,11},{10,... | collective-permute-start | bytes 589832 | tf_op jit(solution)/shard_map/ppermute | solution.py:65
  338.5 18.8 %collective-permute-start.55 = (bf16[96,1024]{1,0:T(8,128)(2,1)S(1)}, bf16[96,1024]{1,0:T(8,128)(2,1)S(1)}, u32[]{:S(2)}, u32[]{:S(2)}) collective-permute-start(bf16[96,1024]{1,0:T(8,128)(2,1)S(1)} %get-tuple-element.558), channel_id=1, source_target_pairs={{0,2},{1,3},{2,0},{3,1},{4,6},{5,7},{6,4},{7,5},{8,10},{9,11},{10,... | collective-permute-start | bytes 589832 | tf_op jit(solution)/shard_map/ppermute | solution.py:65
  339.4 16.8 %collective-permute-start.50 = (bf16[128,1024]{1,0:T(8,128)(2,1)S(1)}, bf16[128,1024]{1,0:T(8,128)(2,1)S(1)}, u32[]{:S(2)}, u32[]{:S(2)}) collective-permute-start(bf16[128,1024]{1,0:T(8,128)(2,1)S(1)} %get-tuple-element.547), channel_id=1, source_target_pairs={{0,8},{1,9},{2,10},{3,11},{4,12},{5,13},{6,14},{7,15},{8,0},{9,1},... | collective-permute-start | bytes 786440 | tf_op jit(solution)/shard_map/ppermute | solution.py:65
  339.4 18.7 %collective-permute-start.45 = (bf16[64,2048]{1,0:T(8,128)(2,1)S(1)}, bf16[64,2048]{1,0:T(8,128)(2,1)S(1)}, u32[]{:S(2)}, u32[]{:S(2)}) collective-permute-start(bf16[64,2048]{1,0:T(8,128)(2,1)S(1)} %get-tuple-element.531), channel_id=1, source_target_pairs={{0,2},{1,3},{2,0},{3,1},{4,6},{5,7},{6,4},{7,5},{8,10},{9,11},{10,... | collective-permute-start | bytes 786440 | tf_op jit(solution)/shard_map/ppermute | solution.py:65
  340.6 12.8 %collective-permute-start.47 = (bf16[128,2176]{1,0:T(8,128)(2,1)S(1)}, bf16[128,2176]{1,0:T(8,128)(2,1)S(1)}, u32[]{:S(2)}, u32[]{:S(2)}) collective-permute-start(bf16[128,2176]{1,0:T(8,128)(2,1)S(1)} %get-tuple-element.535), channel_id=1, source_target_pairs={{0,4},{1,5},{2,6},{3,7},{4,0},{5,1},{6,2},{7,3},{8,12},{9,13},{10,... | collective-permute-start | bytes 1671176 | tf_op jit(solution)/shard_map/ppermute | solution.py:65
  353.6 9.1 %collective-permute-start.48 = (bf16[64,2176]{1,0:T(8,128)(2,1)S(1)}, bf16[64,2176]{1,0:T(8,128)(2,1)S(1)}, u32[]{:S(2)}, u32[]{:S(2)}) collective-permute-start(bf16[64,2176]{1,0:T(8,128)(2,1)S(1)} %get-tuple-element.537), channel_id=1, source_target_pairs={{0,8},{1,9},{2,10},{3,11},{4,12},{5,13},{6,14},{7,15},{8,0},{9,1},... | collective-permute-start | bytes 835592 | tf_op jit(solution)/shard_map/ppermute | solution.py:65
  356.3 12.9 %collective-permute-start.51 = (bf16[64,1024]{1,0:T(8,128)(2,1)S(1)}, bf16[64,1024]{1,0:T(8,128)(2,1)S(1)}, u32[]{:S(2)}, u32[]{:S(2)}) collective-permute-start(bf16[64,1024]{1,0:T(8,128)(2,1)S(1)} %get-tuple-element.549), channel_id=1, source_target_pairs={{0,16},{1,17},{2,18},{3,19},{4,20},{5,21},{6,22},{7,23},{8,24},{9,... | collective-permute-start | bytes 393224 | tf_op jit(solution)/shard_map/ppermute | solution.py:65
  358.8 14.0 %collective-permute-start.46 = (bf16[32,2048]{1,0:T(8,128)(2,1)S(1)}, bf16[32,2048]{1,0:T(8,128)(2,1)S(1)}, u32[]{:S(2)}, u32[]{:S(2)}) collective-permute-start(bf16[32,2048]{1,0:T(8,128)(2,1)S(1)} %get-tuple-element.533), channel_id=1, source_target_pairs={{0,16},{1,17},{2,18},{3,19},{4,20},{5,21},{6,22},{7,23},{8,24},{9,... | collective-permute-start | bytes 393224 | tf_op jit(solution)/shard_map/ppermute | solution.py:65
  363.5 10.8 %collective-permute-start.49 = (bf16[32,2176]{1,0:T(8,128)(2,1)S(1)}, bf16[32,2176]{1,0:T(8,128)(2,1)S(1)}, u32[]{:S(2)}, u32[]{:S(2)}) collective-permute-start(bf16[32,2176]{1,0:T(8,128)(2,1)S(1)} %get-tuple-element.539), channel_id=1, source_target_pairs={{0,16},{1,17},{2,18},{3,19},{4,20},{5,21},{6,22},{7,23},{8,24},{9,... | collective-permute-start | bytes 417800 | tf_op jit(solution)/shard_map/ppermute | solution.py:65
  (69 other events, 1009.5 us)
Sparse Core Ops, SparseCore 0:
  10.9 161.1 all-gather.2
